TPU v7x, 512 devices: a whole 4x4x16 slice. The times are simulated.
512 devices in a mesh: heads: 8 (over y, core), groups: 64 (over z, x).
Axes of the slice: x: 4, y: 4, z: 16, core: 2. Of those that a mesh axis runs over, the one named last changes fastest.
Arguments:
- hidden_rows: bfloat16 [192, 8192], P(None, 'groups'), may hold values from -6 to 6
- qkv_weight: bfloat16 [8192, 10240], P('groups', 'heads'), may hold values from -1 to 1
- out_weight: bfloat16 [8192, 8192], P('heads', 'groups'), may hold values from -0.0625 to 0.0625
- norm_gain: float32 [8192], P('groups'), may hold values from 0.5 to 1.5
- next_weight: bfloat16 [8192, 10240], P('groups', 'heads'), may hold values from -0.0625 to 0.0625
- cache_keys: bfloat16 [49152, 1024], P('groups', 'heads'), may hold values from -6 to 6
- cache_values: bfloat16 [49152, 1024], P('groups', 'heads'), may hold values from -6 to 6
- group_lengths: int32 [128], replicated, may hold values from 128 to 384, as said below
- group_owner: int32 [128], replicated, may hold values from 0 to 63, as said below
- group_start: int32 [128], replicated, may hold values from 0 to 32640, as said below
- listed_rows: int32 [192], replicated, may hold values from 0 to 32767, as said below
Outputs:
- hidden_out: bfloat16 [192, 8192], P(None, 'groups')
- next_qkv: bfloat16 [192, 10240], P('groups', 'heads')
Inputs may be any that keep to these rules, and one draw needn't show every extreme that they name: `group_lengths`: multiples of 128; groups 2k and 2k+1 together hold 512 tokens. `group_owner`: group 2k is held by owner k; every owner holds exactly two groups; one owner holds 768 tokens. The intervals from group_start to group_start + group_lengths - 1 of all groups tile 0 to 32767. `listed_rows`: distinct and increasing.
All inputs are finite; a program needn't handle non-finite values.
Results may differ from a plain program's by a relative error of at most 0.0085.
Values may be sent and summed in bfloat16 or wider, within the bound.
No kernel may reach another device: no remote copies, remote signals or barrier semaphores. Data moves between devices by JAX's collectives and lax.ppermute only.
A program may use at most 64 MiB of HBM per device.

v0:
```python
import functools
import math

import jax
import jax.numpy as jnp
from jax import lax
from jax.sharding import Mesh
from jax.sharding import PartitionSpec as P

D = 8192
HD = 128
GQ = 8
BLK = 128
GROUPS = ("groups_0", "groups_1")


theta_base = 500000.0
epsilon = 1e-05
masked_score = -1e30


def split_up(array, dim, peers):
    before, after = (array.shape[:dim], array.shape[dim + 1 :])
    return jnp.moveaxis(array.reshape(*before, peers, -1, *after), dim, 0)


def sent_and_summed(array, axis, dim):
    pieces = split_up(array, dim, lax.axis_size(axis))
    arrived = lax.all_to_all(pieces, axis, split_axis=0, concat_axis=0, tiled=True)
    return arrived.astype(jnp.float32).sum(axis=0)


def sum_by_axis(array, axes, dim):
    far, near = axes
    pieces = split_up(array, dim, lax.axis_size(far))
    nearer = sent_and_summed(pieces, near, dim + 1)
    arrived = lax.all_to_all(
        nearer.astype(jnp.bfloat16), far, split_axis=0, concat_axis=0, tiled=True
    )
    return arrived.astype(jnp.float32).sum(axis=0)


def sent_to_all(array, axis):
    copies = jnp.broadcast_to(array, (lax.axis_size(axis), *array.shape))
    return lax.all_to_all(copies, axis, split_axis=0, concat_axis=0, tiled=True)


def in_order(pieces, dim):
    lengths = list(pieces.shape[1:])
    lengths[dim] *= pieces.shape[0]
    return jnp.moveaxis(pieces, 0, dim).reshape(lengths)


def gathered_copies(array, axis, dim):
    pieces = sent_to_all(array, axis)
    return in_order(pieces, dim)


def over_axes(array, axes):
    for axis in axes:
        array = lax.pmax(array, axis)
    return array


def sent_and_summed_2(array, axis, dim):
    peers = lax.axis_size(axis)
    pieces = lax.all_to_all(split_up(array, dim, peers), axis, 0, 0, tiled=True)
    return jnp.sum(pieces, axis=0)


def sum_in_two_steps(array, axes, dim):
    far, near = axes
    own = sent_and_summed_2(split_up(array, dim, lax.axis_size(far)), near, dim + 1)
    return jnp.sum(lax.all_to_all(own, far, 0, 0, tiled=True), axis=0)


def in_one_piece(arrays, axis, dim, along):
    widths = [math.prod(a.shape[along:]) for a in arrays]
    both = jnp.concatenate(
        [a.reshape(*a.shape[:along], w) for a, w in zip(arrays, widths)], axis=along
    )
    result = sum_in_two_steps(both, axis, dim)
    pieces = jnp.split(result, [sum(widths[:k]) for k in range(1, len(widths))], axis=along)
    return tuple(
        (b.reshape(*result.shape[:along], *a.shape[along:]) for a, b in zip(arrays, pieces))
    )


def over_copies(array, axis):
    everything = sent_to_all(array, axis)
    return jnp.sum(everything.astype(jnp.float32), axis=0)


def by_axis(array, axes):
    return functools.reduce(lax.psum, axes, array)


def angles(positions, half_dim):
    freq = theta_base ** (-(jnp.arange(half_dim).astype(jnp.float32) * 2.0 / (2 * half_dim)))
    phase = positions.astype(jnp.float32)[:, None] * freq[None, :]
    return (jnp.cos(phase), jnp.sin(phase))


def rotate(vectors, cosine, sine):
    half_dim = vectors.shape[-1] // 2
    lower = vectors[..., :half_dim]
    upper = vectors[..., half_dim:]
    return jnp.concatenate([lower * cosine - upper * sine, upper * cosine + lower * sine], axis=-1)


def layout(
    owner_index, group_lengths, group_owner, group_start, listed_rows, cap_blocks, block_rows
):
    block_len = group_lengths // block_rows
    holder = (group_owner == owner_index).astype(jnp.int32)
    held_blocks = holder * block_len
    offset = jnp.cumsum(held_blocks) - held_blocks
    block_ids = jnp.arange(cap_blocks)[:, None]
    member = (
        (holder[None, :] == 1)
        & (block_ids >= offset[None, :])
        & (block_ids < offset[None, :] + block_len[None, :])
    ).astype(jnp.int32)
    shift_blk = jnp.sum(member * group_start[None, :], axis=1)
    begin_blk = jnp.sum(
        member * (group_start[None, :] + (block_ids - offset[None, :]) * block_rows), axis=1
    )
    live_blk = jnp.sum(member, axis=1) > 0
    inside = jnp.arange(block_rows)[None, :]
    key_pos = (begin_blk[:, None] + inside).reshape(-1)
    key_shift = (shift_blk[:, None] + 0 * inside).reshape(-1)
    key_live = (live_blk[:, None] & (inside >= 0)).reshape(-1)
    listed_hit = jnp.any(key_pos[:, None] == listed_rows[None, :], axis=1)
    return (key_pos, key_shift, key_live & jnp.logical_not(listed_hit))


def on_device(
    hidden_rows,
    qkv_weight,
    out_weight,
    norm_gain,
    next_weight,
    cache_keys,
    cache_values,
    group_lengths,
    group_owner,
    group_start,
    listed_rows,
):
    group_count = lax.axis_size(GROUPS)
    own_index = lax.axis_index(GROUPS)
    row_count = hidden_rows.shape[0]
    local_rows = row_count // group_count
    kv_local = out_weight.shape[0] // (GQ * HD)
    capacity = cache_keys.shape[0]
    first_row = own_index * local_rows
    own_pos = lax.dynamic_slice_in_dim(listed_rows, first_row, local_rows)
    own_cos, own_sin = angles(own_pos, HD // 2)
    mixed = sum_by_axis(
        jnp.dot(hidden_rows, qkv_weight, preferred_element_type=jnp.float32).astype(jnp.bfloat16),
        ("groups_0", "groups_1"),
        0,
    ).reshape(local_rows, kv_local, GQ + 2, HD)
    own_queries = rotate(mixed[:, :, :GQ], own_cos[:, None, None], own_sin[:, None, None]).astype(
        jnp.bfloat16
    )
    queries = gathered_copies(own_queries, GROUPS, 0)
    own_keys = rotate(mixed[:, :, GQ], own_cos[:, None], own_sin[:, None]).astype(jnp.bfloat16)
    own_values = mixed[:, :, GQ + 1].astype(jnp.bfloat16)
    key_pos, key_shift, key_live = layout(
        own_index, group_lengths, group_owner, group_start, listed_rows, capacity // BLK, BLK
    )
    store_cos, store_sin = angles(key_shift, HD // 2)
    rotated = rotate(
        cache_keys.astype(jnp.float32).reshape(capacity, kv_local, HD),
        store_cos[:, None],
        store_sin[:, None],
    ).astype(jnp.bfloat16)
    store_values = cache_values.reshape(capacity, kv_local, HD)
    all_pos = jnp.concatenate([key_pos, own_pos], axis=0)
    all_live = jnp.concatenate([key_live, jnp.ones((local_rows,), bool)], axis=0)
    allowed = all_live[None, :] & (all_pos[None, :] <= listed_rows[:, None])
    scale = HD ** (-0.5)
    peak_list = []
    total_list = []
    numer_list = []
    key_block = jnp.concatenate([rotated[:, 0], own_keys[:, 0]], axis=0)
    value_block = jnp.concatenate([store_values[:, 0], own_values[:, 0]], axis=0)
    for pair_index in range(GQ // 2):
        query_block = queries[:, 0, 2 * pair_index : 2 * pair_index + 2]
        scores = (
            jnp.einsum("rgd,kd->rgk", query_block, key_block, preferred_element_type=jnp.float32)
            * scale
        )
        scores = jnp.where(allowed[:, None, :], scores, masked_score)
        peaks = jnp.max(scores, axis=-1)
        weights = jnp.where(allowed[:, None, :], jnp.exp(scores - peaks[..., None]), 0.0)
        totals = jnp.sum(weights, axis=-1)
        numerator = jnp.einsum(
            "rgk,kd->rgd",
            weights.astype(jnp.bfloat16),
            value_block,
            preferred_element_type=jnp.float32,
        )
        peak_list.append(peaks)
        total_list.append(totals)
        numer_list.append(numerator)
    peaks = jnp.concatenate(peak_list, axis=1)
    totals = jnp.concatenate(total_list, axis=1)
    numerator = jnp.concatenate(numer_list, axis=1)
    highest = over_axes(peaks, GROUPS)
    factor = jnp.exp(peaks - highest)
    numer_share, total_share = in_one_piece(
        (numerator * factor[..., None], totals * factor), ("groups_0", "groups_1"), 0, 2
    )
    heads_share = (
        (numer_share / total_share[..., None])
        .astype(jnp.bfloat16)
        .reshape(local_rows, kv_local * GQ * HD)
    )
    head_term = jnp.dot(
        gathered_copies(heads_share, GROUPS, 0), out_weight, preferred_element_type=jnp.float32
    )
    attended = over_copies(head_term.astype(jnp.bfloat16), "heads").astype(jnp.float32)
    resid = hidden_rows.astype(jnp.float32) + attended
    squares = by_axis(jnp.sum(resid * resid, axis=1), GROUPS)
    normed = (resid * lax.rsqrt(squares / D + epsilon)[:, None] * norm_gain[None, :]).astype(
        jnp.bfloat16
    )
    next_qkv = sum_by_axis(
        jnp.dot(normed, next_weight, preferred_element_type=jnp.float32).astype(jnp.bfloat16),
        ("groups_0", "groups_1"),
        0,
    ).astype(jnp.bfloat16)
    return (resid.astype(jnp.bfloat16), next_qkv)


def solution(mesh):
    split = Mesh(
        mesh.devices.reshape(mesh.shape["heads"], 16, 4), ("heads", "groups_0", "groups_1")
    )
    return jax.shard_map(
        on_device,
        mesh=split,
        in_specs=(
            P(None, GROUPS),
            P(GROUPS, "heads"),
            P("heads", GROUPS),
            P(GROUPS),
            P(GROUPS, "heads"),
            P(GROUPS, "heads"),
            P(GROUPS, "heads"),
            P(),
            P(),
            P(),
            P(),
        ),
        out_specs=(P(None, GROUPS), P(GROUPS, "heads")),
        check_vma=False,
    )
```

profile of v0, /device:TPU:6, one launch (start us, length us, event | category | flops | bytes accessed | tf_op | source)
XLA Modules:
  0.0 279.6 jit_solution(2588547614130906398)
XLA Ops:
  0.6 1.0 copy-done
  1.6 1.1 convolution_convert_fusion.1
  2.7 0.2 reshape_reshape.7
  3.0 1.0 copy.96
  3.9 9.3 %all-to-all-start = ((bf16[4,16,3,1280]{3,1,2,0:T(8,128)(2,1)}), bf16[4,16,3,1280]{3,1,2,0:T(8,128)(2,1)S(1)}, u32[]{:S(2)}, u32[]{:S(2)}) async-start(bf16[4,16,3,1280]{3,1,2,0:T(8,128)(2,1)} %copy.96), calls=%async_computation | async-start | bytes 983040 | tf_op jit(solution)/shard_map/all_to_all | solution.py:29
  13.3 0.1 copy.95
  13.4 0.2 reduce-window.9
  13.5 0.1 reduce.3
  13.7 0.2 select_reduce_fusion.1
  14.0 0.2 compare_reduce_fusion
  14.2 4.8 %all-to-all-done = bf16[4,16,3,1280]{3,1,2,0:T(8,128)(2,1)S(1)} async-done(((bf16[4,16,3,1280]{3,1,2,0:T(8,128)(2,1)}), bf16[4,16,3,1280]{3,1,2,0:T(8,128)(2,1)S(1)}, u32[]{:S(2)}, u32[]{:S(2)}) %all-to-all-start) | async-done | bytes 491552 | tf_op jit(solution)/shard_map/all_to_all | solution.py:29
  19.1 0.7 copy.97
  19.9 11.9 %all-to-all-start.1 = ((bf16[16,3,1280]{2,1,0:T(4,128)(2,1)}), bf16[16,3,1280]{2,1,0:T(4,128)(2,1)S(1)}, u32[]{:S(2)}, u32[]{:S(2)}) async-start(bf16[16,3,1280]{2,1,0:T(4,128)(2,1)} %copy.97), calls=%async_computation.1 | async-start | bytes 327680 | tf_op jit(solution)/shard_map/all_to_all | solution.py:37
  31.9 0.1 multiply_cosine_fusion.2
  32.0 14.4 %all-to-all-done.1 = bf16[16,3,1280]{2,1,0:T(4,128)(2,1)S(1)} async-done(((bf16[16,3,1280]{2,1,0:T(4,128)(2,1)}), bf16[16,3,1280]{2,1,0:T(4,128)(2,1)S(1)}, u32[]{:S(2)}, u32[]{:S(2)}) %all-to-all-start.1) | async-done | bytes 122912 | tf_op jit(solution)/shard_map/all_to_all | solution.py:37
  46.7 0.8 broadcast_in_dim.49
  47.5 6.9 %all-to-all-start.2 = ((bf16[64,3,1,8,128]{4,3,1,2,0:T(8,128)(2,1)}), bf16[64,3,1,8,128]{4,3,1,2,0:T(8,128)(2,1)S(1)}, u32[]{:S(2)}, u32[]{:S(2)}) async-start(bf16[64,3,1,8,128]{4,3,1,2,0:T(8,128)(2,1)} %broadcast_in_dim.49), calls=%async_computation.2 | async-start | bytes 786432 | tf_op jit(solution)/shard_map/all_to_all | solution.py:45
  54.4 0.2 compare_and_fusion
  54.7 1.8 fusion.41
  56.5 0.1 fusion.61
  56.6 0.1 maximum_bitcast_fusion.1
  56.8 23.1 %all-to-all-done.2 = bf16[64,3,1,8,128]{4,3,1,2,0:T(8,128)(2,1)S(1)} async-done(((bf16[64,3,1,8,128]{4,3,1,2,0:T(8,128)(2,1)}), bf16[64,3,1,8,128]{4,3,1,2,0:T(8,128)(2,1)S(1)}, u32[]{:S(2)}, u32[]{:S(2)}) %all-to-all-start.2) | async-done | bytes 393248 | tf_op jit(solution)/shard_map/all_to_all | solution.py:45
  79.8 0.3 fusion.72
  80.1 0.5 fusion.76
  80.6 0.5 fusion.75
  81.2 0.5 fusion.74
  81.7 0.5 fusion.73
  82.2 0.4 copy-done.10
  82.6 0.5 fusion.12
  83.2 0.5 fusion.14
  83.7 0.5 fusion.16
  84.2 1.8 fusion.4
  86.0 0.5 fusion.18
  86.5 0.2 copy.106
  86.7 0.2 copy.104
  86.9 0.2 copy.102
  87.0 0.2 copy.100
  87.2 28.1 %pmax.14 = f32[192,8]{0,1:T(8,128)S(1)} all-reduce(f32[192,8]{0,1:T(8,128)S(1)} %pad_maximum_fusion.1), channel_id=1, replica_groups=mesh['heads'=8,'groups_0'=16,'groups_1'=4] {'groups_0'}, use_global_device_ids=true, to_apply=%region_11.12 | all-reduce | flops 1536 | bytes 12288 | tf_op jit(solution)/shard_map/pmax | solution.py:61
  115.3 7.9 %pmax.15 = f32[192,8]{0,1:T(8,128)S(1)} all-reduce(f32[192,8]{0,1:T(8,128)S(1)} %pmax.14), channel_id=1, replica_groups=mesh['heads'=8,'groups_0'=16,'groups_1'=4] {'groups_1'}, use_global_device_ids=true, to_apply=%region_12.13 | all-reduce | flops 1536 | bytes 12288 | tf_op jit(solution)/shard_map/pmax | solution.py:61
  123.2 0.1 copy.107
  123.4 0.3 reshape.410
  123.7 3.2 %copy.109 = f32[16,4,3,8,1]{4,3,2,1,0:T(8,128)S(1)} copy(f32[16,4,3,8,1]{2,1,0,3,4:T(4,128)S(1)} %reshape.410) | data formatting | bytes 12288 | tf_op jit(solution)/shard_map/concatenate | solution.py:79
  126.9 0.4 maximum_multiply_fusion
  127.3 0.1 maximum_bitcast_fusion
  127.4 0.1 copy.110
  127.6 17.6 %all_to_all.45 = f32[4,16,3,8,129]{4,3,2,1,0:T(8,128)S(1)} all-to-all(f32[4,16,3,8,129]{4,3,2,1,0:T(8,128)S(1)} %copy.110), channel_id=1, replica_groups=mesh['heads'=8,'groups_0'=16,'groups_1'=4] {'groups_1'}, dimensions={0} | all-to-all | bytes 1585152 | tf_op jit(solution)/shard_map/all_to_all | solution.py:67
  145.2 0.1 reduce_sum.153
  145.4 19.7 %all_to_all.46 = f32[16,3,8,129]{3,2,1,0:T(8,128)S(1)} all-to-all(f32[16,3,8,129]{3,2,1,0:T(8,128)S(1)} %reduce_sum.153), channel_id=1, replica_groups=mesh['heads'=8,'groups_0'=16,'groups_1'=4] {'groups_0'}, dimensions={0} | all-to-all | bytes 396288 | tf_op jit(solution)/shard_map/all_to_all | solution.py:74
  165.1 0.1 slice_reduce_fusion
  165.3 0.1 broadcast_in_dim.96
  165.4 33.2 %all_to_all.47 = bf16[64,3,1024]{2,1,0:T(4,128)(2,1)S(1)} all-to-all(bf16[64,3,1024]{2,1,0:T(4,128)(2,1)S(1)} %broadcast_in_dim.96), channel_id=1, replica_groups=mesh['heads'=8,'groups_0'=16,'groups_1'=4] {'groups_0','groups_1'}, dimensions={0} | all-to-all | bytes 786432 | tf_op jit(solution)/shard_map/all_to_all | solution.py:45
  198.6 0.3 reshape.405
  199.0 0.3 convolution_convert_fusion.2
  199.3 13.2 %all_to_all.48 = bf16[8,192,128]{2,1,0:T(8,128)(2,1)S(1)} all-to-all(bf16[8,192,128]{2,1,0:T(8,128)(2,1)S(1)} %broadcast_in_dim.97), channel_id=1, replica_groups=mesh['heads'=8,'groups_0'=16,'groups_1'=4] {'heads'}, dimensions={0} | all-to-all | bytes 786432 | tf_op jit(solution)/shard_map/all_to_all | solution.py:45
  212.6 0.6 multiply_reduce_fusion
  213.2 27.2 %psum.14 = f32[192]{0:T(256)S(1)} all-reduce(f32[192]{0:T(256)S(1)} %get-tuple-element.23), channel_id=1, replica_groups=mesh['heads'=8,'groups_0'=16,'groups_1'=4] {'groups_0'}, use_global_device_ids=true, to_apply=%region_21.22 | all-reduce | flops 192 | bytes 1536 | tf_op jit(solution)/shard_map/psum | solution.py:95
  240.4 7.7 %psum.15 = f32[192]{0:T(256)S(1)} all-reduce(f32[192]{0:T(256)S(1)} %psum.14), channel_id=1, replica_groups=mesh['heads'=8,'groups_0'=16,'groups_1'=4] {'groups_1'}, use_global_device_ids=true, to_apply=%region_22.23 | all-reduce | flops 192 | bytes 1536 | tf_op jit(solution)/shard_map/psum | solution.py:95
  248.1 0.3 convolution_convert_fusion
  248.5 0.2 reshape_reshape.8
  248.7 0.2 copy.111
  248.9 11.5 %all_to_all.49 = bf16[4,16,3,1280]{3,1,2,0:T(8,128)(2,1)S(1)} all-to-all(bf16[4,16,3,1280]{3,1,2,0:T(8,128)(2,1)S(1)} %copy.111), channel_id=1, replica_groups=mesh['heads'=8,'groups_0'=16,'groups_1'=4] {'groups_1'}, dimensions={0} | all-to-all | bytes 983040 | tf_op jit(solution)/shard_map/all_to_all | solution.py:29
  260.5 0.1 copy.112
  260.6 18.3 %all_to_all.50 = bf16[16,3,1280]{2,1,0:T(4,128)(2,1)S(1)} all-to-all(bf16[16,3,1280]{2,1,0:T(4,128)(2,1)S(1)} %copy.112), channel_id=1, replica_groups=mesh['heads'=8,'groups_0'=16,'groups_1'=4] {'groups_0'}, dimensions={0} | all-to-all | bytes 245760 | tf_op jit(solution)/shard_map/all_to_all | solution.py:37
  278.9 0.7 reduce_sum.158
  (50 shorter events, 1.2 us)
Async XLA Ops:
  0.6 1.0 copy-start
  2.7 10.5 %copy-start.6 = (s32[128]{0:T(128)S(1)}, s32[128]{0:T(128)}, u32[]{:S(2)}) copy-start(s32[128]{0:T(128)} %param.19) | copy-start | bytes 1540
  2.7 10.5 %copy-start.8 = (s32[128]{0:T(128)S(1)}, s32[128]{0:T(128)}, u32[]{:S(2)}) copy-start(s32[128]{0:T(128)} %param.18) | copy-start | bytes 1540
  2.9 10.7 %copy-start.9 = (s32[128]{0:T(128)S(1)}, s32[128]{0:T(128)}, u32[]{:S(2)}) copy-start(s32[128]{0:T(128)} %param.20) | copy-start | bytes 1540
  2.9 11.0 %copy-start.5 = (s32[192]{0:T(256)S(1)}, s32[192]{0:T(256)}, u32[]{:S(2)}) copy-start(s32[192]{0:T(256)} %param.21) | copy-start | bytes 2308
  3.9 15.1 %all-to-all-start = ((bf16[4,16,3,1280]{3,1,2,0:T(8,128)(2,1)}), bf16[4,16,3,1280]{3,1,2,0:T(8,128)(2,1)S(1)}, u32[]{:S(2)}, u32[]{:S(2)}) async-start(bf16[4,16,3,1280]{3,1,2,0:T(8,128)(2,1)} %copy.96), calls=%async_computation | async-start | bytes 983040 | tf_op jit(solution)/shard_map/all_to_all | solution.py:29
  14.2 40.4 %copy-start.4 = (bf16[768,128]{1,0:T(8,128)(2,1)S(1)}, bf16[768,128]{1,0:T(8,128)(2,1)}, u32[]{:S(2)}) copy-start(bf16[768,128]{1,0:T(8,128)(2,1)} %param.16) | copy-start | bytes 589828
  19.9 26.6 %all-to-all-start.1 = ((bf16[16,3,1280]{2,1,0:T(4,128)(2,1)}), bf16[16,3,1280]{2,1,0:T(4,128)(2,1)S(1)}, u32[]{:S(2)}, u32[]{:S(2)}) async-start(bf16[16,3,1280]{2,1,0:T(4,128)(2,1)} %copy.97), calls=%async_computation.1 | async-start | bytes 327680 | tf_op jit(solution)/shard_map/all_to_all | solution.py:37
  47.5 32.4 %all-to-all-start.2 = ((bf16[64,3,1,8,128]{4,3,1,2,0:T(8,128)(2,1)}), bf16[64,3,1,8,128]{4,3,1,2,0:T(8,128)(2,1)S(1)}, u32[]{:S(2)}, u32[]{:S(2)}) async-start(bf16[64,3,1,8,128]{4,3,1,2,0:T(8,128)(2,1)} %broadcast_in_dim.49), calls=%async_computation.2 | async-start | bytes 786432 | tf_op jit(solution)/shard_map/all_to_all | solution.py:45
  81.7 0.9 copy-start.10
  165.1 33.8 %copy-start.3 = (bf16[1024,128]{1,0:T(8,128)(2,1)S(1)}, bf16[1024,128]{1,0:T(8,128)(2,1)}, u32[]{:S(2)}) copy-start(bf16[1024,128]{1,0:T(8,128)(2,1)} %param.13) | copy-start | bytes 786436
  199.0 13.6 %copy-start.1 = (bf16[192,128]{1,0:T(8,128)(2,1)S(1)}, bf16[192,128]{1,0:T(8,128)(2,1)}, u32[]{:S(2)}) copy-start(bf16[192,128]{1,0:T(8,128)(2,1)} %param.11) | copy-start | bytes 147460
  199.0 49.1 %copy-start.2 = (bf16[128,1280]{1,0:T(8,128)(2,1)S(1)}, bf16[128,1280]{1,0:T(8,128)(2,1)}, u32[]{:S(2)}) copy-start(bf16[128,1280]{1,0:T(8,128)(2,1)} %param.15) | copy-start | bytes 983044
  199.0 49.1 %copy-start.7 = (f32[128]{0:T(128)S(1)}, f32[128]{0:T(128)}, u32[]{:S(2)}) copy-start(f32[128]{0:T(128)} %param.14) | copy-start | bytes 1540
where the time goes:
time: 281 us; the launch traced here: 280 us
  blocking collectives  184 us (65%)
  waiting for transfers between devices  42.4 us (15%)
  starting transfers between devices  28.1 us (10%)
  local copies, waits for them, and re-layouts  10.1 us (4%)
  other arithmetic  7.57 us (3%)
  matrix products  5.86 us (2%)
    all_to_all x2, blocking collectives, sent_to_all(): return lax.all_to_all(copies, axis, split_axis=0, concat_axis=0, tiled=True)  46.4 us
    pmax x2, blocking collectives, over_axes(): array = lax.pmax(array, axis)  36 us
    psum x2, blocking collectives, by_axis(): return functools.reduce(lax.psum, axes, array)  34.9 us
    all_to_all x1, waiting for transfers between devices, sent_to_all(): return lax.all_to_all(copies, axis, split_axis=0, concat_axis=0, tiled=True)  23.1 us
    all_to_all x1, blocking collectives, sum_in_two_steps(): return jnp.sum(lax.all_to_all(own, far, 0, 0, tiled=True), axis=0)  19.7 us
    all_to_all x1, blocking collectives, sum_by_axis(): lax.all_to_all(nearer.astype(jnp.bfloat16), far, split_axis=0, concat_axi...  18.3 us
    all_to_all x1, blocking collectives, sent_and_summed_2(): pieces = lax.all_to_all(split_up(array, dim, peers), axis, 0, 0, tiled=True)  17.6 us
    all_to_all x1, waiting for transfers between devices, sum_by_axis(): lax.all_to_all(nearer.astype(jnp.bfloat16), far, split_axis=0, concat_axi...  14.4 us
  transfers between devices with their start and end apart: 3, of which 3 were waited for; matrix products, arithmetic and copies ran while one was open for 1% of the time, Pallas kernels for 0%

commit v1 on v0

v1 whole, which is shorter than its diff:
```python
import functools

import jax
import jax.numpy as jnp
from jax import lax
from jax.experimental import pallas as pl
from jax.experimental.pallas import tpu as pltpu
from jax.sharding import Mesh
from jax.sharding import PartitionSpec as P

D = 8192
HD = 128
GQ = 8
BLK = 128
NZ = 16
NX = 4
NH = 8
RI = 3
XR = NZ * RI
TILE = 16
GROUPS = ("z", "x")
theta_base = 500000.0
epsilon = 1e-05
masked_score = -1e30
least_peak = -1e28
never = 2**30
LOG2E = 1.4426950408889634

bf16 = jnp.bfloat16
f32 = jnp.float32


def vmem_call(kernel, out_shape, operands, scratch=(), limit=32):
    space = pl.BlockSpec(memory_space=pltpu.VMEM)
    outs = jax.tree.map(lambda _: space, out_shape)
    return pl.pallas_call(
        kernel,
        out_shape=out_shape,
        in_specs=[space] * len(operands),
        out_specs=outs,
        scratch_shapes=list(scratch),
        compiler_params=pltpu.CompilerParams(vmem_limit_bytes=limit * 2**20),
    )(*operands)


def shaped(shape, dtype):
    return jax.ShapeDtypeStruct(shape, dtype)


def three_pieces(value):
    high = value.astype(bf16).astype(f32)
    rest = value - high
    middle = rest.astype(bf16).astype(f32)
    low = (rest - middle).astype(bf16).astype(f32)
    return high, middle, low


def angles(positions, half_dim):
    freq = theta_base ** (-(jnp.arange(half_dim).astype(f32) * 2.0 / (2 * half_dim)))
    phase = positions.astype(f32)[:, None] * freq[None, :]
    return (jnp.cos(phase), jnp.sin(phase))


def rope_factors(positions):
    cosine, sine = angles(positions, HD // 2)
    return jnp.concatenate([cosine, cosine], -1), jnp.concatenate([-sine, sine], -1)


def rotate_kernel(keys_ref, cos_ref, sin_ref, out_ref):
    for b in range(keys_ref.shape[0] // BLK):
        block = keys_ref[b * BLK : (b + 1) * BLK, :].astype(f32)
        turned = (
            block * cos_ref[b : b + 1, :]
            + pltpu.roll(block, HD // 2, 1) * sin_ref[b : b + 1, :]
        )
        turned = turned.astype(bf16).astype(f32)
        out_ref[:, b * BLK : (b + 1) * BLK] = turned.T.astype(bf16)


def project_kernel(hidden_ref, weight_ref, gain_ref, out_ref):
    rows = hidden_ref.shape[0]
    new = lax.broadcasted_iota(jnp.int32, (rows, 1), 0)
    src = (new % NZ) * (NX * RI) + (new // XR) * RI + (new % XR) // NZ
    chosen = lax.broadcasted_iota(jnp.int32, (rows, rows), 1) == src
    moved = jnp.dot(
        jnp.where(chosen, 1.0, 0.0).astype(bf16), hidden_ref[...], preferred_element_type=f32
    ).astype(bf16)
    high, middle, low = three_pieces(gain_ref[...])
    sub = lax.broadcasted_iota(jnp.int32, (TILE, HD), 0)
    gain = jnp.where(
        sub == 0, high, jnp.where(sub == 1, middle, jnp.where(sub == 2, low, 0.0))
    ).astype(bf16)
    zero = jnp.zeros((TILE, HD), bf16)
    for x in range(NX):
        part = moved[x * XR : (x + 1) * XR, :]
        product = jnp.dot(part, weight_ref[...], preferred_element_type=f32).astype(bf16)
        for i in range(RI):
            band = product[i * TILE : (i + 1) * TILE, :]
            for j in range(GQ + 2):
                slot = 2 * (i * 4) + j if j < GQ else 2 * (12 + i) + (j - GQ)
                out_ref[x, slot] = band[:, j * HD : (j + 1) * HD]
            out_ref[x, 32 + i] = part[i * TILE : (i + 1) * TILE, :]
        out_ref[x, 30] = zero
        out_ref[x, 31] = zero
        out_ref[x, 35] = gain


def sum_x_kernel(in_ref, tiles_ref, hidden_ref, gain_ref):
    for t in range(32):
        total = in_ref[0, t].astype(f32)
        for x in range(1, NX):
            total = total + in_ref[x, t].astype(f32)
        tiles_ref[t // 2, t % 2] = total.astype(bf16)
    for x in range(NX):
        for i in range(RI):
            hidden_ref[x, i] = in_ref[x, 32 + i]
        pieces = in_ref[x, 35].astype(f32)
        gain_ref[x : x + 1, :] = pieces[0:1] + pieces[1:2] + pieces[2:3]


def rope_kernel(in_ref, factors_ref, copies_ref, own_ref):
    for s in range(2):
        total = in_ref[0, s].astype(f32)
        for z in range(1, NZ):
            total = total + in_ref[z, s].astype(f32)
        turned = total * factors_ref[s, 0] + pltpu.roll(total, HD // 2, 1) * factors_ref[s, 1]
        turned = turned.astype(bf16)
        own_ref[s] = turned
        for z in range(NZ):
            copies_ref[z, s] = turned


def attend_kernel(
    queries_ref, keys_ref, values_ref, new_ref, keypos_ref, rowpos_ref, out_ref, score_ref
):
    held = keys_ref.shape[2]
    blocks = held // BLK
    scale = HD ** (-0.5) * LOG2E
    contract_last = (((1,), (1,)), ((), ()))
    new_keys = jnp.concatenate([new_ref[x, 0] for x in range(NX)], axis=0)
    new_values = jnp.concatenate([new_ref[x, 1] for x in range(NX)], axis=0)
    fresh = new_keys.shape[0]
    for i in range(RI):
        queries = jnp.concatenate(
            [queries_ref[4 * i + g // 2, g % 2] for g in range(GQ)], axis=0
        )
        row_pos = jnp.concatenate([rowpos_ref[i]] * GQ, axis=0)
        peak = jnp.full((HD, BLK), least_peak, f32)
        for x in range(NX):
            score = jnp.dot(queries, keys_ref[x], preferred_element_type=f32)
            for b in range(blocks):
                n = x * blocks + b
                cut = jnp.where(
                    keypos_ref[n : n + 1, :] <= row_pos,
                    score[:, b * BLK : (b + 1) * BLK],
                    masked_score,
                )
                score_ref[:, n * BLK : (n + 1) * BLK] = cut
                peak = jnp.maximum(peak, cut)
        n = NX * blocks
        score = lax.dot_general(queries, new_keys, contract_last, preferred_element_type=f32)
        last = jnp.where(keypos_ref[n : n + 1, :fresh] <= row_pos[:, :fresh], score, masked_score)
        top = jnp.maximum(
            jnp.max(peak, axis=1, keepdims=True), jnp.max(last, axis=1, keepdims=True)
        )
        top = top * scale
        weight = jnp.exp2(last * scale - top)
        total_last = jnp.sum(weight, axis=1, keepdims=True)
        numer = jnp.dot(weight.astype(bf16), new_values, preferred_element_type=f32)
        total = jnp.zeros((HD, BLK), f32)
        for x in range(NX):
            weights = []
            for b in range(blocks):
                n = x * blocks + b
                weight = jnp.exp2(score_ref[:, n * BLK : (n + 1) * BLK] * scale - top)
                total = total + weight
                weights.append(weight.astype(bf16))
            numer = numer + jnp.dot(
                jnp.concatenate(weights, axis=1), values_ref[x], preferred_element_type=f32
            )
        total = jnp.sum(total, axis=1, keepdims=True) + total_last
        some = total > 0.0
        share = numer * jnp.where(some, 1.0 / jnp.where(some, total, 1.0), 0.0)
        level = top + jnp.where(some, jnp.log2(jnp.where(some, total, 1.0)), 0.0)
        share_at = (NX * blocks + i) * BLK
        score_ref[:, share_at : share_at + BLK] = share
        level_at = (NX * blocks + RI + i) * BLK
        score_ref[:, level_at : level_at + BLK] = jnp.broadcast_to(level, (HD, BLK))
    lane = lax.broadcasted_iota(jnp.int32, (8, HD), 1)
    for z in range(NZ):
        parts = []
        tail = jnp.zeros((8, HD), f32)
        for k in range(RI):
            row = 24 * z + 8 * k
            i, r = row // HD, row % HD
            share_at = (NX * blocks + i) * BLK
            level_at = (NX * blocks + RI + i) * BLK
            parts.append(score_ref[r : r + 8, share_at : share_at + BLK])
            for p, piece in enumerate(three_pieces(score_ref[r : r + 8, level_at : level_at + BLK])):
                tail = jnp.where(lane == 3 * k + p, piece, tail)
        out_ref[z] = jnp.concatenate(parts + [tail], axis=0).astype(bf16)


def combine_kernel(in_ref, out_ref):
    level = [[None] * RI for _ in range(NZ)]
    top = [None] * RI
    for z in range(NZ):
        tail = in_ref[z].astype(f32)[24:32, :]
        for k in range(RI):
            value = tail[:, 3 * k : 3 * k + 1] + tail[:, 3 * k + 1 : 3 * k + 2]
            value = value + tail[:, 3 * k + 2 : 3 * k + 3]
            level[z][k] = value
            top[k] = value if z == 0 else jnp.maximum(top[k], value)
    numer = jnp.zeros((8 * RI, HD), f32)
    total = jnp.zeros((8 * RI, 1), f32)
    for z in range(NZ):
        factor = jnp.concatenate([jnp.exp2(level[z][k] - top[k]) for k in range(RI)], axis=0)
        numer = numer + in_ref[z].astype(f32)[: 8 * RI, :] * factor
        total = total + factor
    result = (numer / total).astype(bf16)
    for z in range(NZ):
        out_ref[z] = result


def output_kernel(heads_ref, weight_ref, out_ref):
    rows = heads_ref[...]
    bands = []
    for i in range(RI):
        at = i * GQ * TILE
        bands.append(
            jnp.concatenate([rows[at + g * TILE : at + (g + 1) * TILE, :] for g in range(GQ)], axis=1)
        )
    attended = jnp.concatenate(bands, axis=0)
    for x in range(NX):
        term = jnp.dot(attended, weight_ref[x], preferred_element_type=f32).astype(bf16)
        for h in range(NH):
            out_ref[h, :, x * HD : (x + 1) * HD] = term


def next_kernel(terms_ref, hidden_ref, gain_ref, weight_ref, resid_ref, out_ref, cut_ref):
    attended = terms_ref[0].astype(f32)
    for h in range(1, NH):
        attended = attended + terms_ref[h].astype(f32)
    squares = jnp.zeros((XR, 1), f32)
    product = jnp.zeros((XR, weight_ref.shape[2]), f32)
    for x in range(NX):
        before = jnp.concatenate([hidden_ref[x, i] for i in range(RI)], axis=0).astype(f32)
        resid = before + attended[:, x * HD : (x + 1) * HD]
        resid_ref[x] = resid.astype(bf16)
        squares = squares + jnp.sum(resid * resid, axis=1, keepdims=True)
        gained = (resid * gain_ref[x : x + 1, :]).astype(bf16)
        product = product + jnp.dot(gained, weight_ref[x], preferred_element_type=f32)
    for i in range(RI):
        for j in range(GQ + 2):
            cut_ref[:, i * (GQ + 2) + j, :] = product[
                i * TILE : (i + 1) * TILE, j * HD : (j + 1) * HD
            ]
    lane = lax.broadcasted_iota(jnp.int32, (TILE, HD), 1)
    tail = jnp.zeros((TILE, HD), f32)
    for i in range(RI):
        for p, piece in enumerate(three_pieces(squares[i * TILE : (i + 1) * TILE, :])):
            tail = jnp.where(lane == 3 * i + p, piece, tail)
    cut_ref[:, 30, :] = tail
    cut_ref[:, 31, :] = jnp.zeros((TILE, HD), f32)
    out_ref[...] = cut_ref[...].astype(bf16)


def finish_kernel(in_ref, out_ref):
    total = in_ref[0].astype(f32)
    for z in range(1, NZ):
        total = total + in_ref[z].astype(f32)
    rows = []
    for i in range(RI):
        squares = total[30:31, 3 * i : 3 * i + 1] + total[30:31, 3 * i + 1 : 3 * i + 2]
        squares = squares + total[30:31, 3 * i + 2 : 3 * i + 3]
        factor = lax.rsqrt(squares / D + epsilon)
        at = i * (GQ + 2)
        rows.append(
            jnp.concatenate(
                [total[at + j : at + j + 1, :] * factor for j in range(GQ + 2)], axis=1
            )
        )
    out_ref[...] = jnp.concatenate(rows, axis=0).astype(bf16)


def reorder_kernel(in_ref, out_ref):
    rows = out_ref.shape[0]
    new = lax.broadcasted_iota(jnp.int32, (rows, 1), 0)
    src = ((new // RI) % NX) * XR + (new % RI) * NZ + new // (NX * RI)
    chosen = lax.broadcasted_iota(jnp.int32, (rows, rows), 1) == src
    data = jnp.concatenate([in_ref[x] for x in range(NX)], axis=0)
    out_ref[...] = jnp.dot(
        jnp.where(chosen, 1.0, 0.0).astype(bf16), data, preferred_element_type=f32
    ).astype(bf16)


def key_layout(z, group_lengths, group_owner, group_start, listed_rows, blocks):
    owners = z * NX + jnp.arange(NX, dtype=jnp.int32)
    length = group_lengths // BLK
    holder = (group_owner[None, :] == owners[:, None]).astype(jnp.int32)
    count = group_owner.shape[0]
    before = jnp.arange(count)[None, :] < jnp.arange(count)[:, None]
    held = holder * length[None, :]
    offset = jnp.sum(jnp.where(before[None], held[:, None, :], 0), axis=2)
    ids = jnp.arange(blocks, dtype=jnp.int32)[None, :, None]
    member = (
        (holder[:, None, :] == 1)
        & (ids >= offset[:, None, :])
        & (ids < offset[:, None, :] + length[None, None, :])
    ).astype(jnp.int32)
    start = group_start[None, None, :]
    shift = jnp.sum(member * start, axis=2)
    begin = jnp.sum(member * (start + (ids - offset[:, None, :]) * BLK), axis=2)
    live = jnp.sum(member, axis=2) > 0
    position = begin[:, :, None] + jnp.arange(BLK, dtype=jnp.int32)
    hit = jnp.any(position[..., None] == listed_rows, axis=-1)
    position = jnp.where(live[:, :, None] & ~hit, position, never)
    return shift, position.reshape(NX * blocks, BLK)


def on_device(
    hidden_rows,
    qkv_weight,
    out_weight,
    norm_gain,
    next_weight,
    cache_keys,
    cache_values,
    group_lengths,
    group_owner,
    group_start,
    listed_rows,
):
    z = lax.axis_index("z")
    x = lax.axis_index("x")
    held = cache_keys.shape[0]
    blocks = held // BLK
    a2a = functools.partial(lax.all_to_all, split_axis=0, concat_axis=0, tiled=True)

    payload = vmem_call(
        project_kernel,
        shaped((NX, 36, TILE, HD), bf16),
        (hidden_rows, qkv_weight, norm_gain.reshape(1, HD)),
    )
    payload = a2a(payload, "x")

    shift, key_pos = key_layout(
        z, group_lengths, group_owner, group_start, listed_rows, blocks
    )
    own_shift = lax.dynamic_slice_in_dim(shift, x, 1, axis=0)[0]
    by_zxi = listed_rows.reshape(NZ, NX, RI)
    row_pos = lax.dynamic_slice_in_dim(by_zxi, x, 1, axis=1)[:, 0].T
    tile_row = jnp.where(z < 12, z // 4, jnp.minimum(z - 12, RI - 1))
    tile_pos = lax.dynamic_slice_in_dim(row_pos, tile_row, 1, axis=0)[0]
    new_pos = lax.dynamic_slice_in_dim(by_zxi, tile_row, 1, axis=2)[:, :, 0].T.reshape(-1)
    new_pos = jnp.where((z >= 12) & (z < 12 + RI), new_pos, never)
    new_pos = jnp.concatenate([new_pos, jnp.full((BLK - NZ * NX,), never, jnp.int32)])
    key_pos = jnp.concatenate([key_pos, new_pos[None]], axis=0)
    wide_row_pos = jnp.broadcast_to(row_pos[:, :, None], (RI, NZ, BLK))
    cosine, sine = rope_factors(jnp.concatenate([own_shift, tile_pos]))
    keys_turned = vmem_call(
        rotate_kernel,
        shaped((HD, held), bf16),
        (cache_keys, cosine[:blocks], sine[:blocks]),
    )
    turns = jnp.stack([cosine[blocks:], sine[blocks:]])
    still = jnp.stack([jnp.ones_like(turns[0]), jnp.zeros_like(turns[0])])
    factors = jnp.stack([turns, jnp.where(z < 12, turns, still)])
    keys_x = lax.all_gather(keys_turned, "x", axis=0)
    values_x = lax.all_gather(cache_values, "x", axis=0)
    out_weight_x = lax.all_gather(out_weight, "x", axis=0)
    next_weight_x = lax.all_gather(next_weight, "x", axis=0)

    tiles, hidden_x, gain_x = vmem_call(
        sum_x_kernel,
        (
            shaped((NZ, 2, TILE, HD), bf16),
            shaped((NX, RI, TILE, HD), bf16),
            shaped((NX, HD), f32),
        ),
        (payload,),
    )
    copies, own = vmem_call(
        rope_kernel,
        (shaped((NZ, 2, TILE, HD), bf16), shaped((2, TILE, HD), bf16)),
        (a2a(tiles, "z"), factors),
    )
    new_x = lax.all_gather(own, "x", axis=0)
    queries = a2a(copies, "z")
    parts = vmem_call(
        attend_kernel,
        shaped((NZ, 32, HD), bf16),
        (queries, keys_x, values_x, new_x, key_pos, wide_row_pos),
        scratch=[pltpu.VMEM((HD, (NX * blocks + 2 * RI) * BLK), f32)],
    )
    share = vmem_call(
        combine_kernel, shaped((NZ, 8 * RI, HD), bf16), (a2a(parts, "z"),)
    )
    heads_out = a2a(share, "z").reshape(XR * GQ, HD)
    terms = vmem_call(
        output_kernel, shaped((NH, XR, NX * HD), bf16), (heads_out, out_weight_x)
    )
    resid, products = vmem_call(
        next_kernel,
        (shaped((NX, XR, HD), bf16), shaped((NZ, 32, HD), bf16)),
        (a2a(terms, "heads"), hidden_x, gain_x, next_weight_x),
        scratch=[pltpu.VMEM((NZ, 32, HD), f32)],
    )
    resid = a2a(resid, "x")
    hidden_out = vmem_call(reorder_kernel, shaped(hidden_rows.shape, bf16), (resid,))
    next_qkv = vmem_call(
        finish_kernel, shaped((RI, (GQ + 2) * HD), bf16), (a2a(products, "z"),)
    )
    return hidden_out, next_qkv


def solution(mesh):
    split = Mesh(mesh.devices.reshape(NH, NZ, NX), ("heads", "z", "x"))
    return jax.shard_map(
        on_device,
        mesh=split,
        in_specs=(
            P(None, GROUPS),
            P(GROUPS, "heads"),
            P("heads", GROUPS),
            P(GROUPS),
            P(GROUPS, "heads"),
            P(GROUPS, "heads"),
            P(GROUPS, "heads"),
            P(),
            P(),
            P(),
            P(),
        ),
        out_specs=(P(None, GROUPS), P(GROUPS, "heads")),
        check_vma=False,
    )
```

time: 281 us -> 196 us (0.70)
  blocking collectives: 184 us -> 75.5 us
  between operations: 1.11 us -> 14.3 us
  Pallas kernels: 0 us -> 10.1 us
  starting transfers between devices: 28.1 us -> 37.5 us
  waiting for transfers between devices: 42.4 us -> 48.3 us
  matrix products: 5.86 us -> 0 us
  other arithmetic: 7.57 us -> 1.87 us
  local copies, waits for them, and re-layouts: 10.1 us -> 6.53 us
    all_to_all x6 -> x2, blocking collectives: 114 us -> 32.9 us  [the longest x1 25.2 us: on_device(): a2a(parts, 'z')]
    all_gather x0 -> x3, blocking collectives: none -> 42.5 us  [the longest x1 16.6 us: on_device(): values_x = lax.all_gather(cache_values, 'x', axis=0)]
    pmax x2 -> x0, blocking collectives: 36 us -> none  [over_axes(): array = lax.pmax(array, axis)]
    psum x2 -> x0, blocking collectives: 34.9 us -> none  [by_axis(): return functools.reduce(lax.psum, axes, array)]
    pallas_call x0 -> x10, Pallas kernels: none -> 10.1 us  [vmem_call(): pl.pallas_call(kernel, out_shape=out_shape, in_specs=[space] * len(operan...]
    all_to_all x3 -> x6, starting transfers between devices: 28.1 us -> 37.5 us  [the longest x1 12.3 us: on_device(): a2a(tiles, 'z')]
    dot_general x11 -> x0, matrix products: 5.86 us -> none  [the longest x4 2.12 us: on_device(): jnp.einsum('rgd,kd->rgk', query_block, key_block, preferred_element_type=...]
    all_to_all x3 -> x6, waiting for transfers between devices: 42.4 us -> 46.9 us  [the longest x1 13 us: on_device(): heads_out = a2a(share, 'z').reshape(XR * GQ, HD)]
  transfers between devices with their start and end apart: 3 -> 8, of which waited for: 3 -> 4; matrix products, arithmetic and copies ran while one was open for 1% -> 2% of each run, Pallas kernels for 0% -> 4%
where the time goes in v1:
time: 196 us; the launch traced here: 194 us
  blocking collectives  75.5 us (39%)
  waiting for transfers between devices  48.3 us (25%)
  starting transfers between devices  37.5 us (19%)
  between operations  14.3 us (7%)
  Pallas kernels  10.1 us (5%)
  local copies, waits for them, and re-layouts  6.53 us (3%)
    all_to_all x1, blocking collectives, on_device(): a2a(parts, 'z')  25.2 us
    all_gather x1, blocking collectives, on_device(): values_x = lax.all_gather(cache_values, 'x', axis=0)  16.6 us
    all_gather x1, blocking collectives, on_device(): keys_x = lax.all_gather(keys_turned, 'x', axis=0)  14.1 us
    all_to_all x1, waiting for transfers between devices, on_device(): heads_out = a2a(share, 'z').reshape(XR * GQ, HD)  13 us
    all_to_all x1, waiting for transfers between devices, on_device(): a2a(products, 'z')  12.9 us
    all_to_all x1, starting transfers between devices, on_device(): a2a(tiles, 'z')  12.3 us
    all_to_all x1, waiting for transfers between devices, on_device(): a2a(tiles, 'z')  12 us
    all_gather x1, blocking collectives, on_device(): new_x = lax.all_gather(own, 'x', axis=0)  11.9 us
  transfers between devices with their start and end apart: 8, of which 4 were waited for; matrix products, arithmetic and copies ran while one was open for 2% of the time, Pallas kernels for 4%

profile of v1, /device:TPU:6, one launch (start us, length us, event | category | flops | bytes accessed | tf_op | source)
XLA Modules:
  0.0 194.2 jit_solution(2912957925214612373)
XLA Ops:
  7.2 0.0 all-gather.8.cloned.1.call-start
  7.2 0.7 all-gather.8.cloned.1.call-update
  7.9 0.0 copy-start.8
  7.9 1.0 copy-done.2
  8.9 0.8 copy-done.4
  9.7 0.7 copy-done.5
  10.4 1.3 shard_map.122
  11.7 9.3 %all-to-all-start = ((bf16[4,36,16,128]{3,2,1,0:T(8,128)(2,1)}), bf16[4,36,16,128]{3,2,1,0:T(8,128)(2,1)S(1)}, u32[]{:S(2)}, u32[]{:S(2)}) async-start(bf16[4,36,16,128]{3,2,1,0:T(8,128)(2,1)} %shard_map.122), calls=%async_computation | async-start | bytes 1179648 | tf_op jit(solution)/shard_map/all_to_all | solution.py:345
  21.0 0.7 all-gather.10.cloned.1.call-update
  21.8 0.2 reshape.190
  22.0 0.1 fusion.5
  22.1 0.1 compare_select_fusion
  22.1 0.1 select_reduce_fusion
  22.3 0.0 copy-done.10
  22.3 0.4 select_reduce_fusion.1
  22.7 0.2 dynamic-slice_reduce_fusion.1
  22.9 0.1 copy.25
  23.0 0.1 iota_add_fusion
  23.1 0.4 dynamic-slice_reduce_fusion
  23.5 0.1 add_convert_fusion
  23.6 0.1 multiply_cosine_fusion
  23.7 0.1 fusion.7
  23.8 0.0 copy-done.7
  23.8 0.1 pad_maximum_fusion.1
  23.9 0.3 shard_map.125
  24.2 0.0 copy-start.6
  24.3 0.1 dynamic-slice_select_fusion
  24.4 14.1 %all-gather = bf16[512,768]{1,0:T(8,128)(2,1)S(1)} all-gather(bf16[128,768]{1,0:T(8,128)(2,1)S(1)} %shard_map.125), channel_id=2, replica_groups=mesh['heads'=8,'z'=16,'x'=4] {'x'}, dimensions={0}, use_global_device_ids=true | all-gather | bytes 983040 | tf_op jit(solution)/shard_map/all_gather | solution.py:369
  38.4 0.0 all-to-all-done.in_ref
  38.4 0.7 shard_map.123
  39.2 12.3 %all-to-all-start.1 = ((bf16[16,2,16,128]{3,2,1,0:T(8,128)(2,1)}), bf16[16,2,16,128]{3,2,1,0:T(8,128)(2,1)S(1)}, u32[]{:S(2)}, u32[]{:S(2)}) async-start(bf16[16,2,16,128]{3,2,1,0:T(8,128)(2,1)} %get-tuple-element.9), calls=%async_computation.1 | async-start | bytes 262144 | tf_op jit(solution)/shard_map/all_to_all | solution.py:386
  51.4 0.5 compare_reduce_fusion
  52.0 0.1 add.78
  52.0 0.1 copy.27
  52.1 0.1 select_n.81
  52.2 0.1 copy.24
  52.4 0.1 gt.11
  52.4 0.1 copy.28
  52.5 0.1 add_select_fusion
  52.6 12.0 %all-to-all-done.1.in_ref = bf16[16,2,16,128]{3,2,1,0:T(8,128)(2,1)S(1)} async-done(((bf16[16,2,16,128]{3,2,1,0:T(8,128)(2,1)}), bf16[16,2,16,128]{3,2,1,0:T(8,128)(2,1)S(1)}, u32[]{:S(2)}, u32[]{:S(2)}) %all-to-all-start.1) | async-done | bytes 131104 | tf_op jit(solution)/shard_map/all_to_all | solution.py:386
  64.6 0.8 shard_map.124
  65.4 3.9 %all-to-all-start.2 = ((bf16[16,2,16,128]{3,2,1,0:T(8,128)(2,1)}), bf16[16,2,16,128]{3,2,1,0:T(8,128)(2,1)S(1)}, u32[]{:S(2)}, u32[]{:S(2)}) async-start(bf16[16,2,16,128]{3,2,1,0:T(8,128)(2,1)} %get-tuple-element.10), calls=%async_computation.2 | async-start | bytes 262144 | tf_op jit(solution)/shard_map/all_to_all | solution.py:389
  69.3 16.6 %all-gather.1 = bf16[3072,128]{1,0:T(8,128)(2,1)S(1)} all-gather(bf16[768,128]{1,0:T(8,128)(2,1)S(1)} %copy-done.6), channel_id=3, replica_groups=mesh['heads'=8,'z'=16,'x'=4] {'x'}, dimensions={0}, use_global_device_ids=true | all-gather | bytes 983040 | tf_op jit(solution)/shard_map/all_gather | solution.py:370
  85.9 11.9 %all-gather.2 = bf16[8,16,128]{2,1,0:T(8,128)(2,1)S(1)} all-gather(bf16[2,16,128]{2,1,0:T(8,128)(2,1)S(1)} %get-tuple-element.11), channel_id=4, replica_groups=mesh['heads'=8,'z'=16,'x'=4] {'x'}, dimensions={0}, use_global_device_ids=true | all-gather | bytes 40960 | tf_op jit(solution)/shard_map/all_gather | solution.py:388
  97.8 0.0 all-to-all-done.2.queries_ref
  97.8 0.1 broadcast_in_dim.38.rowpos_ref
  97.9 2.4 %shard_map.126 = bf16[16,32,128]{2,1,0:T(8,128)(2,1)S(1)} custom-call(bf16[16,2,16,128]{3,2,1,0:T(8,128)(2,1)S(1)} %all-to-all-done.2.queries_ref, bf16[4,128,768]{2,1,0:T(8,128)(2,1)S(1)} %bitcast.25, bf16[4,768,128]{2,1,0:T(8,128)(2,1)S(1)} %bitcast.26, bf16[4,2,16,128]{3,2,1,0:T(8,128)(2,1)S(1)} %bitcast.30, s32[25,128]{1,0:T(8,128)S(1)} %pad_add_fusion.keypos_ref, ...), custom_call_target="tpu_custom_call" | custom-call | tf_op jit(solution)/shard_map/pallas_call | solution.py:36
  100.3 25.2 %all_to_all.40.in_ref = bf16[16,32,128]{2,1,0:T(8,128)(2,1)S(1)} all-to-all(bf16[16,32,128]{2,1,0:T(8,128)(2,1)S(1)} %shard_map.126), channel_id=1, replica_groups=mesh['heads'=8,'z'=16,'x'=4] {'z'}, dimensions={0} | all-to-all | bytes 262144 | tf_op jit(solution)/shard_map/all_to_all | solution.py:397
  125.4 0.9 shard_map.127
  126.4 4.0 %all-to-all-start.4 = ((bf16[16,24,128]{2,1,0:T(8,128)(2,1)}), bf16[16,24,128]{2,1,0:T(8,128)(2,1)S(1)}, u32[]{:S(2)}, u32[]{:S(2)}) async-start(bf16[16,24,128]{2,1,0:T(8,128)(2,1)} %shard_map.127), calls=%async_computation.4 | async-start | bytes 196608 | tf_op jit(solution)/shard_map/all_to_all | solution.py:399
  130.4 0.0 all-gather.8.cloned.1.call-done
  130.4 13.0 %all-to-all-done.4 = bf16[16,24,128]{2,1,0:T(8,128)(2,1)S(1)} async-done(((bf16[16,24,128]{2,1,0:T(8,128)(2,1)}), bf16[16,24,128]{2,1,0:T(8,128)(2,1)S(1)}, u32[]{:S(2)}, u32[]{:S(2)}) %all-to-all-start.4) | async-done | bytes 98336 | tf_op jit(solution)/shard_map/all_to_all | solution.py:399
  143.4 1.2 copy-done.1
  144.6 1.0 shard_map.128
  145.7 4.5 %all-to-all-start.5 = ((bf16[8,48,512]{2,1,0:T(8,128)(2,1)}), bf16[8,48,512]{2,1,0:T(8,128)(2,1)S(1)}, u32[]{:S(2)}, u32[]{:S(2)}) async-start(bf16[8,48,512]{2,1,0:T(8,128)(2,1)} %shard_map.128), calls=%async_computation.5 | async-start | bytes 786432 | tf_op jit(solution)/shard_map/all_to_all | solution.py:406
  150.2 0.0 all-gather.10.cloned.1.call-done
  150.2 8.9 %all-to-all-done.5.terms_ref = bf16[8,48,512]{2,1,0:T(8,128)(2,1)S(1)} async-done(((bf16[8,48,512]{2,1,0:T(8,128)(2,1)}), bf16[8,48,512]{2,1,0:T(8,128)(2,1)S(1)}, u32[]{:S(2)}, u32[]{:S(2)}) %all-to-all-start.5) | async-done | bytes 393248 | tf_op jit(solution)/shard_map/all_to_all | solution.py:406
  159.1 1.3 copy-done
  160.4 1.1 shard_map.129
  161.5 7.8 %all_to_all.41.in_ref = bf16[4,48,128]{2,1,0:T(8,128)(2,1)S(1)} all-to-all(bf16[4,48,128]{2,1,0:T(8,128)(2,1)S(1)} %get-tuple-element.14), channel_id=1, replica_groups=mesh['heads'=8,'z'=16,'x'=4] {'x'}, dimensions={0} | all-to-all | bytes 98304 | tf_op jit(solution)/shard_map/all_to_all | solution.py:409
  169.3 3.5 %all-to-all-start.7 = ((bf16[16,32,128]{2,1,0:T(8,128)(2,1)}), bf16[16,32,128]{2,1,0:T(8,128)(2,1)S(1)}, u32[]{:S(2)}, u32[]{:S(2)}) async-start(bf16[16,32,128]{2,1,0:T(8,128)(2,1)} %get-tuple-element.15), calls=%async_computation.7 | async-start | bytes 262144 | tf_op jit(solution)/shard_map/all_to_all | solution.py:412
  172.8 0.8 shard_map.130
  173.7 12.9 %all-to-all-done.7.in_ref = bf16[16,32,128]{2,1,0:T(8,128)(2,1)S(1)} async-done(((bf16[16,32,128]{2,1,0:T(8,128)(2,1)}), bf16[16,32,128]{2,1,0:T(8,128)(2,1)S(1)}, u32[]{:S(2)}, u32[]{:S(2)}) %all-to-all-start.7) | async-done | bytes 131104 | tf_op jit(solution)/shard_map/all_to_all | solution.py:412
  186.6 0.8 shard_map.131
  (30 shorter events, 0.1 us)
Async XLA Ops:
  7.2 123.2 %all-gather.8.cloned.1.call-start = ((), (), s32[]{:S(2)}) async-start(), calls=%async_computation.8 | async-start | bytes 1310720 | tf_op jit(solution)/shard_map/all_gather | solution.py:371
  7.9 13.9 %copy-start.8 = (s32[192]{0:T(256)S(1)}, s32[192]{0:T(256)}, u32[]{:S(2)}) copy-start(s32[192]{0:T(256)} %param.21) | copy-start | bytes 2308
  7.9 14.1 %copy-start.9 = (s32[128]{0:T(128)S(1)}, s32[128]{0:T(128)}, u32[]{:S(2)}) copy-start(s32[128]{0:T(128)} %param.19) | copy-start | bytes 1540
  7.9 1.0 copy-start.2
  8.9 0.8 copy-start.4
  9.7 0.7 copy-start.5
  10.4 11.6 %copy-start.11 = (s32[128]{0:T(128)S(1)}, s32[128]{0:T(128)}, u32[]{:S(2)}) copy-start(s32[128]{0:T(128)} %param.18) | copy-start | bytes 1540
  10.4 11.9 %copy-start.10 = (s32[128]{0:T(128)S(1)}, s32[128]{0:T(128)}, u32[]{:S(2)}) copy-start(s32[128]{0:T(128)} %param.20) | copy-start | bytes 1540
  10.4 13.4 %copy-start.7 = (f32[1,2,16,128]{3,2,1,0:T(8,128)S(1)}, f32[1,2,16,128]{3,2,1,0:T(8,128)}, u32[]{:S(2)}) copy-start(f32[1,2,16,128]{3,2,1,0:T(8,128)} %constant.87.clone.1) | copy-start | bytes 49156
  10.4 13.5 %copy-start.3 = (bf16[768,128]{1,0:T(8,128)(2,1)S(1)}, bf16[768,128]{1,0:T(8,128)(2,1)}, u32[]{:S(2)}) copy-start(bf16[768,128]{1,0:T(8,128)(2,1)} %keys_ref.1) | copy-start | bytes 589828
  11.7 26.8 %all-to-all-start = ((bf16[4,36,16,128]{3,2,1,0:T(8,128)(2,1)}), bf16[4,36,16,128]{3,2,1,0:T(8,128)(2,1)S(1)}, u32[]{:S(2)}, u32[]{:S(2)}) async-start(bf16[4,36,16,128]{3,2,1,0:T(8,128)(2,1)} %shard_map.122), calls=%async_computation | async-start | bytes 1179648 | tf_op jit(solution)/shard_map/all_to_all | solution.py:345
  21.0 129.2 %all-gather.10.cloned.1.call-start = ((), (), s32[]{:S(2)}) async-start(), calls=%async_computation.9 | async-start | bytes 1638400 | tf_op jit(solution)/shard_map/all_gather | solution.py:372
  24.2 45.1 %copy-start.6 = (bf16[768,128]{1,0:T(8,128)(2,1)S(1)}, bf16[768,128]{1,0:T(8,128)(2,1)}, u32[]{:S(2)}) copy-start(bf16[768,128]{1,0:T(8,128)(2,1)} %param.17) | copy-start | bytes 589828
  39.2 25.5 %all-to-all-start.1 = ((bf16[16,2,16,128]{3,2,1,0:T(8,128)(2,1)}), bf16[16,2,16,128]{3,2,1,0:T(8,128)(2,1)S(1)}, u32[]{:S(2)}, u32[]{:S(2)}) async-start(bf16[16,2,16,128]{3,2,1,0:T(8,128)(2,1)} %get-tuple-element.9), calls=%async_computation.1 | async-start | bytes 262144 | tf_op jit(solution)/shard_map/all_to_all | solution.py:386
  65.4 32.4 %all-to-all-start.2 = ((bf16[16,2,16,128]{3,2,1,0:T(8,128)(2,1)}), bf16[16,2,16,128]{3,2,1,0:T(8,128)(2,1)S(1)}, u32[]{:S(2)}, u32[]{:S(2)}) async-start(bf16[16,2,16,128]{3,2,1,0:T(8,128)(2,1)} %get-tuple-element.10), calls=%async_computation.2 | async-start | bytes 262144 | tf_op jit(solution)/shard_map/all_to_all | solution.py:389
  126.4 17.0 %all-to-all-start.4 = ((bf16[16,24,128]{2,1,0:T(8,128)(2,1)}), bf16[16,24,128]{2,1,0:T(8,128)(2,1)S(1)}, u32[]{:S(2)}, u32[]{:S(2)}) async-start(bf16[16,24,128]{2,1,0:T(8,128)(2,1)} %shard_map.127), calls=%async_computation.4 | async-start | bytes 196608 | tf_op jit(solution)/shard_map/all_to_all | solution.py:399
  143.4 1.2 copy-start.1
  145.7 13.4 %all-to-all-start.5 = ((bf16[8,48,512]{2,1,0:T(8,128)(2,1)}), bf16[8,48,512]{2,1,0:T(8,128)(2,1)S(1)}, u32[]{:S(2)}, u32[]{:S(2)}) async-start(bf16[8,48,512]{2,1,0:T(8,128)(2,1)} %shard_map.128), calls=%async_computation.5 | async-start | bytes 786432 | tf_op jit(solution)/shard_map/all_to_all | solution.py:406
  159.1 1.3 copy-start
  169.3 17.3 %all-to-all-start.7 = ((bf16[16,32,128]{2,1,0:T(8,128)(2,1)}), bf16[16,32,128]{2,1,0:T(8,128)(2,1)S(1)}, u32[]{:S(2)}, u32[]{:S(2)}) async-start(bf16[16,32,128]{2,1,0:T(8,128)(2,1)} %get-tuple-element.15), calls=%async_computation.7 | async-start | bytes 262144 | tf_op jit(solution)/shard_map/all_to_all | solution.py:412
Sparse Core Ops, SparseCore 0:
  10.1 35.6 all-gather.7
  47.9 37.8 all-gather.9

commit v2 on v1

--- a/solution.py
+++ b/solution.py
@@ -30,13 +30,15 @@
 f32 = jnp.float32
 
 
-def vmem_call(kernel, out_shape, operands, scratch=(), limit=32):
+def vmem_call(kernel, out_shape, operands, scratch=(), limit=32, scalars=0, hbm=False):
     space = pl.BlockSpec(memory_space=pltpu.VMEM)
     outs = jax.tree.map(lambda _: space, out_shape)
+    rest = pl.BlockSpec(memory_space=pltpu.HBM) if hbm else space
+    small = pl.BlockSpec(memory_space=pltpu.SMEM)
     return pl.pallas_call(
         kernel,
         out_shape=out_shape,
-        in_specs=[space] * len(operands),
+        in_specs=[small] * scalars + [rest] * (len(operands) - scalars),
         out_specs=outs,
         scratch_shapes=list(scratch),
         compiler_params=pltpu.CompilerParams(vmem_limit_bytes=limit * 2**20),
@@ -66,24 +68,37 @@
     return jnp.concatenate([cosine, cosine], -1), jnp.concatenate([-sine, sine], -1)
 
 
-def rotate_kernel(keys_ref, cos_ref, sin_ref, out_ref):
-    for b in range(keys_ref.shape[0] // BLK):
+def rotate_kernel(keys_ref, values_ref, cos_ref, sin_ref, out_ref):
+    blocks = keys_ref.shape[0] // BLK
+    for b in range(blocks):
+        out_ref[blocks + b] = values_ref[b * BLK : (b + 1) * BLK, :]
         block = keys_ref[b * BLK : (b + 1) * BLK, :].astype(f32)
         turned = (
             block * cos_ref[b : b + 1, :]
             + pltpu.roll(block, HD // 2, 1) * sin_ref[b : b + 1, :]
         )
         turned = turned.astype(bf16).astype(f32)
-        out_ref[:, b * BLK : (b + 1) * BLK] = turned.T.astype(bf16)
-
-
-def project_kernel(hidden_ref, weight_ref, gain_ref, out_ref):
+        out_ref[b] = turned.T.astype(bf16)
+
+
+def project_kernel(hidden_hbm, weight_hbm, gain_hbm, out_ref, hidden_ref, weight_ref, gain_ref, sems):
+    copies = [
+        pltpu.make_async_copy(src, dst, sems.at[n])
+        for n, (src, dst) in enumerate(
+            ((hidden_hbm, hidden_ref), (gain_hbm, gain_ref), (weight_hbm, weight_ref))
+        )
+    ]
+    for copy in copies:
+        copy.start()
     rows = hidden_ref.shape[0]
     new = lax.broadcasted_iota(jnp.int32, (rows, 1), 0)
     src = (new % NZ) * (NX * RI) + (new // XR) * RI + (new % XR) // NZ
     chosen = lax.broadcasted_iota(jnp.int32, (rows, rows), 1) == src
+    choice = jnp.where(chosen, 1.0, 0.0).astype(bf16)
+    copies[0].wait()
+    copies[1].wait()
     moved = jnp.dot(
-        jnp.where(chosen, 1.0, 0.0).astype(bf16), hidden_ref[...], preferred_element_type=f32
+        choice, hidden_ref[...], preferred_element_type=f32
     ).astype(bf16)
     high, middle, low = three_pieces(gain_ref[...])
     sub = lax.broadcasted_iota(jnp.int32, (TILE, HD), 0)
@@ -91,6 +106,7 @@
         sub == 0, high, jnp.where(sub == 1, middle, jnp.where(sub == 2, low, 0.0))
     ).astype(bf16)
     zero = jnp.zeros((TILE, HD), bf16)
+    copies[2].wait()
     for x in range(NX):
         part = moved[x * XR : (x + 1) * XR, :]
         product = jnp.dot(part, weight_ref[...], preferred_element_type=f32).astype(bf16)
@@ -105,17 +121,18 @@
         out_ref[x, 35] = gain
 
 
-def sum_x_kernel(in_ref, tiles_ref, hidden_ref, gain_ref):
+def sum_x_kernel(x_ref, in_ref, tiles_ref, hidden_ref, gain_ref):
     for t in range(32):
         total = in_ref[0, t].astype(f32)
         for x in range(1, NX):
             total = total + in_ref[x, t].astype(f32)
         tiles_ref[t // 2, t % 2] = total.astype(bf16)
-    for x in range(NX):
+    for s in range(NX):
+        src = (x_ref[0] + NX - s) % NX
         for i in range(RI):
-            hidden_ref[x, i] = in_ref[x, 32 + i]
-        pieces = in_ref[x, 35].astype(f32)
-        gain_ref[x : x + 1, :] = pieces[0:1] + pieces[1:2] + pieces[2:3]
+            hidden_ref[s, i] = in_ref[src, 32 + i]
+        pieces = in_ref[src, 35].astype(f32)
+        gain_ref[s : s + 1, :] = pieces[0:1] + pieces[1:2] + pieces[2:3]
 
 
 def rope_kernel(in_ref, factors_ref, copies_ref, own_ref):
@@ -130,15 +147,13 @@
             copies_ref[z, s] = turned
 
 
-def attend_kernel(
-    queries_ref, keys_ref, values_ref, new_ref, keypos_ref, rowpos_ref, out_ref, score_ref
-):
-    held = keys_ref.shape[2]
-    blocks = held // BLK
+def attend_kernel(queries_ref, keypos_ref, rowpos_ref, *refs):
+    cache_refs, new_refs, (out_ref, score_ref) = refs[:NX], refs[NX : 2 * NX], refs[2 * NX :]
+    blocks = cache_refs[0].shape[0] // 2
     scale = HD ** (-0.5) * LOG2E
     contract_last = (((1,), (1,)), ((), ()))
-    new_keys = jnp.concatenate([new_ref[x, 0] for x in range(NX)], axis=0)
-    new_values = jnp.concatenate([new_ref[x, 1] for x in range(NX)], axis=0)
+    new_keys = jnp.concatenate([ref[0] for ref in new_refs], axis=0)
+    new_values = jnp.concatenate([ref[1] for ref in new_refs], axis=0)
     fresh = new_keys.shape[0]
     for i in range(RI):
         queries = jnp.concatenate(
@@ -147,7 +162,8 @@
         row_pos = jnp.concatenate([rowpos_ref[i]] * GQ, axis=0)
         peak = jnp.full((HD, BLK), least_peak, f32)
         for x in range(NX):
-            score = jnp.dot(queries, keys_ref[x], preferred_element_type=f32)
+            keys = jnp.concatenate([cache_refs[x][b] for b in range(blocks)], axis=1)
+            score = jnp.dot(queries, keys, preferred_element_type=f32)
             for b in range(blocks):
                 n = x * blocks + b
                 cut = jnp.where(
@@ -175,8 +191,9 @@
                 weight = jnp.exp2(score_ref[:, n * BLK : (n + 1) * BLK] * scale - top)
                 total = total + weight
                 weights.append(weight.astype(bf16))
+            values = jnp.concatenate([cache_refs[x][blocks + b] for b in range(blocks)], axis=0)
             numer = numer + jnp.dot(
-                jnp.concatenate(weights, axis=1), values_ref[x], preferred_element_type=f32
+                jnp.concatenate(weights, axis=1), values, preferred_element_type=f32
             )
         total = jnp.sum(total, axis=1, keepdims=True) + total_last
         some = total > 0.0
@@ -222,7 +239,8 @@
         out_ref[z] = result
 
 
-def output_kernel(heads_ref, weight_ref, out_ref):
+def output_kernel(heads_ref, *refs):
+    weight_refs, out_ref = refs[:NX], refs[NX]
     rows = heads_ref[...]
     bands = []
     for i in range(RI):
@@ -232,24 +250,25 @@
         )
     attended = jnp.concatenate(bands, axis=0)
     for x in range(NX):
-        term = jnp.dot(attended, weight_ref[x], preferred_element_type=f32).astype(bf16)
+        term = jnp.dot(attended, weight_refs[x][...], preferred_element_type=f32).astype(bf16)
         for h in range(NH):
             out_ref[h, :, x * HD : (x + 1) * HD] = term
 
 
-def next_kernel(terms_ref, hidden_ref, gain_ref, weight_ref, resid_ref, out_ref, cut_ref):
+def next_kernel(terms_ref, hidden_ref, gain_ref, *refs):
+    weight_refs, resid_refs, (out_ref, cut_ref) = refs[:NX], refs[NX : 2 * NX], refs[2 * NX :]
     attended = terms_ref[0].astype(f32)
     for h in range(1, NH):
         attended = attended + terms_ref[h].astype(f32)
     squares = jnp.zeros((XR, 1), f32)
-    product = jnp.zeros((XR, weight_ref.shape[2]), f32)
+    product = jnp.zeros((XR, weight_refs[0].shape[1]), f32)
     for x in range(NX):
         before = jnp.concatenate([hidden_ref[x, i] for i in range(RI)], axis=0).astype(f32)
         resid = before + attended[:, x * HD : (x + 1) * HD]
-        resid_ref[x] = resid.astype(bf16)
+        resid_refs[x][...] = resid.astype(bf16)
         squares = squares + jnp.sum(resid * resid, axis=1, keepdims=True)
         gained = (resid * gain_ref[x : x + 1, :]).astype(bf16)
-        product = product + jnp.dot(gained, weight_ref[x], preferred_element_type=f32)
+        product = product + jnp.dot(gained, weight_refs[x][...], preferred_element_type=f32)
     for i in range(RI):
         for j in range(GQ + 2):
             cut_ref[:, i * (GQ + 2) + j, :] = product[
@@ -283,19 +302,20 @@
     out_ref[...] = jnp.concatenate(rows, axis=0).astype(bf16)
 
 
-def reorder_kernel(in_ref, out_ref):
+def reorder_kernel(x_ref, *refs):
+    in_refs, out_ref = refs[:NX], refs[NX]
     rows = out_ref.shape[0]
     new = lax.broadcasted_iota(jnp.int32, (rows, 1), 0)
-    src = ((new // RI) % NX) * XR + (new % RI) * NZ + new // (NX * RI)
+    source = ((new // RI) % NX + NX - x_ref[0]) % NX
+    src = source * XR + (new % RI) * NZ + new // (NX * RI)
     chosen = lax.broadcasted_iota(jnp.int32, (rows, rows), 1) == src
-    data = jnp.concatenate([in_ref[x] for x in range(NX)], axis=0)
+    data = jnp.concatenate([ref[...] for ref in in_refs], axis=0)
     out_ref[...] = jnp.dot(
         jnp.where(chosen, 1.0, 0.0).astype(bf16), data, preferred_element_type=f32
     ).astype(bf16)
 
 
-def key_layout(z, group_lengths, group_owner, group_start, listed_rows, blocks):
-    owners = z * NX + jnp.arange(NX, dtype=jnp.int32)
+def key_layout(owners, group_lengths, group_owner, group_start, listed_rows, blocks):
     length = group_lengths // BLK
     holder = (group_owner[None, :] == owners[:, None]).astype(jnp.int32)
     count = group_owner.shape[0]
@@ -337,40 +357,54 @@
     blocks = held // BLK
     a2a = functools.partial(lax.all_to_all, split_axis=0, concat_axis=0, tiled=True)
 
+    def shifted(array, step):
+        return lax.ppermute(array, "x", [(n, (n + step) % NX) for n in range(NX)])
+
+    def from_x(array):
+        return [array] + [shifted(array, step) for step in range(1, NX)]
+
     payload = vmem_call(
         project_kernel,
         shaped((NX, 36, TILE, HD), bf16),
         (hidden_rows, qkv_weight, norm_gain.reshape(1, HD)),
+        scratch=[
+            pltpu.VMEM(hidden_rows.shape, bf16),
+            pltpu.VMEM(qkv_weight.shape, bf16),
+            pltpu.VMEM((1, HD), f32),
+            pltpu.SemaphoreType.DMA((3,)),
+        ],
+        hbm=True,
+        limit=60,
     )
     payload = a2a(payload, "x")
 
+    sources = (x + NX - jnp.arange(NX, dtype=jnp.int32)) % NX
     shift, key_pos = key_layout(
-        z, group_lengths, group_owner, group_start, listed_rows, blocks
-    )
-    own_shift = lax.dynamic_slice_in_dim(shift, x, 1, axis=0)[0]
-    by_zxi = listed_rows.reshape(NZ, NX, RI)
-    row_pos = lax.dynamic_slice_in_dim(by_zxi, x, 1, axis=1)[:, 0].T
+        z * NX + sources, group_lengths, group_owner, group_start, listed_rows, blocks
+    )
+    by_xiz = listed_rows.reshape(NZ, NX, RI).transpose(1, 2, 0)
+    row_pos = lax.dynamic_slice_in_dim(by_xiz, x, 1, axis=0)[0]
     tile_row = jnp.where(z < 12, z // 4, jnp.minimum(z - 12, RI - 1))
-    tile_pos = lax.dynamic_slice_in_dim(row_pos, tile_row, 1, axis=0)[0]
-    new_pos = lax.dynamic_slice_in_dim(by_zxi, tile_row, 1, axis=2)[:, :, 0].T.reshape(-1)
-    new_pos = jnp.where((z >= 12) & (z < 12 + RI), new_pos, never)
+    tile_pos = lax.dynamic_slice_in_dim(by_xiz, tile_row, 1, axis=1)[:, 0]
+    tile_pos = jnp.sum(
+        jnp.where(sources[:, None, None] == jnp.arange(NX)[None, :, None], tile_pos[None], 0), axis=1
+    )
+    fresh = (z >= 12) & (z < 12 + RI)
+    new_pos = jnp.where(fresh, tile_pos.reshape(-1), never)
     new_pos = jnp.concatenate([new_pos, jnp.full((BLK - NZ * NX,), never, jnp.int32)])
     key_pos = jnp.concatenate([key_pos, new_pos[None]], axis=0)
     wide_row_pos = jnp.broadcast_to(row_pos[:, :, None], (RI, NZ, BLK))
-    cosine, sine = rope_factors(jnp.concatenate([own_shift, tile_pos]))
-    keys_turned = vmem_call(
+    cosine, sine = rope_factors(jnp.concatenate([shift[0], tile_pos[0]]))
+    cache = vmem_call(
         rotate_kernel,
-        shaped((HD, held), bf16),
-        (cache_keys, cosine[:blocks], sine[:blocks]),
+        shaped((2 * blocks, BLK, HD), bf16),
+        (cache_keys, cache_values, cosine[:blocks], sine[:blocks]),
     )
     turns = jnp.stack([cosine[blocks:], sine[blocks:]])
     still = jnp.stack([jnp.ones_like(turns[0]), jnp.zeros_like(turns[0])])
     factors = jnp.stack([turns, jnp.where(z < 12, turns, still)])
-    keys_x = lax.all_gather(keys_turned, "x", axis=0)
-    values_x = lax.all_gather(cache_values, "x", axis=0)
-    out_weight_x = lax.all_gather(out_weight, "x", axis=0)
-    next_weight_x = lax.all_gather(next_weight, "x", axis=0)
-
+
+    x_scalar = x.reshape(1).astype(jnp.int32)
     tiles, hidden_x, gain_x = vmem_call(
         sum_x_kernel,
         (
@@ -378,36 +412,45 @@
             shaped((NX, RI, TILE, HD), bf16),
             shaped((NX, HD), f32),
         ),
-        (payload,),
-    )
+        (x_scalar, payload),
+        scalars=1,
+    )
+    tiles, cache = lax.optimization_barrier((tiles, cache))
+    caches = from_x(cache)
     copies, own = vmem_call(
         rope_kernel,
         (shaped((NZ, 2, TILE, HD), bf16), shaped((2, TILE, HD), bf16)),
         (a2a(tiles, "z"), factors),
     )
-    new_x = lax.all_gather(own, "x", axis=0)
     queries = a2a(copies, "z")
+    news = from_x(own)
     parts = vmem_call(
         attend_kernel,
         shaped((NZ, 32, HD), bf16),
-        (queries, keys_x, values_x, new_x, key_pos, wide_row_pos),
+        (queries, key_pos, wide_row_pos, *caches, *news),
         scratch=[pltpu.VMEM((HD, (NX * blocks + 2 * RI) * BLK), f32)],
     )
-    share = vmem_call(
-        combine_kernel, shaped((NZ, 8 * RI, HD), bf16), (a2a(parts, "z"),)
-    )
-    heads_out = a2a(share, "z").reshape(XR * GQ, HD)
+    parts, out_weight = lax.optimization_barrier((parts, out_weight))
+    out_weights = from_x(out_weight)
+    parts, out_weights = lax.optimization_barrier((a2a(parts, "z"), out_weights))
+    share = vmem_call(combine_kernel, shaped((NZ, 8 * RI, HD), bf16), (parts,))
+    share, next_weight = lax.optimization_barrier((share, next_weight))
+    next_weights = from_x(next_weight)
+    heads_out, next_weights = lax.optimization_barrier((a2a(share, "z"), next_weights))
+    heads_out = heads_out.reshape(XR * GQ, HD)
     terms = vmem_call(
-        output_kernel, shaped((NH, XR, NX * HD), bf16), (heads_out, out_weight_x)
-    )
-    resid, products = vmem_call(
+        output_kernel, shaped((NH, XR, NX * HD), bf16), (heads_out, *out_weights)
+    )
+    *resids, products = vmem_call(
         next_kernel,
-        (shaped((NX, XR, HD), bf16), shaped((NZ, 32, HD), bf16)),
-        (a2a(terms, "heads"), hidden_x, gain_x, next_weight_x),
+        (*[shaped((XR, HD), bf16)] * NX, shaped((NZ, 32, HD), bf16)),
+        (a2a(terms, "heads"), hidden_x, gain_x, *next_weights),
         scratch=[pltpu.VMEM((NZ, 32, HD), f32)],
     )
-    resid = a2a(resid, "x")
-    hidden_out = vmem_call(reorder_kernel, shaped(hidden_rows.shape, bf16), (resid,))
+    resids = [resids[0]] + [shifted(resids[s], NX - s) for s in range(1, NX)]
+    hidden_out = vmem_call(
+        reorder_kernel, shaped(hidden_rows.shape, bf16), (x_scalar, *resids), scalars=1
+    )
     next_qkv = vmem_call(
         finish_kernel, shaped((RI, (GQ + 2) * HD), bf16), (a2a(products, "z"),)
     )

time: 196 us -> 174 us (0.89)
  starting transfers between devices: 37.5 us -> 116 us
  blocking collectives: 75.5 us -> 13.2 us
  waiting for transfers between devices: 48.3 us -> 26.6 us
  between operations: 14.3 us -> 1.1 us
  local copies, waits for them, and re-layouts: 6.53 us -> 1.14 us
    ppermute x0 -> x15, starting transfers between devices: none -> 50 us  [shifted(): return lax.ppermute(array, 'x', [(n, (n + step) % NX) for n in range(NX)])]
    all_gather x3 -> x0, blocking collectives: 42.5 us -> none  [the longest x1 16.6 us: on_device(): values_x = lax.all_gather(cache_values, 'x', axis=0)]
    all_to_all x2, waiting for transfers between devices: 21.9 us -> 0.01 us  [the longest x1 0.01 us: on_device(): a2a(parts, 'z')]
    all_to_all x2 -> x1, blocking collectives: 32.9 us -> 13.2 us  [on_device(): a2a(terms, 'heads')]
    ppermute x0 -> x15, waiting for transfers between devices: none -> 18.5 us  [shifted(): return lax.ppermute(array, 'x', [(n, (n + step) % NX) for n in range(NX)])]
    all_to_all x2, starting transfers between devices: 8.51 us -> 22.5 us  [the longest x1 12 us: on_device(): a2a(share, 'z')]
    all_to_all x1, waiting for transfers between devices: 12.9 us -> 0.01 us  [on_device(): a2a(products, 'z')]
    all_to_all x1, waiting for transfers between devices: 12 us -> 2.62 us  [on_device(): a2a(tiles, 'z')]
  transfers between devices with their start and end apart: 8 -> 21, of which waited for: 4 -> 9; matrix products, arithmetic and copies ran while one was open for 2% -> 2% of each run, Pallas kernels for 4% -> 1%
where the time goes in v2:
time: 174 us; the launch traced here: 171 us
  starting transfers between devices  116 us (67%)
  waiting for transfers between devices  26.6 us (15%)
  blocking collectives  13.2 us (8%)
  Pallas kernels  11.1 us (6%)
  other arithmetic  2.1 us (1%)
    ppermute x15, starting transfers between devices, shifted(): return lax.ppermute(array, 'x', [(n, (n + step) % NX) for n in range(NX)])  50 us
    ppermute x15, waiting for transfers between devices, shifted(): return lax.ppermute(array, 'x', [(n, (n + step) % NX) for n in range(NX)])  18.5 us
    all_to_all x1, blocking collectives, on_device(): a2a(terms, 'heads')  13.2 us
    all_to_all x1, starting transfers between devices, on_device(): a2a(tiles, 'z')  12.4 us
    all_to_all x1, starting transfers between devices, on_device(): a2a(products, 'z')  12 us
    all_to_all x1, starting transfers between devices, on_device(): a2a(share, 'z')  12 us
    pallas_call x10, Pallas kernels, vmem_call(): pl.pallas_call(kernel, out_shape=out_shape, in_specs=[small] * scalars +...  11.1 us
    all_to_all x1, starting transfers between devices, on_device(): a2a(parts, 'z')  10.5 us
  transfers between devices with their start and end apart: 21, of which 9 were waited for; matrix products, arithmetic and copies ran while one was open for 2% of the time, Pallas kernels for 1%

profile of v2, /device:TPU:6, one launch (start us, length us, event | category | flops | bytes accessed | tf_op | source)
XLA Modules:
  0.0 171.1 jit_solution(12110292308029801085)
XLA Ops:
  0.6 2.2 %shard_map.122 = bf16[4,36,16,128]{3,2,1,0:T(8,128)(2,1)} custom-call(bf16[192,128]{1,0:T(8,128)(2,1)} %hidden_hbm.1, bf16[128,1280]{1,0:T(8,128)(2,1)} %weight_hbm.1, f32[1,128]{1,0:T(1,128)} %bitcast.26), custom_call_target="tpu_custom_call" | custom-call | tf_op jit(solution)/shard_map/pallas_call | solution.py:38
  2.9 9.4 %all-to-all-start = ((bf16[4,36,16,128]{3,2,1,0:T(8,128)(2,1)}), bf16[4,36,16,128]{3,2,1,0:T(8,128)(2,1)S(1)}, u32[]{:S(2)}, u32[]{:S(2)}) async-start(bf16[4,36,16,128]{3,2,1,0:T(8,128)(2,1)} %shard_map.122), calls=%async_computation | async-start | bytes 1179648 | tf_op jit(solution)/shard_map/all_to_all | solution.py:379
  12.5 0.1 fusion.5
  12.7 0.1 select_reduce_fusion
  12.8 0.4 select_reduce_fusion.1
  13.2 0.1 slice_reduce_fusion
  13.3 0.2 reshape.240
  13.5 0.1 dynamic-slice_bitcast_fusion
  13.6 0.1 copy.20
  13.7 0.1 select_reduce_fusion.3
  13.8 0.1 add_convert_fusion
  13.9 0.1 fusion.4
  14.0 0.1 pad_maximum_fusion.3.sin_ref
  14.1 0.1 fusion.7
  14.2 0.1 pad_maximum_fusion.4.cos_ref
  14.2 0.1 fusion.2
  14.3 0.1 copy.22
  14.4 0.1 iota_add_fusion
  14.5 0.3 shard_map.124.refs_0_
  14.9 3.9 %all-to-all-done.in_ref = bf16[4,36,16,128]{3,2,1,0:T(8,128)(2,1)S(1)} async-done(((bf16[4,36,16,128]{3,2,1,0:T(8,128)(2,1)}), bf16[4,36,16,128]{3,2,1,0:T(8,128)(2,1)S(1)}, u32[]{:S(2)}, u32[]{:S(2)}) %all-to-all-start) | async-done | bytes 589856 | tf_op jit(solution)/shard_map/all_to_all | solution.py:379
  18.7 0.7 shard_map.123
  19.4 12.4 %all-to-all-start.1 = ((bf16[16,2,16,128]{3,2,1,0:T(8,128)(2,1)}), bf16[16,2,16,128]{3,2,1,0:T(8,128)(2,1)S(1)}, u32[]{:S(2)}, u32[]{:S(2)}) async-start(bf16[16,2,16,128]{3,2,1,0:T(8,128)(2,1)} %get-tuple-element.29), calls=%async_computation.1 | async-start | bytes 262144 | tf_op jit(solution)/shard_map/all_to_all | solution.py:423
  31.9 0.5 compare_reduce_fusion
  32.4 0.1 add.89
  32.5 0.1 copy.21
  32.6 0.1 gt.11
  32.7 0.1 add_select_fusion
  32.8 1.9 %collective-permute-start.2 = (bf16[12,128,128]{2,1,0:T(8,128)(2,1)S(1)}, bf16[12,128,128]{2,1,0:T(8,128)(2,1)S(1)}, u32[]{:S(2)}, u32[]{:S(2)}) collective-permute-start(bf16[12,128,128]{2,1,0:T(8,128)(2,1)S(1)} %shard_map.124.refs_0_), channel_id=1, source_target_pairs={{0,3},{1,0},{2,1},{3,2},{4,7},{5,4},{6,5},{7,6},{8,11},{9,8},{10,9... | collective-permute-start | bytes 1179656 | tf_op jit(solution)/shard_map/ppermute | solution.py:361
  34.7 5.4 %collective-permute-start.1 = (bf16[12,128,128]{2,1,0:T(8,128)(2,1)S(1)}, bf16[12,128,128]{2,1,0:T(8,128)(2,1)S(1)}, u32[]{:S(2)}, u32[]{:S(2)}) collective-permute-start(bf16[12,128,128]{2,1,0:T(8,128)(2,1)S(1)} %shard_map.124.refs_0_), channel_id=1, source_target_pairs={{0,2},{1,3},{2,0},{3,1},{4,6},{5,7},{6,4},{7,5},{8,10},{9,11},{10,... | collective-permute-start | bytes 1179656 | tf_op jit(solution)/shard_map/ppermute | solution.py:361
  40.1 3.1 %collective-permute-start = (bf16[12,128,128]{2,1,0:T(8,128)(2,1)S(1)}, bf16[12,128,128]{2,1,0:T(8,128)(2,1)S(1)}, u32[]{:S(2)}, u32[]{:S(2)}) collective-permute-start(bf16[12,128,128]{2,1,0:T(8,128)(2,1)S(1)} %shard_map.124.refs_0_), channel_id=1, source_target_pairs={{0,1},{1,2},{2,3},{3,0},{4,5},{5,6},{6,7},{7,4},{8,9},{9,10},{10,1... | collective-permute-start | bytes 1179656 | tf_op jit(solution)/shard_map/ppermute | solution.py:361
  43.2 2.6 %all-to-all-done.1.in_ref = bf16[16,2,16,128]{3,2,1,0:T(8,128)(2,1)S(1)} async-done(((bf16[16,2,16,128]{3,2,1,0:T(8,128)(2,1)}), bf16[16,2,16,128]{3,2,1,0:T(8,128)(2,1)S(1)}, u32[]{:S(2)}, u32[]{:S(2)}) %all-to-all-start.1) | async-done | bytes 131104 | tf_op jit(solution)/shard_map/all_to_all | solution.py:423
  45.8 0.8 shard_map.125
  46.6 9.4 %all-to-all-start.2 = ((bf16[16,2,16,128]{3,2,1,0:T(8,128)(2,1)}), bf16[16,2,16,128]{3,2,1,0:T(8,128)(2,1)S(1)}, u32[]{:S(2)}, u32[]{:S(2)}) async-start(bf16[16,2,16,128]{3,2,1,0:T(8,128)(2,1)} %get-tuple-element.30), calls=%async_computation.2 | async-start | bytes 262144 | tf_op jit(solution)/shard_map/all_to_all | solution.py:425
  56.0 0.1 select_n.84
  56.1 2.8 %collective-permute-start.5 = (bf16[2,16,128]{2,1,0:T(8,128)(2,1)S(1)}, bf16[2,16,128]{2,1,0:T(8,128)(2,1)S(1)}, u32[]{:S(2)}, u32[]{:S(2)}) collective-permute-start(bf16[2,16,128]{2,1,0:T(8,128)(2,1)S(1)} %get-tuple-element.32.refs_4_), channel_id=1, source_target_pairs={{0,3},{1,0},{2,1},{3,2},{4,7},{5,4},{6,5},{7,6},{8,11},{9,8},{10,9... | collective-permute-start | bytes 24584 | tf_op jit(solution)/shard_map/ppermute | solution.py:361
  58.9 2.5 %collective-permute-start.4 = (bf16[2,16,128]{2,1,0:T(8,128)(2,1)S(1)}, bf16[2,16,128]{2,1,0:T(8,128)(2,1)S(1)}, u32[]{:S(2)}, u32[]{:S(2)}) collective-permute-start(bf16[2,16,128]{2,1,0:T(8,128)(2,1)S(1)} %get-tuple-element.32.refs_4_), channel_id=1, source_target_pairs={{0,2},{1,3},{2,0},{3,1},{4,6},{5,7},{6,4},{7,5},{8,10},{9,11},{10,... | collective-permute-start | bytes 24584 | tf_op jit(solution)/shard_map/ppermute | solution.py:361
  61.5 4.5 %collective-permute-start.3 = (bf16[2,16,128]{2,1,0:T(8,128)(2,1)S(1)}, bf16[2,16,128]{2,1,0:T(8,128)(2,1)S(1)}, u32[]{:S(2)}, u32[]{:S(2)}) collective-permute-start(bf16[2,16,128]{2,1,0:T(8,128)(2,1)S(1)} %get-tuple-element.32.refs_4_), channel_id=1, source_target_pairs={{0,1},{1,2},{2,3},{3,0},{4,5},{5,6},{6,7},{7,4},{8,9},{9,10},{10,1... | collective-permute-start | bytes 24584 | tf_op jit(solution)/shard_map/ppermute | solution.py:361
  66.0 0.1 copy.24
  66.1 1.5 collective-permute-done.3.refs_5_
  67.6 1.7 all-to-all-done.2.queries_ref
  69.3 3.1 %shard_map.126 = bf16[16,32,128]{2,1,0:T(8,128)(2,1)} custom-call(bf16[16,2,16,128]{3,2,1,0:T(8,128)(2,1)S(1)} %all-to-all-done.2.queries_ref, s32[25,128]{1,0:T(8,128)S(1)} %pad_add_fusion.keypos_ref, s32[3,16,128]{2,1,0:T(8,128)S(1)} %broadcast_in_dim.95.rowpos_ref, bf16[12,128,128]{2,1,0:T(8,128)(2,1)S(1)} %shard_map.124.refs_0_, ...), custom_call_target="tpu_custom_call" | custom-call | tf_op jit(solution)/shard_map/pallas_call | solution.py:38
  72.5 10.5 %all-to-all-start.3 = ((bf16[16,32,128]{2,1,0:T(8,128)(2,1)}), bf16[16,32,128]{2,1,0:T(8,128)(2,1)S(1)}, u32[]{:S(2)}, u32[]{:S(2)}) async-start(bf16[16,32,128]{2,1,0:T(8,128)(2,1)} %shard_map.126), calls=%async_computation.3 | async-start | bytes 262144 | tf_op jit(solution)/shard_map/all_to_all | solution.py:435
  83.0 3.9 %collective-permute-start.8 = (bf16[1024,128]{1,0:T(8,128)(2,1)S(1)}, bf16[1024,128]{1,0:T(8,128)(2,1)S(1)}, u32[]{:S(2)}, u32[]{:S(2)}) collective-permute-start(bf16[1024,128]{1,0:T(8,128)(2,1)S(1)} %copy-done.1), channel_id=1, source_target_pairs={{0,3},{1,0},{2,1},{3,2},{4,7},{5,4},{6,5},{7,6},{8,11},{9,8},{10,9... | collective-permute-start | bytes 786440 | tf_op jit(solution)/shard_map/ppermute | solution.py:361
  86.9 4.6 %collective-permute-start.7 = (bf16[1024,128]{1,0:T(8,128)(2,1)S(1)}, bf16[1024,128]{1,0:T(8,128)(2,1)S(1)}, u32[]{:S(2)}, u32[]{:S(2)}) collective-permute-start(bf16[1024,128]{1,0:T(8,128)(2,1)S(1)} %copy-done.1), channel_id=1, source_target_pairs={{0,2},{1,3},{2,0},{3,1},{4,6},{5,7},{6,4},{7,5},{8,10},{9,11},{10,... | collective-permute-start | bytes 786440 | tf_op jit(solution)/shard_map/ppermute | solution.py:361
  91.5 2.2 %collective-permute-start.6 = (bf16[1024,128]{1,0:T(8,128)(2,1)S(1)}, bf16[1024,128]{1,0:T(8,128)(2,1)S(1)}, u32[]{:S(2)}, u32[]{:S(2)}) collective-permute-start(bf16[1024,128]{1,0:T(8,128)(2,1)S(1)} %copy-done.1), channel_id=1, source_target_pairs={{0,1},{1,2},{2,3},{3,0},{4,5},{5,6},{6,7},{7,4},{8,9},{9,10},{10,1... | collective-permute-start | bytes 786440 | tf_op jit(solution)/shard_map/ppermute | solution.py:361
  93.7 3.0 %collective-permute-done.7.refs_2_ = bf16[1024,128]{1,0:T(8,128)(2,1)S(1)} collective-permute-done((bf16[1024,128]{1,0:T(8,128)(2,1)S(1)}, bf16[1024,128]{1,0:T(8,128)(2,1)S(1)}, u32[]{:S(2)}, u32[]{:S(2)}) %collective-permute-start.7) | collective-permute-done | bytes 262176 | tf_op jit(solution)/shard_map/ppermute | solution.py:361
  96.7 3.0 %collective-permute-done.6.refs_1_ = bf16[1024,128]{1,0:T(8,128)(2,1)S(1)} collective-permute-done((bf16[1024,128]{1,0:T(8,128)(2,1)S(1)}, bf16[1024,128]{1,0:T(8,128)(2,1)S(1)}, u32[]{:S(2)}, u32[]{:S(2)}) %collective-permute-start.6) | collective-permute-done | bytes 262176 | tf_op jit(solution)/shard_map/ppermute | solution.py:361
  99.8 0.9 shard_map.127
  100.7 12.0 %all-to-all-start.4 = ((bf16[16,24,128]{2,1,0:T(8,128)(2,1)}), bf16[16,24,128]{2,1,0:T(8,128)(2,1)S(1)}, u32[]{:S(2)}, u32[]{:S(2)}) async-start(bf16[16,24,128]{2,1,0:T(8,128)(2,1)} %shard_map.127), calls=%async_computation.4 | async-start | bytes 196608 | tf_op jit(solution)/shard_map/all_to_all | solution.py:439
  112.7 1.9 %collective-permute-start.11 = (bf16[128,1280]{1,0:T(8,128)(2,1)S(1)}, bf16[128,1280]{1,0:T(8,128)(2,1)S(1)}, u32[]{:S(2)}, u32[]{:S(2)}) collective-permute-start(bf16[128,1280]{1,0:T(8,128)(2,1)S(1)} %copy-done), channel_id=1, source_target_pairs={{0,3},{1,0},{2,1},{3,2},{4,7},{5,4},{6,5},{7,6},{8,11},{9,8},{10,9... | collective-permute-start | bytes 983048 | tf_op jit(solution)/shard_map/ppermute | solution.py:361
  114.7 4.8 %collective-permute-start.10 = (bf16[128,1280]{1,0:T(8,128)(2,1)S(1)}, bf16[128,1280]{1,0:T(8,128)(2,1)S(1)}, u32[]{:S(2)}, u32[]{:S(2)}) collective-permute-start(bf16[128,1280]{1,0:T(8,128)(2,1)S(1)} %copy-done), channel_id=1, source_target_pairs={{0,2},{1,3},{2,0},{3,1},{4,6},{5,7},{6,4},{7,5},{8,10},{9,11},{10,... | collective-permute-start | bytes 983048 | tf_op jit(solution)/shard_map/ppermute | solution.py:361
  119.5 2.5 %collective-permute-start.9 = (bf16[128,1280]{1,0:T(8,128)(2,1)S(1)}, bf16[128,1280]{1,0:T(8,128)(2,1)S(1)}, u32[]{:S(2)}, u32[]{:S(2)}) collective-permute-start(bf16[128,1280]{1,0:T(8,128)(2,1)S(1)} %copy-done), channel_id=1, source_target_pairs={{0,1},{1,2},{2,3},{3,0},{4,5},{5,6},{6,7},{7,4},{8,9},{9,10},{10,1... | collective-permute-start | bytes 983048 | tf_op jit(solution)/shard_map/ppermute | solution.py:361
  122.0 4.5 %collective-permute-done.11.refs_3_ = bf16[128,1280]{1,0:T(8,128)(2,1)S(1)} collective-permute-done((bf16[128,1280]{1,0:T(8,128)(2,1)S(1)}, bf16[128,1280]{1,0:T(8,128)(2,1)S(1)}, u32[]{:S(2)}, u32[]{:S(2)}) %collective-permute-start.11) | collective-permute-done | bytes 327712 | tf_op jit(solution)/shard_map/ppermute | solution.py:361
  126.4 2.8 %collective-permute-done.9.refs_1_ = bf16[128,1280]{1,0:T(8,128)(2,1)S(1)} collective-permute-done((bf16[128,1280]{1,0:T(8,128)(2,1)S(1)}, bf16[128,1280]{1,0:T(8,128)(2,1)S(1)}, u32[]{:S(2)}, u32[]{:S(2)}) %collective-permute-start.9) | collective-permute-done | bytes 327712 | tf_op jit(solution)/shard_map/ppermute | solution.py:361
  129.2 0.3 shard_map.128
  129.5 13.2 %all_to_all.35.terms_ref = bf16[8,48,512]{2,1,0:T(8,128)(2,1)S(1)} all-to-all(bf16[8,48,512]{2,1,0:T(8,128)(2,1)S(1)} %shard_map.128), channel_id=1, replica_groups=mesh['heads'=8,'z'=16,'x'=4] {'heads'}, dimensions={0} | all-to-all | bytes 786432 | tf_op jit(solution)/shard_map/all_to_all | solution.py:447
  142.7 1.1 shard_map.129
  143.8 12.0 %all-to-all-start.6 = ((bf16[16,32,128]{2,1,0:T(8,128)(2,1)}), bf16[16,32,128]{2,1,0:T(8,128)(2,1)S(1)}, u32[]{:S(2)}, u32[]{:S(2)}) async-start(bf16[16,32,128]{2,1,0:T(8,128)(2,1)} %get-tuple-element.53), calls=%async_computation.6 | async-start | bytes 262144 | tf_op jit(solution)/shard_map/all_to_all | solution.py:455
  155.8 2.3 %collective-permute-start.12 = (bf16[48,128]{1,0:T(8,128)(2,1)S(1)}, bf16[48,128]{1,0:T(8,128)(2,1)S(1)}, u32[]{:S(2)}, u32[]{:S(2)}) collective-permute-start(bf16[48,128]{1,0:T(8,128)(2,1)S(1)} %get-tuple-element.50), channel_id=1, source_target_pairs={{0,3},{1,0},{2,1},{3,2},{4,7},{5,4},{6,5},{7,6},{8,11},{9,8},{10,9... | collective-permute-start | bytes 36872 | tf_op jit(solution)/shard_map/ppermute | solution.py:361
  158.2 5.6 %collective-permute-start.13 = (bf16[48,128]{1,0:T(8,128)(2,1)S(1)}, bf16[48,128]{1,0:T(8,128)(2,1)S(1)}, u32[]{:S(2)}, u32[]{:S(2)}) collective-permute-start(bf16[48,128]{1,0:T(8,128)(2,1)S(1)} %get-tuple-element.51), channel_id=1, source_target_pairs={{0,2},{1,3},{2,0},{3,1},{4,6},{5,7},{6,4},{7,5},{8,10},{9,11},{10,... | collective-permute-start | bytes 36872 | tf_op jit(solution)/shard_map/ppermute | solution.py:361
  163.8 1.9 %collective-permute-start.14 = (bf16[48,128]{1,0:T(8,128)(2,1)S(1)}, bf16[48,128]{1,0:T(8,128)(2,1)S(1)}, u32[]{:S(2)}, u32[]{:S(2)}) collective-permute-start(bf16[48,128]{1,0:T(8,128)(2,1)S(1)} %get-tuple-element.52), channel_id=1, source_target_pairs={{0,1},{1,2},{2,3},{3,0},{4,5},{5,6},{6,7},{7,4},{8,9},{9,10},{10,1... | collective-permute-start | bytes 36872 | tf_op jit(solution)/shard_map/ppermute | solution.py:361
  165.7 3.6 %collective-permute-done.14.refs_3_ = bf16[48,128]{1,0:T(8,128)(2,1)S(1)} collective-permute-done((bf16[48,128]{1,0:T(8,128)(2,1)S(1)}, bf16[48,128]{1,0:T(8,128)(2,1)S(1)}, u32[]{:S(2)}, u32[]{:S(2)}) %collective-permute-start.14) | collective-permute-done | bytes 12320 | tf_op jit(solution)/shard_map/ppermute | solution.py:361
  169.4 0.9 shard_map.130
  170.3 0.8 shard_map.131
  (49 shorter events, 0.4 us)
Async XLA Ops:
  2.8 9.6 %copy-start.8 = (s32[128]{0:T(128)S(1)}, s32[128]{0:T(128)}, u32[]{:S(2)}) copy-start(s32[128]{0:T(128)} %param.18) | copy-start | bytes 1540
  2.9 9.6 %copy-start.6 = (s32[128]{0:T(128)S(1)}, s32[128]{0:T(128)}, u32[]{:S(2)}) copy-start(s32[128]{0:T(128)} %param.19) | copy-start | bytes 1540
  2.9 9.9 %copy-start.7 = (s32[128]{0:T(128)S(1)}, s32[128]{0:T(128)}, u32[]{:S(2)}) copy-start(s32[128]{0:T(128)} %param.20) | copy-start | bytes 1540
  2.9 10.5 %copy-start.5 = (s32[192]{0:T(256)S(1)}, s32[192]{0:T(256)}, u32[]{:S(2)}) copy-start(s32[192]{0:T(256)} %param.21) | copy-start | bytes 2308
  2.9 11.6 %copy-start.2 = (bf16[768,128]{1,0:T(8,128)(2,1)S(1)}, bf16[768,128]{1,0:T(8,128)(2,1)}, u32[]{:S(2)}) copy-start(bf16[768,128]{1,0:T(8,128)(2,1)} %keys_ref.1) | copy-start | bytes 589828
  2.9 11.6 %copy-start.3 = (bf16[768,128]{1,0:T(8,128)(2,1)S(1)}, bf16[768,128]{1,0:T(8,128)(2,1)}, u32[]{:S(2)}) copy-start(bf16[768,128]{1,0:T(8,128)(2,1)} %values_ref.1) | copy-start | bytes 589828
  2.9 15.8 %all-to-all-start = ((bf16[4,36,16,128]{3,2,1,0:T(8,128)(2,1)}), bf16[4,36,16,128]{3,2,1,0:T(8,128)(2,1)S(1)}, u32[]{:S(2)}, u32[]{:S(2)}) async-start(bf16[4,36,16,128]{3,2,1,0:T(8,128)(2,1)} %shard_map.122), calls=%async_computation | async-start | bytes 1179648 | tf_op jit(solution)/shard_map/all_to_all | solution.py:379
  12.7 2.2 %copy-start.4 = (f32[1,2,16,128]{3,2,1,0:T(8,128)S(1)}, f32[1,2,16,128]{3,2,1,0:T(8,128)}, u32[]{:S(2)}) copy-start(f32[1,2,16,128]{3,2,1,0:T(8,128)} %constant.84.clone.1) | copy-start | bytes 49156
  19.4 26.4 %all-to-all-start.1 = ((bf16[16,2,16,128]{3,2,1,0:T(8,128)(2,1)}), bf16[16,2,16,128]{3,2,1,0:T(8,128)(2,1)S(1)}, u32[]{:S(2)}, u32[]{:S(2)}) async-start(bf16[16,2,16,128]{3,2,1,0:T(8,128)(2,1)} %get-tuple-element.29), calls=%async_computation.1 | async-start | bytes 262144 | tf_op jit(solution)/shard_map/all_to_all | solution.py:423
  32.8 28.7 %collective-permute-start.2 = (bf16[12,128,128]{2,1,0:T(8,128)(2,1)S(1)}, bf16[12,128,128]{2,1,0:T(8,128)(2,1)S(1)}, u32[]{:S(2)}, u32[]{:S(2)}) collective-permute-start(bf16[12,128,128]{2,1,0:T(8,128)(2,1)S(1)} %shard_map.124.refs_0_), channel_id=1, source_target_pairs={{0,3},{1,0},{2,1},{3,2},{4,7},{5,4},{6,5},{7,6},{8,11},{9,8},{10,9... | collective-permute-start | bytes 1179656 | tf_op jit(solution)/shard_map/ppermute | solution.py:361
  34.7 31.4 %collective-permute-start.1 = (bf16[12,128,128]{2,1,0:T(8,128)(2,1)S(1)}, bf16[12,128,128]{2,1,0:T(8,128)(2,1)S(1)}, u32[]{:S(2)}, u32[]{:S(2)}) collective-permute-start(bf16[12,128,128]{2,1,0:T(8,128)(2,1)S(1)} %shard_map.124.refs_0_), channel_id=1, source_target_pairs={{0,2},{1,3},{2,0},{3,1},{4,6},{5,7},{6,4},{7,5},{8,10},{9,11},{10,... | collective-permute-start | bytes 1179656 | tf_op jit(solution)/shard_map/ppermute | solution.py:361
  40.1 26.0 %collective-permute-start = (bf16[12,128,128]{2,1,0:T(8,128)(2,1)S(1)}, bf16[12,128,128]{2,1,0:T(8,128)(2,1)S(1)}, u32[]{:S(2)}, u32[]{:S(2)}) collective-permute-start(bf16[12,128,128]{2,1,0:T(8,128)(2,1)S(1)} %shard_map.124.refs_0_), channel_id=1, source_target_pairs={{0,1},{1,2},{2,3},{3,0},{4,5},{5,6},{6,7},{7,4},{8,9},{9,10},{10,1... | collective-permute-start | bytes 1179656 | tf_op jit(solution)/shard_map/ppermute | solution.py:361
  46.6 22.7 %all-to-all-start.2 = ((bf16[16,2,16,128]{3,2,1,0:T(8,128)(2,1)}), bf16[16,2,16,128]{3,2,1,0:T(8,128)(2,1)S(1)}, u32[]{:S(2)}, u32[]{:S(2)}) async-start(bf16[16,2,16,128]{3,2,1,0:T(8,128)(2,1)} %get-tuple-element.30), calls=%async_computation.2 | async-start | bytes 262144 | tf_op jit(solution)/shard_map/all_to_all | solution.py:425
  56.1 10.0 %collective-permute-start.5 = (bf16[2,16,128]{2,1,0:T(8,128)(2,1)S(1)}, bf16[2,16,128]{2,1,0:T(8,128)(2,1)S(1)}, u32[]{:S(2)}, u32[]{:S(2)}) collective-permute-start(bf16[2,16,128]{2,1,0:T(8,128)(2,1)S(1)} %get-tuple-element.32.refs_4_), channel_id=1, source_target_pairs={{0,3},{1,0},{2,1},{3,2},{4,7},{5,4},{6,5},{7,6},{8,11},{9,8},{10,9... | collective-permute-start | bytes 24584 | tf_op jit(solution)/shard_map/ppermute | solution.py:361
  58.9 7.2 %collective-permute-start.4 = (bf16[2,16,128]{2,1,0:T(8,128)(2,1)S(1)}, bf16[2,16,128]{2,1,0:T(8,128)(2,1)S(1)}, u32[]{:S(2)}, u32[]{:S(2)}) collective-permute-start(bf16[2,16,128]{2,1,0:T(8,128)(2,1)S(1)} %get-tuple-element.32.refs_4_), channel_id=1, source_target_pairs={{0,2},{1,3},{2,0},{3,1},{4,6},{5,7},{6,4},{7,5},{8,10},{9,11},{10,... | collective-permute-start | bytes 24584 | tf_op jit(solution)/shard_map/ppermute | solution.py:361
  61.5 6.2 %collective-permute-start.3 = (bf16[2,16,128]{2,1,0:T(8,128)(2,1)S(1)}, bf16[2,16,128]{2,1,0:T(8,128)(2,1)S(1)}, u32[]{:S(2)}, u32[]{:S(2)}) collective-permute-start(bf16[2,16,128]{2,1,0:T(8,128)(2,1)S(1)} %get-tuple-element.32.refs_4_), channel_id=1, source_target_pairs={{0,1},{1,2},{2,3},{3,0},{4,5},{5,6},{6,7},{7,4},{8,9},{9,10},{10,1... | collective-permute-start | bytes 24584 | tf_op jit(solution)/shard_map/ppermute | solution.py:361
  69.3 13.6 %copy-start.1 = (bf16[1024,128]{1,0:T(8,128)(2,1)S(1)}, bf16[1024,128]{1,0:T(8,128)(2,1)}, u32[]{:S(2)}) copy-start(bf16[1024,128]{1,0:T(8,128)(2,1)} %refs_0_) | copy-start | bytes 786436
  72.5 40.2 %copy-start = (bf16[128,1280]{1,0:T(8,128)(2,1)S(1)}, bf16[128,1280]{1,0:T(8,128)(2,1)}, u32[]{:S(2)}) copy-start(bf16[128,1280]{1,0:T(8,128)(2,1)} %refs_0_.1) | copy-start | bytes 983044
  72.5 27.3 %all-to-all-start.3 = ((bf16[16,32,128]{2,1,0:T(8,128)(2,1)}), bf16[16,32,128]{2,1,0:T(8,128)(2,1)S(1)}, u32[]{:S(2)}, u32[]{:S(2)}) async-start(bf16[16,32,128]{2,1,0:T(8,128)(2,1)} %shard_map.126), calls=%async_computation.3 | async-start | bytes 262144 | tf_op jit(solution)/shard_map/all_to_all | solution.py:435
  83.0 10.7 %collective-permute-start.8 = (bf16[1024,128]{1,0:T(8,128)(2,1)S(1)}, bf16[1024,128]{1,0:T(8,128)(2,1)S(1)}, u32[]{:S(2)}, u32[]{:S(2)}) collective-permute-start(bf16[1024,128]{1,0:T(8,128)(2,1)S(1)} %copy-done.1), channel_id=1, source_target_pairs={{0,3},{1,0},{2,1},{3,2},{4,7},{5,4},{6,5},{7,6},{8,11},{9,8},{10,9... | collective-permute-start | bytes 786440 | tf_op jit(solution)/shard_map/ppermute | solution.py:361
  86.9 9.8 %collective-permute-start.7 = (bf16[1024,128]{1,0:T(8,128)(2,1)S(1)}, bf16[1024,128]{1,0:T(8,128)(2,1)S(1)}, u32[]{:S(2)}, u32[]{:S(2)}) collective-permute-start(bf16[1024,128]{1,0:T(8,128)(2,1)S(1)} %copy-done.1), channel_id=1, source_target_pairs={{0,2},{1,3},{2,0},{3,1},{4,6},{5,7},{6,4},{7,5},{8,10},{9,11},{10,... | collective-permute-start | bytes 786440 | tf_op jit(solution)/shard_map/ppermute | solution.py:361
  91.5 8.3 %collective-permute-start.6 = (bf16[1024,128]{1,0:T(8,128)(2,1)S(1)}, bf16[1024,128]{1,0:T(8,128)(2,1)S(1)}, u32[]{:S(2)}, u32[]{:S(2)}) collective-permute-start(bf16[1024,128]{1,0:T(8,128)(2,1)S(1)} %copy-done.1), channel_id=1, source_target_pairs={{0,1},{1,2},{2,3},{3,0},{4,5},{5,6},{6,7},{7,4},{8,9},{9,10},{10,1... | collective-permute-start | bytes 786440 | tf_op jit(solution)/shard_map/ppermute | solution.py:361
  100.7 28.5 %all-to-all-start.4 = ((bf16[16,24,128]{2,1,0:T(8,128)(2,1)}), bf16[16,24,128]{2,1,0:T(8,128)(2,1)S(1)}, u32[]{:S(2)}, u32[]{:S(2)}) async-start(bf16[16,24,128]{2,1,0:T(8,128)(2,1)} %shard_map.127), calls=%async_computation.4 | async-start | bytes 196608 | tf_op jit(solution)/shard_map/all_to_all | solution.py:439
  112.7 13.7 %collective-permute-start.11 = (bf16[128,1280]{1,0:T(8,128)(2,1)S(1)}, bf16[128,1280]{1,0:T(8,128)(2,1)S(1)}, u32[]{:S(2)}, u32[]{:S(2)}) collective-permute-start(bf16[128,1280]{1,0:T(8,128)(2,1)S(1)} %copy-done), channel_id=1, source_target_pairs={{0,3},{1,0},{2,1},{3,2},{4,7},{5,4},{6,5},{7,6},{8,11},{9,8},{10,9... | collective-permute-start | bytes 983048 | tf_op jit(solution)/shard_map/ppermute | solution.py:361
  114.7 11.8 %collective-permute-start.10 = (bf16[128,1280]{1,0:T(8,128)(2,1)S(1)}, bf16[128,1280]{1,0:T(8,128)(2,1)S(1)}, u32[]{:S(2)}, u32[]{:S(2)}) collective-permute-start(bf16[128,1280]{1,0:T(8,128)(2,1)S(1)} %copy-done), channel_id=1, source_target_pairs={{0,2},{1,3},{2,0},{3,1},{4,6},{5,7},{6,4},{7,5},{8,10},{9,11},{10,... | collective-permute-start | bytes 983048 | tf_op jit(solution)/shard_map/ppermute | solution.py:361
  119.5 9.7 %collective-permute-start.9 = (bf16[128,1280]{1,0:T(8,128)(2,1)S(1)}, bf16[128,1280]{1,0:T(8,128)(2,1)S(1)}, u32[]{:S(2)}, u32[]{:S(2)}) collective-permute-start(bf16[128,1280]{1,0:T(8,128)(2,1)S(1)} %copy-done), channel_id=1, source_target_pairs={{0,1},{1,2},{2,3},{3,0},{4,5},{5,6},{6,7},{7,4},{8,9},{9,10},{10,1... | collective-permute-start | bytes 983048 | tf_op jit(solution)/shard_map/ppermute | solution.py:361
  143.8 26.5 %all-to-all-start.6 = ((bf16[16,32,128]{2,1,0:T(8,128)(2,1)}), bf16[16,32,128]{2,1,0:T(8,128)(2,1)S(1)}, u32[]{:S(2)}, u32[]{:S(2)}) async-start(bf16[16,32,128]{2,1,0:T(8,128)(2,1)} %get-tuple-element.53), calls=%async_computation.6 | async-start | bytes 262144 | tf_op jit(solution)/shard_map/all_to_all | solution.py:455
  155.8 9.9 %collective-permute-start.12 = (bf16[48,128]{1,0:T(8,128)(2,1)S(1)}, bf16[48,128]{1,0:T(8,128)(2,1)S(1)}, u32[]{:S(2)}, u32[]{:S(2)}) collective-permute-start(bf16[48,128]{1,0:T(8,128)(2,1)S(1)} %get-tuple-element.50), channel_id=1, source_target_pairs={{0,3},{1,0},{2,1},{3,2},{4,7},{5,4},{6,5},{7,6},{8,11},{9,8},{10,9... | collective-permute-start | bytes 36872 | tf_op jit(solution)/shard_map/ppermute | solution.py:361
  158.2 7.6 %collective-permute-start.13 = (bf16[48,128]{1,0:T(8,128)(2,1)S(1)}, bf16[48,128]{1,0:T(8,128)(2,1)S(1)}, u32[]{:S(2)}, u32[]{:S(2)}) collective-permute-start(bf16[48,128]{1,0:T(8,128)(2,1)S(1)} %get-tuple-element.51), channel_id=1, source_target_pairs={{0,2},{1,3},{2,0},{3,1},{4,6},{5,7},{6,4},{7,5},{8,10},{9,11},{10,... | collective-permute-start | bytes 36872 | tf_op jit(solution)/shard_map/ppermute | solution.py:361
  163.8 5.6 %collective-permute-start.14 = (bf16[48,128]{1,0:T(8,128)(2,1)S(1)}, bf16[48,128]{1,0:T(8,128)(2,1)S(1)}, u32[]{:S(2)}, u32[]{:S(2)}) collective-permute-start(bf16[48,128]{1,0:T(8,128)(2,1)S(1)} %get-tuple-element.52), channel_id=1, source_target_pairs={{0,1},{1,2},{2,3},{3,0},{4,5},{5,6},{6,7},{7,4},{8,9},{9,10},{10,1... | collective-permute-start | bytes 36872 | tf_op jit(solution)/shard_map/ppermute | solution.py:361

commit v3 on v2

--- a/solution.py
+++ b/solution.py
@@ -15,9 +15,13 @@
 NZ = 16
 NX = 4
 NH = 8
+FRESH = 16
 RI = 3
 XR = NZ * RI
 TILE = 16
+QT = RI * GQ
+KT = 2 * NX * RI
+HT = QT + KT
 GROUPS = ("z", "x")
 theta_base = 500000.0
 epsilon = 1e-05
@@ -68,7 +72,7 @@
     return jnp.concatenate([cosine, cosine], -1), jnp.concatenate([-sine, sine], -1)
 
 
-def rotate_kernel(keys_ref, values_ref, cos_ref, sin_ref, out_ref):
+def bundle_kernel(keys_ref, values_ref, cos_ref, sin_ref, out_weight_ref, next_weight_ref, out_ref, weights_ref):
     blocks = keys_ref.shape[0] // BLK
     for b in range(blocks):
         out_ref[blocks + b] = values_ref[b * BLK : (b + 1) * BLK, :]
@@ -79,6 +83,10 @@
         )
         turned = turned.astype(bf16).astype(f32)
         out_ref[b] = turned.T.astype(bf16)
+    for g in range(GQ):
+        weights_ref[g] = out_weight_ref[g * HD : (g + 1) * HD, :]
+    for j in range(GQ + 2):
+        weights_ref[GQ + j] = next_weight_ref[:, j * HD : (j + 1) * HD]
 
 
 def project_kernel(hidden_hbm, weight_hbm, gain_hbm, out_ref, hidden_ref, weight_ref, gain_ref, sems):
@@ -105,60 +113,68 @@
     gain = jnp.where(
         sub == 0, high, jnp.where(sub == 1, middle, jnp.where(sub == 2, low, 0.0))
     ).astype(bf16)
-    zero = jnp.zeros((TILE, HD), bf16)
     copies[2].wait()
     for x in range(NX):
         part = moved[x * XR : (x + 1) * XR, :]
         product = jnp.dot(part, weight_ref[...], preferred_element_type=f32).astype(bf16)
         for i in range(RI):
             band = product[i * TILE : (i + 1) * TILE, :]
-            for j in range(GQ + 2):
-                slot = 2 * (i * 4) + j if j < GQ else 2 * (12 + i) + (j - GQ)
-                out_ref[x, slot] = band[:, j * HD : (j + 1) * HD]
-            out_ref[x, 32 + i] = part[i * TILE : (i + 1) * TILE, :]
-        out_ref[x, 30] = zero
-        out_ref[x, 31] = zero
-        out_ref[x, 35] = gain
-
-
-def sum_x_kernel(x_ref, in_ref, tiles_ref, hidden_ref, gain_ref):
-    for t in range(32):
-        total = in_ref[0, t].astype(f32)
+            for j in range(GQ):
+                out_ref[x, i * GQ + j] = band[:, j * HD : (j + 1) * HD]
+            for j in range(2):
+                tile = band[:, (GQ + j) * HD : (GQ + j + 1) * HD]
+                for to in range(NX):
+                    out_ref[to, QT + j * NX * RI + x * RI + i] = tile
+            out_ref[x, HT + i] = part[i * TILE : (i + 1) * TILE, :]
+        out_ref[x, HT + RI] = gain
+
+
+def sum_x_kernel(x_ref, in_ref, tiles_ref, hidden_ref, gain_ref, cut_ref):
+    def total(t):
+        result = in_ref[0, t].astype(f32)
         for x in range(1, NX):
-            total = total + in_ref[x, t].astype(f32)
-        tiles_ref[t // 2, t % 2] = total.astype(bf16)
+            result = result + in_ref[x, t].astype(f32)
+        return result
+
+    for k in range(KT):
+        cut_ref[:, k, :] = total(QT + k)
+    rows = [total(t) for t in range(QT)]
+    halves = [row[h * 8 : (h + 1) * 8, :] for row in rows for h in range(2)]
+    for z in range(NZ):
+        block = halves[z * RI : (z + 1) * RI] + [cut_ref[z]]
+        tiles_ref[z] = jnp.concatenate(block, axis=0).astype(bf16)
     for s in range(NX):
         src = (x_ref[0] + NX - s) % NX
         for i in range(RI):
-            hidden_ref[s, i] = in_ref[src, 32 + i]
-        pieces = in_ref[src, 35].astype(f32)
+            hidden_ref[s, i] = in_ref[src, HT + i]
+        pieces = in_ref[src, HT + RI].astype(f32)
         gain_ref[s : s + 1, :] = pieces[0:1] + pieces[1:2] + pieces[2:3]
 
 
-def rope_kernel(in_ref, factors_ref, copies_ref, own_ref):
-    for s in range(2):
-        total = in_ref[0, s].astype(f32)
-        for z in range(1, NZ):
-            total = total + in_ref[z, s].astype(f32)
-        turned = total * factors_ref[s, 0] + pltpu.roll(total, HD // 2, 1) * factors_ref[s, 1]
-        turned = turned.astype(bf16)
-        own_ref[s] = turned
-        for z in range(NZ):
-            copies_ref[z, s] = turned
-
-
-def attend_kernel(queries_ref, keypos_ref, rowpos_ref, *refs):
-    cache_refs, new_refs, (out_ref, score_ref) = refs[:NX], refs[NX : 2 * NX], refs[2 * NX :]
+def rope_kernel(in_ref, cos_ref, sin_ref, copies_ref, new_ref):
+    total = in_ref[0].astype(f32)
+    for z in range(1, NZ):
+        total = total + in_ref[z].astype(f32)
+    turned = total * cos_ref[...] + pltpu.roll(total, HD // 2, 1) * sin_ref[...]
+    queries = turned[: 8 * RI, :].astype(bf16)
+    for z in range(NZ):
+        copies_ref[z] = queries
+    new = turned[8 * RI :, :]
+    pad = jnp.zeros((FRESH - NX * RI, HD), f32)
+    new_ref[0] = jnp.concatenate([new[: NX * RI, :], pad], axis=0).astype(bf16)
+    new_ref[1] = jnp.concatenate([new[NX * RI :, :], pad], axis=0).astype(bf16)
+
+
+def attend_kernel(queries_ref, keypos_ref, rowpos_ref, new_ref, *refs):
+    cache_refs, (out_ref, score_ref) = refs[:NX], refs[NX:]
     blocks = cache_refs[0].shape[0] // 2
     scale = HD ** (-0.5) * LOG2E
     contract_last = (((1,), (1,)), ((), ()))
-    new_keys = jnp.concatenate([ref[0] for ref in new_refs], axis=0)
-    new_values = jnp.concatenate([ref[1] for ref in new_refs], axis=0)
+    new_keys, new_values = new_ref[0], new_ref[1]
     fresh = new_keys.shape[0]
+    every = queries_ref[...]
     for i in range(RI):
-        queries = jnp.concatenate(
-            [queries_ref[4 * i + g // 2, g % 2] for g in range(GQ)], axis=0
-        )
+        queries = every[i * HD : (i + 1) * HD, :]
         row_pos = jnp.concatenate([rowpos_ref[i]] * GQ, axis=0)
         peak = jnp.full((HD, BLK), least_peak, f32)
         for x in range(NX):
@@ -240,7 +256,7 @@
 
 
 def output_kernel(heads_ref, *refs):
-    weight_refs, out_ref = refs[:NX], refs[NX]
+    weight_refs, out_ref = [ref.at[pl.ds(0, GQ)] for ref in refs[:NX]], refs[NX]
     rows = heads_ref[...]
     bands = []
     for i in range(RI):
@@ -250,25 +266,27 @@
         )
     attended = jnp.concatenate(bands, axis=0)
     for x in range(NX):
-        term = jnp.dot(attended, weight_refs[x][...], preferred_element_type=f32).astype(bf16)
+        term = jnp.dot(attended, weight_refs[x][...].reshape(GQ * HD, HD), preferred_element_type=f32).astype(bf16)
         for h in range(NH):
             out_ref[h, :, x * HD : (x + 1) * HD] = term
 
 
 def next_kernel(terms_ref, hidden_ref, gain_ref, *refs):
-    weight_refs, resid_refs, (out_ref, cut_ref) = refs[:NX], refs[NX : 2 * NX], refs[2 * NX :]
+    weight_refs = [ref.at[pl.ds(GQ, GQ + 2)] for ref in refs[:NX]]
+    resid_refs, (out_ref, cut_ref) = refs[NX : 2 * NX], refs[2 * NX :]
     attended = terms_ref[0].astype(f32)
     for h in range(1, NH):
         attended = attended + terms_ref[h].astype(f32)
     squares = jnp.zeros((XR, 1), f32)
-    product = jnp.zeros((XR, weight_refs[0].shape[1]), f32)
+    product = jnp.zeros((XR, (GQ + 2) * HD), f32)
     for x in range(NX):
         before = jnp.concatenate([hidden_ref[x, i] for i in range(RI)], axis=0).astype(f32)
         resid = before + attended[:, x * HD : (x + 1) * HD]
         resid_refs[x][...] = resid.astype(bf16)
         squares = squares + jnp.sum(resid * resid, axis=1, keepdims=True)
         gained = (resid * gain_ref[x : x + 1, :]).astype(bf16)
-        product = product + jnp.dot(gained, weight_refs[x][...], preferred_element_type=f32)
+        weight = jnp.concatenate([weight_refs[x][j] for j in range(GQ + 2)], axis=1)
+        product = product + jnp.dot(gained, weight, preferred_element_type=f32)
     for i in range(RI):
         for j in range(GQ + 2):
             cut_ref[:, i * (GQ + 2) + j, :] = product[
@@ -360,12 +378,12 @@
     def shifted(array, step):
         return lax.ppermute(array, "x", [(n, (n + step) % NX) for n in range(NX)])
 
-    def from_x(array):
-        return [array] + [shifted(array, step) for step in range(1, NX)]
+    def after(array, first):
+        return lax.optimization_barrier((array, first))[0]
 
     payload = vmem_call(
         project_kernel,
-        shaped((NX, 36, TILE, HD), bf16),
+        shaped((NX, HT + RI + 1, TILE, HD), bf16),
         (hidden_rows, qkv_weight, norm_gain.reshape(1, HD)),
         scratch=[
             pltpu.VMEM(hidden_rows.shape, bf16),
@@ -382,69 +400,64 @@
     shift, key_pos = key_layout(
         z * NX + sources, group_lengths, group_owner, group_start, listed_rows, blocks
     )
-    by_xiz = listed_rows.reshape(NZ, NX, RI).transpose(1, 2, 0)
-    row_pos = lax.dynamic_slice_in_dim(by_xiz, x, 1, axis=0)[0]
-    tile_row = jnp.where(z < 12, z // 4, jnp.minimum(z - 12, RI - 1))
-    tile_pos = lax.dynamic_slice_in_dim(by_xiz, tile_row, 1, axis=1)[:, 0]
-    tile_pos = jnp.sum(
-        jnp.where(sources[:, None, None] == jnp.arange(NX)[None, :, None], tile_pos[None], 0), axis=1
-    )
-    fresh = (z >= 12) & (z < 12 + RI)
-    new_pos = jnp.where(fresh, tile_pos.reshape(-1), never)
-    new_pos = jnp.concatenate([new_pos, jnp.full((BLK - NZ * NX,), never, jnp.int32)])
-    key_pos = jnp.concatenate([key_pos, new_pos[None]], axis=0)
+    by_zxi = listed_rows.reshape(NZ, NX, RI)
+    row_pos = lax.dynamic_slice_in_dim(by_zxi, x, 1, axis=1)[:, 0].T
+    new_pos = lax.dynamic_slice_in_dim(by_zxi, z, 1, axis=0).reshape(-1)
+    own = 8 * RI * z + jnp.arange(8 * RI)
+    chosen = (own // HD * NZ + own % NZ)[:, None] == jnp.arange(XR)[None, :]
+    query_pos = jnp.sum(jnp.where(chosen, row_pos.reshape(1, XR), 0), axis=1)
+    rest = jnp.full((BLK - NX * RI,), never, jnp.int32)
+    key_pos = jnp.concatenate([key_pos, jnp.concatenate([new_pos, rest])[None]], axis=0)
     wide_row_pos = jnp.broadcast_to(row_pos[:, :, None], (RI, NZ, BLK))
-    cosine, sine = rope_factors(jnp.concatenate([shift[0], tile_pos[0]]))
-    cache = vmem_call(
-        rotate_kernel,
-        shaped((2 * blocks, BLK, HD), bf16),
-        (cache_keys, cache_values, cosine[:blocks], sine[:blocks]),
-    )
-    turns = jnp.stack([cosine[blocks:], sine[blocks:]])
-    still = jnp.stack([jnp.ones_like(turns[0]), jnp.zeros_like(turns[0])])
-    factors = jnp.stack([turns, jnp.where(z < 12, turns, still)])
+    cosine, sine = rope_factors(
+        jnp.concatenate([query_pos, new_pos, jnp.zeros((NX * RI,), jnp.int32), shift[0]])
+    )
+    rows = 8 * RI + KT
+    cache, weights = vmem_call(
+        bundle_kernel,
+        (shaped((2 * blocks, BLK, HD), bf16), shaped((2 * GQ + 2, HD, HD), bf16)),
+        (cache_keys, cache_values, cosine[rows:], sine[rows:], out_weight, next_weight),
+    )
 
     x_scalar = x.reshape(1).astype(jnp.int32)
     tiles, hidden_x, gain_x = vmem_call(
         sum_x_kernel,
         (
-            shaped((NZ, 2, TILE, HD), bf16),
+            shaped((NZ, rows, HD), bf16),
             shaped((NX, RI, TILE, HD), bf16),
             shaped((NX, HD), f32),
         ),
         (x_scalar, payload),
+        scratch=[pltpu.VMEM((NZ, KT, HD), f32)],
         scalars=1,
     )
-    tiles, cache = lax.optimization_barrier((tiles, cache))
-    caches = from_x(cache)
-    copies, own = vmem_call(
+    caches = [cache] + [shifted(after(cache, tiles), step) for step in (1, 3)]
+    copies, new = vmem_call(
         rope_kernel,
-        (shaped((NZ, 2, TILE, HD), bf16), shaped((2, TILE, HD), bf16)),
-        (a2a(tiles, "z"), factors),
-    )
-    queries = a2a(copies, "z")
-    news = from_x(own)
+        (shaped((NZ, 8 * RI, HD), bf16), shaped((2, FRESH, HD), bf16)),
+        (a2a(tiles, "z"), cosine[:rows], sine[:rows]),
+    )
+    caches.insert(2, shifted(after(cache, copies), 2))
+    weights_x = [weights, shifted(after(weights, copies), 1)]
+    queries = a2a(copies, "z").reshape(XR * GQ, HD)
     parts = vmem_call(
         attend_kernel,
         shaped((NZ, 32, HD), bf16),
-        (queries, key_pos, wide_row_pos, *caches, *news),
+        (queries, key_pos, wide_row_pos, new, *caches),
         scratch=[pltpu.VMEM((HD, (NX * blocks + 2 * RI) * BLK), f32)],
     )
-    parts, out_weight = lax.optimization_barrier((parts, out_weight))
-    out_weights = from_x(out_weight)
-    parts, out_weights = lax.optimization_barrier((a2a(parts, "z"), out_weights))
-    share = vmem_call(combine_kernel, shaped((NZ, 8 * RI, HD), bf16), (parts,))
-    share, next_weight = lax.optimization_barrier((share, next_weight))
-    next_weights = from_x(next_weight)
-    heads_out, next_weights = lax.optimization_barrier((a2a(share, "z"), next_weights))
-    heads_out = heads_out.reshape(XR * GQ, HD)
+    weights_x += [shifted(after(weights, parts), step) for step in (2, 3)]
+    share = vmem_call(
+        combine_kernel, shaped((NZ, 8 * RI, HD), bf16), (a2a(parts, "z"),)
+    )
+    heads_out = a2a(share, "z").reshape(XR * GQ, HD)
     terms = vmem_call(
-        output_kernel, shaped((NH, XR, NX * HD), bf16), (heads_out, *out_weights)
+        output_kernel, shaped((NH, XR, NX * HD), bf16), (heads_out, *weights_x)
     )
     *resids, products = vmem_call(
         next_kernel,
         (*[shaped((XR, HD), bf16)] * NX, shaped((NZ, 32, HD), bf16)),
-        (a2a(terms, "heads"), hidden_x, gain_x, *next_weights),
+        (a2a(terms, "heads"), hidden_x, gain_x, *weights_x),
         scratch=[pltpu.VMEM((NZ, 32, HD), f32)],
     )
     resids = [resids[0]] + [shifted(resids[s], NX - s) for s in range(1, NX)]

time: 174 us -> 157 us (0.902); the launches traced: 171 us -> 157 us
  starting transfers between devices: 116 us -> 84.7 us
  waiting for transfers between devices: 26.6 us -> 43.3 us
    ppermute x15 -> x9, starting transfers between devices: 50 us -> 29.7 us  [shifted(): return lax.ppermute(array, 'x', [(n, (n + step) % NX) for n in range(NX)])]
    all_to_all x2, waiting for transfers between devices: 1.67 us -> 13.1 us  [the longest x1 8.88 us: on_device(): queries = a2a(copies, 'z').reshape(XR * GQ, HD)]
    all_to_all x2, starting transfers between devices: 21.4 us -> 13.1 us  [the longest x1 8.56 us: on_device(): heads_out = a2a(share, 'z').reshape(XR * GQ, HD)]
    ppermute x15 -> x9, waiting for transfers between devices: 18.5 us -> 11.2 us  [shifted(): return lax.ppermute(array, 'x', [(n, (n + step) % NX) for n in range(NX)])]
    all_to_all x1, waiting for transfers between devices: 2.62 us -> 7.52 us  [on_device(): a2a(tiles, 'z')]
    all_to_all x1, starting transfers between devices: 12 us -> 7.51 us  [on_device(): a2a(products, 'z')]
    all_to_all x1, waiting for transfers between devices: 0.01 us -> 3.46 us  [on_device(): a2a(parts, 'z')]
    all_to_all x1, waiting for transfers between devices: 3.86 us -> 5.91 us  [on_device(): payload = a2a(payload, 'x')]
  transfers between devices with their start and end apart: 21 -> 15, of which waited for: 9 -> 9; matrix products, arithmetic and copies ran while one was open for 2% -> 2% of each run, Pallas kernels for 1% -> 2%
where the time goes in v3:
time: 157 us
  starting transfers between devices  84.7 us (54%)
  waiting for transfers between devices  43.3 us (28%)
  blocking collectives  13.2 us (8%)
  Pallas kernels  11.4 us (7%)
  other arithmetic  2.03 us (1%)
    ppermute x9, starting transfers between devices, shifted(): return lax.ppermute(array, 'x', [(n, (n + step) % NX) for n in range(NX)])  29.7 us
    all_to_all x1, starting transfers between devices, on_device(): a2a(tiles, 'z')  13.8 us
    all_to_all x1, blocking collectives, on_device(): a2a(terms, 'heads')  13.2 us
    pallas_call x10, Pallas kernels, vmem_call(): pl.pallas_call(kernel, out_shape=out_shape, in_specs=[small] * scalars +...  11.4 us
    ppermute x9, waiting for transfers between devices, shifted(): return lax.ppermute(array, 'x', [(n, (n + step) % NX) for n in range(NX)])  11.2 us
    all_to_all x1, starting transfers between devices, on_device(): a2a(parts, 'z')  11.2 us
    all_to_all x1, starting transfers between devices, on_device(): payload = a2a(payload, 'x')  9.47 us
    all_to_all x1, waiting for transfers between devices, on_device(): queries = a2a(copies, 'z').reshape(XR * GQ, HD)  8.88 us
  transfers between devices with their start and end apart: 15, of which 9 were waited for; matrix products, arithmetic and copies ran while one was open for 2% of the time, Pallas kernels for 2%

profile of v3, /device:TPU:6, one launch (start us, length us, event | category | flops | bytes accessed | tf_op | source)
XLA Modules:
  0.0 156.6 jit_solution(5828105196235944019)
XLA Ops:
  0.6 2.3 %shard_map.122 = bf16[4,52,16,128]{3,2,1,0:T(8,128)(2,1)} custom-call(bf16[192,128]{1,0:T(8,128)(2,1)} %hidden_hbm.1, bf16[128,1280]{1,0:T(8,128)(2,1)} %weight_hbm.1, f32[1,128]{1,0:T(1,128)} %bitcast.13), custom_call_target="tpu_custom_call" | custom-call | tf_op jit(solution)/shard_map/pallas_call | solution.py:42
  2.9 0.0 copy-start.7
  2.9 0.0 copy-start.5
  3.0 0.0 copy-start.4
  3.0 0.0 copy-start.6
  3.0 9.5 %all-to-all-start = ((bf16[4,52,16,128]{3,2,1,0:T(8,128)(2,1)}), bf16[4,52,16,128]{3,2,1,0:T(8,128)(2,1)S(1)}, u32[]{:S(2)}, u32[]{:S(2)}) async-start(bf16[4,52,16,128]{3,2,1,0:T(8,128)(2,1)} %shard_map.122), calls=%async_computation | async-start | bytes 1703936 | tf_op jit(solution)/shard_map/all_to_all | solution.py:397
  12.6 0.1 fusion.5
  12.6 0.1 compare_select_fusion
  12.7 0.1 select_reduce_fusion
  12.9 0.2 reshape.214
  13.1 0.1 copy.19
  13.1 0.1 concatenate.25
  13.2 0.1 broadcast_in_dim.38
  13.3 0.4 select_reduce_fusion.1
  13.7 0.1 slice_reduce_fusion
  13.8 0.2 select_reduce_fusion.3
  14.0 0.1 add_convert_fusion
  14.1 0.2 multiply_sine_fusion
  14.3 5.9 %all-to-all-done.in_ref = bf16[4,52,16,128]{3,2,1,0:T(8,128)(2,1)S(1)} async-done(((bf16[4,52,16,128]{3,2,1,0:T(8,128)(2,1)}), bf16[4,52,16,128]{3,2,1,0:T(8,128)(2,1)S(1)}, u32[]{:S(2)}, u32[]{:S(2)}) %all-to-all-start) | async-done | bytes 852000 | tf_op jit(solution)/shard_map/all_to_all | solution.py:397
  20.2 0.9 shard_map.123
  21.1 13.8 %all-to-all-start.1 = ((bf16[16,48,128]{2,1,0:T(8,128)(2,1)}), bf16[16,48,128]{2,1,0:T(8,128)(2,1)S(1)}, u32[]{:S(2)}, u32[]{:S(2)}) async-start(bf16[16,48,128]{2,1,0:T(8,128)(2,1)} %get-tuple-element.18), calls=%async_computation.1 | async-start | bytes 393216 | tf_op jit(solution)/shard_map/all_to_all | solution.py:438
  34.9 0.1 pad_maximum_fusion
  35.0 0.1 copy.21
  35.1 0.3 shard_map.125
  35.4 0.1 fusion
  35.5 0.1 iota_add_fusion
  35.6 0.5 compare_reduce_fusion
  36.1 1.9 %collective-permute-start.2 = (bf16[12,128,128]{2,1,0:T(8,128)(2,1)S(1)}, bf16[12,128,128]{2,1,0:T(8,128)(2,1)S(1)}, u32[]{:S(2)}, u32[]{:S(2)}) collective-permute-start(bf16[12,128,128]{2,1,0:T(8,128)(2,1)S(1)} %get-tuple-element.23.refs_0_), channel_id=1, source_target_pairs={{0,3},{1,0},{2,1},{3,2},{4,7},{5,4},{6,5},{7,6},{8,11},{9,8},{10,9... | collective-permute-start | bytes 1179656 | tf_op jit(solution)/shard_map/ppermute | solution.py:379
  38.0 5.1 %collective-permute-start = (bf16[12,128,128]{2,1,0:T(8,128)(2,1)S(1)}, bf16[12,128,128]{2,1,0:T(8,128)(2,1)S(1)}, u32[]{:S(2)}, u32[]{:S(2)}) collective-permute-start(bf16[12,128,128]{2,1,0:T(8,128)(2,1)S(1)} %get-tuple-element.23.refs_0_), channel_id=1, source_target_pairs={{0,1},{1,2},{2,3},{3,0},{4,5},{5,6},{6,7},{7,4},{8,9},{9,10},{10,1... | collective-permute-start | bytes 1179656 | tf_op jit(solution)/shard_map/ppermute | solution.py:379
  43.2 7.5 %all-to-all-done.1.in_ref = bf16[16,48,128]{2,1,0:T(8,128)(2,1)S(1)} async-done(((bf16[16,48,128]{2,1,0:T(8,128)(2,1)}), bf16[16,48,128]{2,1,0:T(8,128)(2,1)S(1)}, u32[]{:S(2)}, u32[]{:S(2)}) %all-to-all-start.1) | async-done | bytes 196640 | tf_op jit(solution)/shard_map/all_to_all | solution.py:438
  50.7 0.7 shard_map.124
  51.4 4.5 %all-to-all-start.2 = ((bf16[16,24,128]{2,1,0:T(8,128)(2,1)}), bf16[16,24,128]{2,1,0:T(8,128)(2,1)S(1)}, u32[]{:S(2)}, u32[]{:S(2)}) async-start(bf16[16,24,128]{2,1,0:T(8,128)(2,1)} %get-tuple-element.19), calls=%async_computation.2 | async-start | bytes 196608 | tf_op jit(solution)/shard_map/all_to_all | solution.py:442
  55.9 3.8 %collective-permute-start.1 = (bf16[12,128,128]{2,1,0:T(8,128)(2,1)S(1)}, bf16[12,128,128]{2,1,0:T(8,128)(2,1)S(1)}, u32[]{:S(2)}, u32[]{:S(2)}) collective-permute-start(bf16[12,128,128]{2,1,0:T(8,128)(2,1)S(1)} %get-tuple-element.23.refs_0_), channel_id=1, source_target_pairs={{0,2},{1,3},{2,0},{3,1},{4,6},{5,7},{6,4},{7,5},{8,10},{9,11},{10,... | collective-permute-start | bytes 1179656 | tf_op jit(solution)/shard_map/ppermute | solution.py:379
  59.8 0.1 add.119
  59.9 0.1 copy.20
  60.0 0.1 gt.11
  60.1 0.1 add_select_fusion
  60.2 0.0 collective-permute-done.2.refs_3_
  60.2 0.0 collective-permute-done.refs_1_
  60.2 8.9 %all-to-all-done.2 = bf16[16,24,128]{2,1,0:T(8,128)(2,1)S(1)} async-done(((bf16[16,24,128]{2,1,0:T(8,128)(2,1)}), bf16[16,24,128]{2,1,0:T(8,128)(2,1)S(1)}, u32[]{:S(2)}, u32[]{:S(2)}) %all-to-all-start.2) | async-done | bytes 98336 | tf_op jit(solution)/shard_map/all_to_all | solution.py:442
  69.1 0.1 broadcast_in_dim.50.rowpos_ref
  69.2 3.1 %shard_map.126 = bf16[16,32,128]{2,1,0:T(8,128)(2,1)} custom-call(bf16[384,128]{1,0:T(8,128)(2,1)S(1)} %bitcast.9, s32[25,128]{1,0:T(8,128)S(1)} %pad_add_fusion.keypos_ref, s32[3,16,128]{2,1,0:T(8,128)S(1)} %broadcast_in_dim.50.rowpos_ref, bf16[2,16,128]{2,1,0:T(8,128)(2,1)S(1)} %get-tuple-element.20.new_ref, ...), custom_call_target="tpu_custom_call" | custom-call | tf_op jit(solution)/shard_map/pallas_call | solution.py:42
  72.3 11.2 %all-to-all-start.3 = ((bf16[16,32,128]{2,1,0:T(8,128)(2,1)}), bf16[16,32,128]{2,1,0:T(8,128)(2,1)S(1)}, u32[]{:S(2)}, u32[]{:S(2)}) async-start(bf16[16,32,128]{2,1,0:T(8,128)(2,1)} %shard_map.126), calls=%async_computation.3 | async-start | bytes 262144 | tf_op jit(solution)/shard_map/all_to_all | solution.py:451
  83.5 4.0 %collective-permute-start.3 = (bf16[18,128,128]{2,1,0:T(8,128)(2,1)S(1)}, bf16[18,128,128]{2,1,0:T(8,128)(2,1)S(1)}, u32[]{:S(2)}, u32[]{:S(2)}) collective-permute-start(bf16[18,128,128]{2,1,0:T(8,128)(2,1)S(1)} %get-tuple-element.26.refs_0_), channel_id=1, source_target_pairs={{0,1},{1,2},{2,3},{3,0},{4,5},{5,6},{6,7},{7,4},{8,9},{9,10},{10,1... | collective-permute-start | bytes 1769480 | tf_op jit(solution)/shard_map/ppermute | solution.py:379
  87.5 1.9 %collective-permute-start.5 = (bf16[18,128,128]{2,1,0:T(8,128)(2,1)S(1)}, bf16[18,128,128]{2,1,0:T(8,128)(2,1)S(1)}, u32[]{:S(2)}, u32[]{:S(2)}) collective-permute-start(bf16[18,128,128]{2,1,0:T(8,128)(2,1)S(1)} %get-tuple-element.26.refs_0_), channel_id=1, source_target_pairs={{0,3},{1,0},{2,1},{3,2},{4,7},{5,4},{6,5},{7,6},{8,11},{9,8},{10,9... | collective-permute-start | bytes 1769480 | tf_op jit(solution)/shard_map/ppermute | solution.py:379
  89.4 3.9 %collective-permute-start.4 = (bf16[18,128,128]{2,1,0:T(8,128)(2,1)S(1)}, bf16[18,128,128]{2,1,0:T(8,128)(2,1)S(1)}, u32[]{:S(2)}, u32[]{:S(2)}) collective-permute-start(bf16[18,128,128]{2,1,0:T(8,128)(2,1)S(1)} %get-tuple-element.26.refs_0_), channel_id=1, source_target_pairs={{0,2},{1,3},{2,0},{3,1},{4,6},{5,7},{6,4},{7,5},{8,10},{9,11},{10,... | collective-permute-start | bytes 1769480 | tf_op jit(solution)/shard_map/ppermute | solution.py:379
  93.3 3.5 %all-to-all-done.3.in_ref = bf16[16,32,128]{2,1,0:T(8,128)(2,1)S(1)} async-done(((bf16[16,32,128]{2,1,0:T(8,128)(2,1)}), bf16[16,32,128]{2,1,0:T(8,128)(2,1)S(1)}, u32[]{:S(2)}, u32[]{:S(2)}) %all-to-all-start.3) | async-done | bytes 131104 | tf_op jit(solution)/shard_map/all_to_all | solution.py:451
  96.8 0.9 shard_map.127
  97.7 8.6 %all-to-all-start.4 = ((bf16[16,24,128]{2,1,0:T(8,128)(2,1)}), bf16[16,24,128]{2,1,0:T(8,128)(2,1)S(1)}, u32[]{:S(2)}, u32[]{:S(2)}) async-start(bf16[16,24,128]{2,1,0:T(8,128)(2,1)} %shard_map.127), calls=%async_computation.4 | async-start | bytes 196608 | tf_op jit(solution)/shard_map/all_to_all | solution.py:453
  106.3 3.4 %collective-permute-done.3.refs_1_ = bf16[18,128,128]{2,1,0:T(8,128)(2,1)S(1)} collective-permute-done((bf16[18,128,128]{2,1,0:T(8,128)(2,1)S(1)}, bf16[18,128,128]{2,1,0:T(8,128)(2,1)S(1)}, u32[]{:S(2)}, u32[]{:S(2)}) %collective-permute-start.3) | collective-permute-done | bytes 589856 | tf_op jit(solution)/shard_map/ppermute | solution.py:379
  109.7 5.3 %collective-permute-done.5.refs_3_ = bf16[18,128,128]{2,1,0:T(8,128)(2,1)S(1)} collective-permute-done((bf16[18,128,128]{2,1,0:T(8,128)(2,1)S(1)}, bf16[18,128,128]{2,1,0:T(8,128)(2,1)S(1)}, u32[]{:S(2)}, u32[]{:S(2)}) %collective-permute-start.5) | collective-permute-done | bytes 589856 | tf_op jit(solution)/shard_map/ppermute | solution.py:379
  115.0 4.2 %all-to-all-done.4 = bf16[16,24,128]{2,1,0:T(8,128)(2,1)S(1)} async-done(((bf16[16,24,128]{2,1,0:T(8,128)(2,1)}), bf16[16,24,128]{2,1,0:T(8,128)(2,1)S(1)}, u32[]{:S(2)}, u32[]{:S(2)}) %all-to-all-start.4) | async-done | bytes 98336 | tf_op jit(solution)/shard_map/all_to_all | solution.py:453
  119.2 0.3 shard_map.128
  119.5 13.2 %all_to_all.35.terms_ref = bf16[8,48,512]{2,1,0:T(8,128)(2,1)S(1)} all-to-all(bf16[8,48,512]{2,1,0:T(8,128)(2,1)S(1)} %shard_map.128), channel_id=1, replica_groups=mesh['heads'=8,'z'=16,'x'=4] {'heads'}, dimensions={0} | all-to-all | bytes 786432 | tf_op jit(solution)/shard_map/all_to_all | solution.py:460
  132.7 1.1 shard_map.129
  133.8 7.5 %all-to-all-start.6 = ((bf16[16,32,128]{2,1,0:T(8,128)(2,1)}), bf16[16,32,128]{2,1,0:T(8,128)(2,1)S(1)}, u32[]{:S(2)}, u32[]{:S(2)}) async-start(bf16[16,32,128]{2,1,0:T(8,128)(2,1)} %get-tuple-element.33), calls=%async_computation.6 | async-start | bytes 262144 | tf_op jit(solution)/shard_map/all_to_all | solution.py:468
  141.3 1.9 %collective-permute-start.6 = (bf16[48,128]{1,0:T(8,128)(2,1)S(1)}, bf16[48,128]{1,0:T(8,128)(2,1)S(1)}, u32[]{:S(2)}, u32[]{:S(2)}) collective-permute-start(bf16[48,128]{1,0:T(8,128)(2,1)S(1)} %get-tuple-element.30), channel_id=1, source_target_pairs={{0,3},{1,0},{2,1},{3,2},{4,7},{5,4},{6,5},{7,6},{8,11},{9,8},{10,9... | collective-permute-start | bytes 36872 | tf_op jit(solution)/shard_map/ppermute | solution.py:379
  143.3 2.9 %collective-permute-start.7 = (bf16[48,128]{1,0:T(8,128)(2,1)S(1)}, bf16[48,128]{1,0:T(8,128)(2,1)S(1)}, u32[]{:S(2)}, u32[]{:S(2)}) collective-permute-start(bf16[48,128]{1,0:T(8,128)(2,1)S(1)} %get-tuple-element.31), channel_id=1, source_target_pairs={{0,2},{1,3},{2,0},{3,1},{4,6},{5,7},{6,4},{7,5},{8,10},{9,11},{10,... | collective-permute-start | bytes 36872 | tf_op jit(solution)/shard_map/ppermute | solution.py:379
  146.2 4.1 %collective-permute-start.8 = (bf16[48,128]{1,0:T(8,128)(2,1)S(1)}, bf16[48,128]{1,0:T(8,128)(2,1)S(1)}, u32[]{:S(2)}, u32[]{:S(2)}) collective-permute-start(bf16[48,128]{1,0:T(8,128)(2,1)S(1)} %get-tuple-element.32), channel_id=1, source_target_pairs={{0,1},{1,2},{2,3},{3,0},{4,5},{5,6},{6,7},{7,4},{8,9},{9,10},{10,1... | collective-permute-start | bytes 36872 | tf_op jit(solution)/shard_map/ppermute | solution.py:379
  150.4 0.0 collective-permute-done.7.refs_2_
  150.4 2.5 %collective-permute-done.8.refs_3_ = bf16[48,128]{1,0:T(8,128)(2,1)S(1)} collective-permute-done((bf16[48,128]{1,0:T(8,128)(2,1)S(1)}, bf16[48,128]{1,0:T(8,128)(2,1)S(1)}, u32[]{:S(2)}, u32[]{:S(2)}) %collective-permute-start.8) | collective-permute-done | bytes 12320 | tf_op jit(solution)/shard_map/ppermute | solution.py:379
  152.8 0.9 shard_map.130
  153.7 2.1 %all-to-all-done.6.in_ref = bf16[16,32,128]{2,1,0:T(8,128)(2,1)S(1)} async-done(((bf16[16,32,128]{2,1,0:T(8,128)(2,1)}), bf16[16,32,128]{2,1,0:T(8,128)(2,1)S(1)}, u32[]{:S(2)}, u32[]{:S(2)}) %all-to-all-start.6) | async-done | bytes 131104 | tf_op jit(solution)/shard_map/all_to_all | solution.py:468
  155.8 0.8 shard_map.131
  (29 shorter events, 0.2 us)
Async XLA Ops:
  2.9 9.6 %copy-start.7 = (s32[128]{0:T(128)S(1)}, s32[128]{0:T(128)}, u32[]{:S(2)}) copy-start(s32[128]{0:T(128)} %param.18) | copy-start | bytes 1540
  2.9 9.6 %copy-start.5 = (s32[128]{0:T(128)S(1)}, s32[128]{0:T(128)}, u32[]{:S(2)}) copy-start(s32[128]{0:T(128)} %param.19) | copy-start | bytes 1540
  3.0 9.9 %copy-start.4 = (s32[192]{0:T(256)S(1)}, s32[192]{0:T(256)}, u32[]{:S(2)}) copy-start(s32[192]{0:T(256)} %param.21) | copy-start | bytes 2308
  3.0 10.3 %copy-start.6 = (s32[128]{0:T(128)S(1)}, s32[128]{0:T(128)}, u32[]{:S(2)}) copy-start(s32[128]{0:T(128)} %param.20) | copy-start | bytes 1540
  3.0 17.2 %all-to-all-start = ((bf16[4,52,16,128]{3,2,1,0:T(8,128)(2,1)}), bf16[4,52,16,128]{3,2,1,0:T(8,128)(2,1)S(1)}, u32[]{:S(2)}, u32[]{:S(2)}) async-start(bf16[4,52,16,128]{3,2,1,0:T(8,128)(2,1)} %shard_map.122), calls=%async_computation | async-start | bytes 1703936 | tf_op jit(solution)/shard_map/all_to_all | solution.py:397
  12.4 22.6 %copy-start = (bf16[128,1280]{1,0:T(8,128)(2,1)S(1)}, bf16[128,1280]{1,0:T(8,128)(2,1)}, u32[]{:S(2)}) copy-start(bf16[128,1280]{1,0:T(8,128)(2,1)} %next_weight_ref.1) | copy-start | bytes 983044
  12.4 22.6 %copy-start.1 = (bf16[1024,128]{1,0:T(8,128)(2,1)S(1)}, bf16[1024,128]{1,0:T(8,128)(2,1)}, u32[]{:S(2)}) copy-start(bf16[1024,128]{1,0:T(8,128)(2,1)} %out_weight_ref.1) | copy-start | bytes 786436
  12.4 22.6 %copy-start.2 = (bf16[768,128]{1,0:T(8,128)(2,1)S(1)}, bf16[768,128]{1,0:T(8,128)(2,1)}, u32[]{:S(2)}) copy-start(bf16[768,128]{1,0:T(8,128)(2,1)} %keys_ref.1) | copy-start | bytes 589828
  12.5 22.6 %copy-start.3 = (bf16[768,128]{1,0:T(8,128)(2,1)S(1)}, bf16[768,128]{1,0:T(8,128)(2,1)}, u32[]{:S(2)}) copy-start(bf16[768,128]{1,0:T(8,128)(2,1)} %values_ref.1) | copy-start | bytes 589828
  21.1 29.6 %all-to-all-start.1 = ((bf16[16,48,128]{2,1,0:T(8,128)(2,1)}), bf16[16,48,128]{2,1,0:T(8,128)(2,1)S(1)}, u32[]{:S(2)}, u32[]{:S(2)}) async-start(bf16[16,48,128]{2,1,0:T(8,128)(2,1)} %get-tuple-element.18), calls=%async_computation.1 | async-start | bytes 393216 | tf_op jit(solution)/shard_map/all_to_all | solution.py:438
  36.1 24.1 %collective-permute-start.2 = (bf16[12,128,128]{2,1,0:T(8,128)(2,1)S(1)}, bf16[12,128,128]{2,1,0:T(8,128)(2,1)S(1)}, u32[]{:S(2)}, u32[]{:S(2)}) collective-permute-start(bf16[12,128,128]{2,1,0:T(8,128)(2,1)S(1)} %get-tuple-element.23.refs_0_), channel_id=1, source_target_pairs={{0,3},{1,0},{2,1},{3,2},{4,7},{5,4},{6,5},{7,6},{8,11},{9,8},{10,9... | collective-permute-start | bytes 1179656 | tf_op jit(solution)/shard_map/ppermute | solution.py:379
  38.0 22.2 %collective-permute-start = (bf16[12,128,128]{2,1,0:T(8,128)(2,1)S(1)}, bf16[12,128,128]{2,1,0:T(8,128)(2,1)S(1)}, u32[]{:S(2)}, u32[]{:S(2)}) collective-permute-start(bf16[12,128,128]{2,1,0:T(8,128)(2,1)S(1)} %get-tuple-element.23.refs_0_), channel_id=1, source_target_pairs={{0,1},{1,2},{2,3},{3,0},{4,5},{5,6},{6,7},{7,4},{8,9},{9,10},{10,1... | collective-permute-start | bytes 1179656 | tf_op jit(solution)/shard_map/ppermute | solution.py:379
  51.4 17.7 %all-to-all-start.2 = ((bf16[16,24,128]{2,1,0:T(8,128)(2,1)}), bf16[16,24,128]{2,1,0:T(8,128)(2,1)S(1)}, u32[]{:S(2)}, u32[]{:S(2)}) async-start(bf16[16,24,128]{2,1,0:T(8,128)(2,1)} %get-tuple-element.19), calls=%async_computation.2 | async-start | bytes 196608 | tf_op jit(solution)/shard_map/all_to_all | solution.py:442
  55.9 13.1 %collective-permute-start.1 = (bf16[12,128,128]{2,1,0:T(8,128)(2,1)S(1)}, bf16[12,128,128]{2,1,0:T(8,128)(2,1)S(1)}, u32[]{:S(2)}, u32[]{:S(2)}) collective-permute-start(bf16[12,128,128]{2,1,0:T(8,128)(2,1)S(1)} %get-tuple-element.23.refs_0_), channel_id=1, source_target_pairs={{0,2},{1,3},{2,0},{3,1},{4,6},{5,7},{6,4},{7,5},{8,10},{9,11},{10,... | collective-permute-start | bytes 1179656 | tf_op jit(solution)/shard_map/ppermute | solution.py:379
  72.3 24.5 %all-to-all-start.3 = ((bf16[16,32,128]{2,1,0:T(8,128)(2,1)}), bf16[16,32,128]{2,1,0:T(8,128)(2,1)S(1)}, u32[]{:S(2)}, u32[]{:S(2)}) async-start(bf16[16,32,128]{2,1,0:T(8,128)(2,1)} %shard_map.126), calls=%async_computation.3 | async-start | bytes 262144 | tf_op jit(solution)/shard_map/all_to_all | solution.py:451
  83.5 26.2 %collective-permute-start.3 = (bf16[18,128,128]{2,1,0:T(8,128)(2,1)S(1)}, bf16[18,128,128]{2,1,0:T(8,128)(2,1)S(1)}, u32[]{:S(2)}, u32[]{:S(2)}) collective-permute-start(bf16[18,128,128]{2,1,0:T(8,128)(2,1)S(1)} %get-tuple-element.26.refs_0_), channel_id=1, source_target_pairs={{0,1},{1,2},{2,3},{3,0},{4,5},{5,6},{6,7},{7,4},{8,9},{9,10},{10,1... | collective-permute-start | bytes 1769480 | tf_op jit(solution)/shard_map/ppermute | solution.py:379
  87.5 27.5 %collective-permute-start.5 = (bf16[18,128,128]{2,1,0:T(8,128)(2,1)S(1)}, bf16[18,128,128]{2,1,0:T(8,128)(2,1)S(1)}, u32[]{:S(2)}, u32[]{:S(2)}) collective-permute-start(bf16[18,128,128]{2,1,0:T(8,128)(2,1)S(1)} %get-tuple-element.26.refs_0_), channel_id=1, source_target_pairs={{0,3},{1,0},{2,1},{3,2},{4,7},{5,4},{6,5},{7,6},{8,11},{9,8},{10,9... | collective-permute-start | bytes 1769480 | tf_op jit(solution)/shard_map/ppermute | solution.py:379
  89.4 25.6 %collective-permute-start.4 = (bf16[18,128,128]{2,1,0:T(8,128)(2,1)S(1)}, bf16[18,128,128]{2,1,0:T(8,128)(2,1)S(1)}, u32[]{:S(2)}, u32[]{:S(2)}) collective-permute-start(bf16[18,128,128]{2,1,0:T(8,128)(2,1)S(1)} %get-tuple-element.26.refs_0_), channel_id=1, source_target_pairs={{0,2},{1,3},{2,0},{3,1},{4,6},{5,7},{6,4},{7,5},{8,10},{9,11},{10,... | collective-permute-start | bytes 1769480 | tf_op jit(solution)/shard_map/ppermute | solution.py:379
  97.7 21.5 %all-to-all-start.4 = ((bf16[16,24,128]{2,1,0:T(8,128)(2,1)}), bf16[16,24,128]{2,1,0:T(8,128)(2,1)S(1)}, u32[]{:S(2)}, u32[]{:S(2)}) async-start(bf16[16,24,128]{2,1,0:T(8,128)(2,1)} %shard_map.127), calls=%async_computation.4 | async-start | bytes 196608 | tf_op jit(solution)/shard_map/all_to_all | solution.py:453
  133.8 22.0 %all-to-all-start.6 = ((bf16[16,32,128]{2,1,0:T(8,128)(2,1)}), bf16[16,32,128]{2,1,0:T(8,128)(2,1)S(1)}, u32[]{:S(2)}, u32[]{:S(2)}) async-start(bf16[16,32,128]{2,1,0:T(8,128)(2,1)} %get-tuple-element.33), calls=%async_computation.6 | async-start | bytes 262144 | tf_op jit(solution)/shard_map/all_to_all | solution.py:468
  141.3 9.0 %collective-permute-start.6 = (bf16[48,128]{1,0:T(8,128)(2,1)S(1)}, bf16[48,128]{1,0:T(8,128)(2,1)S(1)}, u32[]{:S(2)}, u32[]{:S(2)}) collective-permute-start(bf16[48,128]{1,0:T(8,128)(2,1)S(1)} %get-tuple-element.30), channel_id=1, source_target_pairs={{0,3},{1,0},{2,1},{3,2},{4,7},{5,4},{6,5},{7,6},{8,11},{9,8},{10,9... | collective-permute-start | bytes 36872 | tf_op jit(solution)/shard_map/ppermute | solution.py:379
  143.3 7.1 %collective-permute-start.7 = (bf16[48,128]{1,0:T(8,128)(2,1)S(1)}, bf16[48,128]{1,0:T(8,128)(2,1)S(1)}, u32[]{:S(2)}, u32[]{:S(2)}) collective-permute-start(bf16[48,128]{1,0:T(8,128)(2,1)S(1)} %get-tuple-element.31), channel_id=1, source_target_pairs={{0,2},{1,3},{2,0},{3,1},{4,6},{5,7},{6,4},{7,5},{8,10},{9,11},{10,... | collective-permute-start | bytes 36872 | tf_op jit(solution)/shard_map/ppermute | solution.py:379
  146.2 6.6 %collective-permute-start.8 = (bf16[48,128]{1,0:T(8,128)(2,1)S(1)}, bf16[48,128]{1,0:T(8,128)(2,1)S(1)}, u32[]{:S(2)}, u32[]{:S(2)}) collective-permute-start(bf16[48,128]{1,0:T(8,128)(2,1)S(1)} %get-tuple-element.32), channel_id=1, source_target_pairs={{0,1},{1,2},{2,3},{3,0},{4,5},{5,6},{6,7},{7,4},{8,9},{9,10},{10,1... | collective-permute-start | bytes 36872 | tf_op jit(solution)/shard_map/ppermute | solution.py:379

commit v4 on v3

--- a/solution.py
+++ b/solution.py
@@ -72,7 +72,7 @@
     return jnp.concatenate([cosine, cosine], -1), jnp.concatenate([-sine, sine], -1)
 
 
-def bundle_kernel(keys_ref, values_ref, cos_ref, sin_ref, out_weight_ref, next_weight_ref, out_ref, weights_ref):
+def bundle_kernel(keys_ref, values_ref, cos_ref, sin_ref, out_ref):
     blocks = keys_ref.shape[0] // BLK
     for b in range(blocks):
         out_ref[blocks + b] = values_ref[b * BLK : (b + 1) * BLK, :]
@@ -83,10 +83,6 @@
         )
         turned = turned.astype(bf16).astype(f32)
         out_ref[b] = turned.T.astype(bf16)
-    for g in range(GQ):
-        weights_ref[g] = out_weight_ref[g * HD : (g + 1) * HD, :]
-    for j in range(GQ + 2):
-        weights_ref[GQ + j] = next_weight_ref[:, j * HD : (j + 1) * HD]
 
 
 def project_kernel(hidden_hbm, weight_hbm, gain_hbm, out_ref, hidden_ref, weight_ref, gain_ref, sems):
@@ -256,7 +252,7 @@
 
 
 def output_kernel(heads_ref, *refs):
-    weight_refs, out_ref = [ref.at[pl.ds(0, GQ)] for ref in refs[:NX]], refs[NX]
+    weight_refs, out_ref = refs[:NX], refs[NX]
     rows = heads_ref[...]
     bands = []
     for i in range(RI):
@@ -266,14 +262,13 @@
         )
     attended = jnp.concatenate(bands, axis=0)
     for x in range(NX):
-        term = jnp.dot(attended, weight_refs[x][...].reshape(GQ * HD, HD), preferred_element_type=f32).astype(bf16)
+        term = jnp.dot(attended, weight_refs[x][...], preferred_element_type=f32).astype(bf16)
         for h in range(NH):
             out_ref[h, :, x * HD : (x + 1) * HD] = term
 
 
 def next_kernel(terms_ref, hidden_ref, gain_ref, *refs):
-    weight_refs = [ref.at[pl.ds(GQ, GQ + 2)] for ref in refs[:NX]]
-    resid_refs, (out_ref, cut_ref) = refs[NX : 2 * NX], refs[2 * NX :]
+    weight_refs, resid_refs, (out_ref, cut_ref) = refs[:NX], refs[NX : 2 * NX], refs[2 * NX :]
     attended = terms_ref[0].astype(f32)
     for h in range(1, NH):
         attended = attended + terms_ref[h].astype(f32)
@@ -285,8 +280,7 @@
         resid_refs[x][...] = resid.astype(bf16)
         squares = squares + jnp.sum(resid * resid, axis=1, keepdims=True)
         gained = (resid * gain_ref[x : x + 1, :]).astype(bf16)
-        weight = jnp.concatenate([weight_refs[x][j] for j in range(GQ + 2)], axis=1)
-        product = product + jnp.dot(gained, weight, preferred_element_type=f32)
+        product = product + jnp.dot(gained, weight_refs[x][...], preferred_element_type=f32)
     for i in range(RI):
         for j in range(GQ + 2):
             cut_ref[:, i * (GQ + 2) + j, :] = product[
@@ -378,8 +372,8 @@
     def shifted(array, step):
         return lax.ppermute(array, "x", [(n, (n + step) % NX) for n in range(NX)])
 
-    def after(array, first):
-        return lax.optimization_barrier((array, first))[0]
+    def after(array, *first):
+        return lax.optimization_barrier((array, *first))[0]
 
     payload = vmem_call(
         project_kernel,
@@ -413,10 +407,10 @@
         jnp.concatenate([query_pos, new_pos, jnp.zeros((NX * RI,), jnp.int32), shift[0]])
     )
     rows = 8 * RI + KT
-    cache, weights = vmem_call(
+    cache = vmem_call(
         bundle_kernel,
-        (shaped((2 * blocks, BLK, HD), bf16), shaped((2 * GQ + 2, HD, HD), bf16)),
-        (cache_keys, cache_values, cosine[rows:], sine[rows:], out_weight, next_weight),
+        shaped((2 * blocks, BLK, HD), bf16),
+        (cache_keys, cache_values, cosine[rows:], sine[rows:]),
     )
 
     x_scalar = x.reshape(1).astype(jnp.int32)
@@ -431,33 +425,37 @@
         scratch=[pltpu.VMEM((NZ, KT, HD), f32)],
         scalars=1,
     )
-    caches = [cache] + [shifted(after(cache, tiles), step) for step in (1, 3)]
+    caches = {0: cache} | {step: shifted(after(cache, tiles), step) for step in (2, 1)}
     copies, new = vmem_call(
         rope_kernel,
         (shaped((NZ, 8 * RI, HD), bf16), shaped((2, FRESH, HD), bf16)),
         (a2a(tiles, "z"), cosine[:rows], sine[:rows]),
     )
-    caches.insert(2, shifted(after(cache, copies), 2))
-    weights_x = [weights, shifted(after(weights, copies), 1)]
+    caches[3] = shifted(after(cache, copies), 3)
     queries = a2a(copies, "z").reshape(XR * GQ, HD)
     parts = vmem_call(
         attend_kernel,
         shaped((NZ, 32, HD), bf16),
-        (queries, key_pos, wide_row_pos, new, *caches),
+        (queries, key_pos, wide_row_pos, new, *(caches[step] for step in range(NX))),
         scratch=[pltpu.VMEM((HD, (NX * blocks + 2 * RI) * BLK), f32)],
     )
-    weights_x += [shifted(after(weights, parts), step) for step in (2, 3)]
+    outs = {0: out_weight} | {step: shifted(after(out_weight, parts), step) for step in (2, 1)}
     share = vmem_call(
         combine_kernel, shaped((NZ, 8 * RI, HD), bf16), (a2a(parts, "z"),)
     )
+    outs[3] = shifted(after(out_weight, share), 3)
+    nexts = {0: next_weight, 2: shifted(after(next_weight, share, outs[1], outs[2]), 2)}
     heads_out = a2a(share, "z").reshape(XR * GQ, HD)
     terms = vmem_call(
-        output_kernel, shaped((NH, XR, NX * HD), bf16), (heads_out, *weights_x)
-    )
+        output_kernel,
+        shaped((NH, XR, NX * HD), bf16),
+        (heads_out, *(outs[step] for step in range(NX))),
+    )
+    nexts |= {step: shifted(after(next_weight, terms, nexts[2]), step) for step in (1, 3)}
     *resids, products = vmem_call(
         next_kernel,
         (*[shaped((XR, HD), bf16)] * NX, shaped((NZ, 32, HD), bf16)),
-        (a2a(terms, "heads"), hidden_x, gain_x, *weights_x),
+        (a2a(terms, "heads"), hidden_x, gain_x, *(nexts[step] for step in range(NX))),
         scratch=[pltpu.VMEM((NZ, 32, HD), f32)],
     )
     resids = [resids[0]] + [shifted(resids[s], NX - s) for s in range(1, NX)]

time: 157 us -> 167 us (1.064)
  blocking collectives: 13.2 us -> 0 us
  waiting for transfers between devices: 43.3 us -> 54.2 us
  starting transfers between devices: 84.7 us -> 95 us
    all_to_all x1 -> x0, blocking collectives: 13.2 us -> none  [on_device(): a2a(terms, 'heads')]
    ppermute x9 -> x12, waiting for transfers between devices: 11.2 us -> 19.7 us  [shifted(): return lax.ppermute(array, 'x', [(n, (n + step) % NX) for n in range(NX)])]
    ppermute x9 -> x12, starting transfers between devices: 29.7 us -> 36.8 us  [shifted(): return lax.ppermute(array, 'x', [(n, (n + step) % NX) for n in range(NX)])]
    all_to_all x1, waiting for transfers between devices: 3.46 us -> 8.13 us  [on_device(): a2a(parts, 'z')]
    all_to_all x1, starting transfers between devices: 8.56 us -> 4.02 us  [on_device(): heads_out = a2a(share, 'z').reshape(XR * GQ, HD)]
    all_to_all x0 -> x1, starting transfers between devices: none -> 4.46 us  [on_device(): a2a(terms, 'heads')]
    all_to_all x1, waiting for transfers between devices: 4.24 us -> 0.01 us  [on_device(): heads_out = a2a(share, 'z').reshape(XR * GQ, HD)]
    all_to_all x1, starting transfers between devices: 7.51 us -> 10.9 us  [on_device(): a2a(products, 'z')]
  transfers between devices with their start and end apart: 15 -> 19, of which waited for: 9 -> 9; matrix products, arithmetic and copies ran while one was open for 2% -> 2% of each run, Pallas kernels for 2% -> 2%
where the time goes in v4:
time: 167 us; the launch traced here: 165 us
  starting transfers between devices  95 us (57%)
  waiting for transfers between devices  54.2 us (32%)
  Pallas kernels  12.1 us (7%)
  other arithmetic  2.03 us (1%)
    ppermute x12, starting transfers between devices, shifted(): return lax.ppermute(array, 'x', [(n, (n + step) % NX) for n in range(NX)])  36.8 us
    ppermute x12, waiting for transfers between devices, shifted(): return lax.ppermute(array, 'x', [(n, (n + step) % NX) for n in range(NX)])  19.7 us
    all_to_all x1, starting transfers between devices, on_device(): a2a(tiles, 'z')  13.8 us
    pallas_call x10, Pallas kernels, vmem_call(): pl.pallas_call(kernel, out_shape=out_shape, in_specs=[small] * scalars +...  12.1 us
    all_to_all x1, starting transfers between devices, on_device(): a2a(parts, 'z')  11.2 us
    all_to_all x1, starting transfers between devices, on_device(): a2a(products, 'z')  10.9 us
    all_to_all x1, waiting for transfers between devices, on_device(): queries = a2a(copies, 'z').reshape(XR * GQ, HD)  10.2 us
    all_to_all x1, starting transfers between devices, on_device(): payload = a2a(payload, 'x')  9.47 us
  transfers between devices with their start and end apart: 19, of which 9 were waited for; matrix products, arithmetic and copies ran while one was open for 2% of the time, Pallas kernels for 2%

profile of v4, /device:TPU:6, one launch (start us, length us, event | category | flops | bytes accessed | tf_op | source)
XLA Modules:
  0.0 165.4 jit_solution(11675529825618183600)
XLA Ops:
  0.6 2.3 %shard_map.122 = bf16[4,52,16,128]{3,2,1,0:T(8,128)(2,1)} custom-call(bf16[192,128]{1,0:T(8,128)(2,1)} %hidden_hbm.1, bf16[128,1280]{1,0:T(8,128)(2,1)} %weight_hbm.1, f32[1,128]{1,0:T(1,128)} %bitcast.13), custom_call_target="tpu_custom_call" | custom-call | tf_op jit(solution)/shard_map/pallas_call | solution.py:42
  2.9 0.0 copy-start.7
  2.9 0.0 copy-start.5
  3.0 0.0 copy-start.4
  3.0 0.0 copy-start.6
  3.0 9.5 %all-to-all-start = ((bf16[4,52,16,128]{3,2,1,0:T(8,128)(2,1)}), bf16[4,52,16,128]{3,2,1,0:T(8,128)(2,1)S(1)}, u32[]{:S(2)}, u32[]{:S(2)}) async-start(bf16[4,52,16,128]{3,2,1,0:T(8,128)(2,1)} %shard_map.122), calls=%async_computation | async-start | bytes 1703936 | tf_op jit(solution)/shard_map/all_to_all | solution.py:391
  12.5 0.1 fusion.5
  12.6 0.1 compare_select_fusion
  12.7 0.1 select_reduce_fusion
  12.9 0.2 reshape.214
  13.0 0.1 concatenate.25
  13.1 0.1 copy.19
  13.2 0.1 broadcast_in_dim.38
  13.3 0.4 select_reduce_fusion.1
  13.7 0.1 slice_reduce_fusion
  13.8 0.2 select_reduce_fusion.3
  14.0 0.1 add_convert_fusion
  14.1 0.2 multiply_sine_fusion
  14.3 5.9 %all-to-all-done.in_ref = bf16[4,52,16,128]{3,2,1,0:T(8,128)(2,1)S(1)} async-done(((bf16[4,52,16,128]{3,2,1,0:T(8,128)(2,1)}), bf16[4,52,16,128]{3,2,1,0:T(8,128)(2,1)S(1)}, u32[]{:S(2)}, u32[]{:S(2)}) %all-to-all-start) | async-done | bytes 852000 | tf_op jit(solution)/shard_map/all_to_all | solution.py:391
  20.2 0.9 shard_map.123
  21.1 13.8 %all-to-all-start.1 = ((bf16[16,48,128]{2,1,0:T(8,128)(2,1)}), bf16[16,48,128]{2,1,0:T(8,128)(2,1)S(1)}, u32[]{:S(2)}, u32[]{:S(2)}) async-start(bf16[16,48,128]{2,1,0:T(8,128)(2,1)} %get-tuple-element.18), calls=%async_computation.1 | async-start | bytes 393216 | tf_op jit(solution)/shard_map/all_to_all | solution.py:432
  34.9 0.1 pad_maximum_fusion
  35.0 0.1 copy.21
  35.0 0.3 shard_map.125.refs_0_
  35.4 0.1 fusion
  35.5 0.1 iota_add_fusion
  35.5 0.5 compare_reduce_fusion
  36.1 4.0 %collective-permute-start = (bf16[12,128,128]{2,1,0:T(8,128)(2,1)S(1)}, bf16[12,128,128]{2,1,0:T(8,128)(2,1)S(1)}, u32[]{:S(2)}, u32[]{:S(2)}) collective-permute-start(bf16[12,128,128]{2,1,0:T(8,128)(2,1)S(1)} %shard_map.125.refs_0_), channel_id=1, source_target_pairs={{0,1},{1,2},{2,3},{3,0},{4,5},{5,6},{6,7},{7,4},{8,9},{9,10},{10,1... | collective-permute-start | bytes 1179656 | tf_op jit(solution)/shard_map/ppermute | solution.py:373
  40.0 1.9 %collective-permute-start.1 = (bf16[12,128,128]{2,1,0:T(8,128)(2,1)S(1)}, bf16[12,128,128]{2,1,0:T(8,128)(2,1)S(1)}, u32[]{:S(2)}, u32[]{:S(2)}) collective-permute-start(bf16[12,128,128]{2,1,0:T(8,128)(2,1)S(1)} %shard_map.125.refs_0_), channel_id=1, source_target_pairs={{0,2},{1,3},{2,0},{3,1},{4,6},{5,7},{6,4},{7,5},{8,10},{9,11},{10,... | collective-permute-start | bytes 1179656 | tf_op jit(solution)/shard_map/ppermute | solution.py:373
  42.0 8.7 %all-to-all-done.1.in_ref = bf16[16,48,128]{2,1,0:T(8,128)(2,1)S(1)} async-done(((bf16[16,48,128]{2,1,0:T(8,128)(2,1)}), bf16[16,48,128]{2,1,0:T(8,128)(2,1)S(1)}, u32[]{:S(2)}, u32[]{:S(2)}) %all-to-all-start.1) | async-done | bytes 196640 | tf_op jit(solution)/shard_map/all_to_all | solution.py:432
  50.7 0.7 shard_map.124
  51.4 4.4 %all-to-all-start.2 = ((bf16[16,24,128]{2,1,0:T(8,128)(2,1)}), bf16[16,24,128]{2,1,0:T(8,128)(2,1)S(1)}, u32[]{:S(2)}, u32[]{:S(2)}) async-start(bf16[16,24,128]{2,1,0:T(8,128)(2,1)} %get-tuple-element.19), calls=%async_computation.2 | async-start | bytes 196608 | tf_op jit(solution)/shard_map/all_to_all | solution.py:435
  55.8 2.3 %collective-permute-start.2 = (bf16[12,128,128]{2,1,0:T(8,128)(2,1)S(1)}, bf16[12,128,128]{2,1,0:T(8,128)(2,1)S(1)}, u32[]{:S(2)}, u32[]{:S(2)}) collective-permute-start(bf16[12,128,128]{2,1,0:T(8,128)(2,1)S(1)} %shard_map.125.refs_0_), channel_id=1, source_target_pairs={{0,3},{1,0},{2,1},{3,2},{4,7},{5,4},{6,5},{7,6},{8,11},{9,8},{10,9... | collective-permute-start | bytes 1179656 | tf_op jit(solution)/shard_map/ppermute | solution.py:373
  58.1 0.1 add.119
  58.2 0.1 copy.20
  58.3 0.1 gt.11
  58.4 0.1 add_select_fusion
  58.5 10.2 %all-to-all-done.2 = bf16[16,24,128]{2,1,0:T(8,128)(2,1)S(1)} async-done(((bf16[16,24,128]{2,1,0:T(8,128)(2,1)}), bf16[16,24,128]{2,1,0:T(8,128)(2,1)S(1)}, u32[]{:S(2)}, u32[]{:S(2)}) %all-to-all-start.2) | async-done | bytes 98336 | tf_op jit(solution)/shard_map/all_to_all | solution.py:435
  68.7 0.1 broadcast_in_dim.50.rowpos_ref
  68.8 3.1 %shard_map.126 = bf16[16,32,128]{2,1,0:T(8,128)(2,1)} custom-call(bf16[384,128]{1,0:T(8,128)(2,1)S(1)} %bitcast.9, s32[25,128]{1,0:T(8,128)S(1)} %pad_add_fusion.keypos_ref, s32[3,16,128]{2,1,0:T(8,128)S(1)} %broadcast_in_dim.50.rowpos_ref, bf16[2,16,128]{2,1,0:T(8,128)(2,1)S(1)} %get-tuple-element.20.new_ref, bf16[12,128,128]{2,1,0:T(8,128)(2,1)S(1)} %shard_map.125.refs_0_, ...), custom_call_target="tpu_custom_call" | custom-call | tf_op jit(solution)/shard_map/pallas_call | solution.py:42
  71.9 11.2 %all-to-all-start.3 = ((bf16[16,32,128]{2,1,0:T(8,128)(2,1)}), bf16[16,32,128]{2,1,0:T(8,128)(2,1)S(1)}, u32[]{:S(2)}, u32[]{:S(2)}) async-start(bf16[16,32,128]{2,1,0:T(8,128)(2,1)} %shard_map.126), calls=%async_computation.3 | async-start | bytes 262144 | tf_op jit(solution)/shard_map/all_to_all | solution.py:444
  83.2 2.8 %collective-permute-start.3 = (bf16[1024,128]{1,0:T(8,128)(2,1)S(1)}, bf16[1024,128]{1,0:T(8,128)(2,1)S(1)}, u32[]{:S(2)}, u32[]{:S(2)}) collective-permute-start(bf16[1024,128]{1,0:T(8,128)(2,1)S(1)} %copy-done.1), channel_id=1, source_target_pairs={{0,1},{1,2},{2,3},{3,0},{4,5},{5,6},{6,7},{7,4},{8,9},{9,10},{10,1... | collective-permute-start | bytes 786440 | tf_op jit(solution)/shard_map/ppermute | solution.py:373
  85.9 2.2 %collective-permute-start.4 = (bf16[1024,128]{1,0:T(8,128)(2,1)S(1)}, bf16[1024,128]{1,0:T(8,128)(2,1)S(1)}, u32[]{:S(2)}, u32[]{:S(2)}) collective-permute-start(bf16[1024,128]{1,0:T(8,128)(2,1)S(1)} %copy-done.1), channel_id=1, source_target_pairs={{0,2},{1,3},{2,0},{3,1},{4,6},{5,7},{6,4},{7,5},{8,10},{9,11},{10,... | collective-permute-start | bytes 786440 | tf_op jit(solution)/shard_map/ppermute | solution.py:373
  88.1 8.1 %all-to-all-done.3.in_ref = bf16[16,32,128]{2,1,0:T(8,128)(2,1)S(1)} async-done(((bf16[16,32,128]{2,1,0:T(8,128)(2,1)}), bf16[16,32,128]{2,1,0:T(8,128)(2,1)S(1)}, u32[]{:S(2)}, u32[]{:S(2)}) %all-to-all-start.3) | async-done | bytes 131104 | tf_op jit(solution)/shard_map/all_to_all | solution.py:444
  96.3 0.9 shard_map.127
  97.2 4.0 %all-to-all-start.4 = ((bf16[16,24,128]{2,1,0:T(8,128)(2,1)}), bf16[16,24,128]{2,1,0:T(8,128)(2,1)S(1)}, u32[]{:S(2)}, u32[]{:S(2)}) async-start(bf16[16,24,128]{2,1,0:T(8,128)(2,1)} %shard_map.127), calls=%async_computation.4 | async-start | bytes 196608 | tf_op jit(solution)/shard_map/all_to_all | solution.py:448
  101.3 5.0 %collective-permute-start.6 = (bf16[128,1280]{1,0:T(8,128)(2,1)S(1)}, bf16[128,1280]{1,0:T(8,128)(2,1)S(1)}, u32[]{:S(2)}, u32[]{:S(2)}) collective-permute-start(bf16[128,1280]{1,0:T(8,128)(2,1)S(1)} %copy-done), channel_id=1, source_target_pairs={{0,2},{1,3},{2,0},{3,1},{4,6},{5,7},{6,4},{7,5},{8,10},{9,11},{10,... | collective-permute-start | bytes 983048 | tf_op jit(solution)/shard_map/ppermute | solution.py:373
  106.3 3.1 %collective-permute-start.5 = (bf16[1024,128]{1,0:T(8,128)(2,1)S(1)}, bf16[1024,128]{1,0:T(8,128)(2,1)S(1)}, u32[]{:S(2)}, u32[]{:S(2)}) collective-permute-start(bf16[1024,128]{1,0:T(8,128)(2,1)S(1)} %copy-done.1), channel_id=1, source_target_pairs={{0,3},{1,0},{2,1},{3,2},{4,7},{5,4},{6,5},{7,6},{8,11},{9,8},{10,9... | collective-permute-start | bytes 786440 | tf_op jit(solution)/shard_map/ppermute | solution.py:373
  109.4 7.2 %collective-permute-done.5.refs_3_ = bf16[1024,128]{1,0:T(8,128)(2,1)S(1)} collective-permute-done((bf16[1024,128]{1,0:T(8,128)(2,1)S(1)}, bf16[1024,128]{1,0:T(8,128)(2,1)S(1)}, u32[]{:S(2)}, u32[]{:S(2)}) %collective-permute-start.5) | collective-permute-done | bytes 262176 | tf_op jit(solution)/shard_map/ppermute | solution.py:373
  116.6 1.0 shard_map.128
  117.6 4.5 %all-to-all-start.5 = ((bf16[8,48,512]{2,1,0:T(8,128)(2,1)}), bf16[8,48,512]{2,1,0:T(8,128)(2,1)S(1)}, u32[]{:S(2)}, u32[]{:S(2)}) async-start(bf16[8,48,512]{2,1,0:T(8,128)(2,1)} %shard_map.128), calls=%async_computation.5 | async-start | bytes 786432 | tf_op jit(solution)/shard_map/all_to_all | solution.py:458
  122.1 3.0 %collective-permute-start.7 = (bf16[128,1280]{1,0:T(8,128)(2,1)S(1)}, bf16[128,1280]{1,0:T(8,128)(2,1)S(1)}, u32[]{:S(2)}, u32[]{:S(2)}) collective-permute-start(bf16[128,1280]{1,0:T(8,128)(2,1)S(1)} %copy-done), channel_id=1, source_target_pairs={{0,1},{1,2},{2,3},{3,0},{4,5},{5,6},{6,7},{7,4},{8,9},{9,10},{10,1... | collective-permute-start | bytes 983048 | tf_op jit(solution)/shard_map/ppermute | solution.py:373
  125.1 2.8 %collective-permute-start.8 = (bf16[128,1280]{1,0:T(8,128)(2,1)S(1)}, bf16[128,1280]{1,0:T(8,128)(2,1)S(1)}, u32[]{:S(2)}, u32[]{:S(2)}) collective-permute-start(bf16[128,1280]{1,0:T(8,128)(2,1)S(1)} %copy-done), channel_id=1, source_target_pairs={{0,3},{1,0},{2,1},{3,2},{4,7},{5,4},{6,5},{7,6},{8,11},{9,8},{10,9... | collective-permute-start | bytes 983048 | tf_op jit(solution)/shard_map/ppermute | solution.py:373
  127.9 6.1 %collective-permute-done.7.refs_1_ = bf16[128,1280]{1,0:T(8,128)(2,1)S(1)} collective-permute-done((bf16[128,1280]{1,0:T(8,128)(2,1)S(1)}, bf16[128,1280]{1,0:T(8,128)(2,1)S(1)}, u32[]{:S(2)}, u32[]{:S(2)}) %collective-permute-start.7) | collective-permute-done | bytes 327712 | tf_op jit(solution)/shard_map/ppermute | solution.py:373
  134.1 4.0 %collective-permute-done.8.refs_3_ = bf16[128,1280]{1,0:T(8,128)(2,1)S(1)} collective-permute-done((bf16[128,1280]{1,0:T(8,128)(2,1)S(1)}, bf16[128,1280]{1,0:T(8,128)(2,1)S(1)}, u32[]{:S(2)}, u32[]{:S(2)}) %collective-permute-start.8) | collective-permute-done | bytes 327712 | tf_op jit(solution)/shard_map/ppermute | solution.py:373
  138.0 1.1 shard_map.129
  139.1 10.9 %all-to-all-start.6 = ((bf16[16,32,128]{2,1,0:T(8,128)(2,1)}), bf16[16,32,128]{2,1,0:T(8,128)(2,1)S(1)}, u32[]{:S(2)}, u32[]{:S(2)}) async-start(bf16[16,32,128]{2,1,0:T(8,128)(2,1)} %get-tuple-element.33), calls=%async_computation.6 | async-start | bytes 262144 | tf_op jit(solution)/shard_map/all_to_all | solution.py:466
  150.0 2.4 %collective-permute-start.9 = (bf16[48,128]{1,0:T(8,128)(2,1)S(1)}, bf16[48,128]{1,0:T(8,128)(2,1)S(1)}, u32[]{:S(2)}, u32[]{:S(2)}) collective-permute-start(bf16[48,128]{1,0:T(8,128)(2,1)S(1)} %get-tuple-element.30), channel_id=1, source_target_pairs={{0,3},{1,0},{2,1},{3,2},{4,7},{5,4},{6,5},{7,6},{8,11},{9,8},{10,9... | collective-permute-start | bytes 36872 | tf_op jit(solution)/shard_map/ppermute | solution.py:373
  152.5 4.1 %collective-permute-start.10 = (bf16[48,128]{1,0:T(8,128)(2,1)S(1)}, bf16[48,128]{1,0:T(8,128)(2,1)S(1)}, u32[]{:S(2)}, u32[]{:S(2)}) collective-permute-start(bf16[48,128]{1,0:T(8,128)(2,1)S(1)} %get-tuple-element.31), channel_id=1, source_target_pairs={{0,2},{1,3},{2,0},{3,1},{4,6},{5,7},{6,4},{7,5},{8,10},{9,11},{10,... | collective-permute-start | bytes 36872 | tf_op jit(solution)/shard_map/ppermute | solution.py:373
  156.6 3.1 %collective-permute-start.11 = (bf16[48,128]{1,0:T(8,128)(2,1)S(1)}, bf16[48,128]{1,0:T(8,128)(2,1)S(1)}, u32[]{:S(2)}, u32[]{:S(2)}) collective-permute-start(bf16[48,128]{1,0:T(8,128)(2,1)S(1)} %get-tuple-element.32), channel_id=1, source_target_pairs={{0,1},{1,2},{2,3},{3,0},{4,5},{5,6},{6,7},{7,4},{8,9},{9,10},{10,1... | collective-permute-start | bytes 36872 | tf_op jit(solution)/shard_map/ppermute | solution.py:373
  159.8 2.4 %collective-permute-done.11.refs_3_ = bf16[48,128]{1,0:T(8,128)(2,1)S(1)} collective-permute-done((bf16[48,128]{1,0:T(8,128)(2,1)S(1)}, bf16[48,128]{1,0:T(8,128)(2,1)S(1)}, u32[]{:S(2)}, u32[]{:S(2)}) %collective-permute-start.11) | collective-permute-done | bytes 12320 | tf_op jit(solution)/shard_map/ppermute | solution.py:373
  162.2 0.9 shard_map.130
  163.1 1.5 all-to-all-done.6.in_ref
  164.6 0.8 shard_map.131
  (36 shorter events, 0.2 us)
Async XLA Ops:
  2.9 9.6 %copy-start.7 = (s32[128]{0:T(128)S(1)}, s32[128]{0:T(128)}, u32[]{:S(2)}) copy-start(s32[128]{0:T(128)} %param.18) | copy-start | bytes 1540
  2.9 9.6 %copy-start.5 = (s32[128]{0:T(128)S(1)}, s32[128]{0:T(128)}, u32[]{:S(2)}) copy-start(s32[128]{0:T(128)} %param.19) | copy-start | bytes 1540
  3.0 9.9 %copy-start.4 = (s32[192]{0:T(256)S(1)}, s32[192]{0:T(256)}, u32[]{:S(2)}) copy-start(s32[192]{0:T(256)} %param.21) | copy-start | bytes 2308
  3.0 10.3 %copy-start.6 = (s32[128]{0:T(128)S(1)}, s32[128]{0:T(128)}, u32[]{:S(2)}) copy-start(s32[128]{0:T(128)} %param.20) | copy-start | bytes 1540
  3.0 17.2 %all-to-all-start = ((bf16[4,52,16,128]{3,2,1,0:T(8,128)(2,1)}), bf16[4,52,16,128]{3,2,1,0:T(8,128)(2,1)S(1)}, u32[]{:S(2)}, u32[]{:S(2)}) async-start(bf16[4,52,16,128]{3,2,1,0:T(8,128)(2,1)} %shard_map.122), calls=%async_computation | async-start | bytes 1703936 | tf_op jit(solution)/shard_map/all_to_all | solution.py:391
  12.4 22.6 %copy-start.2 = (bf16[768,128]{1,0:T(8,128)(2,1)S(1)}, bf16[768,128]{1,0:T(8,128)(2,1)}, u32[]{:S(2)}) copy-start(bf16[768,128]{1,0:T(8,128)(2,1)} %keys_ref.1) | copy-start | bytes 589828
  12.4 22.6 %copy-start.3 = (bf16[768,128]{1,0:T(8,128)(2,1)S(1)}, bf16[768,128]{1,0:T(8,128)(2,1)}, u32[]{:S(2)}) copy-start(bf16[768,128]{1,0:T(8,128)(2,1)} %values_ref.1) | copy-start | bytes 589828
  21.1 29.6 %all-to-all-start.1 = ((bf16[16,48,128]{2,1,0:T(8,128)(2,1)}), bf16[16,48,128]{2,1,0:T(8,128)(2,1)S(1)}, u32[]{:S(2)}, u32[]{:S(2)}) async-start(bf16[16,48,128]{2,1,0:T(8,128)(2,1)} %get-tuple-element.18), calls=%async_computation.1 | async-start | bytes 393216 | tf_op jit(solution)/shard_map/all_to_all | solution.py:432
  36.1 22.4 %collective-permute-start = (bf16[12,128,128]{2,1,0:T(8,128)(2,1)S(1)}, bf16[12,128,128]{2,1,0:T(8,128)(2,1)S(1)}, u32[]{:S(2)}, u32[]{:S(2)}) collective-permute-start(bf16[12,128,128]{2,1,0:T(8,128)(2,1)S(1)} %shard_map.125.refs_0_), channel_id=1, source_target_pairs={{0,1},{1,2},{2,3},{3,0},{4,5},{5,6},{6,7},{7,4},{8,9},{9,10},{10,1... | collective-permute-start | bytes 1179656 | tf_op jit(solution)/shard_map/ppermute | solution.py:373
  40.0 18.5 %collective-permute-start.1 = (bf16[12,128,128]{2,1,0:T(8,128)(2,1)S(1)}, bf16[12,128,128]{2,1,0:T(8,128)(2,1)S(1)}, u32[]{:S(2)}, u32[]{:S(2)}) collective-permute-start(bf16[12,128,128]{2,1,0:T(8,128)(2,1)S(1)} %shard_map.125.refs_0_), channel_id=1, source_target_pairs={{0,2},{1,3},{2,0},{3,1},{4,6},{5,7},{6,4},{7,5},{8,10},{9,11},{10,... | collective-permute-start | bytes 1179656 | tf_op jit(solution)/shard_map/ppermute | solution.py:373
  51.4 17.3 %all-to-all-start.2 = ((bf16[16,24,128]{2,1,0:T(8,128)(2,1)}), bf16[16,24,128]{2,1,0:T(8,128)(2,1)S(1)}, u32[]{:S(2)}, u32[]{:S(2)}) async-start(bf16[16,24,128]{2,1,0:T(8,128)(2,1)} %get-tuple-element.19), calls=%async_computation.2 | async-start | bytes 196608 | tf_op jit(solution)/shard_map/all_to_all | solution.py:435
  55.8 12.9 %collective-permute-start.2 = (bf16[12,128,128]{2,1,0:T(8,128)(2,1)S(1)}, bf16[12,128,128]{2,1,0:T(8,128)(2,1)S(1)}, u32[]{:S(2)}, u32[]{:S(2)}) collective-permute-start(bf16[12,128,128]{2,1,0:T(8,128)(2,1)S(1)} %shard_map.125.refs_0_), channel_id=1, source_target_pairs={{0,3},{1,0},{2,1},{3,2},{4,7},{5,4},{6,5},{7,6},{8,11},{9,8},{10,9... | collective-permute-start | bytes 1179656 | tf_op jit(solution)/shard_map/ppermute | solution.py:373
  68.8 14.4 %copy-start.1 = (bf16[1024,128]{1,0:T(8,128)(2,1)S(1)}, bf16[1024,128]{1,0:T(8,128)(2,1)}, u32[]{:S(2)}) copy-start(bf16[1024,128]{1,0:T(8,128)(2,1)} %refs_0_.2) | copy-start | bytes 786436
  68.8 32.5 %copy-start = (bf16[128,1280]{1,0:T(8,128)(2,1)S(1)}, bf16[128,1280]{1,0:T(8,128)(2,1)}, u32[]{:S(2)}) copy-start(bf16[128,1280]{1,0:T(8,128)(2,1)} %refs_0_.3) | copy-start | bytes 983044
  71.9 24.4 %all-to-all-start.3 = ((bf16[16,32,128]{2,1,0:T(8,128)(2,1)}), bf16[16,32,128]{2,1,0:T(8,128)(2,1)S(1)}, u32[]{:S(2)}, u32[]{:S(2)}) async-start(bf16[16,32,128]{2,1,0:T(8,128)(2,1)} %shard_map.126), calls=%async_computation.3 | async-start | bytes 262144 | tf_op jit(solution)/shard_map/all_to_all | solution.py:444
  83.2 18.1 %collective-permute-start.3 = (bf16[1024,128]{1,0:T(8,128)(2,1)S(1)}, bf16[1024,128]{1,0:T(8,128)(2,1)S(1)}, u32[]{:S(2)}, u32[]{:S(2)}) collective-permute-start(bf16[1024,128]{1,0:T(8,128)(2,1)S(1)} %copy-done.1), channel_id=1, source_target_pairs={{0,1},{1,2},{2,3},{3,0},{4,5},{5,6},{6,7},{7,4},{8,9},{9,10},{10,1... | collective-permute-start | bytes 786440 | tf_op jit(solution)/shard_map/ppermute | solution.py:373
  85.9 15.3 %collective-permute-start.4 = (bf16[1024,128]{1,0:T(8,128)(2,1)S(1)}, bf16[1024,128]{1,0:T(8,128)(2,1)S(1)}, u32[]{:S(2)}, u32[]{:S(2)}) collective-permute-start(bf16[1024,128]{1,0:T(8,128)(2,1)S(1)} %copy-done.1), channel_id=1, source_target_pairs={{0,2},{1,3},{2,0},{3,1},{4,6},{5,7},{6,4},{7,5},{8,10},{9,11},{10,... | collective-permute-start | bytes 786440 | tf_op jit(solution)/shard_map/ppermute | solution.py:373
  97.2 19.4 %all-to-all-start.4 = ((bf16[16,24,128]{2,1,0:T(8,128)(2,1)}), bf16[16,24,128]{2,1,0:T(8,128)(2,1)S(1)}, u32[]{:S(2)}, u32[]{:S(2)}) async-start(bf16[16,24,128]{2,1,0:T(8,128)(2,1)} %shard_map.127), calls=%async_computation.4 | async-start | bytes 196608 | tf_op jit(solution)/shard_map/all_to_all | solution.py:448
  101.3 20.8 %collective-permute-start.6 = (bf16[128,1280]{1,0:T(8,128)(2,1)S(1)}, bf16[128,1280]{1,0:T(8,128)(2,1)S(1)}, u32[]{:S(2)}, u32[]{:S(2)}) collective-permute-start(bf16[128,1280]{1,0:T(8,128)(2,1)S(1)} %copy-done), channel_id=1, source_target_pairs={{0,2},{1,3},{2,0},{3,1},{4,6},{5,7},{6,4},{7,5},{8,10},{9,11},{10,... | collective-permute-start | bytes 983048 | tf_op jit(solution)/shard_map/ppermute | solution.py:373
  106.3 10.3 %collective-permute-start.5 = (bf16[1024,128]{1,0:T(8,128)(2,1)S(1)}, bf16[1024,128]{1,0:T(8,128)(2,1)S(1)}, u32[]{:S(2)}, u32[]{:S(2)}) collective-permute-start(bf16[1024,128]{1,0:T(8,128)(2,1)S(1)} %copy-done.1), channel_id=1, source_target_pairs={{0,3},{1,0},{2,1},{3,2},{4,7},{5,4},{6,5},{7,6},{8,11},{9,8},{10,9... | collective-permute-start | bytes 786440 | tf_op jit(solution)/shard_map/ppermute | solution.py:373
  117.6 20.4 %all-to-all-start.5 = ((bf16[8,48,512]{2,1,0:T(8,128)(2,1)}), bf16[8,48,512]{2,1,0:T(8,128)(2,1)S(1)}, u32[]{:S(2)}, u32[]{:S(2)}) async-start(bf16[8,48,512]{2,1,0:T(8,128)(2,1)} %shard_map.128), calls=%async_computation.5 | async-start | bytes 786432 | tf_op jit(solution)/shard_map/all_to_all | solution.py:458
  122.1 12.0 %collective-permute-start.7 = (bf16[128,1280]{1,0:T(8,128)(2,1)S(1)}, bf16[128,1280]{1,0:T(8,128)(2,1)S(1)}, u32[]{:S(2)}, u32[]{:S(2)}) collective-permute-start(bf16[128,1280]{1,0:T(8,128)(2,1)S(1)} %copy-done), channel_id=1, source_target_pairs={{0,1},{1,2},{2,3},{3,0},{4,5},{5,6},{6,7},{7,4},{8,9},{9,10},{10,1... | collective-permute-start | bytes 983048 | tf_op jit(solution)/shard_map/ppermute | solution.py:373
  125.1 12.9 %collective-permute-start.8 = (bf16[128,1280]{1,0:T(8,128)(2,1)S(1)}, bf16[128,1280]{1,0:T(8,128)(2,1)S(1)}, u32[]{:S(2)}, u32[]{:S(2)}) collective-permute-start(bf16[128,1280]{1,0:T(8,128)(2,1)S(1)} %copy-done), channel_id=1, source_target_pairs={{0,3},{1,0},{2,1},{3,2},{4,7},{5,4},{6,5},{7,6},{8,11},{9,8},{10,9... | collective-permute-start | bytes 983048 | tf_op jit(solution)/shard_map/ppermute | solution.py:373
  139.1 25.5 %all-to-all-start.6 = ((bf16[16,32,128]{2,1,0:T(8,128)(2,1)}), bf16[16,32,128]{2,1,0:T(8,128)(2,1)S(1)}, u32[]{:S(2)}, u32[]{:S(2)}) async-start(bf16[16,32,128]{2,1,0:T(8,128)(2,1)} %get-tuple-element.33), calls=%async_computation.6 | async-start | bytes 262144 | tf_op jit(solution)/shard_map/all_to_all | solution.py:466
  150.0 9.7 %collective-permute-start.9 = (bf16[48,128]{1,0:T(8,128)(2,1)S(1)}, bf16[48,128]{1,0:T(8,128)(2,1)S(1)}, u32[]{:S(2)}, u32[]{:S(2)}) collective-permute-start(bf16[48,128]{1,0:T(8,128)(2,1)S(1)} %get-tuple-element.30), channel_id=1, source_target_pairs={{0,3},{1,0},{2,1},{3,2},{4,7},{5,4},{6,5},{7,6},{8,11},{9,8},{10,9... | collective-permute-start | bytes 36872 | tf_op jit(solution)/shard_map/ppermute | solution.py:373
  152.5 7.3 %collective-permute-start.10 = (bf16[48,128]{1,0:T(8,128)(2,1)S(1)}, bf16[48,128]{1,0:T(8,128)(2,1)S(1)}, u32[]{:S(2)}, u32[]{:S(2)}) collective-permute-start(bf16[48,128]{1,0:T(8,128)(2,1)S(1)} %get-tuple-element.31), channel_id=1, source_target_pairs={{0,2},{1,3},{2,0},{3,1},{4,6},{5,7},{6,4},{7,5},{8,10},{9,11},{10,... | collective-permute-start | bytes 36872 | tf_op jit(solution)/shard_map/ppermute | solution.py:373
  156.6 5.6 %collective-permute-start.11 = (bf16[48,128]{1,0:T(8,128)(2,1)S(1)}, bf16[48,128]{1,0:T(8,128)(2,1)S(1)}, u32[]{:S(2)}, u32[]{:S(2)}) collective-permute-start(bf16[48,128]{1,0:T(8,128)(2,1)S(1)} %get-tuple-element.32), channel_id=1, source_target_pairs={{0,1},{1,2},{2,3},{3,0},{4,5},{5,6},{6,7},{7,4},{8,9},{9,10},{10,1... | collective-permute-start | bytes 36872 | tf_op jit(solution)/shard_map/ppermute | solution.py:373

commit v5 on v3

--- a/solution.py
+++ b/solution.py
@@ -34,7 +34,7 @@
 f32 = jnp.float32
 
 
-def vmem_call(kernel, out_shape, operands, scratch=(), limit=32, scalars=0, hbm=False):
+def vmem_call(kernel, out_shape, operands, scratch=(), limit=12, scalars=0, hbm=False):
     space = pl.BlockSpec(memory_space=pltpu.VMEM)
     outs = jax.tree.map(lambda _: space, out_shape)
     rest = pl.BlockSpec(memory_space=pltpu.HBM) if hbm else space
@@ -72,21 +72,29 @@
     return jnp.concatenate([cosine, cosine], -1), jnp.concatenate([-sine, sine], -1)
 
 
-def bundle_kernel(keys_ref, values_ref, cos_ref, sin_ref, out_weight_ref, next_weight_ref, out_ref, weights_ref):
+def bundle_kernel(keys_ref, values_ref, cos_ref, sin_ref, out_weight_ref, next_weight_ref, cache_ref, weights_ref, both_ref):
     blocks = keys_ref.shape[0] // BLK
     for b in range(blocks):
-        out_ref[blocks + b] = values_ref[b * BLK : (b + 1) * BLK, :]
+        values = values_ref[b * BLK : (b + 1) * BLK, :]
+        cache_ref[blocks + b] = values
+        both_ref[blocks + b] = values
         block = keys_ref[b * BLK : (b + 1) * BLK, :].astype(f32)
         turned = (
             block * cos_ref[b : b + 1, :]
             + pltpu.roll(block, HD // 2, 1) * sin_ref[b : b + 1, :]
         )
         turned = turned.astype(bf16).astype(f32)
-        out_ref[b] = turned.T.astype(bf16)
+        turned = turned.T.astype(bf16)
+        cache_ref[b] = turned
+        both_ref[b] = turned
     for g in range(GQ):
-        weights_ref[g] = out_weight_ref[g * HD : (g + 1) * HD, :]
+        block = out_weight_ref[g * HD : (g + 1) * HD, :]
+        weights_ref[g] = block
+        both_ref[2 * blocks + g] = block
     for j in range(GQ + 2):
-        weights_ref[GQ + j] = next_weight_ref[:, j * HD : (j + 1) * HD]
+        block = next_weight_ref[:, j * HD : (j + 1) * HD]
+        weights_ref[GQ + j] = block
+        both_ref[2 * blocks + GQ + j] = block
 
 
 def project_kernel(hidden_hbm, weight_hbm, gain_hbm, out_ref, hidden_ref, weight_ref, gain_ref, sems):
@@ -167,7 +175,7 @@
 
 def attend_kernel(queries_ref, keypos_ref, rowpos_ref, new_ref, *refs):
     cache_refs, (out_ref, score_ref) = refs[:NX], refs[NX:]
-    blocks = cache_refs[0].shape[0] // 2
+    blocks = (keypos_ref.shape[0] - 1) // NX
     scale = HD ** (-0.5) * LOG2E
     contract_last = (((1,), (1,)), ((), ()))
     new_keys, new_values = new_ref[0], new_ref[1]
@@ -255,8 +263,12 @@
         out_ref[z] = result
 
 
+def weight_blocks(refs, first, count):
+    return [ref.at[pl.ds(ref.shape[0] - (2 * GQ + 2) + first, count)] for ref in refs]
+
+
 def output_kernel(heads_ref, *refs):
-    weight_refs, out_ref = [ref.at[pl.ds(0, GQ)] for ref in refs[:NX]], refs[NX]
+    weight_refs, out_ref = weight_blocks(refs[:NX], 0, GQ), refs[NX]
     rows = heads_ref[...]
     bands = []
     for i in range(RI):
@@ -272,7 +284,7 @@
 
 
 def next_kernel(terms_ref, hidden_ref, gain_ref, *refs):
-    weight_refs = [ref.at[pl.ds(GQ, GQ + 2)] for ref in refs[:NX]]
+    weight_refs = weight_blocks(refs[:NX], GQ, GQ + 2)
     resid_refs, (out_ref, cut_ref) = refs[NX : 2 * NX], refs[2 * NX :]
     attended = terms_ref[0].astype(f32)
     for h in range(1, NH):
@@ -378,9 +390,6 @@
     def shifted(array, step):
         return lax.ppermute(array, "x", [(n, (n + step) % NX) for n in range(NX)])
 
-    def after(array, first):
-        return lax.optimization_barrier((array, first))[0]
-
     payload = vmem_call(
         project_kernel,
         shaped((NX, HT + RI + 1, TILE, HD), bf16),
@@ -413,9 +422,10 @@
         jnp.concatenate([query_pos, new_pos, jnp.zeros((NX * RI,), jnp.int32), shift[0]])
     )
     rows = 8 * RI + KT
-    cache, weights = vmem_call(
+    counts = (2 * blocks, 2 * GQ + 2, 2 * blocks + 2 * GQ + 2)
+    cache, weights, both = vmem_call(
         bundle_kernel,
-        (shaped((2 * blocks, BLK, HD), bf16), shaped((2 * GQ + 2, HD, HD), bf16)),
+        tuple(shaped((count, HD, HD), bf16) for count in counts),
         (cache_keys, cache_values, cosine[rows:], sine[rows:], out_weight, next_weight),
     )
 
@@ -431,14 +441,13 @@
         scratch=[pltpu.VMEM((NZ, KT, HD), f32)],
         scalars=1,
     )
-    caches = [cache] + [shifted(after(cache, tiles), step) for step in (1, 3)]
+    tiles, cache, both = lax.optimization_barrier((tiles, cache, both))
+    caches = [cache, shifted(cache, 1), shifted(cache, 2), shifted(both, 3)]
     copies, new = vmem_call(
         rope_kernel,
         (shaped((NZ, 8 * RI, HD), bf16), shaped((2, FRESH, HD), bf16)),
         (a2a(tiles, "z"), cosine[:rows], sine[:rows]),
     )
-    caches.insert(2, shifted(after(cache, copies), 2))
-    weights_x = [weights, shifted(after(weights, copies), 1)]
     queries = a2a(copies, "z").reshape(XR * GQ, HD)
     parts = vmem_call(
         attend_kernel,
@@ -446,7 +455,8 @@
         (queries, key_pos, wide_row_pos, new, *caches),
         scratch=[pltpu.VMEM((HD, (NX * blocks + 2 * RI) * BLK), f32)],
     )
-    weights_x += [shifted(after(weights, parts), step) for step in (2, 3)]
+    parts, weights = lax.optimization_barrier((parts, weights))
+    weights_x = [weights, shifted(weights, 1), shifted(weights, 2), caches[3]]
     share = vmem_call(
         combine_kernel, shaped((NZ, 8 * RI, HD), bf16), (a2a(parts, "z"),)
     )

time: 157 us -> 155 us (0.987); the launches traced: 157 us -> 152 us
  starting transfers between devices: 84.7 us -> 74.9 us
  waiting for transfers between devices: 43.3 us -> 47.7 us
    all_to_all x1, waiting for transfers between devices: 4.24 us -> 12.9 us  [on_device(): heads_out = a2a(share, 'z').reshape(XR * GQ, HD)]
    all_to_all x1, waiting for transfers between devices: 8.88 us -> 2.38 us  [on_device(): queries = a2a(copies, 'z').reshape(XR * GQ, HD)]
    all_to_all x1, waiting for transfers between devices: 3.46 us -> 8.75 us  [on_device(): a2a(parts, 'z')]
    all_to_all x1, starting transfers between devices: 8.56 us -> 3.99 us  [on_device(): heads_out = a2a(share, 'z').reshape(XR * GQ, HD)]
    all_to_all x1, starting transfers between devices: 7.51 us -> 3.51 us  [on_device(): a2a(products, 'z')]
    ppermute x9 -> x8, waiting for transfers between devices: 11.2 us -> 14.1 us  [shifted(): return lax.ppermute(array, 'x', [(n, (n + step) % NX) for n in range(NX)])]
    all_to_all x1, starting transfers between devices: 4.52 us -> 6.85 us  [on_device(): queries = a2a(copies, 'z').reshape(XR * GQ, HD)]
    all_to_all x1, waiting for transfers between devices: 7.52 us -> 5.18 us  [on_device(): a2a(tiles, 'z')]
  transfers between devices with their start and end apart: 15 -> 14, of which waited for: 9 -> 8; matrix products, arithmetic and copies ran while one was open for 2% -> 2% of each run, Pallas kernels for 2% -> 2%
where the time goes in v5:
time: 155 us; the launch traced here: 152 us
  starting transfers between devices  74.9 us (48%)
  waiting for transfers between devices  47.7 us (31%)
  blocking collectives  13.2 us (9%)
  Pallas kernels  11.5 us (7%)
  other arithmetic  2.02 us (1%)
  local copies, waits for them, and re-layouts  2 us (1%)
    ppermute x8, starting transfers between devices, shifted(): return lax.ppermute(array, 'x', [(n, (n + step) % NX) for n in range(NX)])  27.9 us
    ppermute x8, waiting for transfers between devices, shifted(): return lax.ppermute(array, 'x', [(n, (n + step) % NX) for n in range(NX)])  14.1 us
    all_to_all x1, starting transfers between devices, on_device(): a2a(tiles, 'z')  13.8 us
    all_to_all x1, blocking collectives, on_device(): a2a(terms, 'heads')  13.2 us
    all_to_all x1, waiting for transfers between devices, on_device(): heads_out = a2a(share, 'z').reshape(XR * GQ, HD)  12.9 us
    pallas_call x10, Pallas kernels, vmem_call(): pl.pallas_call(kernel, out_shape=out_shape, in_specs=[small] * scalars +...  11.5 us
    all_to_all x1, starting transfers between devices, on_device(): payload = a2a(payload, 'x')  9.47 us
    all_to_all x1, starting transfers between devices, on_device(): a2a(parts, 'z')  9.37 us
  transfers between devices with their start and end apart: 14, of which 8 were waited for; matrix products, arithmetic and copies ran while one was open for 2% of the time, Pallas kernels for 2%

profile of v5, /device:TPU:6, one launch (start us, length us, event | category | flops | bytes accessed | tf_op | source)
XLA Modules:
  0.0 152.3 jit_solution(12692457335195056393)
XLA Ops:
  0.6 2.4 %shard_map.122 = bf16[4,52,16,128]{3,2,1,0:T(8,128)(2,1)} custom-call(bf16[192,128]{1,0:T(8,128)(2,1)} %hidden_hbm.1, bf16[128,1280]{1,0:T(8,128)(2,1)} %weight_hbm.1, f32[1,128]{1,0:T(1,128)} %bitcast.13), custom_call_target="tpu_custom_call" | custom-call | tf_op jit(solution)/shard_map/pallas_call | solution.py:42
  3.0 0.0 copy-start.8
  3.0 0.0 copy-start.6
  3.0 0.0 copy-start.7
  3.0 0.0 copy-start.5
  3.0 0.0 copy-start
  3.0 0.0 copy-start.1
  3.1 0.0 copy-start.2
  3.1 0.0 copy-start.3
  3.1 9.5 %all-to-all-start = ((bf16[4,52,16,128]{3,2,1,0:T(8,128)(2,1)}), bf16[4,52,16,128]{3,2,1,0:T(8,128)(2,1)S(1)}, u32[]{:S(2)}, u32[]{:S(2)}) async-start(bf16[4,52,16,128]{3,2,1,0:T(8,128)(2,1)} %shard_map.122), calls=%async_computation | async-start | bytes 1703936 | tf_op jit(solution)/shard_map/all_to_all | solution.py:406
  12.6 0.1 fusion.3
  12.7 0.1 compare_select_fusion
  12.8 0.1 select_reduce_fusion
  13.0 0.4 select_reduce_fusion.1
  13.3 0.1 slice_reduce_fusion
  13.5 0.2 reshape.214
  13.6 0.1 copy.19
  13.7 0.1 broadcast_in_dim.38
  13.8 0.1 concatenate.25
  13.9 0.2 select_reduce_fusion.3
  14.1 0.1 add_convert_fusion
  14.2 0.2 fusion.2
  14.4 0.1 pad_maximum_fusion.2
  14.5 0.4 shard_map.124
  14.9 0.9 copy-done.4
  15.8 4.5 %all-to-all-done.in_ref = bf16[4,52,16,128]{3,2,1,0:T(8,128)(2,1)S(1)} async-done(((bf16[4,52,16,128]{3,2,1,0:T(8,128)(2,1)}), bf16[4,52,16,128]{3,2,1,0:T(8,128)(2,1)S(1)}, u32[]{:S(2)}, u32[]{:S(2)}) %all-to-all-start) | async-done | bytes 852000 | tf_op jit(solution)/shard_map/all_to_all | solution.py:406
  20.3 0.9 shard_map.123
  21.2 13.8 %all-to-all-start.1 = ((bf16[16,48,128]{2,1,0:T(8,128)(2,1)}), bf16[16,48,128]{2,1,0:T(8,128)(2,1)S(1)}, u32[]{:S(2)}, u32[]{:S(2)}) async-start(bf16[16,48,128]{2,1,0:T(8,128)(2,1)} %get-tuple-element.23), calls=%async_computation.1 | async-start | bytes 393216 | tf_op jit(solution)/shard_map/all_to_all | solution.py:449
  35.0 0.1 copy.21
  35.1 1.9 %collective-permute-start.2 = (bf16[30,128,128]{2,1,0:T(8,128)(2,1)}, bf16[30,128,128]{2,1,0:T(8,128)(2,1)S(1)}, u32[]{:S(2)}, u32[]{:S(2)}) collective-permute-start(bf16[30,128,128]{2,1,0:T(8,128)(2,1)} %copy-done.4), channel_id=1, source_target_pairs={{0,3},{1,0},{2,1},{3,2},{4,7},{5,4},{6,5},{7,6},{8,11},{9,8},{10,9... | collective-permute-start | bytes 2949128 | tf_op jit(solution)/shard_map/ppermute | solution.py:391
  37.0 0.1 iota_add_fusion
  37.1 0.1 pad_maximum_fusion
  37.2 0.5 compare_reduce_fusion
  37.7 5.1 %collective-permute-start = (bf16[12,128,128]{2,1,0:T(8,128)(2,1)S(1)}, bf16[12,128,128]{2,1,0:T(8,128)(2,1)S(1)}, u32[]{:S(2)}, u32[]{:S(2)}) collective-permute-start(bf16[12,128,128]{2,1,0:T(8,128)(2,1)S(1)} %get-tuple-element.26.refs_0_), channel_id=1, source_target_pairs={{0,1},{1,2},{2,3},{3,0},{4,5},{5,6},{6,7},{7,4},{8,9},{9,10},{10,1... | collective-permute-start | bytes 1179656 | tf_op jit(solution)/shard_map/ppermute | solution.py:391
  42.8 2.8 %collective-permute-start.1 = (bf16[12,128,128]{2,1,0:T(8,128)(2,1)S(1)}, bf16[12,128,128]{2,1,0:T(8,128)(2,1)S(1)}, u32[]{:S(2)}, u32[]{:S(2)}) collective-permute-start(bf16[12,128,128]{2,1,0:T(8,128)(2,1)S(1)} %get-tuple-element.26.refs_0_), channel_id=1, source_target_pairs={{0,2},{1,3},{2,0},{3,1},{4,6},{5,7},{6,4},{7,5},{8,10},{9,11},{10,... | collective-permute-start | bytes 1179656 | tf_op jit(solution)/shard_map/ppermute | solution.py:391
  45.6 5.2 %all-to-all-done.1.in_ref = bf16[16,48,128]{2,1,0:T(8,128)(2,1)S(1)} async-done(((bf16[16,48,128]{2,1,0:T(8,128)(2,1)}), bf16[16,48,128]{2,1,0:T(8,128)(2,1)S(1)}, u32[]{:S(2)}, u32[]{:S(2)}) %all-to-all-start.1) | async-done | bytes 196640 | tf_op jit(solution)/shard_map/all_to_all | solution.py:449
  50.8 0.7 shard_map.125
  51.5 6.9 %all-to-all-start.2 = ((bf16[16,24,128]{2,1,0:T(8,128)(2,1)}), bf16[16,24,128]{2,1,0:T(8,128)(2,1)S(1)}, u32[]{:S(2)}, u32[]{:S(2)}) async-start(bf16[16,24,128]{2,1,0:T(8,128)(2,1)} %get-tuple-element.24), calls=%async_computation.2 | async-start | bytes 196608 | tf_op jit(solution)/shard_map/all_to_all | solution.py:451
  58.4 0.1 add.119
  58.5 0.1 copy.20
  58.6 0.1 gt.11
  58.7 0.1 add_select_fusion
  58.8 10.3 %collective-permute-done.1.refs_2_ = bf16[12,128,128]{2,1,0:T(8,128)(2,1)S(1)} collective-permute-done((bf16[12,128,128]{2,1,0:T(8,128)(2,1)S(1)}, bf16[12,128,128]{2,1,0:T(8,128)(2,1)S(1)}, u32[]{:S(2)}, u32[]{:S(2)}) %collective-permute-start.1) | collective-permute-done | bytes 393248 | tf_op jit(solution)/shard_map/ppermute | solution.py:391
  69.1 2.4 %all-to-all-done.2 = bf16[16,24,128]{2,1,0:T(8,128)(2,1)S(1)} async-done(((bf16[16,24,128]{2,1,0:T(8,128)(2,1)}), bf16[16,24,128]{2,1,0:T(8,128)(2,1)S(1)}, u32[]{:S(2)}, u32[]{:S(2)}) %all-to-all-start.2) | async-done | bytes 98336 | tf_op jit(solution)/shard_map/all_to_all | solution.py:451
  71.5 0.1 broadcast_in_dim.50.rowpos_ref
  71.6 3.1 %shard_map.126 = bf16[16,32,128]{2,1,0:T(8,128)(2,1)} custom-call(bf16[384,128]{1,0:T(8,128)(2,1)S(1)} %bitcast.9, s32[25,128]{1,0:T(8,128)S(1)} %pad_add_fusion.keypos_ref, s32[3,16,128]{2,1,0:T(8,128)S(1)} %broadcast_in_dim.50.rowpos_ref, bf16[2,16,128]{2,1,0:T(8,128)(2,1)S(1)} %get-tuple-element.25.new_ref, ...), custom_call_target="tpu_custom_call" | custom-call | tf_op jit(solution)/shard_map/pallas_call | solution.py:42
  74.7 9.4 %all-to-all-start.3 = ((bf16[16,32,128]{2,1,0:T(8,128)(2,1)}), bf16[16,32,128]{2,1,0:T(8,128)(2,1)S(1)}, u32[]{:S(2)}, u32[]{:S(2)}) async-start(bf16[16,32,128]{2,1,0:T(8,128)(2,1)} %shard_map.126), calls=%async_computation.3 | async-start | bytes 262144 | tf_op jit(solution)/shard_map/all_to_all | solution.py:461
  84.1 1.9 %collective-permute-start.3 = (bf16[18,128,128]{2,1,0:T(8,128)(2,1)S(1)}, bf16[18,128,128]{2,1,0:T(8,128)(2,1)S(1)}, u32[]{:S(2)}, u32[]{:S(2)}) collective-permute-start(bf16[18,128,128]{2,1,0:T(8,128)(2,1)S(1)} %get-tuple-element.30.refs_0_), channel_id=1, source_target_pairs={{0,1},{1,2},{2,3},{3,0},{4,5},{5,6},{6,7},{7,4},{8,9},{9,10},{10,1... | collective-permute-start | bytes 1769480 | tf_op jit(solution)/shard_map/ppermute | solution.py:391
  86.0 2.5 %collective-permute-start.4 = (bf16[18,128,128]{2,1,0:T(8,128)(2,1)S(1)}, bf16[18,128,128]{2,1,0:T(8,128)(2,1)S(1)}, u32[]{:S(2)}, u32[]{:S(2)}) collective-permute-start(bf16[18,128,128]{2,1,0:T(8,128)(2,1)S(1)} %get-tuple-element.30.refs_0_), channel_id=1, source_target_pairs={{0,2},{1,3},{2,0},{3,1},{4,6},{5,7},{6,4},{7,5},{8,10},{9,11},{10,... | collective-permute-start | bytes 1769480 | tf_op jit(solution)/shard_map/ppermute | solution.py:391
  88.5 8.7 %all-to-all-done.3.in_ref = bf16[16,32,128]{2,1,0:T(8,128)(2,1)S(1)} async-done(((bf16[16,32,128]{2,1,0:T(8,128)(2,1)}), bf16[16,32,128]{2,1,0:T(8,128)(2,1)S(1)}, u32[]{:S(2)}, u32[]{:S(2)}) %all-to-all-start.3) | async-done | bytes 131104 | tf_op jit(solution)/shard_map/all_to_all | solution.py:461
  97.2 0.9 shard_map.127
  98.2 4.0 %all-to-all-start.4 = ((bf16[16,24,128]{2,1,0:T(8,128)(2,1)}), bf16[16,24,128]{2,1,0:T(8,128)(2,1)S(1)}, u32[]{:S(2)}, u32[]{:S(2)}) async-start(bf16[16,24,128]{2,1,0:T(8,128)(2,1)} %shard_map.127), calls=%async_computation.4 | async-start | bytes 196608 | tf_op jit(solution)/shard_map/all_to_all | solution.py:463
  102.2 0.1 collective-permute-done.3.refs_1_
  102.3 12.9 %all-to-all-done.4 = bf16[16,24,128]{2,1,0:T(8,128)(2,1)S(1)} async-done(((bf16[16,24,128]{2,1,0:T(8,128)(2,1)}), bf16[16,24,128]{2,1,0:T(8,128)(2,1)S(1)}, u32[]{:S(2)}, u32[]{:S(2)}) %all-to-all-start.4) | async-done | bytes 98336 | tf_op jit(solution)/shard_map/all_to_all | solution.py:463
  115.1 0.3 shard_map.128
  115.4 13.2 %all_to_all.35.terms_ref = bf16[8,48,512]{2,1,0:T(8,128)(2,1)S(1)} all-to-all(bf16[8,48,512]{2,1,0:T(8,128)(2,1)S(1)} %shard_map.128), channel_id=1, replica_groups=mesh['heads'=8,'z'=16,'x'=4] {'heads'}, dimensions={0} | all-to-all | bytes 786432 | tf_op jit(solution)/shard_map/all_to_all | solution.py:470
  128.7 1.1 shard_map.129
  129.8 3.5 %all-to-all-start.6 = ((bf16[16,32,128]{2,1,0:T(8,128)(2,1)}), bf16[16,32,128]{2,1,0:T(8,128)(2,1)S(1)}, u32[]{:S(2)}, u32[]{:S(2)}) async-start(bf16[16,32,128]{2,1,0:T(8,128)(2,1)} %get-tuple-element.37), calls=%async_computation.6 | async-start | bytes 262144 | tf_op jit(solution)/shard_map/all_to_all | solution.py:478
  133.3 5.7 %collective-permute-start.5 = (bf16[48,128]{1,0:T(8,128)(2,1)S(1)}, bf16[48,128]{1,0:T(8,128)(2,1)S(1)}, u32[]{:S(2)}, u32[]{:S(2)}) collective-permute-start(bf16[48,128]{1,0:T(8,128)(2,1)S(1)} %get-tuple-element.34), channel_id=1, source_target_pairs={{0,3},{1,0},{2,1},{3,2},{4,7},{5,4},{6,5},{7,6},{8,11},{9,8},{10,9... | collective-permute-start | bytes 36872 | tf_op jit(solution)/shard_map/ppermute | solution.py:391
  139.0 6.0 %collective-permute-start.6 = (bf16[48,128]{1,0:T(8,128)(2,1)S(1)}, bf16[48,128]{1,0:T(8,128)(2,1)S(1)}, u32[]{:S(2)}, u32[]{:S(2)}) collective-permute-start(bf16[48,128]{1,0:T(8,128)(2,1)S(1)} %get-tuple-element.35), channel_id=1, source_target_pairs={{0,2},{1,3},{2,0},{3,1},{4,6},{5,7},{6,4},{7,5},{8,10},{9,11},{10,... | collective-permute-start | bytes 36872 | tf_op jit(solution)/shard_map/ppermute | solution.py:391
  145.1 1.9 %collective-permute-start.7 = (bf16[48,128]{1,0:T(8,128)(2,1)S(1)}, bf16[48,128]{1,0:T(8,128)(2,1)S(1)}, u32[]{:S(2)}, u32[]{:S(2)}) collective-permute-start(bf16[48,128]{1,0:T(8,128)(2,1)S(1)} %get-tuple-element.36), channel_id=1, source_target_pairs={{0,1},{1,2},{2,3},{3,0},{4,5},{5,6},{6,7},{7,4},{8,9},{9,10},{10,1... | collective-permute-start | bytes 36872 | tf_op jit(solution)/shard_map/ppermute | solution.py:391
  147.0 3.6 %collective-permute-done.7.refs_3_ = bf16[48,128]{1,0:T(8,128)(2,1)S(1)} collective-permute-done((bf16[48,128]{1,0:T(8,128)(2,1)S(1)}, bf16[48,128]{1,0:T(8,128)(2,1)S(1)}, u32[]{:S(2)}, u32[]{:S(2)}) %collective-permute-start.7) | collective-permute-done | bytes 12320 | tf_op jit(solution)/shard_map/ppermute | solution.py:391
  150.7 0.9 shard_map.130
  151.6 0.8 shard_map.131
  (29 shorter events, 0.2 us)
Async XLA Ops:
  3.0 9.6 %copy-start.8 = (s32[128]{0:T(128)S(1)}, s32[128]{0:T(128)}, u32[]{:S(2)}) copy-start(s32[128]{0:T(128)} %param.18) | copy-start | bytes 1540
  3.0 9.6 %copy-start.6 = (s32[128]{0:T(128)S(1)}, s32[128]{0:T(128)}, u32[]{:S(2)}) copy-start(s32[128]{0:T(128)} %param.19) | copy-start | bytes 1540
  3.0 9.9 %copy-start.7 = (s32[128]{0:T(128)S(1)}, s32[128]{0:T(128)}, u32[]{:S(2)}) copy-start(s32[128]{0:T(128)} %param.20) | copy-start | bytes 1540
  3.0 10.4 %copy-start.5 = (s32[192]{0:T(256)S(1)}, s32[192]{0:T(256)}, u32[]{:S(2)}) copy-start(s32[192]{0:T(256)} %param.21) | copy-start | bytes 2308
  3.0 11.4 %copy-start = (bf16[128,1280]{1,0:T(8,128)(2,1)S(1)}, bf16[128,1280]{1,0:T(8,128)(2,1)}, u32[]{:S(2)}) copy-start(bf16[128,1280]{1,0:T(8,128)(2,1)} %next_weight_ref.1) | copy-start | bytes 983044
  3.0 11.4 %copy-start.1 = (bf16[1024,128]{1,0:T(8,128)(2,1)S(1)}, bf16[1024,128]{1,0:T(8,128)(2,1)}, u32[]{:S(2)}) copy-start(bf16[1024,128]{1,0:T(8,128)(2,1)} %out_weight_ref.1) | copy-start | bytes 786436
  3.1 11.4 %copy-start.2 = (bf16[768,128]{1,0:T(8,128)(2,1)S(1)}, bf16[768,128]{1,0:T(8,128)(2,1)}, u32[]{:S(2)}) copy-start(bf16[768,128]{1,0:T(8,128)(2,1)} %keys_ref.1) | copy-start | bytes 589828
  3.1 11.4 %copy-start.3 = (bf16[768,128]{1,0:T(8,128)(2,1)S(1)}, bf16[768,128]{1,0:T(8,128)(2,1)}, u32[]{:S(2)}) copy-start(bf16[768,128]{1,0:T(8,128)(2,1)} %values_ref.1) | copy-start | bytes 589828
  3.1 17.2 %all-to-all-start = ((bf16[4,52,16,128]{3,2,1,0:T(8,128)(2,1)}), bf16[4,52,16,128]{3,2,1,0:T(8,128)(2,1)S(1)}, u32[]{:S(2)}, u32[]{:S(2)}) async-start(bf16[4,52,16,128]{3,2,1,0:T(8,128)(2,1)} %shard_map.122), calls=%async_computation | async-start | bytes 1703936 | tf_op jit(solution)/shard_map/all_to_all | solution.py:406
  14.9 1.0 copy-start.4
  21.2 29.6 %all-to-all-start.1 = ((bf16[16,48,128]{2,1,0:T(8,128)(2,1)}), bf16[16,48,128]{2,1,0:T(8,128)(2,1)S(1)}, u32[]{:S(2)}, u32[]{:S(2)}) async-start(bf16[16,48,128]{2,1,0:T(8,128)(2,1)} %get-tuple-element.23), calls=%async_computation.1 | async-start | bytes 393216 | tf_op jit(solution)/shard_map/all_to_all | solution.py:449
  35.1 34.1 %collective-permute-start.2 = (bf16[30,128,128]{2,1,0:T(8,128)(2,1)}, bf16[30,128,128]{2,1,0:T(8,128)(2,1)S(1)}, u32[]{:S(2)}, u32[]{:S(2)}) collective-permute-start(bf16[30,128,128]{2,1,0:T(8,128)(2,1)} %copy-done.4), channel_id=1, source_target_pairs={{0,3},{1,0},{2,1},{3,2},{4,7},{5,4},{6,5},{7,6},{8,11},{9,8},{10,9... | collective-permute-start | bytes 2949128 | tf_op jit(solution)/shard_map/ppermute | solution.py:391
  37.7 21.1 %collective-permute-start = (bf16[12,128,128]{2,1,0:T(8,128)(2,1)S(1)}, bf16[12,128,128]{2,1,0:T(8,128)(2,1)S(1)}, u32[]{:S(2)}, u32[]{:S(2)}) collective-permute-start(bf16[12,128,128]{2,1,0:T(8,128)(2,1)S(1)} %get-tuple-element.26.refs_0_), channel_id=1, source_target_pairs={{0,1},{1,2},{2,3},{3,0},{4,5},{5,6},{6,7},{7,4},{8,9},{9,10},{10,1... | collective-permute-start | bytes 1179656 | tf_op jit(solution)/shard_map/ppermute | solution.py:391
  42.8 26.3 %collective-permute-start.1 = (bf16[12,128,128]{2,1,0:T(8,128)(2,1)S(1)}, bf16[12,128,128]{2,1,0:T(8,128)(2,1)S(1)}, u32[]{:S(2)}, u32[]{:S(2)}) collective-permute-start(bf16[12,128,128]{2,1,0:T(8,128)(2,1)S(1)} %get-tuple-element.26.refs_0_), channel_id=1, source_target_pairs={{0,2},{1,3},{2,0},{3,1},{4,6},{5,7},{6,4},{7,5},{8,10},{9,11},{10,... | collective-permute-start | bytes 1179656 | tf_op jit(solution)/shard_map/ppermute | solution.py:391
  51.5 20.0 %all-to-all-start.2 = ((bf16[16,24,128]{2,1,0:T(8,128)(2,1)}), bf16[16,24,128]{2,1,0:T(8,128)(2,1)S(1)}, u32[]{:S(2)}, u32[]{:S(2)}) async-start(bf16[16,24,128]{2,1,0:T(8,128)(2,1)} %get-tuple-element.24), calls=%async_computation.2 | async-start | bytes 196608 | tf_op jit(solution)/shard_map/all_to_all | solution.py:451
  74.7 22.5 %all-to-all-start.3 = ((bf16[16,32,128]{2,1,0:T(8,128)(2,1)}), bf16[16,32,128]{2,1,0:T(8,128)(2,1)S(1)}, u32[]{:S(2)}, u32[]{:S(2)}) async-start(bf16[16,32,128]{2,1,0:T(8,128)(2,1)} %shard_map.126), calls=%async_computation.3 | async-start | bytes 262144 | tf_op jit(solution)/shard_map/all_to_all | solution.py:461
  84.1 18.2 %collective-permute-start.3 = (bf16[18,128,128]{2,1,0:T(8,128)(2,1)S(1)}, bf16[18,128,128]{2,1,0:T(8,128)(2,1)S(1)}, u32[]{:S(2)}, u32[]{:S(2)}) collective-permute-start(bf16[18,128,128]{2,1,0:T(8,128)(2,1)S(1)} %get-tuple-element.30.refs_0_), channel_id=1, source_target_pairs={{0,1},{1,2},{2,3},{3,0},{4,5},{5,6},{6,7},{7,4},{8,9},{9,10},{10,1... | collective-permute-start | bytes 1769480 | tf_op jit(solution)/shard_map/ppermute | solution.py:391
  86.0 16.2 %collective-permute-start.4 = (bf16[18,128,128]{2,1,0:T(8,128)(2,1)S(1)}, bf16[18,128,128]{2,1,0:T(8,128)(2,1)S(1)}, u32[]{:S(2)}, u32[]{:S(2)}) collective-permute-start(bf16[18,128,128]{2,1,0:T(8,128)(2,1)S(1)} %get-tuple-element.30.refs_0_), channel_id=1, source_target_pairs={{0,2},{1,3},{2,0},{3,1},{4,6},{5,7},{6,4},{7,5},{8,10},{9,11},{10,... | collective-permute-start | bytes 1769480 | tf_op jit(solution)/shard_map/ppermute | solution.py:391
  98.2 17.0 %all-to-all-start.4 = ((bf16[16,24,128]{2,1,0:T(8,128)(2,1)}), bf16[16,24,128]{2,1,0:T(8,128)(2,1)S(1)}, u32[]{:S(2)}, u32[]{:S(2)}) async-start(bf16[16,24,128]{2,1,0:T(8,128)(2,1)} %shard_map.127), calls=%async_computation.4 | async-start | bytes 196608 | tf_op jit(solution)/shard_map/all_to_all | solution.py:463
  129.8 21.8 %all-to-all-start.6 = ((bf16[16,32,128]{2,1,0:T(8,128)(2,1)}), bf16[16,32,128]{2,1,0:T(8,128)(2,1)S(1)}, u32[]{:S(2)}, u32[]{:S(2)}) async-start(bf16[16,32,128]{2,1,0:T(8,128)(2,1)} %get-tuple-element.37), calls=%async_computation.6 | async-start | bytes 262144 | tf_op jit(solution)/shard_map/all_to_all | solution.py:478
  133.3 13.7 %collective-permute-start.5 = (bf16[48,128]{1,0:T(8,128)(2,1)S(1)}, bf16[48,128]{1,0:T(8,128)(2,1)S(1)}, u32[]{:S(2)}, u32[]{:S(2)}) collective-permute-start(bf16[48,128]{1,0:T(8,128)(2,1)S(1)} %get-tuple-element.34), channel_id=1, source_target_pairs={{0,3},{1,0},{2,1},{3,2},{4,7},{5,4},{6,5},{7,6},{8,11},{9,8},{10,9... | collective-permute-start | bytes 36872 | tf_op jit(solution)/shard_map/ppermute | solution.py:391
  139.0 8.0 %collective-permute-start.6 = (bf16[48,128]{1,0:T(8,128)(2,1)S(1)}, bf16[48,128]{1,0:T(8,128)(2,1)S(1)}, u32[]{:S(2)}, u32[]{:S(2)}) collective-permute-start(bf16[48,128]{1,0:T(8,128)(2,1)S(1)} %get-tuple-element.35), channel_id=1, source_target_pairs={{0,2},{1,3},{2,0},{3,1},{4,6},{5,7},{6,4},{7,5},{8,10},{9,11},{10,... | collective-permute-start | bytes 36872 | tf_op jit(solution)/shard_map/ppermute | solution.py:391
  145.1 5.6 %collective-permute-start.7 = (bf16[48,128]{1,0:T(8,128)(2,1)S(1)}, bf16[48,128]{1,0:T(8,128)(2,1)S(1)}, u32[]{:S(2)}, u32[]{:S(2)}) collective-permute-start(bf16[48,128]{1,0:T(8,128)(2,1)S(1)} %get-tuple-element.36), channel_id=1, source_target_pairs={{0,1},{1,2},{2,3},{3,0},{4,5},{5,6},{6,7},{7,4},{8,9},{9,10},{10,1... | collective-permute-start | bytes 36872 | tf_op jit(solution)/shard_map/ppermute | solution.py:391

commit v6 on v5

--- a/solution.py
+++ b/solution.py
@@ -94,7 +94,6 @@
     for j in range(GQ + 2):
         block = next_weight_ref[:, j * HD : (j + 1) * HD]
         weights_ref[GQ + j] = block
-        both_ref[2 * blocks + GQ + j] = block
 
 
 def project_kernel(hidden_hbm, weight_hbm, gain_hbm, out_ref, hidden_ref, weight_ref, gain_ref, sems):
@@ -263,12 +262,10 @@
         out_ref[z] = result
 
 
-def weight_blocks(refs, first, count):
-    return [ref.at[pl.ds(ref.shape[0] - (2 * GQ + 2) + first, count)] for ref in refs]
-
-
 def output_kernel(heads_ref, *refs):
-    weight_refs, out_ref = weight_blocks(refs[:NX], 0, GQ), refs[NX]
+    weight_refs, out_ref = [ref.at[pl.ds(0, GQ)] for ref in refs[: NX - 1]], refs[NX]
+    last = refs[NX - 1]
+    weight_refs.append(last.at[pl.ds(last.shape[0] - GQ, GQ)])
     rows = heads_ref[...]
     bands = []
     for i in range(RI):
@@ -284,7 +281,9 @@
 
 
 def next_kernel(terms_ref, hidden_ref, gain_ref, *refs):
-    weight_refs = weight_blocks(refs[:NX], GQ, GQ + 2)
+    wide = range(GQ, 2 * GQ + 2)
+    weights = [jnp.concatenate([ref[j] for j in wide], axis=1) for ref in refs[: NX - 1]]
+    weights.append(refs[NX - 1][...])
     resid_refs, (out_ref, cut_ref) = refs[NX : 2 * NX], refs[2 * NX :]
     attended = terms_ref[0].astype(f32)
     for h in range(1, NH):
@@ -297,8 +296,7 @@
         resid_refs[x][...] = resid.astype(bf16)
         squares = squares + jnp.sum(resid * resid, axis=1, keepdims=True)
         gained = (resid * gain_ref[x : x + 1, :]).astype(bf16)
-        weight = jnp.concatenate([weight_refs[x][j] for j in range(GQ + 2)], axis=1)
-        product = product + jnp.dot(gained, weight, preferred_element_type=f32)
+        product = product + jnp.dot(gained, weights[x], preferred_element_type=f32)
     for i in range(RI):
         for j in range(GQ + 2):
             cut_ref[:, i * (GQ + 2) + j, :] = product[
@@ -422,7 +420,7 @@
         jnp.concatenate([query_pos, new_pos, jnp.zeros((NX * RI,), jnp.int32), shift[0]])
     )
     rows = 8 * RI + KT
-    counts = (2 * blocks, 2 * GQ + 2, 2 * blocks + 2 * GQ + 2)
+    counts = (2 * blocks, 2 * GQ + 2, 2 * blocks + GQ)
     cache, weights, both = vmem_call(
         bundle_kernel,
         tuple(shaped((count, HD, HD), bf16) for count in counts),
@@ -456,18 +454,20 @@
         scratch=[pltpu.VMEM((HD, (NX * blocks + 2 * RI) * BLK), f32)],
     )
     parts, weights = lax.optimization_barrier((parts, weights))
-    weights_x = [weights, shifted(weights, 1), shifted(weights, 2), caches[3]]
+    weights_x = [weights, shifted(weights, 1), shifted(weights, 2)]
     share = vmem_call(
         combine_kernel, shaped((NZ, 8 * RI, HD), bf16), (a2a(parts, "z"),)
     )
+    share, next_weight = lax.optimization_barrier((share, next_weight))
+    next_last = shifted(next_weight, 3)
     heads_out = a2a(share, "z").reshape(XR * GQ, HD)
     terms = vmem_call(
-        output_kernel, shaped((NH, XR, NX * HD), bf16), (heads_out, *weights_x)
+        output_kernel, shaped((NH, XR, NX * HD), bf16), (heads_out, *weights_x, caches[3])
     )
     *resids, products = vmem_call(
         next_kernel,
         (*[shaped((XR, HD), bf16)] * NX, shaped((NZ, 32, HD), bf16)),
-        (a2a(terms, "heads"), hidden_x, gain_x, *weights_x),
+        (a2a(terms, "heads"), hidden_x, gain_x, *weights_x, next_last),
         scratch=[pltpu.VMEM((NZ, 32, HD), f32)],
     )
     resids = [resids[0]] + [shifted(resids[s], NX - s) for s in range(1, NX)]

time: 155 us -> 153 us (0.987)
  blocking collectives: 13.2 us -> 0 us
  waiting for transfers between devices: 47.7 us -> 56.8 us
  starting transfers between devices: 74.9 us -> 77.4 us
  Pallas kernels: 11.5 us -> 13.1 us
    all_to_all x1 -> x0, blocking collectives: 13.2 us -> none  [on_device(): a2a(terms, 'heads')]
    all_to_all x1, waiting for transfers between devices: 2.38 us -> 8.75 us  [on_device(): queries = a2a(copies, 'z').reshape(XR * GQ, HD)]
    all_to_all x1, starting transfers between devices: 9.37 us -> 3.51 us  [on_device(): a2a(parts, 'z')]
    all_to_all x0 -> x1, starting transfers between devices: none -> 4.46 us  [on_device(): a2a(terms, 'heads')]
    ppermute x8 -> x9, waiting for transfers between devices: 14.1 us -> 17.6 us  [shifted(): return lax.ppermute(array, 'x', [(n, (n + step) % NX) for n in range(NX)])]
    all_to_all x1, waiting for transfers between devices: 8.75 us -> 6.3 us  [on_device(): a2a(parts, 'z')]
    all_to_all x1, starting transfers between devices: 3.99 us -> 5.65 us  [on_device(): heads_out = a2a(share, 'z').reshape(XR * GQ, HD)]
    pallas_call x10, Pallas kernels: 11.5 us -> 13.1 us  [vmem_call(): pl.pallas_call(kernel, out_shape=out_shape, in_specs=[small] * scalars +...]
  transfers between devices with their start and end apart: 14 -> 16, of which waited for: 8 -> 10; matrix products, arithmetic and copies ran while one was open for 2% -> 2% of each run, Pallas kernels for 2% -> 3%
where the time goes in v6:
time: 153 us; the launch traced here: 151 us
  starting transfers between devices  77.4 us (51%)
  waiting for transfers between devices  56.8 us (37%)
  Pallas kernels  13.1 us (9%)
  other arithmetic  2.02 us (1%)
    ppermute x9, starting transfers between devices, shifted(): return lax.ppermute(array, 'x', [(n, (n + step) % NX) for n in range(NX)])  28.7 us
    ppermute x9, waiting for transfers between devices, shifted(): return lax.ppermute(array, 'x', [(n, (n + step) % NX) for n in range(NX)])  17.6 us
    all_to_all x1, starting transfers between devices, on_device(): a2a(tiles, 'z')  13.8 us
    pallas_call x10, Pallas kernels, vmem_call(): pl.pallas_call(kernel, out_shape=out_shape, in_specs=[small] * scalars +...  13.1 us
    all_to_all x1, waiting for transfers between devices, on_device(): heads_out = a2a(share, 'z').reshape(XR * GQ, HD)  13 us
    all_to_all x1, starting transfers between devices, on_device(): payload = a2a(payload, 'x')  9.47 us
    all_to_all x1, waiting for transfers between devices, on_device(): queries = a2a(copies, 'z').reshape(XR * GQ, HD)  8.75 us
    all_to_all x1, starting transfers between devices, on_device(): queries = a2a(copies, 'z').reshape(XR * GQ, HD)  6.86 us
  transfers between devices with their start and end apart: 16, of which 10 were waited for; matrix products, arithmetic and copies ran while one was open for 2% of the time, Pallas kernels for 3%

profile of v6, /device:TPU:6, one launch (start us, length us, event | category | flops | bytes accessed | tf_op | source)
XLA Modules:
  0.0 151.3 jit_solution(15725829492200412854)
XLA Ops:
  0.6 2.3 %shard_map.122 = bf16[4,52,16,128]{3,2,1,0:T(8,128)(2,1)} custom-call(bf16[192,128]{1,0:T(8,128)(2,1)} %hidden_hbm.1, bf16[128,1280]{1,0:T(8,128)(2,1)} %weight_hbm.1, f32[1,128]{1,0:T(1,128)} %bitcast.13), custom_call_target="tpu_custom_call" | custom-call | tf_op jit(solution)/shard_map/pallas_call | solution.py:42
  2.9 0.0 copy-start.7
  3.0 0.0 copy-start.5
  3.0 0.0 copy-start.6
  3.0 0.0 copy-start.4
  3.0 0.0 copy-start
  3.0 0.0 copy-start.1
  3.0 9.5 %all-to-all-start = ((bf16[4,52,16,128]{3,2,1,0:T(8,128)(2,1)}), bf16[4,52,16,128]{3,2,1,0:T(8,128)(2,1)S(1)}, u32[]{:S(2)}, u32[]{:S(2)}) async-start(bf16[4,52,16,128]{3,2,1,0:T(8,128)(2,1)} %shard_map.122), calls=%async_computation | async-start | bytes 1703936 | tf_op jit(solution)/shard_map/all_to_all | solution.py:404
  12.6 0.1 fusion.3
  12.7 0.1 compare_select_fusion
  12.7 0.1 select_reduce_fusion
  12.9 0.4 select_reduce_fusion.1
  13.3 0.1 slice_reduce_fusion
  13.4 0.2 reshape.214
  13.6 0.1 concatenate.25
  13.7 0.1 copy.19
  13.8 0.1 broadcast_in_dim.38
  13.9 0.2 select_reduce_fusion.3
  14.1 0.1 add_convert_fusion
  14.1 0.2 fusion.2
  14.3 0.1 pad_maximum_fusion.2
  14.4 1.3 shard_map.124
  15.7 4.6 %all-to-all-done.in_ref = bf16[4,52,16,128]{3,2,1,0:T(8,128)(2,1)S(1)} async-done(((bf16[4,52,16,128]{3,2,1,0:T(8,128)(2,1)}), bf16[4,52,16,128]{3,2,1,0:T(8,128)(2,1)S(1)}, u32[]{:S(2)}, u32[]{:S(2)}) %all-to-all-start) | async-done | bytes 852000 | tf_op jit(solution)/shard_map/all_to_all | solution.py:404
  20.3 0.9 shard_map.123
  21.1 13.8 %all-to-all-start.1 = ((bf16[16,48,128]{2,1,0:T(8,128)(2,1)}), bf16[16,48,128]{2,1,0:T(8,128)(2,1)S(1)}, u32[]{:S(2)}, u32[]{:S(2)}) async-start(bf16[16,48,128]{2,1,0:T(8,128)(2,1)} %get-tuple-element.25), calls=%async_computation.1 | async-start | bytes 393216 | tf_op jit(solution)/shard_map/all_to_all | solution.py:447
  35.0 0.1 copy.21
  35.0 0.1 pad_maximum_fusion
  35.1 0.1 iota_add_fusion
  35.2 0.5 compare_reduce_fusion
  35.7 1.9 %collective-permute-start.2 = (bf16[20,128,128]{2,1,0:T(8,128)(2,1)}, bf16[20,128,128]{2,1,0:T(8,128)(2,1)S(1)}, u32[]{:S(2)}, u32[]{:S(2)}) collective-permute-start(bf16[20,128,128]{2,1,0:T(8,128)(2,1)} %get-tuple-element.29), channel_id=1, source_target_pairs={{0,3},{1,0},{2,1},{3,2},{4,7},{5,4},{6,5},{7,6},{8,11},{9,8},{10,9... | collective-permute-start | bytes 1966088 | tf_op jit(solution)/shard_map/ppermute | solution.py:389
  37.7 5.1 %collective-permute-start = (bf16[12,128,128]{2,1,0:T(8,128)(2,1)S(1)}, bf16[12,128,128]{2,1,0:T(8,128)(2,1)S(1)}, u32[]{:S(2)}, u32[]{:S(2)}) collective-permute-start(bf16[12,128,128]{2,1,0:T(8,128)(2,1)S(1)} %get-tuple-element.28.refs_0_), channel_id=1, source_target_pairs={{0,1},{1,2},{2,3},{3,0},{4,5},{5,6},{6,7},{7,4},{8,9},{9,10},{10,1... | collective-permute-start | bytes 1179656 | tf_op jit(solution)/shard_map/ppermute | solution.py:389
  42.8 2.8 %collective-permute-start.1 = (bf16[12,128,128]{2,1,0:T(8,128)(2,1)S(1)}, bf16[12,128,128]{2,1,0:T(8,128)(2,1)S(1)}, u32[]{:S(2)}, u32[]{:S(2)}) collective-permute-start(bf16[12,128,128]{2,1,0:T(8,128)(2,1)S(1)} %get-tuple-element.28.refs_0_), channel_id=1, source_target_pairs={{0,2},{1,3},{2,0},{3,1},{4,6},{5,7},{6,4},{7,5},{8,10},{9,11},{10,... | collective-permute-start | bytes 1179656 | tf_op jit(solution)/shard_map/ppermute | solution.py:389
  45.6 5.2 %all-to-all-done.1.in_ref = bf16[16,48,128]{2,1,0:T(8,128)(2,1)S(1)} async-done(((bf16[16,48,128]{2,1,0:T(8,128)(2,1)}), bf16[16,48,128]{2,1,0:T(8,128)(2,1)S(1)}, u32[]{:S(2)}, u32[]{:S(2)}) %all-to-all-start.1) | async-done | bytes 196640 | tf_op jit(solution)/shard_map/all_to_all | solution.py:447
  50.7 0.7 shard_map.125
  51.5 6.9 %all-to-all-start.2 = ((bf16[16,24,128]{2,1,0:T(8,128)(2,1)}), bf16[16,24,128]{2,1,0:T(8,128)(2,1)S(1)}, u32[]{:S(2)}, u32[]{:S(2)}) async-start(bf16[16,24,128]{2,1,0:T(8,128)(2,1)} %get-tuple-element.26), calls=%async_computation.2 | async-start | bytes 196608 | tf_op jit(solution)/shard_map/all_to_all | solution.py:449
  58.4 0.1 add.119
  58.5 0.1 copy.20
  58.6 0.1 gt.11
  58.7 0.1 add_select_fusion
  58.8 4.0 %collective-permute-done.1.refs_2_ = bf16[12,128,128]{2,1,0:T(8,128)(2,1)S(1)} collective-permute-done((bf16[12,128,128]{2,1,0:T(8,128)(2,1)S(1)}, bf16[12,128,128]{2,1,0:T(8,128)(2,1)S(1)}, u32[]{:S(2)}, u32[]{:S(2)}) %collective-permute-start.1) | collective-permute-done | bytes 393248 | tf_op jit(solution)/shard_map/ppermute | solution.py:389
  62.8 8.8 %all-to-all-done.2 = bf16[16,24,128]{2,1,0:T(8,128)(2,1)S(1)} async-done(((bf16[16,24,128]{2,1,0:T(8,128)(2,1)}), bf16[16,24,128]{2,1,0:T(8,128)(2,1)S(1)}, u32[]{:S(2)}, u32[]{:S(2)}) %all-to-all-start.2) | async-done | bytes 98336 | tf_op jit(solution)/shard_map/all_to_all | solution.py:449
  71.5 0.1 broadcast_in_dim.50.rowpos_ref
  71.6 3.1 %shard_map.126 = bf16[16,32,128]{2,1,0:T(8,128)(2,1)} custom-call(bf16[384,128]{1,0:T(8,128)(2,1)S(1)} %bitcast.9, s32[25,128]{1,0:T(8,128)S(1)} %pad_add_fusion.keypos_ref, s32[3,16,128]{2,1,0:T(8,128)S(1)} %broadcast_in_dim.50.rowpos_ref, bf16[2,16,128]{2,1,0:T(8,128)(2,1)S(1)} %get-tuple-element.27.new_ref, ...), custom_call_target="tpu_custom_call" | custom-call | tf_op jit(solution)/shard_map/pallas_call | solution.py:42
  74.7 3.5 %all-to-all-start.3 = ((bf16[16,32,128]{2,1,0:T(8,128)(2,1)}), bf16[16,32,128]{2,1,0:T(8,128)(2,1)S(1)}, u32[]{:S(2)}, u32[]{:S(2)}) async-start(bf16[16,32,128]{2,1,0:T(8,128)(2,1)} %shard_map.126), calls=%async_computation.3 | async-start | bytes 262144 | tf_op jit(solution)/shard_map/all_to_all | solution.py:459
  78.2 2.4 %collective-permute-start.3 = (bf16[18,128,128]{2,1,0:T(8,128)(2,1)S(1)}, bf16[18,128,128]{2,1,0:T(8,128)(2,1)S(1)}, u32[]{:S(2)}, u32[]{:S(2)}) collective-permute-start(bf16[18,128,128]{2,1,0:T(8,128)(2,1)S(1)} %get-tuple-element.33.refs_0_), channel_id=1, source_target_pairs={{0,1},{1,2},{2,3},{3,0},{4,5},{5,6},{6,7},{7,4},{8,9},{9,10},{10,1... | collective-permute-start | bytes 1769480 | tf_op jit(solution)/shard_map/ppermute | solution.py:389
  80.7 4.3 %collective-permute-start.4 = (bf16[18,128,128]{2,1,0:T(8,128)(2,1)S(1)}, bf16[18,128,128]{2,1,0:T(8,128)(2,1)S(1)}, u32[]{:S(2)}, u32[]{:S(2)}) collective-permute-start(bf16[18,128,128]{2,1,0:T(8,128)(2,1)S(1)} %get-tuple-element.33.refs_0_), channel_id=1, source_target_pairs={{0,2},{1,3},{2,0},{3,1},{4,6},{5,7},{6,4},{7,5},{8,10},{9,11},{10,... | collective-permute-start | bytes 1769480 | tf_op jit(solution)/shard_map/ppermute | solution.py:389
  85.0 6.3 %all-to-all-done.3.in_ref = bf16[16,32,128]{2,1,0:T(8,128)(2,1)S(1)} async-done(((bf16[16,32,128]{2,1,0:T(8,128)(2,1)}), bf16[16,32,128]{2,1,0:T(8,128)(2,1)S(1)}, u32[]{:S(2)}, u32[]{:S(2)}) %all-to-all-start.3) | async-done | bytes 131104 | tf_op jit(solution)/shard_map/all_to_all | solution.py:459
  91.3 0.9 shard_map.127
  92.2 5.6 %all-to-all-start.4 = ((bf16[16,24,128]{2,1,0:T(8,128)(2,1)}), bf16[16,24,128]{2,1,0:T(8,128)(2,1)S(1)}, u32[]{:S(2)}, u32[]{:S(2)}) async-start(bf16[16,24,128]{2,1,0:T(8,128)(2,1)} %shard_map.127), calls=%async_computation.4 | async-start | bytes 196608 | tf_op jit(solution)/shard_map/all_to_all | solution.py:463
  97.9 13.0 %all-to-all-done.4 = bf16[16,24,128]{2,1,0:T(8,128)(2,1)S(1)} async-done(((bf16[16,24,128]{2,1,0:T(8,128)(2,1)}), bf16[16,24,128]{2,1,0:T(8,128)(2,1)S(1)}, u32[]{:S(2)}, u32[]{:S(2)}) %all-to-all-start.4) | async-done | bytes 98336 | tf_op jit(solution)/shard_map/all_to_all | solution.py:463
  110.9 1.0 shard_map.128
  111.9 4.5 %all-to-all-start.5 = ((bf16[8,48,512]{2,1,0:T(8,128)(2,1)}), bf16[8,48,512]{2,1,0:T(8,128)(2,1)S(1)}, u32[]{:S(2)}, u32[]{:S(2)}) async-start(bf16[8,48,512]{2,1,0:T(8,128)(2,1)} %shard_map.128), calls=%async_computation.5 | async-start | bytes 786432 | tf_op jit(solution)/shard_map/all_to_all | solution.py:470
  116.4 3.1 %collective-permute-start.5 = (bf16[128,1280]{1,0:T(8,128)(2,1)S(1)}, bf16[128,1280]{1,0:T(8,128)(2,1)S(1)}, u32[]{:S(2)}, u32[]{:S(2)}) collective-permute-start(bf16[128,1280]{1,0:T(8,128)(2,1)S(1)} %copy-done), channel_id=1, source_target_pairs={{0,3},{1,0},{2,1},{3,2},{4,7},{5,4},{6,5},{7,6},{8,11},{9,8},{10,9... | collective-permute-start | bytes 983048 | tf_op jit(solution)/shard_map/ppermute | solution.py:389
  119.5 10.1 %collective-permute-done.5.refs_3_ = bf16[128,1280]{1,0:T(8,128)(2,1)S(1)} collective-permute-done((bf16[128,1280]{1,0:T(8,128)(2,1)S(1)}, bf16[128,1280]{1,0:T(8,128)(2,1)S(1)}, u32[]{:S(2)}, u32[]{:S(2)}) %collective-permute-start.5) | collective-permute-done | bytes 327712 | tf_op jit(solution)/shard_map/ppermute | solution.py:389
  129.6 1.1 shard_map.129
  130.8 4.9 %all-to-all-start.6 = ((bf16[16,32,128]{2,1,0:T(8,128)(2,1)}), bf16[16,32,128]{2,1,0:T(8,128)(2,1)S(1)}, u32[]{:S(2)}, u32[]{:S(2)}) async-start(bf16[16,32,128]{2,1,0:T(8,128)(2,1)} %get-tuple-element.41), calls=%async_computation.6 | async-start | bytes 262144 | tf_op jit(solution)/shard_map/all_to_all | solution.py:478
  135.7 2.3 %collective-permute-start.6 = (bf16[48,128]{1,0:T(8,128)(2,1)S(1)}, bf16[48,128]{1,0:T(8,128)(2,1)S(1)}, u32[]{:S(2)}, u32[]{:S(2)}) collective-permute-start(bf16[48,128]{1,0:T(8,128)(2,1)S(1)} %get-tuple-element.38), channel_id=1, source_target_pairs={{0,3},{1,0},{2,1},{3,2},{4,7},{5,4},{6,5},{7,6},{8,11},{9,8},{10,9... | collective-permute-start | bytes 36872 | tf_op jit(solution)/shard_map/ppermute | solution.py:389
  138.0 4.7 %collective-permute-start.7 = (bf16[48,128]{1,0:T(8,128)(2,1)S(1)}, bf16[48,128]{1,0:T(8,128)(2,1)S(1)}, u32[]{:S(2)}, u32[]{:S(2)}) collective-permute-start(bf16[48,128]{1,0:T(8,128)(2,1)S(1)} %get-tuple-element.39), channel_id=1, source_target_pairs={{0,2},{1,3},{2,0},{3,1},{4,6},{5,7},{6,4},{7,5},{8,10},{9,11},{10,... | collective-permute-start | bytes 36872 | tf_op jit(solution)/shard_map/ppermute | solution.py:389
  142.7 2.1 %collective-permute-start.8 = (bf16[48,128]{1,0:T(8,128)(2,1)S(1)}, bf16[48,128]{1,0:T(8,128)(2,1)S(1)}, u32[]{:S(2)}, u32[]{:S(2)}) collective-permute-start(bf16[48,128]{1,0:T(8,128)(2,1)S(1)} %get-tuple-element.40), channel_id=1, source_target_pairs={{0,1},{1,2},{2,3},{3,0},{4,5},{5,6},{6,7},{7,4},{8,9},{9,10},{10,1... | collective-permute-start | bytes 36872 | tf_op jit(solution)/shard_map/ppermute | solution.py:389
  144.8 0.3 collective-permute-done.7.refs_2_
  145.1 3.2 %collective-permute-done.8.refs_3_ = bf16[48,128]{1,0:T(8,128)(2,1)S(1)} collective-permute-done((bf16[48,128]{1,0:T(8,128)(2,1)S(1)}, bf16[48,128]{1,0:T(8,128)(2,1)S(1)}, u32[]{:S(2)}, u32[]{:S(2)}) %collective-permute-start.8) | collective-permute-done | bytes 12320 | tf_op jit(solution)/shard_map/ppermute | solution.py:389
  148.3 0.9 shard_map.130
  149.2 1.3 all-to-all-done.6.in_ref
  150.6 0.8 shard_map.131
  (30 shorter events, 0.2 us)
Async XLA Ops:
  2.9 9.6 %copy-start.7 = (s32[128]{0:T(128)S(1)}, s32[128]{0:T(128)}, u32[]{:S(2)}) copy-start(s32[128]{0:T(128)} %param.18) | copy-start | bytes 1540
  3.0 9.6 %copy-start.5 = (s32[128]{0:T(128)S(1)}, s32[128]{0:T(128)}, u32[]{:S(2)}) copy-start(s32[128]{0:T(128)} %param.19) | copy-start | bytes 1540
  3.0 9.9 %copy-start.6 = (s32[128]{0:T(128)S(1)}, s32[128]{0:T(128)}, u32[]{:S(2)}) copy-start(s32[128]{0:T(128)} %param.20) | copy-start | bytes 1540
  3.0 10.4 %copy-start.4 = (s32[192]{0:T(256)S(1)}, s32[192]{0:T(256)}, u32[]{:S(2)}) copy-start(s32[192]{0:T(256)} %param.21) | copy-start | bytes 2308
  3.0 11.4 %copy-start = (bf16[128,1280]{1,0:T(8,128)(2,1)S(1)}, bf16[128,1280]{1,0:T(8,128)(2,1)}, u32[]{:S(2)}) copy-start(bf16[128,1280]{1,0:T(8,128)(2,1)} %next_weight_ref.1) | copy-start | bytes 983044
  3.0 11.4 %copy-start.1 = (bf16[1024,128]{1,0:T(8,128)(2,1)S(1)}, bf16[1024,128]{1,0:T(8,128)(2,1)}, u32[]{:S(2)}) copy-start(bf16[1024,128]{1,0:T(8,128)(2,1)} %out_weight_ref.1) | copy-start | bytes 786436
  3.0 11.4 %copy-start.2 = (bf16[768,128]{1,0:T(8,128)(2,1)S(1)}, bf16[768,128]{1,0:T(8,128)(2,1)}, u32[]{:S(2)}) copy-start(bf16[768,128]{1,0:T(8,128)(2,1)} %keys_ref.1) | copy-start | bytes 589828
  3.0 11.4 %copy-start.3 = (bf16[768,128]{1,0:T(8,128)(2,1)S(1)}, bf16[768,128]{1,0:T(8,128)(2,1)}, u32[]{:S(2)}) copy-start(bf16[768,128]{1,0:T(8,128)(2,1)} %values_ref.1) | copy-start | bytes 589828
  3.0 17.2 %all-to-all-start = ((bf16[4,52,16,128]{3,2,1,0:T(8,128)(2,1)}), bf16[4,52,16,128]{3,2,1,0:T(8,128)(2,1)S(1)}, u32[]{:S(2)}, u32[]{:S(2)}) async-start(bf16[4,52,16,128]{3,2,1,0:T(8,128)(2,1)} %shard_map.122), calls=%async_computation | async-start | bytes 1703936 | tf_op jit(solution)/shard_map/all_to_all | solution.py:404
  21.1 29.6 %all-to-all-start.1 = ((bf16[16,48,128]{2,1,0:T(8,128)(2,1)}), bf16[16,48,128]{2,1,0:T(8,128)(2,1)S(1)}, u32[]{:S(2)}, u32[]{:S(2)}) async-start(bf16[16,48,128]{2,1,0:T(8,128)(2,1)} %get-tuple-element.25), calls=%async_computation.1 | async-start | bytes 393216 | tf_op jit(solution)/shard_map/all_to_all | solution.py:447
  35.7 27.0 %collective-permute-start.2 = (bf16[20,128,128]{2,1,0:T(8,128)(2,1)}, bf16[20,128,128]{2,1,0:T(8,128)(2,1)S(1)}, u32[]{:S(2)}, u32[]{:S(2)}) collective-permute-start(bf16[20,128,128]{2,1,0:T(8,128)(2,1)} %get-tuple-element.29), channel_id=1, source_target_pairs={{0,3},{1,0},{2,1},{3,2},{4,7},{5,4},{6,5},{7,6},{8,11},{9,8},{10,9... | collective-permute-start | bytes 1966088 | tf_op jit(solution)/shard_map/ppermute | solution.py:389
  37.7 21.1 %collective-permute-start = (bf16[12,128,128]{2,1,0:T(8,128)(2,1)S(1)}, bf16[12,128,128]{2,1,0:T(8,128)(2,1)S(1)}, u32[]{:S(2)}, u32[]{:S(2)}) collective-permute-start(bf16[12,128,128]{2,1,0:T(8,128)(2,1)S(1)} %get-tuple-element.28.refs_0_), channel_id=1, source_target_pairs={{0,1},{1,2},{2,3},{3,0},{4,5},{5,6},{6,7},{7,4},{8,9},{9,10},{10,1... | collective-permute-start | bytes 1179656 | tf_op jit(solution)/shard_map/ppermute | solution.py:389
  42.8 20.0 %collective-permute-start.1 = (bf16[12,128,128]{2,1,0:T(8,128)(2,1)S(1)}, bf16[12,128,128]{2,1,0:T(8,128)(2,1)S(1)}, u32[]{:S(2)}, u32[]{:S(2)}) collective-permute-start(bf16[12,128,128]{2,1,0:T(8,128)(2,1)S(1)} %get-tuple-element.28.refs_0_), channel_id=1, source_target_pairs={{0,2},{1,3},{2,0},{3,1},{4,6},{5,7},{6,4},{7,5},{8,10},{9,11},{10,... | collective-permute-start | bytes 1179656 | tf_op jit(solution)/shard_map/ppermute | solution.py:389
  51.5 20.0 %all-to-all-start.2 = ((bf16[16,24,128]{2,1,0:T(8,128)(2,1)}), bf16[16,24,128]{2,1,0:T(8,128)(2,1)S(1)}, u32[]{:S(2)}, u32[]{:S(2)}) async-start(bf16[16,24,128]{2,1,0:T(8,128)(2,1)} %get-tuple-element.26), calls=%async_computation.2 | async-start | bytes 196608 | tf_op jit(solution)/shard_map/all_to_all | solution.py:449
  74.7 16.6 %all-to-all-start.3 = ((bf16[16,32,128]{2,1,0:T(8,128)(2,1)}), bf16[16,32,128]{2,1,0:T(8,128)(2,1)S(1)}, u32[]{:S(2)}, u32[]{:S(2)}) async-start(bf16[16,32,128]{2,1,0:T(8,128)(2,1)} %shard_map.126), calls=%async_computation.3 | async-start | bytes 262144 | tf_op jit(solution)/shard_map/all_to_all | solution.py:459
  78.2 19.6 %collective-permute-start.3 = (bf16[18,128,128]{2,1,0:T(8,128)(2,1)S(1)}, bf16[18,128,128]{2,1,0:T(8,128)(2,1)S(1)}, u32[]{:S(2)}, u32[]{:S(2)}) collective-permute-start(bf16[18,128,128]{2,1,0:T(8,128)(2,1)S(1)} %get-tuple-element.33.refs_0_), channel_id=1, source_target_pairs={{0,1},{1,2},{2,3},{3,0},{4,5},{5,6},{6,7},{7,4},{8,9},{9,10},{10,1... | collective-permute-start | bytes 1769480 | tf_op jit(solution)/shard_map/ppermute | solution.py:389
  80.7 17.2 %collective-permute-start.4 = (bf16[18,128,128]{2,1,0:T(8,128)(2,1)S(1)}, bf16[18,128,128]{2,1,0:T(8,128)(2,1)S(1)}, u32[]{:S(2)}, u32[]{:S(2)}) collective-permute-start(bf16[18,128,128]{2,1,0:T(8,128)(2,1)S(1)} %get-tuple-element.33.refs_0_), channel_id=1, source_target_pairs={{0,2},{1,3},{2,0},{3,1},{4,6},{5,7},{6,4},{7,5},{8,10},{9,11},{10,... | collective-permute-start | bytes 1769480 | tf_op jit(solution)/shard_map/ppermute | solution.py:389
  92.2 18.7 %all-to-all-start.4 = ((bf16[16,24,128]{2,1,0:T(8,128)(2,1)}), bf16[16,24,128]{2,1,0:T(8,128)(2,1)S(1)}, u32[]{:S(2)}, u32[]{:S(2)}) async-start(bf16[16,24,128]{2,1,0:T(8,128)(2,1)} %shard_map.127), calls=%async_computation.4 | async-start | bytes 196608 | tf_op jit(solution)/shard_map/all_to_all | solution.py:463
  111.9 17.7 %all-to-all-start.5 = ((bf16[8,48,512]{2,1,0:T(8,128)(2,1)}), bf16[8,48,512]{2,1,0:T(8,128)(2,1)S(1)}, u32[]{:S(2)}, u32[]{:S(2)}) async-start(bf16[8,48,512]{2,1,0:T(8,128)(2,1)} %shard_map.128), calls=%async_computation.5 | async-start | bytes 786432 | tf_op jit(solution)/shard_map/all_to_all | solution.py:470
  116.4 13.2 %collective-permute-start.5 = (bf16[128,1280]{1,0:T(8,128)(2,1)S(1)}, bf16[128,1280]{1,0:T(8,128)(2,1)S(1)}, u32[]{:S(2)}, u32[]{:S(2)}) collective-permute-start(bf16[128,1280]{1,0:T(8,128)(2,1)S(1)} %copy-done), channel_id=1, source_target_pairs={{0,3},{1,0},{2,1},{3,2},{4,7},{5,4},{6,5},{7,6},{8,11},{9,8},{10,9... | collective-permute-start | bytes 983048 | tf_op jit(solution)/shard_map/ppermute | solution.py:389
  130.8 19.8 %all-to-all-start.6 = ((bf16[16,32,128]{2,1,0:T(8,128)(2,1)}), bf16[16,32,128]{2,1,0:T(8,128)(2,1)S(1)}, u32[]{:S(2)}, u32[]{:S(2)}) async-start(bf16[16,32,128]{2,1,0:T(8,128)(2,1)} %get-tuple-element.41), calls=%async_computation.6 | async-start | bytes 262144 | tf_op jit(solution)/shard_map/all_to_all | solution.py:478
  135.7 9.1 %collective-permute-start.6 = (bf16[48,128]{1,0:T(8,128)(2,1)S(1)}, bf16[48,128]{1,0:T(8,128)(2,1)S(1)}, u32[]{:S(2)}, u32[]{:S(2)}) collective-permute-start(bf16[48,128]{1,0:T(8,128)(2,1)S(1)} %get-tuple-element.38), channel_id=1, source_target_pairs={{0,3},{1,0},{2,1},{3,2},{4,7},{5,4},{6,5},{7,6},{8,11},{9,8},{10,9... | collective-permute-start | bytes 36872 | tf_op jit(solution)/shard_map/ppermute | solution.py:389
  138.0 7.1 %collective-permute-start.7 = (bf16[48,128]{1,0:T(8,128)(2,1)S(1)}, bf16[48,128]{1,0:T(8,128)(2,1)S(1)}, u32[]{:S(2)}, u32[]{:S(2)}) collective-permute-start(bf16[48,128]{1,0:T(8,128)(2,1)S(1)} %get-tuple-element.39), channel_id=1, source_target_pairs={{0,2},{1,3},{2,0},{3,1},{4,6},{5,7},{6,4},{7,5},{8,10},{9,11},{10,... | collective-permute-start | bytes 36872 | tf_op jit(solution)/shard_map/ppermute | solution.py:389
  142.7 5.6 %collective-permute-start.8 = (bf16[48,128]{1,0:T(8,128)(2,1)S(1)}, bf16[48,128]{1,0:T(8,128)(2,1)S(1)}, u32[]{:S(2)}, u32[]{:S(2)}) collective-permute-start(bf16[48,128]{1,0:T(8,128)(2,1)S(1)} %get-tuple-element.40), channel_id=1, source_target_pairs={{0,1},{1,2},{2,3},{3,0},{4,5},{5,6},{6,7},{7,4},{8,9},{9,10},{10,1... | collective-permute-start | bytes 36872 | tf_op jit(solution)/shard_map/ppermute | solution.py:389

commit v7 on v3

--- a/solution.py
+++ b/solution.py
@@ -34,7 +34,7 @@
 f32 = jnp.float32
 
 
-def vmem_call(kernel, out_shape, operands, scratch=(), limit=32, scalars=0, hbm=False):
+def vmem_call(kernel, out_shape, operands, scratch=(), limit=12, scalars=0, hbm=False):
     space = pl.BlockSpec(memory_space=pltpu.VMEM)
     outs = jax.tree.map(lambda _: space, out_shape)
     rest = pl.BlockSpec(memory_space=pltpu.HBM) if hbm else space
@@ -72,17 +72,17 @@
     return jnp.concatenate([cosine, cosine], -1), jnp.concatenate([-sine, sine], -1)
 
 
-def bundle_kernel(keys_ref, values_ref, cos_ref, sin_ref, out_weight_ref, next_weight_ref, out_ref, weights_ref):
+def bundle_kernel(keys_ref, values_ref, cos_ref, sin_ref, out_weight_ref, next_weight_ref, cache_ref, weights_ref):
     blocks = keys_ref.shape[0] // BLK
     for b in range(blocks):
-        out_ref[blocks + b] = values_ref[b * BLK : (b + 1) * BLK, :]
+        cache_ref[blocks + b] = values_ref[b * BLK : (b + 1) * BLK, :]
         block = keys_ref[b * BLK : (b + 1) * BLK, :].astype(f32)
         turned = (
             block * cos_ref[b : b + 1, :]
             + pltpu.roll(block, HD // 2, 1) * sin_ref[b : b + 1, :]
         )
         turned = turned.astype(bf16).astype(f32)
-        out_ref[b] = turned.T.astype(bf16)
+        cache_ref[b] = turned.T.astype(bf16)
     for g in range(GQ):
         weights_ref[g] = out_weight_ref[g * HD : (g + 1) * HD, :]
     for j in range(GQ + 2):
@@ -144,7 +144,7 @@
         block = halves[z * RI : (z + 1) * RI] + [cut_ref[z]]
         tiles_ref[z] = jnp.concatenate(block, axis=0).astype(bf16)
     for s in range(NX):
-        src = (x_ref[0] + NX - s) % NX
+        src = x_ref[0] ^ s
         for i in range(RI):
             hidden_ref[s, i] = in_ref[src, HT + i]
         pieces = in_ref[src, HT + RI].astype(f32)
@@ -167,7 +167,7 @@
 
 def attend_kernel(queries_ref, keypos_ref, rowpos_ref, new_ref, *refs):
     cache_refs, (out_ref, score_ref) = refs[:NX], refs[NX:]
-    blocks = cache_refs[0].shape[0] // 2
+    blocks = (keypos_ref.shape[0] - 1) // NX
     scale = HD ** (-0.5) * LOG2E
     contract_last = (((1,), (1,)), ((), ()))
     new_keys, new_values = new_ref[0], new_ref[1]
@@ -256,7 +256,8 @@
 
 
 def output_kernel(heads_ref, *refs):
-    weight_refs, out_ref = [ref.at[pl.ds(0, GQ)] for ref in refs[:NX]], refs[NX]
+    weight_refs, out_ref = refs[:NX], refs[NX]
+    weights = [ref[:GQ].reshape(GQ * HD, HD) for ref in weight_refs]
     rows = heads_ref[...]
     bands = []
     for i in range(RI):
@@ -266,13 +267,14 @@
         )
     attended = jnp.concatenate(bands, axis=0)
     for x in range(NX):
-        term = jnp.dot(attended, weight_refs[x][...].reshape(GQ * HD, HD), preferred_element_type=f32).astype(bf16)
+        term = jnp.dot(attended, weights[x], preferred_element_type=f32).astype(bf16)
         for h in range(NH):
             out_ref[h, :, x * HD : (x + 1) * HD] = term
 
 
 def next_kernel(terms_ref, hidden_ref, gain_ref, *refs):
-    weight_refs = [ref.at[pl.ds(GQ, GQ + 2)] for ref in refs[:NX]]
+    wide = range(GQ, 2 * GQ + 2)
+    weights = [jnp.concatenate([ref[j] for j in wide], axis=1) for ref in refs[:NX]]
     resid_refs, (out_ref, cut_ref) = refs[NX : 2 * NX], refs[2 * NX :]
     attended = terms_ref[0].astype(f32)
     for h in range(1, NH):
@@ -285,8 +287,7 @@
         resid_refs[x][...] = resid.astype(bf16)
         squares = squares + jnp.sum(resid * resid, axis=1, keepdims=True)
         gained = (resid * gain_ref[x : x + 1, :]).astype(bf16)
-        weight = jnp.concatenate([weight_refs[x][j] for j in range(GQ + 2)], axis=1)
-        product = product + jnp.dot(gained, weight, preferred_element_type=f32)
+        product = product + jnp.dot(gained, weights[x], preferred_element_type=f32)
     for i in range(RI):
         for j in range(GQ + 2):
             cut_ref[:, i * (GQ + 2) + j, :] = product[
@@ -324,7 +325,7 @@
     in_refs, out_ref = refs[:NX], refs[NX]
     rows = out_ref.shape[0]
     new = lax.broadcasted_iota(jnp.int32, (rows, 1), 0)
-    source = ((new // RI) % NX + NX - x_ref[0]) % NX
+    source = ((new // RI) % NX) ^ x_ref[0]
     src = source * XR + (new % RI) * NZ + new // (NX * RI)
     chosen = lax.broadcasted_iota(jnp.int32, (rows, rows), 1) == src
     data = jnp.concatenate([ref[...] for ref in in_refs], axis=0)
@@ -375,11 +376,8 @@
     blocks = held // BLK
     a2a = functools.partial(lax.all_to_all, split_axis=0, concat_axis=0, tiled=True)
 
-    def shifted(array, step):
-        return lax.ppermute(array, "x", [(n, (n + step) % NX) for n in range(NX)])
-
-    def after(array, first):
-        return lax.optimization_barrier((array, first))[0]
+    def swapped(array, step):
+        return lax.ppermute(array, "x", [(n, n ^ step) for n in range(NX)])
 
     payload = vmem_call(
         project_kernel,
@@ -396,7 +394,7 @@
     )
     payload = a2a(payload, "x")
 
-    sources = (x + NX - jnp.arange(NX, dtype=jnp.int32)) % NX
+    sources = x ^ jnp.arange(NX, dtype=jnp.int32)
     shift, key_pos = key_layout(
         z * NX + sources, group_lengths, group_owner, group_start, listed_rows, blocks
     )
@@ -431,14 +429,13 @@
         scratch=[pltpu.VMEM((NZ, KT, HD), f32)],
         scalars=1,
     )
-    caches = [cache] + [shifted(after(cache, tiles), step) for step in (1, 3)]
+    tiles, cache = lax.optimization_barrier((tiles, cache))
+    caches = [cache] + [swapped(cache, step) for step in range(1, NX)]
     copies, new = vmem_call(
         rope_kernel,
         (shaped((NZ, 8 * RI, HD), bf16), shaped((2, FRESH, HD), bf16)),
         (a2a(tiles, "z"), cosine[:rows], sine[:rows]),
     )
-    caches.insert(2, shifted(after(cache, copies), 2))
-    weights_x = [weights, shifted(after(weights, copies), 1)]
     queries = a2a(copies, "z").reshape(XR * GQ, HD)
     parts = vmem_call(
         attend_kernel,
@@ -446,7 +443,8 @@
         (queries, key_pos, wide_row_pos, new, *caches),
         scratch=[pltpu.VMEM((HD, (NX * blocks + 2 * RI) * BLK), f32)],
     )
-    weights_x += [shifted(after(weights, parts), step) for step in (2, 3)]
+    parts, weights = lax.optimization_barrier((parts, weights))
+    weights_x = [weights] + [swapped(weights, step) for step in range(1, NX)]
     share = vmem_call(
         combine_kernel, shaped((NZ, 8 * RI, HD), bf16), (a2a(parts, "z"),)
     )
@@ -460,7 +458,7 @@
         (a2a(terms, "heads"), hidden_x, gain_x, *weights_x),
         scratch=[pltpu.VMEM((NZ, 32, HD), f32)],
     )
-    resids = [resids[0]] + [shifted(resids[s], NX - s) for s in range(1, NX)]
+    resids = [resids[0]] + [swapped(resids[s], s) for s in range(1, NX)]
     hidden_out = vmem_call(
         reorder_kernel, shaped(hidden_rows.shape, bf16), (x_scalar, *resids), scalars=1
     )

time: 157 us -> 151 us (0.962)
  starting transfers between devices: 84.7 us -> 77.5 us
    all_to_all x1, starting transfers between devices: 11.2 us -> 3.51 us  [on_device(): a2a(parts, 'z')]
    all_to_all x1, waiting for transfers between devices: 8.88 us -> 12.3 us  [on_device(): queries = a2a(copies, 'z').reshape(XR * GQ, HD)]
    all_to_all x1, starting transfers between devices: 7.51 us -> 5.11 us  [on_device(): a2a(products, 'z')]
    all_to_all x1, starting transfers between devices: 4.52 us -> 6.86 us  [on_device(): queries = a2a(copies, 'z').reshape(XR * GQ, HD)]
    all_to_all x1, waiting for transfers between devices: 7.52 us -> 5.17 us  [on_device(): a2a(tiles, 'z')]
    all_to_all x1, waiting for transfers between devices: 4.24 us -> 6.58 us  [on_device(): heads_out = a2a(share, 'z').reshape(XR * GQ, HD)]
    all_to_all x1, waiting for transfers between devices: 2.05 us -> 0.01 us  [on_device(): a2a(products, 'z')]
where the time goes in v7:
time: 151 us; the launch traced here: 149 us
  starting transfers between devices  77.5 us (51%)
  waiting for transfers between devices  43.4 us (29%)
  blocking collectives  13.2 us (9%)
  Pallas kernels  11.3 us (7%)
  other arithmetic  2.01 us (1%)
    ppermute x9, starting transfers between devices, swapped(): return lax.ppermute(array, 'x', [(n, n ^ step) for n in range(NX)])  30.1 us
    all_to_all x1, starting transfers between devices, on_device(): a2a(tiles, 'z')  13.8 us
    all_to_all x1, blocking collectives, on_device(): a2a(terms, 'heads')  13.2 us
    all_to_all x1, waiting for transfers between devices, on_device(): queries = a2a(copies, 'z').reshape(XR * GQ, HD)  12.3 us
    pallas_call x10, Pallas kernels, vmem_call(): pl.pallas_call(kernel, out_shape=out_shape, in_specs=[small] * scalars +...  11.3 us
    ppermute x9, waiting for transfers between devices, swapped(): return lax.ppermute(array, 'x', [(n, n ^ step) for n in range(NX)])  10.5 us
    all_to_all x1, starting transfers between devices, on_device(): payload = a2a(payload, 'x')  9.47 us
    all_to_all x1, starting transfers between devices, on_device(): heads_out = a2a(share, 'z').reshape(XR * GQ, HD)  8.71 us
  transfers between devices with their start and end apart: 15, of which 9 were waited for; matrix products, arithmetic and copies ran while one was open for 2% of the time, Pallas kernels for 2%

profile of v7, /device:TPU:6, one launch (start us, length us, event | category | flops | bytes accessed | tf_op | source)
XLA Modules:
  0.0 149.5 jit_solution(15057202864580803399)
XLA Ops:
  0.6 2.3 %shard_map.122 = bf16[4,52,16,128]{3,2,1,0:T(8,128)(2,1)} custom-call(bf16[192,128]{1,0:T(8,128)(2,1)} %hidden_hbm.1, bf16[128,1280]{1,0:T(8,128)(2,1)} %weight_hbm.1, f32[1,128]{1,0:T(1,128)} %bitcast.13), custom_call_target="tpu_custom_call" | custom-call | tf_op jit(solution)/shard_map/pallas_call | solution.py:42
  2.9 0.0 copy-start.7
  2.9 0.0 copy-start.5
  3.0 0.0 copy-start.6
  3.0 0.0 copy-start.4
  3.0 0.0 copy-start
  3.0 0.0 copy-start.1
  3.0 0.0 copy-start.2
  3.0 9.5 %all-to-all-start = ((bf16[4,52,16,128]{3,2,1,0:T(8,128)(2,1)}), bf16[4,52,16,128]{3,2,1,0:T(8,128)(2,1)S(1)}, u32[]{:S(2)}, u32[]{:S(2)}) async-start(bf16[4,52,16,128]{3,2,1,0:T(8,128)(2,1)} %shard_map.122), calls=%async_computation | async-start | bytes 1703936 | tf_op jit(solution)/shard_map/all_to_all | solution.py:395
  12.6 0.1 fusion.3
  12.6 0.1 compare_select_fusion
  12.7 0.1 select_reduce_fusion
  12.9 0.4 select_reduce_fusion.1
  13.3 0.1 slice_reduce_fusion
  13.4 0.2 reshape.203
  13.6 0.1 copy.19
  13.7 0.1 concatenate.25
  13.8 0.1 broadcast_in_dim.38
  13.9 0.2 select_reduce_fusion.3
  14.0 0.1 add_convert_fusion
  14.1 0.2 fusion.2
  14.3 0.1 pad_maximum_fusion.2
  14.4 0.3 shard_map.124
  14.8 5.5 %all-to-all-done.in_ref = bf16[4,52,16,128]{3,2,1,0:T(8,128)(2,1)S(1)} async-done(((bf16[4,52,16,128]{3,2,1,0:T(8,128)(2,1)}), bf16[4,52,16,128]{3,2,1,0:T(8,128)(2,1)S(1)}, u32[]{:S(2)}, u32[]{:S(2)}) %all-to-all-start) | async-done | bytes 852000 | tf_op jit(solution)/shard_map/all_to_all | solution.py:395
  20.3 0.9 shard_map.123
  21.1 13.8 %all-to-all-start.1 = ((bf16[16,48,128]{2,1,0:T(8,128)(2,1)}), bf16[16,48,128]{2,1,0:T(8,128)(2,1)S(1)}, u32[]{:S(2)}, u32[]{:S(2)}) async-start(bf16[16,48,128]{2,1,0:T(8,128)(2,1)} %get-tuple-element.20), calls=%async_computation.1 | async-start | bytes 393216 | tf_op jit(solution)/shard_map/all_to_all | solution.py:437
  34.9 0.1 copy.21
  35.0 0.1 pad_maximum_fusion
  35.1 0.1 iota_add_fusion
  35.2 0.5 compare_reduce_fusion
  35.7 4.0 %collective-permute-start.2 = (bf16[12,128,128]{2,1,0:T(8,128)(2,1)S(1)}, bf16[12,128,128]{2,1,0:T(8,128)(2,1)S(1)}, u32[]{:S(2)}, u32[]{:S(2)}) collective-permute-start(bf16[12,128,128]{2,1,0:T(8,128)(2,1)S(1)} %get-tuple-element.23.refs_0_), channel_id=1, source_target_pairs={{0,3},{1,2},{2,1},{3,0},{4,7},{5,6},{6,5},{7,4},{8,11},{9,10},{10,... | collective-permute-start | bytes 1179656 | tf_op jit(solution)/shard_map/ppermute | solution.py:380
  39.7 1.9 %collective-permute-start.1 = (bf16[12,128,128]{2,1,0:T(8,128)(2,1)S(1)}, bf16[12,128,128]{2,1,0:T(8,128)(2,1)S(1)}, u32[]{:S(2)}, u32[]{:S(2)}) collective-permute-start(bf16[12,128,128]{2,1,0:T(8,128)(2,1)S(1)} %get-tuple-element.23.refs_0_), channel_id=1, source_target_pairs={{0,2},{1,3},{2,0},{3,1},{4,6},{5,7},{6,4},{7,5},{8,10},{9,11},{10,... | collective-permute-start | bytes 1179656 | tf_op jit(solution)/shard_map/ppermute | solution.py:380
  41.6 3.9 %collective-permute-start = (bf16[12,128,128]{2,1,0:T(8,128)(2,1)S(1)}, bf16[12,128,128]{2,1,0:T(8,128)(2,1)S(1)}, u32[]{:S(2)}, u32[]{:S(2)}) collective-permute-start(bf16[12,128,128]{2,1,0:T(8,128)(2,1)S(1)} %get-tuple-element.23.refs_0_), channel_id=1, source_target_pairs={{0,1},{1,0},{2,3},{3,2},{4,5},{5,4},{6,7},{7,6},{8,9},{9,8},{10,11... | collective-permute-start | bytes 1179656 | tf_op jit(solution)/shard_map/ppermute | solution.py:380
  45.5 5.2 %all-to-all-done.1.in_ref = bf16[16,48,128]{2,1,0:T(8,128)(2,1)S(1)} async-done(((bf16[16,48,128]{2,1,0:T(8,128)(2,1)}), bf16[16,48,128]{2,1,0:T(8,128)(2,1)S(1)}, u32[]{:S(2)}, u32[]{:S(2)}) %all-to-all-start.1) | async-done | bytes 196640 | tf_op jit(solution)/shard_map/all_to_all | solution.py:437
  50.7 0.7 shard_map.125
  51.5 6.9 %all-to-all-start.2 = ((bf16[16,24,128]{2,1,0:T(8,128)(2,1)}), bf16[16,24,128]{2,1,0:T(8,128)(2,1)S(1)}, u32[]{:S(2)}, u32[]{:S(2)}) async-start(bf16[16,24,128]{2,1,0:T(8,128)(2,1)} %get-tuple-element.21), calls=%async_computation.2 | async-start | bytes 196608 | tf_op jit(solution)/shard_map/all_to_all | solution.py:439
  58.3 0.1 add.107
  58.4 0.1 copy.20
  58.5 0.1 gt.11
  58.6 0.1 add_select_fusion
  58.8 0.4 collective-permute-done.refs_1_
  59.2 12.3 %all-to-all-done.2 = bf16[16,24,128]{2,1,0:T(8,128)(2,1)S(1)} async-done(((bf16[16,24,128]{2,1,0:T(8,128)(2,1)}), bf16[16,24,128]{2,1,0:T(8,128)(2,1)S(1)}, u32[]{:S(2)}, u32[]{:S(2)}) %all-to-all-start.2) | async-done | bytes 98336 | tf_op jit(solution)/shard_map/all_to_all | solution.py:439
  71.5 0.1 broadcast_in_dim.50.rowpos_ref
  71.6 3.1 %shard_map.126 = bf16[16,32,128]{2,1,0:T(8,128)(2,1)} custom-call(bf16[384,128]{1,0:T(8,128)(2,1)S(1)} %bitcast.9, s32[25,128]{1,0:T(8,128)S(1)} %pad_add_fusion.keypos_ref, s32[3,16,128]{2,1,0:T(8,128)S(1)} %broadcast_in_dim.50.rowpos_ref, bf16[2,16,128]{2,1,0:T(8,128)(2,1)S(1)} %get-tuple-element.22.new_ref, ...), custom_call_target="tpu_custom_call" | custom-call | tf_op jit(solution)/shard_map/pallas_call | solution.py:42
  74.7 3.5 %all-to-all-start.3 = ((bf16[16,32,128]{2,1,0:T(8,128)(2,1)}), bf16[16,32,128]{2,1,0:T(8,128)(2,1)S(1)}, u32[]{:S(2)}, u32[]{:S(2)}) async-start(bf16[16,32,128]{2,1,0:T(8,128)(2,1)} %shard_map.126), calls=%async_computation.3 | async-start | bytes 262144 | tf_op jit(solution)/shard_map/all_to_all | solution.py:449
  78.2 4.0 %collective-permute-start.5 = (bf16[18,128,128]{2,1,0:T(8,128)(2,1)S(1)}, bf16[18,128,128]{2,1,0:T(8,128)(2,1)S(1)}, u32[]{:S(2)}, u32[]{:S(2)}) collective-permute-start(bf16[18,128,128]{2,1,0:T(8,128)(2,1)S(1)} %get-tuple-element.26.refs_0_), channel_id=1, source_target_pairs={{0,3},{1,2},{2,1},{3,0},{4,7},{5,6},{6,5},{7,4},{8,11},{9,10},{10,... | collective-permute-start | bytes 1769480 | tf_op jit(solution)/shard_map/ppermute | solution.py:380
  82.2 1.9 %collective-permute-start.4 = (bf16[18,128,128]{2,1,0:T(8,128)(2,1)S(1)}, bf16[18,128,128]{2,1,0:T(8,128)(2,1)S(1)}, u32[]{:S(2)}, u32[]{:S(2)}) collective-permute-start(bf16[18,128,128]{2,1,0:T(8,128)(2,1)S(1)} %get-tuple-element.26.refs_0_), channel_id=1, source_target_pairs={{0,2},{1,3},{2,0},{3,1},{4,6},{5,7},{6,4},{7,5},{8,10},{9,11},{10,... | collective-permute-start | bytes 1769480 | tf_op jit(solution)/shard_map/ppermute | solution.py:380
  84.1 3.9 %collective-permute-start.3 = (bf16[18,128,128]{2,1,0:T(8,128)(2,1)S(1)}, bf16[18,128,128]{2,1,0:T(8,128)(2,1)S(1)}, u32[]{:S(2)}, u32[]{:S(2)}) collective-permute-start(bf16[18,128,128]{2,1,0:T(8,128)(2,1)S(1)} %get-tuple-element.26.refs_0_), channel_id=1, source_target_pairs={{0,1},{1,0},{2,3},{3,2},{4,5},{5,4},{6,7},{7,6},{8,9},{9,8},{10,11... | collective-permute-start | bytes 1769480 | tf_op jit(solution)/shard_map/ppermute | solution.py:380
  88.0 3.2 %all-to-all-done.3.in_ref = bf16[16,32,128]{2,1,0:T(8,128)(2,1)S(1)} async-done(((bf16[16,32,128]{2,1,0:T(8,128)(2,1)}), bf16[16,32,128]{2,1,0:T(8,128)(2,1)S(1)}, u32[]{:S(2)}, u32[]{:S(2)}) %all-to-all-start.3) | async-done | bytes 131104 | tf_op jit(solution)/shard_map/all_to_all | solution.py:449
  91.3 0.9 shard_map.127
  92.2 8.7 %all-to-all-start.4 = ((bf16[16,24,128]{2,1,0:T(8,128)(2,1)}), bf16[16,24,128]{2,1,0:T(8,128)(2,1)S(1)}, u32[]{:S(2)}, u32[]{:S(2)}) async-start(bf16[16,24,128]{2,1,0:T(8,128)(2,1)} %shard_map.127), calls=%async_computation.4 | async-start | bytes 196608 | tf_op jit(solution)/shard_map/all_to_all | solution.py:451
  100.9 3.9 %collective-permute-done.5.refs_3_ = bf16[18,128,128]{2,1,0:T(8,128)(2,1)S(1)} collective-permute-done((bf16[18,128,128]{2,1,0:T(8,128)(2,1)S(1)}, bf16[18,128,128]{2,1,0:T(8,128)(2,1)S(1)}, u32[]{:S(2)}, u32[]{:S(2)}) %collective-permute-start.5) | collective-permute-done | bytes 589856 | tf_op jit(solution)/shard_map/ppermute | solution.py:380
  104.8 2.5 %collective-permute-done.3.refs_1_ = bf16[18,128,128]{2,1,0:T(8,128)(2,1)S(1)} collective-permute-done((bf16[18,128,128]{2,1,0:T(8,128)(2,1)S(1)}, bf16[18,128,128]{2,1,0:T(8,128)(2,1)S(1)}, u32[]{:S(2)}, u32[]{:S(2)}) %collective-permute-start.3) | collective-permute-done | bytes 589856 | tf_op jit(solution)/shard_map/ppermute | solution.py:380
  107.4 6.6 %all-to-all-done.4 = bf16[16,24,128]{2,1,0:T(8,128)(2,1)S(1)} async-done(((bf16[16,24,128]{2,1,0:T(8,128)(2,1)}), bf16[16,24,128]{2,1,0:T(8,128)(2,1)S(1)}, u32[]{:S(2)}, u32[]{:S(2)}) %all-to-all-start.4) | async-done | bytes 98336 | tf_op jit(solution)/shard_map/all_to_all | solution.py:451
  114.0 0.3 shard_map.128
  114.3 13.2 %all_to_all.35.terms_ref = bf16[8,48,512]{2,1,0:T(8,128)(2,1)S(1)} all-to-all(bf16[8,48,512]{2,1,0:T(8,128)(2,1)S(1)} %shard_map.128), channel_id=1, replica_groups=mesh['heads'=8,'z'=16,'x'=4] {'heads'}, dimensions={0} | all-to-all | bytes 786432 | tf_op jit(solution)/shard_map/all_to_all | solution.py:458
  127.5 1.1 shard_map.129
  128.6 5.1 %all-to-all-start.6 = ((bf16[16,32,128]{2,1,0:T(8,128)(2,1)}), bf16[16,32,128]{2,1,0:T(8,128)(2,1)S(1)}, u32[]{:S(2)}, u32[]{:S(2)}) async-start(bf16[16,32,128]{2,1,0:T(8,128)(2,1)} %get-tuple-element.33), calls=%async_computation.6 | async-start | bytes 262144 | tf_op jit(solution)/shard_map/all_to_all | solution.py:466
  133.7 2.2 %collective-permute-start.6 = (bf16[48,128]{1,0:T(8,128)(2,1)S(1)}, bf16[48,128]{1,0:T(8,128)(2,1)S(1)}, u32[]{:S(2)}, u32[]{:S(2)}) collective-permute-start(bf16[48,128]{1,0:T(8,128)(2,1)S(1)} %get-tuple-element.30), channel_id=1, source_target_pairs={{0,1},{1,0},{2,3},{3,2},{4,5},{5,4},{6,7},{7,6},{8,9},{9,8},{10,11... | collective-permute-start | bytes 36872 | tf_op jit(solution)/shard_map/ppermute | solution.py:380
  135.9 5.1 %collective-permute-start.7 = (bf16[48,128]{1,0:T(8,128)(2,1)S(1)}, bf16[48,128]{1,0:T(8,128)(2,1)S(1)}, u32[]{:S(2)}, u32[]{:S(2)}) collective-permute-start(bf16[48,128]{1,0:T(8,128)(2,1)S(1)} %get-tuple-element.31), channel_id=1, source_target_pairs={{0,2},{1,3},{2,0},{3,1},{4,6},{5,7},{6,4},{7,5},{8,10},{9,11},{10,... | collective-permute-start | bytes 36872 | tf_op jit(solution)/shard_map/ppermute | solution.py:380
  141.1 3.1 %collective-permute-start.8 = (bf16[48,128]{1,0:T(8,128)(2,1)S(1)}, bf16[48,128]{1,0:T(8,128)(2,1)S(1)}, u32[]{:S(2)}, u32[]{:S(2)}) collective-permute-start(bf16[48,128]{1,0:T(8,128)(2,1)S(1)} %get-tuple-element.32), channel_id=1, source_target_pairs={{0,3},{1,2},{2,1},{3,0},{4,7},{5,6},{6,5},{7,4},{8,11},{9,10},{10,... | collective-permute-start | bytes 36872 | tf_op jit(solution)/shard_map/ppermute | solution.py:380
  144.2 3.7 %collective-permute-done.8.refs_3_ = bf16[48,128]{1,0:T(8,128)(2,1)S(1)} collective-permute-done((bf16[48,128]{1,0:T(8,128)(2,1)S(1)}, bf16[48,128]{1,0:T(8,128)(2,1)S(1)}, u32[]{:S(2)}, u32[]{:S(2)}) %collective-permute-start.8) | collective-permute-done | bytes 12320 | tf_op jit(solution)/shard_map/ppermute | solution.py:380
  147.9 0.8 shard_map.130
  148.7 0.8 shard_map.131
  (29 shorter events, 0.2 us)
Async XLA Ops:
  2.9 9.6 %copy-start.7 = (s32[128]{0:T(128)S(1)}, s32[128]{0:T(128)}, u32[]{:S(2)}) copy-start(s32[128]{0:T(128)} %param.18) | copy-start | bytes 1540
  2.9 9.6 %copy-start.5 = (s32[128]{0:T(128)S(1)}, s32[128]{0:T(128)}, u32[]{:S(2)}) copy-start(s32[128]{0:T(128)} %param.19) | copy-start | bytes 1540
  3.0 9.9 %copy-start.6 = (s32[128]{0:T(128)S(1)}, s32[128]{0:T(128)}, u32[]{:S(2)}) copy-start(s32[128]{0:T(128)} %param.20) | copy-start | bytes 1540
  3.0 10.4 %copy-start.4 = (s32[192]{0:T(256)S(1)}, s32[192]{0:T(256)}, u32[]{:S(2)}) copy-start(s32[192]{0:T(256)} %param.21) | copy-start | bytes 2308
  3.0 11.4 %copy-start = (bf16[128,1280]{1,0:T(8,128)(2,1)S(1)}, bf16[128,1280]{1,0:T(8,128)(2,1)}, u32[]{:S(2)}) copy-start(bf16[128,1280]{1,0:T(8,128)(2,1)} %next_weight_ref.1) | copy-start | bytes 983044
  3.0 11.4 %copy-start.1 = (bf16[1024,128]{1,0:T(8,128)(2,1)S(1)}, bf16[1024,128]{1,0:T(8,128)(2,1)}, u32[]{:S(2)}) copy-start(bf16[1024,128]{1,0:T(8,128)(2,1)} %out_weight_ref.1) | copy-start | bytes 786436
  3.0 11.4 %copy-start.2 = (bf16[768,128]{1,0:T(8,128)(2,1)S(1)}, bf16[768,128]{1,0:T(8,128)(2,1)}, u32[]{:S(2)}) copy-start(bf16[768,128]{1,0:T(8,128)(2,1)} %keys_ref.1) | copy-start | bytes 589828
  3.0 11.4 %copy-start.3 = (bf16[768,128]{1,0:T(8,128)(2,1)S(1)}, bf16[768,128]{1,0:T(8,128)(2,1)}, u32[]{:S(2)}) copy-start(bf16[768,128]{1,0:T(8,128)(2,1)} %values_ref.1) | copy-start | bytes 589828
  3.0 17.2 %all-to-all-start = ((bf16[4,52,16,128]{3,2,1,0:T(8,128)(2,1)}), bf16[4,52,16,128]{3,2,1,0:T(8,128)(2,1)S(1)}, u32[]{:S(2)}, u32[]{:S(2)}) async-start(bf16[4,52,16,128]{3,2,1,0:T(8,128)(2,1)} %shard_map.122), calls=%async_computation | async-start | bytes 1703936 | tf_op jit(solution)/shard_map/all_to_all | solution.py:395
  21.1 29.6 %all-to-all-start.1 = ((bf16[16,48,128]{2,1,0:T(8,128)(2,1)}), bf16[16,48,128]{2,1,0:T(8,128)(2,1)S(1)}, u32[]{:S(2)}, u32[]{:S(2)}) async-start(bf16[16,48,128]{2,1,0:T(8,128)(2,1)} %get-tuple-element.20), calls=%async_computation.1 | async-start | bytes 393216 | tf_op jit(solution)/shard_map/all_to_all | solution.py:437
  35.7 23.0 %collective-permute-start.2 = (bf16[12,128,128]{2,1,0:T(8,128)(2,1)S(1)}, bf16[12,128,128]{2,1,0:T(8,128)(2,1)S(1)}, u32[]{:S(2)}, u32[]{:S(2)}) collective-permute-start(bf16[12,128,128]{2,1,0:T(8,128)(2,1)S(1)} %get-tuple-element.23.refs_0_), channel_id=1, source_target_pairs={{0,3},{1,2},{2,1},{3,0},{4,7},{5,6},{6,5},{7,4},{8,11},{9,10},{10,... | collective-permute-start | bytes 1179656 | tf_op jit(solution)/shard_map/ppermute | solution.py:380
  39.7 19.1 %collective-permute-start.1 = (bf16[12,128,128]{2,1,0:T(8,128)(2,1)S(1)}, bf16[12,128,128]{2,1,0:T(8,128)(2,1)S(1)}, u32[]{:S(2)}, u32[]{:S(2)}) collective-permute-start(bf16[12,128,128]{2,1,0:T(8,128)(2,1)S(1)} %get-tuple-element.23.refs_0_), channel_id=1, source_target_pairs={{0,2},{1,3},{2,0},{3,1},{4,6},{5,7},{6,4},{7,5},{8,10},{9,11},{10,... | collective-permute-start | bytes 1179656 | tf_op jit(solution)/shard_map/ppermute | solution.py:380
  41.6 17.5 %collective-permute-start = (bf16[12,128,128]{2,1,0:T(8,128)(2,1)S(1)}, bf16[12,128,128]{2,1,0:T(8,128)(2,1)S(1)}, u32[]{:S(2)}, u32[]{:S(2)}) collective-permute-start(bf16[12,128,128]{2,1,0:T(8,128)(2,1)S(1)} %get-tuple-element.23.refs_0_), channel_id=1, source_target_pairs={{0,1},{1,0},{2,3},{3,2},{4,5},{5,4},{6,7},{7,6},{8,9},{9,8},{10,11... | collective-permute-start | bytes 1179656 | tf_op jit(solution)/shard_map/ppermute | solution.py:380
  51.5 20.0 %all-to-all-start.2 = ((bf16[16,24,128]{2,1,0:T(8,128)(2,1)}), bf16[16,24,128]{2,1,0:T(8,128)(2,1)S(1)}, u32[]{:S(2)}, u32[]{:S(2)}) async-start(bf16[16,24,128]{2,1,0:T(8,128)(2,1)} %get-tuple-element.21), calls=%async_computation.2 | async-start | bytes 196608 | tf_op jit(solution)/shard_map/all_to_all | solution.py:439
  74.7 16.6 %all-to-all-start.3 = ((bf16[16,32,128]{2,1,0:T(8,128)(2,1)}), bf16[16,32,128]{2,1,0:T(8,128)(2,1)S(1)}, u32[]{:S(2)}, u32[]{:S(2)}) async-start(bf16[16,32,128]{2,1,0:T(8,128)(2,1)} %shard_map.126), calls=%async_computation.3 | async-start | bytes 262144 | tf_op jit(solution)/shard_map/all_to_all | solution.py:449
  78.2 26.6 %collective-permute-start.5 = (bf16[18,128,128]{2,1,0:T(8,128)(2,1)S(1)}, bf16[18,128,128]{2,1,0:T(8,128)(2,1)S(1)}, u32[]{:S(2)}, u32[]{:S(2)}) collective-permute-start(bf16[18,128,128]{2,1,0:T(8,128)(2,1)S(1)} %get-tuple-element.26.refs_0_), channel_id=1, source_target_pairs={{0,3},{1,2},{2,1},{3,0},{4,7},{5,6},{6,5},{7,4},{8,11},{9,10},{10,... | collective-permute-start | bytes 1769480 | tf_op jit(solution)/shard_map/ppermute | solution.py:380
  82.2 22.7 %collective-permute-start.4 = (bf16[18,128,128]{2,1,0:T(8,128)(2,1)S(1)}, bf16[18,128,128]{2,1,0:T(8,128)(2,1)S(1)}, u32[]{:S(2)}, u32[]{:S(2)}) collective-permute-start(bf16[18,128,128]{2,1,0:T(8,128)(2,1)S(1)} %get-tuple-element.26.refs_0_), channel_id=1, source_target_pairs={{0,2},{1,3},{2,0},{3,1},{4,6},{5,7},{6,4},{7,5},{8,10},{9,11},{10,... | collective-permute-start | bytes 1769480 | tf_op jit(solution)/shard_map/ppermute | solution.py:380
  84.1 23.3 %collective-permute-start.3 = (bf16[18,128,128]{2,1,0:T(8,128)(2,1)S(1)}, bf16[18,128,128]{2,1,0:T(8,128)(2,1)S(1)}, u32[]{:S(2)}, u32[]{:S(2)}) collective-permute-start(bf16[18,128,128]{2,1,0:T(8,128)(2,1)S(1)} %get-tuple-element.26.refs_0_), channel_id=1, source_target_pairs={{0,1},{1,0},{2,3},{3,2},{4,5},{5,4},{6,7},{7,6},{8,9},{9,8},{10,11... | collective-permute-start | bytes 1769480 | tf_op jit(solution)/shard_map/ppermute | solution.py:380
  92.2 21.7 %all-to-all-start.4 = ((bf16[16,24,128]{2,1,0:T(8,128)(2,1)}), bf16[16,24,128]{2,1,0:T(8,128)(2,1)S(1)}, u32[]{:S(2)}, u32[]{:S(2)}) async-start(bf16[16,24,128]{2,1,0:T(8,128)(2,1)} %shard_map.127), calls=%async_computation.4 | async-start | bytes 196608 | tf_op jit(solution)/shard_map/all_to_all | solution.py:451
  128.6 20.1 %all-to-all-start.6 = ((bf16[16,32,128]{2,1,0:T(8,128)(2,1)}), bf16[16,32,128]{2,1,0:T(8,128)(2,1)S(1)}, u32[]{:S(2)}, u32[]{:S(2)}) async-start(bf16[16,32,128]{2,1,0:T(8,128)(2,1)} %get-tuple-element.33), calls=%async_computation.6 | async-start | bytes 262144 | tf_op jit(solution)/shard_map/all_to_all | solution.py:466
  133.7 10.5 %collective-permute-start.6 = (bf16[48,128]{1,0:T(8,128)(2,1)S(1)}, bf16[48,128]{1,0:T(8,128)(2,1)S(1)}, u32[]{:S(2)}, u32[]{:S(2)}) collective-permute-start(bf16[48,128]{1,0:T(8,128)(2,1)S(1)} %get-tuple-element.30), channel_id=1, source_target_pairs={{0,1},{1,0},{2,3},{3,2},{4,5},{5,4},{6,7},{7,6},{8,9},{9,8},{10,11... | collective-permute-start | bytes 36872 | tf_op jit(solution)/shard_map/ppermute | solution.py:380
  135.9 8.3 %collective-permute-start.7 = (bf16[48,128]{1,0:T(8,128)(2,1)S(1)}, bf16[48,128]{1,0:T(8,128)(2,1)S(1)}, u32[]{:S(2)}, u32[]{:S(2)}) collective-permute-start(bf16[48,128]{1,0:T(8,128)(2,1)S(1)} %get-tuple-element.31), channel_id=1, source_target_pairs={{0,2},{1,3},{2,0},{3,1},{4,6},{5,7},{6,4},{7,5},{8,10},{9,11},{10,... | collective-permute-start | bytes 36872 | tf_op jit(solution)/shard_map/ppermute | solution.py:380
  141.1 6.8 %collective-permute-start.8 = (bf16[48,128]{1,0:T(8,128)(2,1)S(1)}, bf16[48,128]{1,0:T(8,128)(2,1)S(1)}, u32[]{:S(2)}, u32[]{:S(2)}) collective-permute-start(bf16[48,128]{1,0:T(8,128)(2,1)S(1)} %get-tuple-element.32), channel_id=1, source_target_pairs={{0,3},{1,2},{2,1},{3,0},{4,7},{5,6},{6,5},{7,4},{8,11},{9,10},{10,... | collective-permute-start | bytes 36872 | tf_op jit(solution)/shard_map/ppermute | solution.py:380

commit v8 on v7

--- a/solution.py
+++ b/solution.py
@@ -379,6 +379,9 @@
     def swapped(array, step):
         return lax.ppermute(array, "x", [(n, n ^ step) for n in range(NX)])
 
+    def after(array, *first):
+        return lax.optimization_barrier((array, *first))[0]
+
     payload = vmem_call(
         project_kernel,
         shaped((NX, HT + RI + 1, TILE, HD), bf16),
@@ -436,6 +439,7 @@
         (shaped((NZ, 8 * RI, HD), bf16), shaped((2, FRESH, HD), bf16)),
         (a2a(tiles, "z"), cosine[:rows], sine[:rows]),
     )
+    weights_x = {0: weights, 2: swapped(after(weights, copies), 2)}
     queries = a2a(copies, "z").reshape(XR * GQ, HD)
     parts = vmem_call(
         attend_kernel,
@@ -443,8 +447,9 @@
         (queries, key_pos, wide_row_pos, new, *caches),
         scratch=[pltpu.VMEM((HD, (NX * blocks + 2 * RI) * BLK), f32)],
     )
-    parts, weights = lax.optimization_barrier((parts, weights))
-    weights_x = [weights] + [swapped(weights, step) for step in range(1, NX)]
+    late = after(weights, parts, weights_x[2])
+    weights_x |= {step: swapped(late, step) for step in (1, 3)}
+    weights_x = [weights_x[step] for step in range(NX)]
     share = vmem_call(
         combine_kernel, shaped((NZ, 8 * RI, HD), bf16), (a2a(parts, "z"),)
     )

time: 151 us -> 146 us (0.967)
  starting transfers between devices: 77.5 us -> 72.1 us
    ppermute x9, waiting for transfers between devices: 10.5 us -> 2.93 us  [swapped(): return lax.ppermute(array, 'x', [(n, n ^ step) for n in range(NX)])]
    all_to_all x1, waiting for transfers between devices: 6.58 us -> 13 us  [on_device(): heads_out = a2a(share, 'z').reshape(XR * GQ, HD)]
    all_to_all x1, waiting for transfers between devices: 3.24 us -> 7.07 us  [on_device(): a2a(parts, 'z')]
    all_to_all x1, starting transfers between devices: 8.71 us -> 4.88 us  [on_device(): heads_out = a2a(share, 'z').reshape(XR * GQ, HD)]
    all_to_all x1, waiting for transfers between devices: 12.3 us -> 8.73 us  [on_device(): queries = a2a(copies, 'z').reshape(XR * GQ, HD)]
    all_to_all x1, starting transfers between devices: 5.11 us -> 3.51 us  [on_device(): a2a(products, 'z')]
  transfers between devices with their start and end apart: 15 -> 15, of which waited for: 9 -> 8; matrix products, arithmetic and copies ran while one was open for 2% -> 2% of each run, Pallas kernels for 2% -> 4%
where the time goes in v8:
time: 146 us; the launch traced here: 144 us
  starting transfers between devices  72.1 us (49%)
  waiting for transfers between devices  42.8 us (29%)
  blocking collectives  13.2 us (9%)
  Pallas kernels  11.3 us (8%)
  other arithmetic  2.01 us (1%)
    ppermute x9, starting transfers between devices, swapped(): return lax.ppermute(array, 'x', [(n, n ^ step) for n in range(NX)])  30.1 us
    all_to_all x1, starting transfers between devices, on_device(): a2a(tiles, 'z')  13.8 us
    all_to_all x1, blocking collectives, on_device(): a2a(terms, 'heads')  13.2 us
    all_to_all x1, waiting for transfers between devices, on_device(): heads_out = a2a(share, 'z').reshape(XR * GQ, HD)  13 us
    pallas_call x10, Pallas kernels, vmem_call(): pl.pallas_call(kernel, out_shape=out_shape, in_specs=[small] * scalars +...  11.3 us
    all_to_all x1, starting transfers between devices, on_device(): payload = a2a(payload, 'x')  9.47 us
    all_to_all x1, waiting for transfers between devices, on_device(): queries = a2a(copies, 'z').reshape(XR * GQ, HD)  8.73 us
    all_to_all x1, waiting for transfers between devices, on_device(): a2a(parts, 'z')  7.07 us
  transfers between devices with their start and end apart: 15, of which 8 were waited for; matrix products, arithmetic and copies ran while one was open for 2% of the time, Pallas kernels for 4%

profile of v8, /device:TPU:6, one launch (start us, length us, event | category | flops | bytes accessed | tf_op | source)
XLA Modules:
  0.0 143.5 jit_solution(13154574159748870222)
XLA Ops:
  0.6 2.3 %shard_map.122 = bf16[4,52,16,128]{3,2,1,0:T(8,128)(2,1)} custom-call(bf16[192,128]{1,0:T(8,128)(2,1)} %hidden_hbm.1, bf16[128,1280]{1,0:T(8,128)(2,1)} %weight_hbm.1, f32[1,128]{1,0:T(1,128)} %bitcast.13), custom_call_target="tpu_custom_call" | custom-call | tf_op jit(solution)/shard_map/pallas_call | solution.py:42
  2.9 0.0 copy-start.7
  2.9 0.0 copy-start.5
  3.0 0.0 copy-start.6
  3.0 0.0 copy-start.4
  3.0 0.0 copy-start
  3.0 0.0 copy-start.1
  3.0 0.0 copy-start.2
  3.0 0.0 copy-start.3
  3.0 9.5 %all-to-all-start = ((bf16[4,52,16,128]{3,2,1,0:T(8,128)(2,1)}), bf16[4,52,16,128]{3,2,1,0:T(8,128)(2,1)S(1)}, u32[]{:S(2)}, u32[]{:S(2)}) async-start(bf16[4,52,16,128]{3,2,1,0:T(8,128)(2,1)} %shard_map.122), calls=%async_computation | async-start | bytes 1703936 | tf_op jit(solution)/shard_map/all_to_all | solution.py:398
  12.6 0.1 fusion.3
  12.6 0.1 compare_select_fusion
  12.7 0.1 select_reduce_fusion
  12.9 0.4 select_reduce_fusion.1
  13.3 0.1 slice_reduce_fusion
  13.4 0.2 reshape.203
  13.6 0.1 copy.19
  13.7 0.1 concatenate.25
  13.8 0.1 broadcast_in_dim.38
  13.9 0.2 select_reduce_fusion.3
  14.0 0.1 add_convert_fusion
  14.1 0.2 fusion.2
  14.3 0.1 pad_maximum_fusion.2
  14.4 0.3 shard_map.124
  14.8 5.5 %all-to-all-done.in_ref = bf16[4,52,16,128]{3,2,1,0:T(8,128)(2,1)S(1)} async-done(((bf16[4,52,16,128]{3,2,1,0:T(8,128)(2,1)}), bf16[4,52,16,128]{3,2,1,0:T(8,128)(2,1)S(1)}, u32[]{:S(2)}, u32[]{:S(2)}) %all-to-all-start) | async-done | bytes 852000 | tf_op jit(solution)/shard_map/all_to_all | solution.py:398
  20.3 0.9 shard_map.123
  21.1 13.8 %all-to-all-start.1 = ((bf16[16,48,128]{2,1,0:T(8,128)(2,1)}), bf16[16,48,128]{2,1,0:T(8,128)(2,1)S(1)}, u32[]{:S(2)}, u32[]{:S(2)}) async-start(bf16[16,48,128]{2,1,0:T(8,128)(2,1)} %get-tuple-element.20), calls=%async_computation.1 | async-start | bytes 393216 | tf_op jit(solution)/shard_map/all_to_all | solution.py:440
  34.9 0.1 copy.21
  35.0 0.1 pad_maximum_fusion
  35.1 0.1 iota_add_fusion
  35.2 0.5 compare_reduce_fusion
  35.7 4.0 %collective-permute-start.2 = (bf16[12,128,128]{2,1,0:T(8,128)(2,1)S(1)}, bf16[12,128,128]{2,1,0:T(8,128)(2,1)S(1)}, u32[]{:S(2)}, u32[]{:S(2)}) collective-permute-start(bf16[12,128,128]{2,1,0:T(8,128)(2,1)S(1)} %get-tuple-element.23.refs_0_), channel_id=1, source_target_pairs={{0,3},{1,2},{2,1},{3,0},{4,7},{5,6},{6,5},{7,4},{8,11},{9,10},{10,... | collective-permute-start | bytes 1179656 | tf_op jit(solution)/shard_map/ppermute | solution.py:380
  39.7 1.9 %collective-permute-start.1 = (bf16[12,128,128]{2,1,0:T(8,128)(2,1)S(1)}, bf16[12,128,128]{2,1,0:T(8,128)(2,1)S(1)}, u32[]{:S(2)}, u32[]{:S(2)}) collective-permute-start(bf16[12,128,128]{2,1,0:T(8,128)(2,1)S(1)} %get-tuple-element.23.refs_0_), channel_id=1, source_target_pairs={{0,2},{1,3},{2,0},{3,1},{4,6},{5,7},{6,4},{7,5},{8,10},{9,11},{10,... | collective-permute-start | bytes 1179656 | tf_op jit(solution)/shard_map/ppermute | solution.py:380
  41.6 3.9 %collective-permute-start = (bf16[12,128,128]{2,1,0:T(8,128)(2,1)S(1)}, bf16[12,128,128]{2,1,0:T(8,128)(2,1)S(1)}, u32[]{:S(2)}, u32[]{:S(2)}) collective-permute-start(bf16[12,128,128]{2,1,0:T(8,128)(2,1)S(1)} %get-tuple-element.23.refs_0_), channel_id=1, source_target_pairs={{0,1},{1,0},{2,3},{3,2},{4,5},{5,4},{6,7},{7,6},{8,9},{9,8},{10,11... | collective-permute-start | bytes 1179656 | tf_op jit(solution)/shard_map/ppermute | solution.py:380
  45.5 5.2 %all-to-all-done.1.in_ref = bf16[16,48,128]{2,1,0:T(8,128)(2,1)S(1)} async-done(((bf16[16,48,128]{2,1,0:T(8,128)(2,1)}), bf16[16,48,128]{2,1,0:T(8,128)(2,1)S(1)}, u32[]{:S(2)}, u32[]{:S(2)}) %all-to-all-start.1) | async-done | bytes 196640 | tf_op jit(solution)/shard_map/all_to_all | solution.py:440
  50.7 0.7 shard_map.125
  51.5 6.9 %all-to-all-start.2 = ((bf16[16,24,128]{2,1,0:T(8,128)(2,1)}), bf16[16,24,128]{2,1,0:T(8,128)(2,1)S(1)}, u32[]{:S(2)}, u32[]{:S(2)}) async-start(bf16[16,24,128]{2,1,0:T(8,128)(2,1)} %get-tuple-element.21), calls=%async_computation.2 | async-start | bytes 196608 | tf_op jit(solution)/shard_map/all_to_all | solution.py:443
  58.3 0.1 add.107
  58.4 0.1 copy.20
  58.5 0.1 gt.11
  58.6 4.0 %collective-permute-start.3 = (bf16[18,128,128]{2,1,0:T(8,128)(2,1)S(1)}, bf16[18,128,128]{2,1,0:T(8,128)(2,1)S(1)}, u32[]{:S(2)}, u32[]{:S(2)}) collective-permute-start(bf16[18,128,128]{2,1,0:T(8,128)(2,1)S(1)} %get-tuple-element.26.refs_0_), channel_id=1, source_target_pairs={{0,2},{1,3},{2,0},{3,1},{4,6},{5,7},{6,4},{7,5},{8,10},{9,11},{10,... | collective-permute-start | bytes 1769480 | tf_op jit(solution)/shard_map/ppermute | solution.py:380
  62.6 0.1 add_select_fusion
  62.8 8.7 %all-to-all-done.2 = bf16[16,24,128]{2,1,0:T(8,128)(2,1)S(1)} async-done(((bf16[16,24,128]{2,1,0:T(8,128)(2,1)}), bf16[16,24,128]{2,1,0:T(8,128)(2,1)S(1)}, u32[]{:S(2)}, u32[]{:S(2)}) %all-to-all-start.2) | async-done | bytes 98336 | tf_op jit(solution)/shard_map/all_to_all | solution.py:443
  71.5 0.1 broadcast_in_dim.50.rowpos_ref
  71.6 3.1 %shard_map.126 = bf16[16,32,128]{2,1,0:T(8,128)(2,1)} custom-call(bf16[384,128]{1,0:T(8,128)(2,1)S(1)} %bitcast.9, s32[25,128]{1,0:T(8,128)S(1)} %pad_add_fusion.keypos_ref, s32[3,16,128]{2,1,0:T(8,128)S(1)} %broadcast_in_dim.50.rowpos_ref, bf16[2,16,128]{2,1,0:T(8,128)(2,1)S(1)} %get-tuple-element.22.new_ref, ...), custom_call_target="tpu_custom_call" | custom-call | tf_op jit(solution)/shard_map/pallas_call | solution.py:42
  74.7 3.5 %all-to-all-start.3 = ((bf16[16,32,128]{2,1,0:T(8,128)(2,1)}), bf16[16,32,128]{2,1,0:T(8,128)(2,1)S(1)}, u32[]{:S(2)}, u32[]{:S(2)}) async-start(bf16[16,32,128]{2,1,0:T(8,128)(2,1)} %shard_map.126), calls=%async_computation.3 | async-start | bytes 262144 | tf_op jit(solution)/shard_map/all_to_all | solution.py:454
  78.2 4.0 %collective-permute-start.5 = (bf16[18,128,128]{2,1,0:T(8,128)(2,1)S(1)}, bf16[18,128,128]{2,1,0:T(8,128)(2,1)S(1)}, u32[]{:S(2)}, u32[]{:S(2)}) collective-permute-start(bf16[18,128,128]{2,1,0:T(8,128)(2,1)S(1)} %get-tuple-element.26.refs_0_), channel_id=1, source_target_pairs={{0,3},{1,2},{2,1},{3,0},{4,7},{5,6},{6,5},{7,4},{8,11},{9,10},{10,... | collective-permute-start | bytes 1769480 | tf_op jit(solution)/shard_map/ppermute | solution.py:380
  82.2 1.9 %collective-permute-start.4 = (bf16[18,128,128]{2,1,0:T(8,128)(2,1)S(1)}, bf16[18,128,128]{2,1,0:T(8,128)(2,1)S(1)}, u32[]{:S(2)}, u32[]{:S(2)}) collective-permute-start(bf16[18,128,128]{2,1,0:T(8,128)(2,1)S(1)} %get-tuple-element.26.refs_0_), channel_id=1, source_target_pairs={{0,1},{1,0},{2,3},{3,2},{4,5},{5,4},{6,7},{7,6},{8,9},{9,8},{10,11... | collective-permute-start | bytes 1769480 | tf_op jit(solution)/shard_map/ppermute | solution.py:380
  84.1 7.1 %all-to-all-done.3.in_ref = bf16[16,32,128]{2,1,0:T(8,128)(2,1)S(1)} async-done(((bf16[16,32,128]{2,1,0:T(8,128)(2,1)}), bf16[16,32,128]{2,1,0:T(8,128)(2,1)S(1)}, u32[]{:S(2)}, u32[]{:S(2)}) %all-to-all-start.3) | async-done | bytes 131104 | tf_op jit(solution)/shard_map/all_to_all | solution.py:454
  91.2 0.9 shard_map.127
  92.1 4.9 %all-to-all-start.4 = ((bf16[16,24,128]{2,1,0:T(8,128)(2,1)}), bf16[16,24,128]{2,1,0:T(8,128)(2,1)S(1)}, u32[]{:S(2)}, u32[]{:S(2)}) async-start(bf16[16,24,128]{2,1,0:T(8,128)(2,1)} %shard_map.127), calls=%async_computation.4 | async-start | bytes 196608 | tf_op jit(solution)/shard_map/all_to_all | solution.py:456
  97.0 13.0 %all-to-all-done.4 = bf16[16,24,128]{2,1,0:T(8,128)(2,1)S(1)} async-done(((bf16[16,24,128]{2,1,0:T(8,128)(2,1)}), bf16[16,24,128]{2,1,0:T(8,128)(2,1)S(1)}, u32[]{:S(2)}, u32[]{:S(2)}) %all-to-all-start.4) | async-done | bytes 98336 | tf_op jit(solution)/shard_map/all_to_all | solution.py:456
  110.0 0.3 shard_map.128
  110.3 13.2 %all_to_all.35.terms_ref = bf16[8,48,512]{2,1,0:T(8,128)(2,1)S(1)} all-to-all(bf16[8,48,512]{2,1,0:T(8,128)(2,1)S(1)} %shard_map.128), channel_id=1, replica_groups=mesh['heads'=8,'z'=16,'x'=4] {'heads'}, dimensions={0} | all-to-all | bytes 786432 | tf_op jit(solution)/shard_map/all_to_all | solution.py:463
  123.5 1.1 shard_map.129
  124.7 3.5 %all-to-all-start.6 = ((bf16[16,32,128]{2,1,0:T(8,128)(2,1)}), bf16[16,32,128]{2,1,0:T(8,128)(2,1)S(1)}, u32[]{:S(2)}, u32[]{:S(2)}) async-start(bf16[16,32,128]{2,1,0:T(8,128)(2,1)} %get-tuple-element.33), calls=%async_computation.6 | async-start | bytes 262144 | tf_op jit(solution)/shard_map/all_to_all | solution.py:471
  128.2 3.9 %collective-permute-start.6 = (bf16[48,128]{1,0:T(8,128)(2,1)S(1)}, bf16[48,128]{1,0:T(8,128)(2,1)S(1)}, u32[]{:S(2)}, u32[]{:S(2)}) collective-permute-start(bf16[48,128]{1,0:T(8,128)(2,1)S(1)} %get-tuple-element.30), channel_id=1, source_target_pairs={{0,1},{1,0},{2,3},{3,2},{4,5},{5,4},{6,7},{7,6},{8,9},{9,8},{10,11... | collective-permute-start | bytes 36872 | tf_op jit(solution)/shard_map/ppermute | solution.py:380
  132.1 2.6 %collective-permute-start.7 = (bf16[48,128]{1,0:T(8,128)(2,1)S(1)}, bf16[48,128]{1,0:T(8,128)(2,1)S(1)}, u32[]{:S(2)}, u32[]{:S(2)}) collective-permute-start(bf16[48,128]{1,0:T(8,128)(2,1)S(1)} %get-tuple-element.31), channel_id=1, source_target_pairs={{0,2},{1,3},{2,0},{3,1},{4,6},{5,7},{6,4},{7,5},{8,10},{9,11},{10,... | collective-permute-start | bytes 36872 | tf_op jit(solution)/shard_map/ppermute | solution.py:380
  134.7 3.9 %collective-permute-start.8 = (bf16[48,128]{1,0:T(8,128)(2,1)S(1)}, bf16[48,128]{1,0:T(8,128)(2,1)S(1)}, u32[]{:S(2)}, u32[]{:S(2)}) collective-permute-start(bf16[48,128]{1,0:T(8,128)(2,1)S(1)} %get-tuple-element.32), channel_id=1, source_target_pairs={{0,3},{1,2},{2,1},{3,0},{4,7},{5,6},{6,5},{7,4},{8,11},{9,10},{10,... | collective-permute-start | bytes 36872 | tf_op jit(solution)/shard_map/ppermute | solution.py:380
  138.6 0.6 collective-permute-done.7.refs_2_
  139.2 2.4 %collective-permute-done.8.refs_3_ = bf16[48,128]{1,0:T(8,128)(2,1)S(1)} collective-permute-done((bf16[48,128]{1,0:T(8,128)(2,1)S(1)}, bf16[48,128]{1,0:T(8,128)(2,1)S(1)}, u32[]{:S(2)}, u32[]{:S(2)}) %collective-permute-start.8) | collective-permute-done | bytes 12320 | tf_op jit(solution)/shard_map/ppermute | solution.py:380
  141.5 0.8 shard_map.130
  142.4 0.3 all-to-all-done.6.in_ref
  142.7 0.8 shard_map.131
  (29 shorter events, 0.2 us)
Async XLA Ops:
  2.9 9.6 %copy-start.7 = (s32[128]{0:T(128)S(1)}, s32[128]{0:T(128)}, u32[]{:S(2)}) copy-start(s32[128]{0:T(128)} %param.18) | copy-start | bytes 1540
  2.9 9.6 %copy-start.5 = (s32[128]{0:T(128)S(1)}, s32[128]{0:T(128)}, u32[]{:S(2)}) copy-start(s32[128]{0:T(128)} %param.19) | copy-start | bytes 1540
  3.0 9.9 %copy-start.6 = (s32[128]{0:T(128)S(1)}, s32[128]{0:T(128)}, u32[]{:S(2)}) copy-start(s32[128]{0:T(128)} %param.20) | copy-start | bytes 1540
  3.0 10.4 %copy-start.4 = (s32[192]{0:T(256)S(1)}, s32[192]{0:T(256)}, u32[]{:S(2)}) copy-start(s32[192]{0:T(256)} %param.21) | copy-start | bytes 2308
  3.0 11.4 %copy-start = (bf16[128,1280]{1,0:T(8,128)(2,1)S(1)}, bf16[128,1280]{1,0:T(8,128)(2,1)}, u32[]{:S(2)}) copy-start(bf16[128,1280]{1,0:T(8,128)(2,1)} %next_weight_ref.1) | copy-start | bytes 983044
  3.0 11.4 %copy-start.1 = (bf16[1024,128]{1,0:T(8,128)(2,1)S(1)}, bf16[1024,128]{1,0:T(8,128)(2,1)}, u32[]{:S(2)}) copy-start(bf16[1024,128]{1,0:T(8,128)(2,1)} %out_weight_ref.1) | copy-start | bytes 786436
  3.0 11.4 %copy-start.2 = (bf16[768,128]{1,0:T(8,128)(2,1)S(1)}, bf16[768,128]{1,0:T(8,128)(2,1)}, u32[]{:S(2)}) copy-start(bf16[768,128]{1,0:T(8,128)(2,1)} %keys_ref.1) | copy-start | bytes 589828
  3.0 11.4 %copy-start.3 = (bf16[768,128]{1,0:T(8,128)(2,1)S(1)}, bf16[768,128]{1,0:T(8,128)(2,1)}, u32[]{:S(2)}) copy-start(bf16[768,128]{1,0:T(8,128)(2,1)} %values_ref.1) | copy-start | bytes 589828
  3.0 17.2 %all-to-all-start = ((bf16[4,52,16,128]{3,2,1,0:T(8,128)(2,1)}), bf16[4,52,16,128]{3,2,1,0:T(8,128)(2,1)S(1)}, u32[]{:S(2)}, u32[]{:S(2)}) async-start(bf16[4,52,16,128]{3,2,1,0:T(8,128)(2,1)} %shard_map.122), calls=%async_computation | async-start | bytes 1703936 | tf_op jit(solution)/shard_map/all_to_all | solution.py:398
  21.1 29.6 %all-to-all-start.1 = ((bf16[16,48,128]{2,1,0:T(8,128)(2,1)}), bf16[16,48,128]{2,1,0:T(8,128)(2,1)S(1)}, u32[]{:S(2)}, u32[]{:S(2)}) async-start(bf16[16,48,128]{2,1,0:T(8,128)(2,1)} %get-tuple-element.20), calls=%async_computation.1 | async-start | bytes 393216 | tf_op jit(solution)/shard_map/all_to_all | solution.py:440
  35.7 27.0 %collective-permute-start.2 = (bf16[12,128,128]{2,1,0:T(8,128)(2,1)S(1)}, bf16[12,128,128]{2,1,0:T(8,128)(2,1)S(1)}, u32[]{:S(2)}, u32[]{:S(2)}) collective-permute-start(bf16[12,128,128]{2,1,0:T(8,128)(2,1)S(1)} %get-tuple-element.23.refs_0_), channel_id=1, source_target_pairs={{0,3},{1,2},{2,1},{3,0},{4,7},{5,6},{6,5},{7,4},{8,11},{9,10},{10,... | collective-permute-start | bytes 1179656 | tf_op jit(solution)/shard_map/ppermute | solution.py:380
  39.7 23.0 %collective-permute-start.1 = (bf16[12,128,128]{2,1,0:T(8,128)(2,1)S(1)}, bf16[12,128,128]{2,1,0:T(8,128)(2,1)S(1)}, u32[]{:S(2)}, u32[]{:S(2)}) collective-permute-start(bf16[12,128,128]{2,1,0:T(8,128)(2,1)S(1)} %get-tuple-element.23.refs_0_), channel_id=1, source_target_pairs={{0,2},{1,3},{2,0},{3,1},{4,6},{5,7},{6,4},{7,5},{8,10},{9,11},{10,... | collective-permute-start | bytes 1179656 | tf_op jit(solution)/shard_map/ppermute | solution.py:380
  41.6 21.1 %collective-permute-start = (bf16[12,128,128]{2,1,0:T(8,128)(2,1)S(1)}, bf16[12,128,128]{2,1,0:T(8,128)(2,1)S(1)}, u32[]{:S(2)}, u32[]{:S(2)}) collective-permute-start(bf16[12,128,128]{2,1,0:T(8,128)(2,1)S(1)} %get-tuple-element.23.refs_0_), channel_id=1, source_target_pairs={{0,1},{1,0},{2,3},{3,2},{4,5},{5,4},{6,7},{7,6},{8,9},{9,8},{10,11... | collective-permute-start | bytes 1179656 | tf_op jit(solution)/shard_map/ppermute | solution.py:380
  51.5 20.0 %all-to-all-start.2 = ((bf16[16,24,128]{2,1,0:T(8,128)(2,1)}), bf16[16,24,128]{2,1,0:T(8,128)(2,1)S(1)}, u32[]{:S(2)}, u32[]{:S(2)}) async-start(bf16[16,24,128]{2,1,0:T(8,128)(2,1)} %get-tuple-element.21), calls=%async_computation.2 | async-start | bytes 196608 | tf_op jit(solution)/shard_map/all_to_all | solution.py:443
  58.6 19.5 %collective-permute-start.3 = (bf16[18,128,128]{2,1,0:T(8,128)(2,1)S(1)}, bf16[18,128,128]{2,1,0:T(8,128)(2,1)S(1)}, u32[]{:S(2)}, u32[]{:S(2)}) collective-permute-start(bf16[18,128,128]{2,1,0:T(8,128)(2,1)S(1)} %get-tuple-element.26.refs_0_), channel_id=1, source_target_pairs={{0,2},{1,3},{2,0},{3,1},{4,6},{5,7},{6,4},{7,5},{8,10},{9,11},{10,... | collective-permute-start | bytes 1769480 | tf_op jit(solution)/shard_map/ppermute | solution.py:380
  74.7 16.5 %all-to-all-start.3 = ((bf16[16,32,128]{2,1,0:T(8,128)(2,1)}), bf16[16,32,128]{2,1,0:T(8,128)(2,1)S(1)}, u32[]{:S(2)}, u32[]{:S(2)}) async-start(bf16[16,32,128]{2,1,0:T(8,128)(2,1)} %shard_map.126), calls=%async_computation.3 | async-start | bytes 262144 | tf_op jit(solution)/shard_map/all_to_all | solution.py:454
  78.2 18.8 %collective-permute-start.5 = (bf16[18,128,128]{2,1,0:T(8,128)(2,1)S(1)}, bf16[18,128,128]{2,1,0:T(8,128)(2,1)S(1)}, u32[]{:S(2)}, u32[]{:S(2)}) collective-permute-start(bf16[18,128,128]{2,1,0:T(8,128)(2,1)S(1)} %get-tuple-element.26.refs_0_), channel_id=1, source_target_pairs={{0,3},{1,2},{2,1},{3,0},{4,7},{5,6},{6,5},{7,4},{8,11},{9,10},{10,... | collective-permute-start | bytes 1769480 | tf_op jit(solution)/shard_map/ppermute | solution.py:380
  82.2 14.8 %collective-permute-start.4 = (bf16[18,128,128]{2,1,0:T(8,128)(2,1)S(1)}, bf16[18,128,128]{2,1,0:T(8,128)(2,1)S(1)}, u32[]{:S(2)}, u32[]{:S(2)}) collective-permute-start(bf16[18,128,128]{2,1,0:T(8,128)(2,1)S(1)} %get-tuple-element.26.refs_0_), channel_id=1, source_target_pairs={{0,1},{1,0},{2,3},{3,2},{4,5},{5,4},{6,7},{7,6},{8,9},{9,8},{10,11... | collective-permute-start | bytes 1769480 | tf_op jit(solution)/shard_map/ppermute | solution.py:380
  92.1 17.9 %all-to-all-start.4 = ((bf16[16,24,128]{2,1,0:T(8,128)(2,1)}), bf16[16,24,128]{2,1,0:T(8,128)(2,1)S(1)}, u32[]{:S(2)}, u32[]{:S(2)}) async-start(bf16[16,24,128]{2,1,0:T(8,128)(2,1)} %shard_map.127), calls=%async_computation.4 | async-start | bytes 196608 | tf_op jit(solution)/shard_map/all_to_all | solution.py:456
  124.7 18.1 %all-to-all-start.6 = ((bf16[16,32,128]{2,1,0:T(8,128)(2,1)}), bf16[16,32,128]{2,1,0:T(8,128)(2,1)S(1)}, u32[]{:S(2)}, u32[]{:S(2)}) async-start(bf16[16,32,128]{2,1,0:T(8,128)(2,1)} %get-tuple-element.33), calls=%async_computation.6 | async-start | bytes 262144 | tf_op jit(solution)/shard_map/all_to_all | solution.py:471
  128.2 10.5 %collective-permute-start.6 = (bf16[48,128]{1,0:T(8,128)(2,1)S(1)}, bf16[48,128]{1,0:T(8,128)(2,1)S(1)}, u32[]{:S(2)}, u32[]{:S(2)}) collective-permute-start(bf16[48,128]{1,0:T(8,128)(2,1)S(1)} %get-tuple-element.30), channel_id=1, source_target_pairs={{0,1},{1,0},{2,3},{3,2},{4,5},{5,4},{6,7},{7,6},{8,9},{9,8},{10,11... | collective-permute-start | bytes 36872 | tf_op jit(solution)/shard_map/ppermute | solution.py:380
  132.1 7.1 %collective-permute-start.7 = (bf16[48,128]{1,0:T(8,128)(2,1)S(1)}, bf16[48,128]{1,0:T(8,128)(2,1)S(1)}, u32[]{:S(2)}, u32[]{:S(2)}) collective-permute-start(bf16[48,128]{1,0:T(8,128)(2,1)S(1)} %get-tuple-element.31), channel_id=1, source_target_pairs={{0,2},{1,3},{2,0},{3,1},{4,6},{5,7},{6,4},{7,5},{8,10},{9,11},{10,... | collective-permute-start | bytes 36872 | tf_op jit(solution)/shard_map/ppermute | solution.py:380
  134.7 6.8 %collective-permute-start.8 = (bf16[48,128]{1,0:T(8,128)(2,1)S(1)}, bf16[48,128]{1,0:T(8,128)(2,1)S(1)}, u32[]{:S(2)}, u32[]{:S(2)}) collective-permute-start(bf16[48,128]{1,0:T(8,128)(2,1)S(1)} %get-tuple-element.32), channel_id=1, source_target_pairs={{0,3},{1,2},{2,1},{3,0},{4,7},{5,6},{6,5},{7,4},{8,11},{9,10},{10,... | collective-permute-start | bytes 36872 | tf_op jit(solution)/shard_map/ppermute | solution.py:380

commit v9 on v8

--- a/solution.py
+++ b/solution.py
@@ -21,8 +21,9 @@
 TILE = 16
 QT = RI * GQ
 KT = 2 * NX * RI
-HT = QT + KT
+WB = 2 * GQ + 3
 GROUPS = ("z", "x")
+HEADS = ("y", "core")
 theta_base = 500000.0
 epsilon = 1e-05
 masked_score = -1e30
@@ -72,7 +73,9 @@
     return jnp.concatenate([cosine, cosine], -1), jnp.concatenate([-sine, sine], -1)
 
 
-def bundle_kernel(keys_ref, values_ref, cos_ref, sin_ref, out_weight_ref, next_weight_ref, cache_ref, weights_ref):
+def bundle_kernel(
+    x_ref, keys_ref, values_ref, cos_ref, sin_ref, out_weight_ref, next_weight_ref, hidden_ref, cache_ref, *bundle_refs
+):
     blocks = keys_ref.shape[0] // BLK
     for b in range(blocks):
         cache_ref[blocks + b] = values_ref[b * BLK : (b + 1) * BLK, :]
@@ -83,13 +86,15 @@
         )
         turned = turned.astype(bf16).astype(f32)
         cache_ref[b] = turned.T.astype(bf16)
-    for g in range(GQ):
-        weights_ref[g] = out_weight_ref[g * HD : (g + 1) * HD, :]
-    for j in range(GQ + 2):
-        weights_ref[GQ + j] = next_weight_ref[:, j * HD : (j + 1) * HD]
-
-
-def project_kernel(hidden_hbm, weight_hbm, gain_hbm, out_ref, hidden_ref, weight_ref, gain_ref, sems):
+    for s, bundle_ref in enumerate(bundle_refs):
+        for g in range(GQ):
+            bundle_ref[g] = out_weight_ref[g * HD : (g + 1) * HD, :]
+        for j in range(GQ + 2):
+            bundle_ref[GQ + j] = next_weight_ref[:, j * HD : (j + 1) * HD]
+        bundle_ref[WB - 1] = hidden_ref[x_ref[0] ^ s]
+
+
+def project_kernel(hidden_hbm, weight_hbm, gain_hbm, out_ref, rows_ref, hidden_ref, weight_ref, gain_ref, sems):
     copies = [
         pltpu.make_async_copy(src, dst, sems.at[n])
         for n, (src, dst) in enumerate(
@@ -125,11 +130,11 @@
                 tile = band[:, (GQ + j) * HD : (GQ + j + 1) * HD]
                 for to in range(NX):
                     out_ref[to, QT + j * NX * RI + x * RI + i] = tile
-            out_ref[x, HT + i] = part[i * TILE : (i + 1) * TILE, :]
-        out_ref[x, HT + RI] = gain
-
-
-def sum_x_kernel(x_ref, in_ref, tiles_ref, hidden_ref, gain_ref, cut_ref):
+        rest = jnp.zeros((HD - XR - TILE, HD), bf16)
+        rows_ref[x] = jnp.concatenate([part, gain, rest], axis=0)
+
+
+def sum_x_kernel(in_ref, tiles_ref, cut_ref):
     def total(t):
         result = in_ref[0, t].astype(f32)
         for x in range(1, NX):
@@ -143,12 +148,6 @@
     for z in range(NZ):
         block = halves[z * RI : (z + 1) * RI] + [cut_ref[z]]
         tiles_ref[z] = jnp.concatenate(block, axis=0).astype(bf16)
-    for s in range(NX):
-        src = x_ref[0] ^ s
-        for i in range(RI):
-            hidden_ref[s, i] = in_ref[src, HT + i]
-        pieces = in_ref[src, HT + RI].astype(f32)
-        gain_ref[s : s + 1, :] = pieces[0:1] + pieces[1:2] + pieces[2:3]
 
 
 def rope_kernel(in_ref, cos_ref, sin_ref, copies_ref, new_ref):
@@ -272,7 +271,7 @@
             out_ref[h, :, x * HD : (x + 1) * HD] = term
 
 
-def next_kernel(terms_ref, hidden_ref, gain_ref, *refs):
+def next_kernel(terms_ref, *refs):
     wide = range(GQ, 2 * GQ + 2)
     weights = [jnp.concatenate([ref[j] for j in wide], axis=1) for ref in refs[:NX]]
     resid_refs, (out_ref, cut_ref) = refs[NX : 2 * NX], refs[2 * NX :]
@@ -282,11 +281,13 @@
     squares = jnp.zeros((XR, 1), f32)
     product = jnp.zeros((XR, (GQ + 2) * HD), f32)
     for x in range(NX):
-        before = jnp.concatenate([hidden_ref[x, i] for i in range(RI)], axis=0).astype(f32)
+        rest = refs[x][WB - 1].astype(f32)
+        before = rest[:XR]
+        gain = rest[XR : XR + 1] + rest[XR + 1 : XR + 2] + rest[XR + 2 : XR + 3]
         resid = before + attended[:, x * HD : (x + 1) * HD]
         resid_refs[x][...] = resid.astype(bf16)
         squares = squares + jnp.sum(resid * resid, axis=1, keepdims=True)
-        gained = (resid * gain_ref[x : x + 1, :]).astype(bf16)
+        gained = (resid * gain).astype(bf16)
         product = product + jnp.dot(gained, weights[x], preferred_element_type=f32)
     for i in range(RI):
         for j in range(GQ + 2):
@@ -382,9 +383,9 @@
     def after(array, *first):
         return lax.optimization_barrier((array, *first))[0]
 
-    payload = vmem_call(
+    payload, hidden_rest = vmem_call(
         project_kernel,
-        shaped((NX, HT + RI + 1, TILE, HD), bf16),
+        (shaped((NX, QT + KT, TILE, HD), bf16), shaped((NX, HD, HD), bf16)),
         (hidden_rows, qkv_weight, norm_gain.reshape(1, HD)),
         scratch=[
             pltpu.VMEM(hidden_rows.shape, bf16),
@@ -414,23 +415,28 @@
         jnp.concatenate([query_pos, new_pos, jnp.zeros((NX * RI,), jnp.int32), shift[0]])
     )
     rows = 8 * RI + KT
-    cache, weights = vmem_call(
+    x_scalar = x.reshape(1).astype(jnp.int32)
+    cache, *bundles = vmem_call(
         bundle_kernel,
-        (shaped((2 * blocks, BLK, HD), bf16), shaped((2 * GQ + 2, HD, HD), bf16)),
-        (cache_keys, cache_values, cosine[rows:], sine[rows:], out_weight, next_weight),
-    )
-
-    x_scalar = x.reshape(1).astype(jnp.int32)
-    tiles, hidden_x, gain_x = vmem_call(
+        (shaped((2 * blocks, BLK, HD), bf16), *[shaped((WB, HD, HD), bf16)] * NX),
+        (
+            x_scalar,
+            cache_keys,
+            cache_values,
+            cosine[rows:],
+            sine[rows:],
+            out_weight,
+            next_weight,
+            hidden_rest,
+        ),
+        scalars=1,
+    )
+
+    tiles = vmem_call(
         sum_x_kernel,
-        (
-            shaped((NZ, rows, HD), bf16),
-            shaped((NX, RI, TILE, HD), bf16),
-            shaped((NX, HD), f32),
-        ),
-        (x_scalar, payload),
+        shaped((NZ, rows, HD), bf16),
+        (payload,),
         scratch=[pltpu.VMEM((NZ, KT, HD), f32)],
-        scalars=1,
     )
     tiles, cache = lax.optimization_barrier((tiles, cache))
     caches = [cache] + [swapped(cache, step) for step in range(1, NX)]
@@ -439,7 +445,7 @@
         (shaped((NZ, 8 * RI, HD), bf16), shaped((2, FRESH, HD), bf16)),
         (a2a(tiles, "z"), cosine[:rows], sine[:rows]),
     )
-    weights_x = {0: weights, 2: swapped(after(weights, copies), 2)}
+    weights_x = {0: bundles[0], 2: swapped(after(bundles[2], copies), 2)}
     queries = a2a(copies, "z").reshape(XR * GQ, HD)
     parts = vmem_call(
         attend_kernel,
@@ -447,8 +453,8 @@
         (queries, key_pos, wide_row_pos, new, *caches),
         scratch=[pltpu.VMEM((HD, (NX * blocks + 2 * RI) * BLK), f32)],
     )
-    late = after(weights, parts, weights_x[2])
-    weights_x |= {step: swapped(late, step) for step in (1, 3)}
+    for step in (1, 3):
+        weights_x[step] = swapped(after(bundles[step], parts, weights_x[2]), step)
     weights_x = [weights_x[step] for step in range(NX)]
     share = vmem_call(
         combine_kernel, shaped((NZ, 8 * RI, HD), bf16), (a2a(parts, "z"),)
@@ -460,37 +466,38 @@
     *resids, products = vmem_call(
         next_kernel,
         (*[shaped((XR, HD), bf16)] * NX, shaped((NZ, 32, HD), bf16)),
-        (a2a(terms, "heads"), hidden_x, gain_x, *weights_x),
+        (a2a(terms, ("core", "y")), *weights_x),
         scratch=[pltpu.VMEM((NZ, 32, HD), f32)],
     )
     resids = [resids[0]] + [swapped(resids[s], s) for s in range(1, NX)]
+    next_qkv = vmem_call(
+        finish_kernel, shaped((RI, (GQ + 2) * HD), bf16), (a2a(products, "z"),)
+    )
+    *resids, next_qkv = lax.optimization_barrier((*resids, next_qkv))
     hidden_out = vmem_call(
         reorder_kernel, shaped(hidden_rows.shape, bf16), (x_scalar, *resids), scalars=1
     )
-    next_qkv = vmem_call(
-        finish_kernel, shaped((RI, (GQ + 2) * HD), bf16), (a2a(products, "z"),)
-    )
     return hidden_out, next_qkv
 
 
 def solution(mesh):
-    split = Mesh(mesh.devices.reshape(NH, NZ, NX), ("heads", "z", "x"))
+    split = Mesh(mesh.devices.reshape(NH // 2, 2, NZ, NX), ("y", "core", "z", "x"))
     return jax.shard_map(
         on_device,
         mesh=split,
         in_specs=(
             P(None, GROUPS),
-            P(GROUPS, "heads"),
-            P("heads", GROUPS),
+            P(GROUPS, HEADS),
+            P(HEADS, GROUPS),
             P(GROUPS),
-            P(GROUPS, "heads"),
-            P(GROUPS, "heads"),
-            P(GROUPS, "heads"),
+            P(GROUPS, HEADS),
+            P(GROUPS, HEADS),
+            P(GROUPS, HEADS),
             P(),
             P(),
             P(),
             P(),
         ),
-        out_specs=(P(None, GROUPS), P(GROUPS, "heads")),
+        out_specs=(P(None, GROUPS), P(GROUPS, HEADS)),
         check_vma=False,
     )

time: 146 us -> 144 us (0.986)
  blocking collectives: 13.2 us -> 30.9 us
  waiting for transfers between devices: 42.8 us -> 26.4 us
  starting transfers between devices: 72.1 us -> 67.5 us
  local copies, waits for them, and re-layouts: 1.05 us -> 3.55 us
    all_to_all x1 -> x2, blocking collectives: 13.2 us -> 30.9 us  [the longest x1 18.3 us: on_device(): heads_out = a2a(share, 'z').reshape(XR * GQ, HD)]
    all_to_all x1 -> x0, waiting for transfers between devices: 13 us -> none  [on_device(): heads_out = a2a(share, 'z').reshape(XR * GQ, HD)]
    all_to_all x1 -> x0, starting transfers between devices: 4.88 us -> none  [on_device(): heads_out = a2a(share, 'z').reshape(XR * GQ, HD)]
    all_to_all x1, waiting for transfers between devices: 0.35 us -> 3.51 us  [on_device(): a2a(products, 'z')]
    all_to_all x1, waiting for transfers between devices: 5.51 us -> 2.46 us  [on_device(): payload = a2a(payload, 'x')]
    ppermute x9, waiting for transfers between devices: 2.93 us -> 0.02 us  [swapped(): return lax.ppermute(array, 'x', [(n, n ^ step) for n in range(NX)])]
    unnamed x16 -> x24, local copies, waits for them, and re-layouts: 0.05 us -> 2.55 us
  transfers between devices with their start and end apart: 15 -> 14, of which waited for: 8 -> 5; matrix products, arithmetic and copies ran while one was open for 2% -> 2% of each run, Pallas kernels for 4% -> 4%
where the time goes in v9:
time: 144 us; the launch traced here: 142 us
  starting transfers between devices  67.5 us (47%)
  blocking collectives  30.9 us (21%)
  waiting for transfers between devices  26.4 us (18%)
  Pallas kernels  10.8 us (8%)
  local copies, waits for them, and re-layouts  3.55 us (2%)
  other arithmetic  2.02 us (1%)
    ppermute x9, starting transfers between devices, swapped(): return lax.ppermute(array, 'x', [(n, n ^ step) for n in range(NX)])  30.7 us
    all_to_all x1, blocking collectives, on_device(): heads_out = a2a(share, 'z').reshape(XR * GQ, HD)  18.3 us
    all_to_all x1, starting transfers between devices, on_device(): a2a(tiles, 'z')  13.4 us
    all_to_all x1, blocking collectives, on_device(): a2a(terms, ('core', 'y'))  12.6 us
    pallas_call x10, Pallas kernels, vmem_call(): pl.pallas_call(kernel, out_shape=out_shape, in_specs=[small] * scalars +...  10.8 us
    all_to_all x1, starting transfers between devices, on_device(): payload = a2a(payload, 'x')  9.46 us
    all_to_all x1, waiting for transfers between devices, on_device(): queries = a2a(copies, 'z').reshape(XR * GQ, HD)  8.72 us
    all_to_all x1, starting transfers between devices, on_device(): queries = a2a(copies, 'z').reshape(XR * GQ, HD)  6.86 us
  transfers between devices with their start and end apart: 14, of which 5 were waited for; matrix products, arithmetic and copies ran while one was open for 2% of the time, Pallas kernels for 4%

profile of v9, /device:TPU:6, one launch (start us, length us, event | category | flops | bytes accessed | tf_op | source)
XLA Modules:
  0.0 142.2 jit_solution(14217339874919662648)
XLA Ops:
  0.6 2.3 %shard_map.122 = (bf16[4,48,16,128]{3,2,1,0:T(8,128)(2,1)}, bf16[4,128,128]{2,1,0:T(8,128)(2,1)}) custom-call(bf16[192,128]{1,0:T(8,128)(2,1)} %hidden_hbm.1, bf16[128,1280]{1,0:T(8,128)(2,1)} %weight_hbm.1, f32[1,128]{1,0:T(1,128)} %bitcast.13), custom_call_target="tpu_custom_call" | custom-call | tf_op jit(solution)/shard_map/pallas_call | solution.py:43
  2.9 0.0 copy-start.11
  2.9 0.0 copy-start.9
  2.9 0.0 copy-start.10
  3.0 0.0 copy-start.8
  3.0 0.0 copy-start
  3.0 0.0 copy-start.1
  3.0 0.0 copy-start.2
  3.0 0.0 copy-start.3
  3.0 9.5 %all-to-all-start = ((bf16[4,48,16,128]{3,2,1,0:T(8,128)(2,1)}), bf16[4,48,16,128]{3,2,1,0:T(8,128)(2,1)S(1)}, u32[]{:S(2)}, u32[]{:S(2)}) async-start(bf16[4,48,16,128]{3,2,1,0:T(8,128)(2,1)} %get-tuple-element.26), calls=%async_computation | async-start | bytes 1572864 | tf_op jit(solution)/shard_map/all_to_all | solution.py:399
  12.6 0.1 fusion.3
  12.6 0.1 compare_select_fusion
  12.7 0.1 select_reduce_fusion
  12.9 0.4 select_reduce_fusion.1
  13.3 0.1 slice_reduce_fusion
  13.4 0.2 reshape.203
  13.6 0.1 copy.19
  13.7 0.1 concatenate.25
  13.8 0.1 broadcast_in_dim.38
  13.9 0.2 select_reduce_fusion.3
  14.1 0.1 add_convert_fusion
  14.1 0.2 fusion.2
  14.3 0.1 pad_maximum_fusion.2
  14.4 0.5 shard_map.124
  15.0 0.8 copy-done.5
  15.8 0.8 copy-done.6
  16.6 0.8 copy-done.7
  17.5 2.5 %all-to-all-done.in_ref = bf16[4,48,16,128]{3,2,1,0:T(8,128)(2,1)S(1)} async-done(((bf16[4,48,16,128]{3,2,1,0:T(8,128)(2,1)}), bf16[4,48,16,128]{3,2,1,0:T(8,128)(2,1)S(1)}, u32[]{:S(2)}, u32[]{:S(2)}) %all-to-all-start) | async-done | bytes 786464 | tf_op jit(solution)/shard_map/all_to_all | solution.py:399
  19.9 0.9 shard_map.123
  20.8 13.4 %all-to-all-start.1 = ((bf16[16,48,128]{2,1,0:T(8,128)(2,1)}), bf16[16,48,128]{2,1,0:T(8,128)(2,1)S(1)}, u32[]{:S(2)}, u32[]{:S(2)}) async-start(bf16[16,48,128]{2,1,0:T(8,128)(2,1)} %shard_map.123), calls=%async_computation.1 | async-start | bytes 393216 | tf_op jit(solution)/shard_map/all_to_all | solution.py:446
  34.2 0.1 copy.21
  34.3 0.1 pad_maximum_fusion
  34.4 0.1 iota_add_fusion
  34.5 0.5 compare_reduce_fusion
  35.0 4.0 %collective-permute-start.2 = (bf16[12,128,128]{2,1,0:T(8,128)(2,1)S(1)}, bf16[12,128,128]{2,1,0:T(8,128)(2,1)S(1)}, u32[]{:S(2)}, u32[]{:S(2)}) collective-permute-start(bf16[12,128,128]{2,1,0:T(8,128)(2,1)S(1)} %get-tuple-element.32.refs_0_), channel_id=1, source_target_pairs={{0,3},{1,2},{2,1},{3,0},{4,7},{5,6},{6,5},{7,4},{8,11},{9,10},{10,... | collective-permute-start | bytes 1179656 | tf_op jit(solution)/shard_map/ppermute | solution.py:381
  39.0 1.9 %collective-permute-start.1 = (bf16[12,128,128]{2,1,0:T(8,128)(2,1)S(1)}, bf16[12,128,128]{2,1,0:T(8,128)(2,1)S(1)}, u32[]{:S(2)}, u32[]{:S(2)}) collective-permute-start(bf16[12,128,128]{2,1,0:T(8,128)(2,1)S(1)} %get-tuple-element.32.refs_0_), channel_id=1, source_target_pairs={{0,2},{1,3},{2,0},{3,1},{4,6},{5,7},{6,4},{7,5},{8,10},{9,11},{10,... | collective-permute-start | bytes 1179656 | tf_op jit(solution)/shard_map/ppermute | solution.py:381
  40.9 3.9 %collective-permute-start = (bf16[12,128,128]{2,1,0:T(8,128)(2,1)S(1)}, bf16[12,128,128]{2,1,0:T(8,128)(2,1)S(1)}, u32[]{:S(2)}, u32[]{:S(2)}) collective-permute-start(bf16[12,128,128]{2,1,0:T(8,128)(2,1)S(1)} %get-tuple-element.32.refs_0_), channel_id=1, source_target_pairs={{0,1},{1,0},{2,3},{3,2},{4,5},{5,4},{6,7},{7,6},{8,9},{9,8},{10,11... | collective-permute-start | bytes 1179656 | tf_op jit(solution)/shard_map/ppermute | solution.py:381
  44.9 5.2 %all-to-all-done.1.in_ref = bf16[16,48,128]{2,1,0:T(8,128)(2,1)S(1)} async-done(((bf16[16,48,128]{2,1,0:T(8,128)(2,1)}), bf16[16,48,128]{2,1,0:T(8,128)(2,1)S(1)}, u32[]{:S(2)}, u32[]{:S(2)}) %all-to-all-start.1) | async-done | bytes 196640 | tf_op jit(solution)/shard_map/all_to_all | solution.py:446
  50.0 0.7 shard_map.125
  50.8 6.9 %all-to-all-start.2 = ((bf16[16,24,128]{2,1,0:T(8,128)(2,1)}), bf16[16,24,128]{2,1,0:T(8,128)(2,1)S(1)}, u32[]{:S(2)}, u32[]{:S(2)}) async-start(bf16[16,24,128]{2,1,0:T(8,128)(2,1)} %get-tuple-element.30), calls=%async_computation.2 | async-start | bytes 196608 | tf_op jit(solution)/shard_map/all_to_all | solution.py:449
  57.6 4.0 %collective-permute-start.3 = (bf16[19,128,128]{2,1,0:T(8,128)(2,1)}, bf16[19,128,128]{2,1,0:T(8,128)(2,1)S(1)}, u32[]{:S(2)}, u32[]{:S(2)}) collective-permute-start(bf16[19,128,128]{2,1,0:T(8,128)(2,1)} %copy-done.7), channel_id=1, source_target_pairs={{0,2},{1,3},{2,0},{3,1},{4,6},{5,7},{6,4},{7,5},{8,10},{9,11},{10,... | collective-permute-start | bytes 1867784 | tf_op jit(solution)/shard_map/ppermute | solution.py:381
  61.6 0.1 add.107
  61.7 0.1 copy.20
  61.8 0.1 gt.11
  61.9 0.1 add_select_fusion
  62.1 8.7 %all-to-all-done.2 = bf16[16,24,128]{2,1,0:T(8,128)(2,1)S(1)} async-done(((bf16[16,24,128]{2,1,0:T(8,128)(2,1)}), bf16[16,24,128]{2,1,0:T(8,128)(2,1)S(1)}, u32[]{:S(2)}, u32[]{:S(2)}) %all-to-all-start.2) | async-done | bytes 98336 | tf_op jit(solution)/shard_map/all_to_all | solution.py:449
  70.8 0.1 broadcast_in_dim.50.rowpos_ref
  70.9 3.1 %shard_map.126 = bf16[16,32,128]{2,1,0:T(8,128)(2,1)} custom-call(bf16[384,128]{1,0:T(8,128)(2,1)S(1)} %bitcast.9, s32[25,128]{1,0:T(8,128)S(1)} %pad_add_fusion.keypos_ref, s32[3,16,128]{2,1,0:T(8,128)S(1)} %broadcast_in_dim.50.rowpos_ref, bf16[2,16,128]{2,1,0:T(8,128)(2,1)S(1)} %get-tuple-element.31.new_ref, ...), custom_call_target="tpu_custom_call" | custom-call | tf_op jit(solution)/shard_map/pallas_call | solution.py:43
  73.9 3.5 %all-to-all-start.3 = ((bf16[16,32,128]{2,1,0:T(8,128)(2,1)}), bf16[16,32,128]{2,1,0:T(8,128)(2,1)S(1)}, u32[]{:S(2)}, u32[]{:S(2)}) async-start(bf16[16,32,128]{2,1,0:T(8,128)(2,1)} %shard_map.126), calls=%async_computation.3 | async-start | bytes 262144 | tf_op jit(solution)/shard_map/all_to_all | solution.py:460
  77.5 2.6 %collective-permute-start.4 = (bf16[19,128,128]{2,1,0:T(8,128)(2,1)}, bf16[19,128,128]{2,1,0:T(8,128)(2,1)S(1)}, u32[]{:S(2)}, u32[]{:S(2)}) collective-permute-start(bf16[19,128,128]{2,1,0:T(8,128)(2,1)} %copy-done.6), channel_id=1, source_target_pairs={{0,1},{1,0},{2,3},{3,2},{4,5},{5,4},{6,7},{7,6},{8,9},{9,8},{10,11... | collective-permute-start | bytes 1867784 | tf_op jit(solution)/shard_map/ppermute | solution.py:381
  80.0 3.9 %collective-permute-start.5 = (bf16[19,128,128]{2,1,0:T(8,128)(2,1)}, bf16[19,128,128]{2,1,0:T(8,128)(2,1)S(1)}, u32[]{:S(2)}, u32[]{:S(2)}) collective-permute-start(bf16[19,128,128]{2,1,0:T(8,128)(2,1)} %copy-done.5), channel_id=1, source_target_pairs={{0,3},{1,2},{2,1},{3,0},{4,7},{5,6},{6,5},{7,4},{8,11},{9,10},{10,... | collective-permute-start | bytes 1867784 | tf_op jit(solution)/shard_map/ppermute | solution.py:381
  83.9 6.5 %all-to-all-done.3.in_ref = bf16[16,32,128]{2,1,0:T(8,128)(2,1)S(1)} async-done(((bf16[16,32,128]{2,1,0:T(8,128)(2,1)}), bf16[16,32,128]{2,1,0:T(8,128)(2,1)S(1)}, u32[]{:S(2)}, u32[]{:S(2)}) %all-to-all-start.3) | async-done | bytes 131104 | tf_op jit(solution)/shard_map/all_to_all | solution.py:460
  90.5 0.3 shard_map.127
  90.7 18.3 %all_to_all.35 = bf16[16,24,128]{2,1,0:T(8,128)(2,1)S(1)} all-to-all(bf16[16,24,128]{2,1,0:T(8,128)(2,1)S(1)} %shard_map.127), channel_id=1, replica_groups=mesh['y'=4,'core'=2,'z'=16,'x'=4] {'z'}, dimensions={0} | all-to-all | bytes 196608 | tf_op jit(solution)/shard_map/all_to_all | solution.py:462
  109.0 0.3 shard_map.128
  109.3 12.6 %all_to_all.36.terms_ref = bf16[8,48,512]{2,1,0:T(8,128)(2,1)S(1)} all-to-all(bf16[8,48,512]{2,1,0:T(8,128)(2,1)S(1)} %shard_map.128), channel_id=1, replica_groups=mesh['y'=4,'core'=2,'z'=16,'x'=4] {'core','y'}, dimensions={0} | all-to-all | bytes 786432 | tf_op jit(solution)/shard_map/all_to_all | solution.py:469
  121.9 1.1 shard_map.129
  123.1 3.5 %all-to-all-start.6 = ((bf16[16,32,128]{2,1,0:T(8,128)(2,1)}), bf16[16,32,128]{2,1,0:T(8,128)(2,1)S(1)}, u32[]{:S(2)}, u32[]{:S(2)}) async-start(bf16[16,32,128]{2,1,0:T(8,128)(2,1)} %get-tuple-element.44), calls=%async_computation.6 | async-start | bytes 262144 | tf_op jit(solution)/shard_map/all_to_all | solution.py:474
  126.6 2.8 %collective-permute-start.6 = (bf16[48,128]{1,0:T(8,128)(2,1)S(1)}, bf16[48,128]{1,0:T(8,128)(2,1)S(1)}, u32[]{:S(2)}, u32[]{:S(2)}) collective-permute-start(bf16[48,128]{1,0:T(8,128)(2,1)S(1)} %get-tuple-element.41), channel_id=1, source_target_pairs={{0,1},{1,0},{2,3},{3,2},{4,5},{5,4},{6,7},{7,6},{8,9},{9,8},{10,11... | collective-permute-start | bytes 36872 | tf_op jit(solution)/shard_map/ppermute | solution.py:381
  129.4 3.8 %collective-permute-start.7 = (bf16[48,128]{1,0:T(8,128)(2,1)S(1)}, bf16[48,128]{1,0:T(8,128)(2,1)S(1)}, u32[]{:S(2)}, u32[]{:S(2)}) collective-permute-start(bf16[48,128]{1,0:T(8,128)(2,1)S(1)} %get-tuple-element.42), channel_id=1, source_target_pairs={{0,2},{1,3},{2,0},{3,1},{4,6},{5,7},{6,4},{7,5},{8,10},{9,11},{10,... | collective-permute-start | bytes 36872 | tf_op jit(solution)/shard_map/ppermute | solution.py:381
  133.2 3.8 %collective-permute-start.8 = (bf16[48,128]{1,0:T(8,128)(2,1)S(1)}, bf16[48,128]{1,0:T(8,128)(2,1)S(1)}, u32[]{:S(2)}, u32[]{:S(2)}) collective-permute-start(bf16[48,128]{1,0:T(8,128)(2,1)S(1)} %get-tuple-element.43), channel_id=1, source_target_pairs={{0,3},{1,2},{2,1},{3,0},{4,7},{5,6},{6,5},{7,4},{8,11},{9,10},{10,... | collective-permute-start | bytes 36872 | tf_op jit(solution)/shard_map/ppermute | solution.py:381
  137.0 3.5 %all-to-all-done.6.in_ref = bf16[16,32,128]{2,1,0:T(8,128)(2,1)S(1)} async-done(((bf16[16,32,128]{2,1,0:T(8,128)(2,1)}), bf16[16,32,128]{2,1,0:T(8,128)(2,1)S(1)}, u32[]{:S(2)}, u32[]{:S(2)}) %all-to-all-start.6) | async-done | bytes 131104 | tf_op jit(solution)/shard_map/all_to_all | solution.py:474
  140.6 0.8 shard_map.130
  141.3 0.8 shard_map.131
  (36 shorter events, 0.2 us)
Async XLA Ops:
  2.9 9.6 %copy-start.11 = (s32[128]{0:T(128)S(1)}, s32[128]{0:T(128)}, u32[]{:S(2)}) copy-start(s32[128]{0:T(128)} %param.18) | copy-start | bytes 1540
  2.9 9.6 %copy-start.9 = (s32[128]{0:T(128)S(1)}, s32[128]{0:T(128)}, u32[]{:S(2)}) copy-start(s32[128]{0:T(128)} %param.19) | copy-start | bytes 1540
  2.9 9.9 %copy-start.10 = (s32[128]{0:T(128)S(1)}, s32[128]{0:T(128)}, u32[]{:S(2)}) copy-start(s32[128]{0:T(128)} %param.20) | copy-start | bytes 1540
  3.0 10.4 %copy-start.8 = (s32[192]{0:T(256)S(1)}, s32[192]{0:T(256)}, u32[]{:S(2)}) copy-start(s32[192]{0:T(256)} %param.21) | copy-start | bytes 2308
  3.0 11.4 %copy-start = (bf16[128,1280]{1,0:T(8,128)(2,1)S(1)}, bf16[128,1280]{1,0:T(8,128)(2,1)}, u32[]{:S(2)}) copy-start(bf16[128,1280]{1,0:T(8,128)(2,1)} %next_weight_ref.1) | copy-start | bytes 983044
  3.0 11.4 %copy-start.1 = (bf16[1024,128]{1,0:T(8,128)(2,1)S(1)}, bf16[1024,128]{1,0:T(8,128)(2,1)}, u32[]{:S(2)}) copy-start(bf16[1024,128]{1,0:T(8,128)(2,1)} %out_weight_ref.1) | copy-start | bytes 786436
  3.0 11.4 %copy-start.2 = (bf16[768,128]{1,0:T(8,128)(2,1)S(1)}, bf16[768,128]{1,0:T(8,128)(2,1)}, u32[]{:S(2)}) copy-start(bf16[768,128]{1,0:T(8,128)(2,1)} %keys_ref.1) | copy-start | bytes 589828
  3.0 11.4 %copy-start.3 = (bf16[768,128]{1,0:T(8,128)(2,1)S(1)}, bf16[768,128]{1,0:T(8,128)(2,1)}, u32[]{:S(2)}) copy-start(bf16[768,128]{1,0:T(8,128)(2,1)} %values_ref.1) | copy-start | bytes 589828
  3.0 11.4 %copy-start.4 = (bf16[4,128,128]{2,1,0:T(8,128)(2,1)S(1)}, bf16[4,128,128]{2,1,0:T(8,128)(2,1)}, u32[]{:S(2)}) copy-start(bf16[4,128,128]{2,1,0:T(8,128)(2,1)} %get-tuple-element.27.hidden_ref) | copy-start | bytes 393220
  3.0 16.9 %all-to-all-start = ((bf16[4,48,16,128]{3,2,1,0:T(8,128)(2,1)}), bf16[4,48,16,128]{3,2,1,0:T(8,128)(2,1)S(1)}, u32[]{:S(2)}, u32[]{:S(2)}) async-start(bf16[4,48,16,128]{3,2,1,0:T(8,128)(2,1)} %get-tuple-element.26), calls=%async_computation | async-start | bytes 1572864 | tf_op jit(solution)/shard_map/all_to_all | solution.py:399
  14.9 0.8 copy-start.5
  15.8 0.8 copy-start.6
  16.6 0.8 copy-start.7
  20.8 29.2 %all-to-all-start.1 = ((bf16[16,48,128]{2,1,0:T(8,128)(2,1)}), bf16[16,48,128]{2,1,0:T(8,128)(2,1)S(1)}, u32[]{:S(2)}, u32[]{:S(2)}) async-start(bf16[16,48,128]{2,1,0:T(8,128)(2,1)} %shard_map.123), calls=%async_computation.1 | async-start | bytes 393216 | tf_op jit(solution)/shard_map/all_to_all | solution.py:446
  35.0 27.0 %collective-permute-start.2 = (bf16[12,128,128]{2,1,0:T(8,128)(2,1)S(1)}, bf16[12,128,128]{2,1,0:T(8,128)(2,1)S(1)}, u32[]{:S(2)}, u32[]{:S(2)}) collective-permute-start(bf16[12,128,128]{2,1,0:T(8,128)(2,1)S(1)} %get-tuple-element.32.refs_0_), channel_id=1, source_target_pairs={{0,3},{1,2},{2,1},{3,0},{4,7},{5,6},{6,5},{7,4},{8,11},{9,10},{10,... | collective-permute-start | bytes 1179656 | tf_op jit(solution)/shard_map/ppermute | solution.py:381
  39.0 23.1 %collective-permute-start.1 = (bf16[12,128,128]{2,1,0:T(8,128)(2,1)S(1)}, bf16[12,128,128]{2,1,0:T(8,128)(2,1)S(1)}, u32[]{:S(2)}, u32[]{:S(2)}) collective-permute-start(bf16[12,128,128]{2,1,0:T(8,128)(2,1)S(1)} %get-tuple-element.32.refs_0_), channel_id=1, source_target_pairs={{0,2},{1,3},{2,0},{3,1},{4,6},{5,7},{6,4},{7,5},{8,10},{9,11},{10,... | collective-permute-start | bytes 1179656 | tf_op jit(solution)/shard_map/ppermute | solution.py:381
  40.9 21.1 %collective-permute-start = (bf16[12,128,128]{2,1,0:T(8,128)(2,1)S(1)}, bf16[12,128,128]{2,1,0:T(8,128)(2,1)S(1)}, u32[]{:S(2)}, u32[]{:S(2)}) collective-permute-start(bf16[12,128,128]{2,1,0:T(8,128)(2,1)S(1)} %get-tuple-element.32.refs_0_), channel_id=1, source_target_pairs={{0,1},{1,0},{2,3},{3,2},{4,5},{5,4},{6,7},{7,6},{8,9},{9,8},{10,11... | collective-permute-start | bytes 1179656 | tf_op jit(solution)/shard_map/ppermute | solution.py:381
  50.8 20.0 %all-to-all-start.2 = ((bf16[16,24,128]{2,1,0:T(8,128)(2,1)}), bf16[16,24,128]{2,1,0:T(8,128)(2,1)S(1)}, u32[]{:S(2)}, u32[]{:S(2)}) async-start(bf16[16,24,128]{2,1,0:T(8,128)(2,1)} %get-tuple-element.30), calls=%async_computation.2 | async-start | bytes 196608 | tf_op jit(solution)/shard_map/all_to_all | solution.py:449
  57.6 19.8 %collective-permute-start.3 = (bf16[19,128,128]{2,1,0:T(8,128)(2,1)}, bf16[19,128,128]{2,1,0:T(8,128)(2,1)S(1)}, u32[]{:S(2)}, u32[]{:S(2)}) collective-permute-start(bf16[19,128,128]{2,1,0:T(8,128)(2,1)} %copy-done.7), channel_id=1, source_target_pairs={{0,2},{1,3},{2,0},{3,1},{4,6},{5,7},{6,4},{7,5},{8,10},{9,11},{10,... | collective-permute-start | bytes 1867784 | tf_op jit(solution)/shard_map/ppermute | solution.py:381
  73.9 16.5 %all-to-all-start.3 = ((bf16[16,32,128]{2,1,0:T(8,128)(2,1)}), bf16[16,32,128]{2,1,0:T(8,128)(2,1)S(1)}, u32[]{:S(2)}, u32[]{:S(2)}) async-start(bf16[16,32,128]{2,1,0:T(8,128)(2,1)} %shard_map.126), calls=%async_computation.3 | async-start | bytes 262144 | tf_op jit(solution)/shard_map/all_to_all | solution.py:460
  77.5 31.5 %collective-permute-start.4 = (bf16[19,128,128]{2,1,0:T(8,128)(2,1)}, bf16[19,128,128]{2,1,0:T(8,128)(2,1)S(1)}, u32[]{:S(2)}, u32[]{:S(2)}) collective-permute-start(bf16[19,128,128]{2,1,0:T(8,128)(2,1)} %copy-done.6), channel_id=1, source_target_pairs={{0,1},{1,0},{2,3},{3,2},{4,5},{5,4},{6,7},{7,6},{8,9},{9,8},{10,11... | collective-permute-start | bytes 1867784 | tf_op jit(solution)/shard_map/ppermute | solution.py:381
  80.0 29.0 %collective-permute-start.5 = (bf16[19,128,128]{2,1,0:T(8,128)(2,1)}, bf16[19,128,128]{2,1,0:T(8,128)(2,1)S(1)}, u32[]{:S(2)}, u32[]{:S(2)}) collective-permute-start(bf16[19,128,128]{2,1,0:T(8,128)(2,1)} %copy-done.5), channel_id=1, source_target_pairs={{0,3},{1,2},{2,1},{3,0},{4,7},{5,6},{6,5},{7,4},{8,11},{9,10},{10,... | collective-permute-start | bytes 1867784 | tf_op jit(solution)/shard_map/ppermute | solution.py:381
  123.1 17.5 %all-to-all-start.6 = ((bf16[16,32,128]{2,1,0:T(8,128)(2,1)}), bf16[16,32,128]{2,1,0:T(8,128)(2,1)S(1)}, u32[]{:S(2)}, u32[]{:S(2)}) async-start(bf16[16,32,128]{2,1,0:T(8,128)(2,1)} %get-tuple-element.44), calls=%async_computation.6 | async-start | bytes 262144 | tf_op jit(solution)/shard_map/all_to_all | solution.py:474
  126.6 14.7 %collective-permute-start.6 = (bf16[48,128]{1,0:T(8,128)(2,1)S(1)}, bf16[48,128]{1,0:T(8,128)(2,1)S(1)}, u32[]{:S(2)}, u32[]{:S(2)}) collective-permute-start(bf16[48,128]{1,0:T(8,128)(2,1)S(1)} %get-tuple-element.41), channel_id=1, source_target_pairs={{0,1},{1,0},{2,3},{3,2},{4,5},{5,4},{6,7},{7,6},{8,9},{9,8},{10,11... | collective-permute-start | bytes 36872 | tf_op jit(solution)/shard_map/ppermute | solution.py:381
  129.4 12.0 %collective-permute-start.7 = (bf16[48,128]{1,0:T(8,128)(2,1)S(1)}, bf16[48,128]{1,0:T(8,128)(2,1)S(1)}, u32[]{:S(2)}, u32[]{:S(2)}) collective-permute-start(bf16[48,128]{1,0:T(8,128)(2,1)S(1)} %get-tuple-element.42), channel_id=1, source_target_pairs={{0,2},{1,3},{2,0},{3,1},{4,6},{5,7},{6,4},{7,5},{8,10},{9,11},{10,... | collective-permute-start | bytes 36872 | tf_op jit(solution)/shard_map/ppermute | solution.py:381
  133.2 8.1 %collective-permute-start.8 = (bf16[48,128]{1,0:T(8,128)(2,1)S(1)}, bf16[48,128]{1,0:T(8,128)(2,1)S(1)}, u32[]{:S(2)}, u32[]{:S(2)}) collective-permute-start(bf16[48,128]{1,0:T(8,128)(2,1)S(1)} %get-tuple-element.43), channel_id=1, source_target_pairs={{0,3},{1,2},{2,1},{3,0},{4,7},{5,6},{6,5},{7,4},{8,11},{9,10},{10,... | collective-permute-start | bytes 36872 | tf_op jit(solution)/shard_map/ppermute | solution.py:381

commit v10 on v9

--- a/solution.py
+++ b/solution.py
@@ -118,20 +118,23 @@
     gain = jnp.where(
         sub == 0, high, jnp.where(sub == 1, middle, jnp.where(sub == 2, low, 0.0))
     ).astype(bf16)
+    rest = jnp.zeros((HD - XR - TILE, HD), bf16)
+    for x in range(NX):
+        rows_ref[x] = jnp.concatenate([moved[x * XR : (x + 1) * XR, :], gain, rest], axis=0)
     copies[2].wait()
-    for x in range(NX):
-        part = moved[x * XR : (x + 1) * XR, :]
-        product = jnp.dot(part, weight_ref[...], preferred_element_type=f32).astype(bf16)
-        for i in range(RI):
-            band = product[i * TILE : (i + 1) * TILE, :]
-            for j in range(GQ):
-                out_ref[x, i * GQ + j] = band[:, j * HD : (j + 1) * HD]
-            for j in range(2):
-                tile = band[:, (GQ + j) * HD : (GQ + j + 1) * HD]
-                for to in range(NX):
-                    out_ref[to, QT + j * NX * RI + x * RI + i] = tile
-        rest = jnp.zeros((HD - XR - TILE, HD), bf16)
-        rows_ref[x] = jnp.concatenate([part, gain, rest], axis=0)
+    for first in range(0, GQ + 2, 2):
+        columns = weight_ref[:, first * HD : (first + 2) * HD]
+        product = jnp.dot(moved, columns, preferred_element_type=f32).astype(bf16)
+        for j in range(first, first + 2):
+            strip = product[:, (j - first) * HD : (j - first + 1) * HD]
+            for x in range(NX):
+                for i in range(RI):
+                    tile = strip[x * XR + i * TILE : x * XR + (i + 1) * TILE, :]
+                    if j < GQ:
+                        out_ref[x, i * GQ + j] = tile
+                    else:
+                        for to in range(NX):
+                            out_ref[to, QT + (j - GQ) * NX * RI + x * RI + i] = tile
 
 
 def sum_x_kernel(in_ref, tiles_ref, cut_ref):
@@ -335,7 +338,7 @@
     ).astype(bf16)
 
 
-def key_layout(owners, group_lengths, group_owner, group_start, listed_rows, blocks):
+def key_layout(owners, group_lengths, group_owner, group_start, blocks):
     length = group_lengths // BLK
     holder = (group_owner[None, :] == owners[:, None]).astype(jnp.int32)
     count = group_owner.shape[0]
@@ -352,10 +355,13 @@
     shift = jnp.sum(member * start, axis=2)
     begin = jnp.sum(member * (start + (ids - offset[:, None, :]) * BLK), axis=2)
     live = jnp.sum(member, axis=2) > 0
+    return shift, begin, live
+
+
+def key_positions(begin, live, listed_rows):
     position = begin[:, :, None] + jnp.arange(BLK, dtype=jnp.int32)
     hit = jnp.any(position[..., None] == listed_rows, axis=-1)
-    position = jnp.where(live[:, :, None] & ~hit, position, never)
-    return shift, position.reshape(NX * blocks, BLK)
+    return jnp.where(live[:, :, None] & ~hit, position, never).reshape(-1, BLK)
 
 
 def on_device(
@@ -399,8 +405,8 @@
     payload = a2a(payload, "x")
 
     sources = x ^ jnp.arange(NX, dtype=jnp.int32)
-    shift, key_pos = key_layout(
-        z * NX + sources, group_lengths, group_owner, group_start, listed_rows, blocks
+    shift, begin, live = key_layout(
+        z * NX + sources, group_lengths, group_owner, group_start, blocks
     )
     by_zxi = listed_rows.reshape(NZ, NX, RI)
     row_pos = lax.dynamic_slice_in_dim(by_zxi, x, 1, axis=1)[:, 0].T
@@ -409,7 +415,6 @@
     chosen = (own // HD * NZ + own % NZ)[:, None] == jnp.arange(XR)[None, :]
     query_pos = jnp.sum(jnp.where(chosen, row_pos.reshape(1, XR), 0), axis=1)
     rest = jnp.full((BLK - NX * RI,), never, jnp.int32)
-    key_pos = jnp.concatenate([key_pos, jnp.concatenate([new_pos, rest])[None]], axis=0)
     wide_row_pos = jnp.broadcast_to(row_pos[:, :, None], (RI, NZ, BLK))
     cosine, sine = rope_factors(
         jnp.concatenate([query_pos, new_pos, jnp.zeros((NX * RI,), jnp.int32), shift[0]])
@@ -447,6 +452,8 @@
     )
     weights_x = {0: bundles[0], 2: swapped(after(bundles[2], copies), 2)}
     queries = a2a(copies, "z").reshape(XR * GQ, HD)
+    key_pos = key_positions(begin, live, after(listed_rows, copies))
+    key_pos = jnp.concatenate([key_pos, jnp.concatenate([new_pos, rest])[None]], axis=0)
     parts = vmem_call(
         attend_kernel,
         shaped((NZ, 32, HD), bf16),

time: 144 us -> 144 us (level)
  no operation moved by 1% of the time
where the time goes in v10:
time: 144 us; the launch traced here: 142 us
  starting transfers between devices  67.2 us (47%)
  blocking collectives  30.7 us (21%)
  waiting for transfers between devices  26.6 us (18%)
  Pallas kernels  10.8 us (8%)
  local copies, waits for them, and re-layouts  3.55 us (2%)
  other arithmetic  2.01 us (1%)
    ppermute x9, starting transfers between devices, swapped(): return lax.ppermute(array, 'x', [(n, n ^ step) for n in range(NX)])  30.7 us
    all_to_all x1, blocking collectives, on_device(): heads_out = a2a(share, 'z').reshape(XR * GQ, HD)  18.1 us
    all_to_all x1, starting transfers between devices, on_device(): a2a(tiles, 'z')  13.5 us
    all_to_all x1, blocking collectives, on_device(): a2a(terms, ('core', 'y'))  12.6 us
    pallas_call x10, Pallas kernels, vmem_call(): pl.pallas_call(kernel, out_shape=out_shape, in_specs=[small] * scalars +...  10.8 us
    all_to_all x1, starting transfers between devices, on_device(): payload = a2a(payload, 'x')  9.46 us
    all_to_all x1, waiting for transfers between devices, on_device(): queries = a2a(copies, 'z').reshape(XR * GQ, HD)  8.51 us
    all_to_all x1, waiting for transfers between devices, on_device(): a2a(parts, 'z')  6.68 us
  transfers between devices with their start and end apart: 14, of which 5 were waited for; matrix products, arithmetic and copies ran while one was open for 2% of the time, Pallas kernels for 4%

profile of v10, /device:TPU:6, one launch (start us, length us, event | category | flops | bytes accessed | tf_op | source)
XLA Modules:
  0.0 141.9 jit_solution(17002546179968052585)
XLA Ops:
  0.6 2.2 %shard_map.122 = (bf16[4,48,16,128]{3,2,1,0:T(8,128)(2,1)}, bf16[4,128,128]{2,1,0:T(8,128)(2,1)}) custom-call(bf16[192,128]{1,0:T(8,128)(2,1)} %hidden_hbm.1, bf16[128,1280]{1,0:T(8,128)(2,1)} %weight_hbm.1, f32[1,128]{1,0:T(1,128)} %bitcast.13), custom_call_target="tpu_custom_call" | custom-call | tf_op jit(solution)/shard_map/pallas_call | solution.py:43
  2.9 0.0 copy-start.11
  2.9 0.0 copy-start.9
  2.9 0.0 copy-start.10
  2.9 0.0 copy-start.8
  2.9 0.0 copy-start
  2.9 0.0 copy-start.1
  3.0 0.0 copy-start.2
  3.0 0.0 copy-start.3
  3.0 9.5 %all-to-all-start = ((bf16[4,48,16,128]{3,2,1,0:T(8,128)(2,1)}), bf16[4,48,16,128]{3,2,1,0:T(8,128)(2,1)S(1)}, u32[]{:S(2)}, u32[]{:S(2)}) async-start(bf16[4,48,16,128]{3,2,1,0:T(8,128)(2,1)} %get-tuple-element.27), calls=%async_computation | async-start | bytes 1572864 | tf_op jit(solution)/shard_map/all_to_all | solution.py:405
  12.5 0.1 fusion.3
  12.6 0.1 compare_select_fusion
  12.7 0.1 select_reduce_fusion
  12.8 0.4 select_reduce_fusion.1
  13.2 0.1 slice_reduce_fusion
  13.4 0.2 reshape.203
  13.6 0.1 copy.19
  13.7 0.1 concatenate.25
  13.7 0.1 broadcast_in_dim.41
  13.8 0.2 select_reduce_fusion.3
  14.0 0.1 add_convert_fusion
  14.1 0.2 fusion.2
  14.3 0.1 pad_maximum_fusion.2
  14.4 0.5 shard_map.124
  14.9 0.8 copy-done.5
  15.7 0.8 copy-done.6
  16.6 0.8 copy-done.7
  17.4 2.5 %all-to-all-done.in_ref = bf16[4,48,16,128]{3,2,1,0:T(8,128)(2,1)S(1)} async-done(((bf16[4,48,16,128]{3,2,1,0:T(8,128)(2,1)}), bf16[4,48,16,128]{3,2,1,0:T(8,128)(2,1)S(1)}, u32[]{:S(2)}, u32[]{:S(2)}) %all-to-all-start) | async-done | bytes 786464 | tf_op jit(solution)/shard_map/all_to_all | solution.py:405
  19.9 0.9 shard_map.123
  20.7 13.5 %all-to-all-start.1 = ((bf16[16,48,128]{2,1,0:T(8,128)(2,1)}), bf16[16,48,128]{2,1,0:T(8,128)(2,1)S(1)}, u32[]{:S(2)}, u32[]{:S(2)}) async-start(bf16[16,48,128]{2,1,0:T(8,128)(2,1)} %shard_map.123), calls=%async_computation.1 | async-start | bytes 393216 | tf_op jit(solution)/shard_map/all_to_all | solution.py:451
  34.2 0.1 copy.21
  34.3 0.1 add.107
  34.4 0.1 copy.20
  34.5 0.1 gt.11
  34.6 0.1 pad_maximum_fusion
  34.7 0.1 iota_add_fusion
  34.7 4.0 %collective-permute-start.2 = (bf16[12,128,128]{2,1,0:T(8,128)(2,1)S(1)}, bf16[12,128,128]{2,1,0:T(8,128)(2,1)S(1)}, u32[]{:S(2)}, u32[]{:S(2)}) collective-permute-start(bf16[12,128,128]{2,1,0:T(8,128)(2,1)S(1)} %get-tuple-element.34.refs_0_), channel_id=1, source_target_pairs={{0,3},{1,2},{2,1},{3,0},{4,7},{5,6},{6,5},{7,4},{8,11},{9,10},{10,... | collective-permute-start | bytes 1179656 | tf_op jit(solution)/shard_map/ppermute | solution.py:387
  38.7 1.9 %collective-permute-start.1 = (bf16[12,128,128]{2,1,0:T(8,128)(2,1)S(1)}, bf16[12,128,128]{2,1,0:T(8,128)(2,1)S(1)}, u32[]{:S(2)}, u32[]{:S(2)}) collective-permute-start(bf16[12,128,128]{2,1,0:T(8,128)(2,1)S(1)} %get-tuple-element.34.refs_0_), channel_id=1, source_target_pairs={{0,2},{1,3},{2,0},{3,1},{4,6},{5,7},{6,4},{7,5},{8,10},{9,11},{10,... | collective-permute-start | bytes 1179656 | tf_op jit(solution)/shard_map/ppermute | solution.py:387
  40.7 3.9 %collective-permute-start = (bf16[12,128,128]{2,1,0:T(8,128)(2,1)S(1)}, bf16[12,128,128]{2,1,0:T(8,128)(2,1)S(1)}, u32[]{:S(2)}, u32[]{:S(2)}) collective-permute-start(bf16[12,128,128]{2,1,0:T(8,128)(2,1)S(1)} %get-tuple-element.34.refs_0_), channel_id=1, source_target_pairs={{0,1},{1,0},{2,3},{3,2},{4,5},{5,4},{6,7},{7,6},{8,9},{9,8},{10,11... | collective-permute-start | bytes 1179656 | tf_op jit(solution)/shard_map/ppermute | solution.py:387
  44.6 5.4 %all-to-all-done.1.in_ref = bf16[16,48,128]{2,1,0:T(8,128)(2,1)S(1)} async-done(((bf16[16,48,128]{2,1,0:T(8,128)(2,1)}), bf16[16,48,128]{2,1,0:T(8,128)(2,1)S(1)}, u32[]{:S(2)}, u32[]{:S(2)}) %all-to-all-start.1) | async-done | bytes 196640 | tf_op jit(solution)/shard_map/all_to_all | solution.py:451
  50.0 0.7 shard_map.125
  50.7 6.6 %all-to-all-start.2 = ((bf16[16,24,128]{2,1,0:T(8,128)(2,1)}), bf16[16,24,128]{2,1,0:T(8,128)(2,1)S(1)}, u32[]{:S(2)}, u32[]{:S(2)}) async-start(bf16[16,24,128]{2,1,0:T(8,128)(2,1)} %get-tuple-element.31), calls=%async_computation.2 | async-start | bytes 196608 | tf_op jit(solution)/shard_map/all_to_all | solution.py:454
  57.4 4.0 %collective-permute-start.3 = (bf16[19,128,128]{2,1,0:T(8,128)(2,1)}, bf16[19,128,128]{2,1,0:T(8,128)(2,1)S(1)}, u32[]{:S(2)}, u32[]{:S(2)}) collective-permute-start(bf16[19,128,128]{2,1,0:T(8,128)(2,1)} %copy-done.7), channel_id=1, source_target_pairs={{0,2},{1,3},{2,0},{3,1},{4,6},{5,7},{6,4},{7,5},{8,10},{9,11},{10,... | collective-permute-start | bytes 1867784 | tf_op jit(solution)/shard_map/ppermute | solution.py:387
  61.4 0.5 compare_reduce_fusion
  61.9 0.1 add_select_fusion
  62.0 8.5 %all-to-all-done.2 = bf16[16,24,128]{2,1,0:T(8,128)(2,1)S(1)} async-done(((bf16[16,24,128]{2,1,0:T(8,128)(2,1)}), bf16[16,24,128]{2,1,0:T(8,128)(2,1)S(1)}, u32[]{:S(2)}, u32[]{:S(2)}) %all-to-all-start.2) | async-done | bytes 98336 | tf_op jit(solution)/shard_map/all_to_all | solution.py:454
  70.5 0.1 broadcast_in_dim.49.rowpos_ref
  70.6 3.1 %shard_map.126 = bf16[16,32,128]{2,1,0:T(8,128)(2,1)} custom-call(bf16[384,128]{1,0:T(8,128)(2,1)S(1)} %bitcast.9, s32[25,128]{1,0:T(8,128)S(1)} %pad_add_fusion.keypos_ref, s32[3,16,128]{2,1,0:T(8,128)S(1)} %broadcast_in_dim.49.rowpos_ref, bf16[2,16,128]{2,1,0:T(8,128)(2,1)S(1)} %get-tuple-element.33.new_ref, ...), custom_call_target="tpu_custom_call" | custom-call | tf_op jit(solution)/shard_map/pallas_call | solution.py:43
  73.7 3.5 %all-to-all-start.3 = ((bf16[16,32,128]{2,1,0:T(8,128)(2,1)}), bf16[16,32,128]{2,1,0:T(8,128)(2,1)S(1)}, u32[]{:S(2)}, u32[]{:S(2)}) async-start(bf16[16,32,128]{2,1,0:T(8,128)(2,1)} %shard_map.126), calls=%async_computation.3 | async-start | bytes 262144 | tf_op jit(solution)/shard_map/all_to_all | solution.py:467
  77.2 2.8 %collective-permute-start.4 = (bf16[19,128,128]{2,1,0:T(8,128)(2,1)}, bf16[19,128,128]{2,1,0:T(8,128)(2,1)S(1)}, u32[]{:S(2)}, u32[]{:S(2)}) collective-permute-start(bf16[19,128,128]{2,1,0:T(8,128)(2,1)} %copy-done.6), channel_id=1, source_target_pairs={{0,1},{1,0},{2,3},{3,2},{4,5},{5,4},{6,7},{7,6},{8,9},{9,8},{10,11... | collective-permute-start | bytes 1867784 | tf_op jit(solution)/shard_map/ppermute | solution.py:387
  80.0 3.7 %collective-permute-start.5 = (bf16[19,128,128]{2,1,0:T(8,128)(2,1)}, bf16[19,128,128]{2,1,0:T(8,128)(2,1)S(1)}, u32[]{:S(2)}, u32[]{:S(2)}) collective-permute-start(bf16[19,128,128]{2,1,0:T(8,128)(2,1)} %copy-done.5), channel_id=1, source_target_pairs={{0,3},{1,2},{2,1},{3,0},{4,7},{5,6},{6,5},{7,4},{8,11},{9,10},{10,... | collective-permute-start | bytes 1867784 | tf_op jit(solution)/shard_map/ppermute | solution.py:387
  83.7 6.7 %all-to-all-done.3.in_ref = bf16[16,32,128]{2,1,0:T(8,128)(2,1)S(1)} async-done(((bf16[16,32,128]{2,1,0:T(8,128)(2,1)}), bf16[16,32,128]{2,1,0:T(8,128)(2,1)S(1)}, u32[]{:S(2)}, u32[]{:S(2)}) %all-to-all-start.3) | async-done | bytes 131104 | tf_op jit(solution)/shard_map/all_to_all | solution.py:467
  90.3 0.3 shard_map.127
  90.6 18.1 %all_to_all.35 = bf16[16,24,128]{2,1,0:T(8,128)(2,1)S(1)} all-to-all(bf16[16,24,128]{2,1,0:T(8,128)(2,1)S(1)} %shard_map.127), channel_id=1, replica_groups=mesh['y'=4,'core'=2,'z'=16,'x'=4] {'z'}, dimensions={0} | all-to-all | bytes 196608 | tf_op jit(solution)/shard_map/all_to_all | solution.py:469
  108.7 0.3 shard_map.128
  109.0 12.6 %all_to_all.36.terms_ref = bf16[8,48,512]{2,1,0:T(8,128)(2,1)S(1)} all-to-all(bf16[8,48,512]{2,1,0:T(8,128)(2,1)S(1)} %shard_map.128), channel_id=1, replica_groups=mesh['y'=4,'core'=2,'z'=16,'x'=4] {'core','y'}, dimensions={0} | all-to-all | bytes 786432 | tf_op jit(solution)/shard_map/all_to_all | solution.py:476
  121.7 1.1 shard_map.129
  122.8 3.5 %all-to-all-start.6 = ((bf16[16,32,128]{2,1,0:T(8,128)(2,1)}), bf16[16,32,128]{2,1,0:T(8,128)(2,1)S(1)}, u32[]{:S(2)}, u32[]{:S(2)}) async-start(bf16[16,32,128]{2,1,0:T(8,128)(2,1)} %get-tuple-element.46), calls=%async_computation.6 | async-start | bytes 262144 | tf_op jit(solution)/shard_map/all_to_all | solution.py:481
  126.3 2.8 %collective-permute-start.6 = (bf16[48,128]{1,0:T(8,128)(2,1)S(1)}, bf16[48,128]{1,0:T(8,128)(2,1)S(1)}, u32[]{:S(2)}, u32[]{:S(2)}) collective-permute-start(bf16[48,128]{1,0:T(8,128)(2,1)S(1)} %get-tuple-element.43), channel_id=1, source_target_pairs={{0,1},{1,0},{2,3},{3,2},{4,5},{5,4},{6,7},{7,6},{8,9},{9,8},{10,11... | collective-permute-start | bytes 36872 | tf_op jit(solution)/shard_map/ppermute | solution.py:387
  129.1 4.1 %collective-permute-start.7 = (bf16[48,128]{1,0:T(8,128)(2,1)S(1)}, bf16[48,128]{1,0:T(8,128)(2,1)S(1)}, u32[]{:S(2)}, u32[]{:S(2)}) collective-permute-start(bf16[48,128]{1,0:T(8,128)(2,1)S(1)} %get-tuple-element.44), channel_id=1, source_target_pairs={{0,2},{1,3},{2,0},{3,1},{4,6},{5,7},{6,4},{7,5},{8,10},{9,11},{10,... | collective-permute-start | bytes 36872 | tf_op jit(solution)/shard_map/ppermute | solution.py:387
  133.2 3.6 %collective-permute-start.8 = (bf16[48,128]{1,0:T(8,128)(2,1)S(1)}, bf16[48,128]{1,0:T(8,128)(2,1)S(1)}, u32[]{:S(2)}, u32[]{:S(2)}) collective-permute-start(bf16[48,128]{1,0:T(8,128)(2,1)S(1)} %get-tuple-element.45), channel_id=1, source_target_pairs={{0,3},{1,2},{2,1},{3,0},{4,7},{5,6},{6,5},{7,4},{8,11},{9,10},{10,... | collective-permute-start | bytes 36872 | tf_op jit(solution)/shard_map/ppermute | solution.py:387
  136.8 3.5 %all-to-all-done.6.in_ref = bf16[16,32,128]{2,1,0:T(8,128)(2,1)S(1)} async-done(((bf16[16,32,128]{2,1,0:T(8,128)(2,1)}), bf16[16,32,128]{2,1,0:T(8,128)(2,1)S(1)}, u32[]{:S(2)}, u32[]{:S(2)}) %all-to-all-start.6) | async-done | bytes 131104 | tf_op jit(solution)/shard_map/all_to_all | solution.py:481
  140.3 0.8 shard_map.130
  141.1 0.8 shard_map.131
  (36 shorter events, 0.2 us)
Async XLA Ops:
  2.9 9.6 %copy-start.11 = (s32[128]{0:T(128)S(1)}, s32[128]{0:T(128)}, u32[]{:S(2)}) copy-start(s32[128]{0:T(128)} %param.18) | copy-start | bytes 1540
  2.9 9.6 %copy-start.9 = (s32[128]{0:T(128)S(1)}, s32[128]{0:T(128)}, u32[]{:S(2)}) copy-start(s32[128]{0:T(128)} %param.19) | copy-start | bytes 1540
  2.9 9.9 %copy-start.10 = (s32[128]{0:T(128)S(1)}, s32[128]{0:T(128)}, u32[]{:S(2)}) copy-start(s32[128]{0:T(128)} %param.20) | copy-start | bytes 1540
  2.9 10.4 %copy-start.8 = (s32[192]{0:T(256)S(1)}, s32[192]{0:T(256)}, u32[]{:S(2)}) copy-start(s32[192]{0:T(256)} %param.21) | copy-start | bytes 2308
  2.9 11.4 %copy-start = (bf16[128,1280]{1,0:T(8,128)(2,1)S(1)}, bf16[128,1280]{1,0:T(8,128)(2,1)}, u32[]{:S(2)}) copy-start(bf16[128,1280]{1,0:T(8,128)(2,1)} %next_weight_ref.1) | copy-start | bytes 983044
  2.9 11.4 %copy-start.1 = (bf16[1024,128]{1,0:T(8,128)(2,1)S(1)}, bf16[1024,128]{1,0:T(8,128)(2,1)}, u32[]{:S(2)}) copy-start(bf16[1024,128]{1,0:T(8,128)(2,1)} %out_weight_ref.1) | copy-start | bytes 786436
  3.0 11.4 %copy-start.2 = (bf16[768,128]{1,0:T(8,128)(2,1)S(1)}, bf16[768,128]{1,0:T(8,128)(2,1)}, u32[]{:S(2)}) copy-start(bf16[768,128]{1,0:T(8,128)(2,1)} %keys_ref.1) | copy-start | bytes 589828
  3.0 11.4 %copy-start.3 = (bf16[768,128]{1,0:T(8,128)(2,1)S(1)}, bf16[768,128]{1,0:T(8,128)(2,1)}, u32[]{:S(2)}) copy-start(bf16[768,128]{1,0:T(8,128)(2,1)} %values_ref.1) | copy-start | bytes 589828
  3.0 11.4 %copy-start.4 = (bf16[4,128,128]{2,1,0:T(8,128)(2,1)S(1)}, bf16[4,128,128]{2,1,0:T(8,128)(2,1)}, u32[]{:S(2)}) copy-start(bf16[4,128,128]{2,1,0:T(8,128)(2,1)} %get-tuple-element.28.hidden_ref) | copy-start | bytes 393220
  3.0 16.9 %all-to-all-start = ((bf16[4,48,16,128]{3,2,1,0:T(8,128)(2,1)}), bf16[4,48,16,128]{3,2,1,0:T(8,128)(2,1)S(1)}, u32[]{:S(2)}, u32[]{:S(2)}) async-start(bf16[4,48,16,128]{3,2,1,0:T(8,128)(2,1)} %get-tuple-element.27), calls=%async_computation | async-start | bytes 1572864 | tf_op jit(solution)/shard_map/all_to_all | solution.py:405
  14.9 0.8 copy-start.5
  15.7 0.8 copy-start.6
  16.6 0.8 copy-start.7
  20.7 29.2 %all-to-all-start.1 = ((bf16[16,48,128]{2,1,0:T(8,128)(2,1)}), bf16[16,48,128]{2,1,0:T(8,128)(2,1)S(1)}, u32[]{:S(2)}, u32[]{:S(2)}) async-start(bf16[16,48,128]{2,1,0:T(8,128)(2,1)} %shard_map.123), calls=%async_computation.1 | async-start | bytes 393216 | tf_op jit(solution)/shard_map/all_to_all | solution.py:451
  34.7 27.2 %collective-permute-start.2 = (bf16[12,128,128]{2,1,0:T(8,128)(2,1)S(1)}, bf16[12,128,128]{2,1,0:T(8,128)(2,1)S(1)}, u32[]{:S(2)}, u32[]{:S(2)}) collective-permute-start(bf16[12,128,128]{2,1,0:T(8,128)(2,1)S(1)} %get-tuple-element.34.refs_0_), channel_id=1, source_target_pairs={{0,3},{1,2},{2,1},{3,0},{4,7},{5,6},{6,5},{7,4},{8,11},{9,10},{10,... | collective-permute-start | bytes 1179656 | tf_op jit(solution)/shard_map/ppermute | solution.py:387
  38.7 23.3 %collective-permute-start.1 = (bf16[12,128,128]{2,1,0:T(8,128)(2,1)S(1)}, bf16[12,128,128]{2,1,0:T(8,128)(2,1)S(1)}, u32[]{:S(2)}, u32[]{:S(2)}) collective-permute-start(bf16[12,128,128]{2,1,0:T(8,128)(2,1)S(1)} %get-tuple-element.34.refs_0_), channel_id=1, source_target_pairs={{0,2},{1,3},{2,0},{3,1},{4,6},{5,7},{6,4},{7,5},{8,10},{9,11},{10,... | collective-permute-start | bytes 1179656 | tf_op jit(solution)/shard_map/ppermute | solution.py:387
  40.7 21.4 %collective-permute-start = (bf16[12,128,128]{2,1,0:T(8,128)(2,1)S(1)}, bf16[12,128,128]{2,1,0:T(8,128)(2,1)S(1)}, u32[]{:S(2)}, u32[]{:S(2)}) collective-permute-start(bf16[12,128,128]{2,1,0:T(8,128)(2,1)S(1)} %get-tuple-element.34.refs_0_), channel_id=1, source_target_pairs={{0,1},{1,0},{2,3},{3,2},{4,5},{5,4},{6,7},{7,6},{8,9},{9,8},{10,11... | collective-permute-start | bytes 1179656 | tf_op jit(solution)/shard_map/ppermute | solution.py:387
  50.7 19.8 %all-to-all-start.2 = ((bf16[16,24,128]{2,1,0:T(8,128)(2,1)}), bf16[16,24,128]{2,1,0:T(8,128)(2,1)S(1)}, u32[]{:S(2)}, u32[]{:S(2)}) async-start(bf16[16,24,128]{2,1,0:T(8,128)(2,1)} %get-tuple-element.31), calls=%async_computation.2 | async-start | bytes 196608 | tf_op jit(solution)/shard_map/all_to_all | solution.py:454
  57.4 19.8 %collective-permute-start.3 = (bf16[19,128,128]{2,1,0:T(8,128)(2,1)}, bf16[19,128,128]{2,1,0:T(8,128)(2,1)S(1)}, u32[]{:S(2)}, u32[]{:S(2)}) collective-permute-start(bf16[19,128,128]{2,1,0:T(8,128)(2,1)} %copy-done.7), channel_id=1, source_target_pairs={{0,2},{1,3},{2,0},{3,1},{4,6},{5,7},{6,4},{7,5},{8,10},{9,11},{10,... | collective-permute-start | bytes 1867784 | tf_op jit(solution)/shard_map/ppermute | solution.py:387
  73.7 16.7 %all-to-all-start.3 = ((bf16[16,32,128]{2,1,0:T(8,128)(2,1)}), bf16[16,32,128]{2,1,0:T(8,128)(2,1)S(1)}, u32[]{:S(2)}, u32[]{:S(2)}) async-start(bf16[16,32,128]{2,1,0:T(8,128)(2,1)} %shard_map.126), calls=%async_computation.3 | async-start | bytes 262144 | tf_op jit(solution)/shard_map/all_to_all | solution.py:467
  77.2 31.5 %collective-permute-start.4 = (bf16[19,128,128]{2,1,0:T(8,128)(2,1)}, bf16[19,128,128]{2,1,0:T(8,128)(2,1)S(1)}, u32[]{:S(2)}, u32[]{:S(2)}) collective-permute-start(bf16[19,128,128]{2,1,0:T(8,128)(2,1)} %copy-done.6), channel_id=1, source_target_pairs={{0,1},{1,0},{2,3},{3,2},{4,5},{5,4},{6,7},{7,6},{8,9},{9,8},{10,11... | collective-permute-start | bytes 1867784 | tf_op jit(solution)/shard_map/ppermute | solution.py:387
  80.0 28.8 %collective-permute-start.5 = (bf16[19,128,128]{2,1,0:T(8,128)(2,1)}, bf16[19,128,128]{2,1,0:T(8,128)(2,1)S(1)}, u32[]{:S(2)}, u32[]{:S(2)}) collective-permute-start(bf16[19,128,128]{2,1,0:T(8,128)(2,1)} %copy-done.5), channel_id=1, source_target_pairs={{0,3},{1,2},{2,1},{3,0},{4,7},{5,6},{6,5},{7,4},{8,11},{9,10},{10,... | collective-permute-start | bytes 1867784 | tf_op jit(solution)/shard_map/ppermute | solution.py:387
  122.8 17.5 %all-to-all-start.6 = ((bf16[16,32,128]{2,1,0:T(8,128)(2,1)}), bf16[16,32,128]{2,1,0:T(8,128)(2,1)S(1)}, u32[]{:S(2)}, u32[]{:S(2)}) async-start(bf16[16,32,128]{2,1,0:T(8,128)(2,1)} %get-tuple-element.46), calls=%async_computation.6 | async-start | bytes 262144 | tf_op jit(solution)/shard_map/all_to_all | solution.py:481
  126.3 14.7 %collective-permute-start.6 = (bf16[48,128]{1,0:T(8,128)(2,1)S(1)}, bf16[48,128]{1,0:T(8,128)(2,1)S(1)}, u32[]{:S(2)}, u32[]{:S(2)}) collective-permute-start(bf16[48,128]{1,0:T(8,128)(2,1)S(1)} %get-tuple-element.43), channel_id=1, source_target_pairs={{0,1},{1,0},{2,3},{3,2},{4,5},{5,4},{6,7},{7,6},{8,9},{9,8},{10,11... | collective-permute-start | bytes 36872 | tf_op jit(solution)/shard_map/ppermute | solution.py:387
  129.1 12.0 %collective-permute-start.7 = (bf16[48,128]{1,0:T(8,128)(2,1)S(1)}, bf16[48,128]{1,0:T(8,128)(2,1)S(1)}, u32[]{:S(2)}, u32[]{:S(2)}) collective-permute-start(bf16[48,128]{1,0:T(8,128)(2,1)S(1)} %get-tuple-element.44), channel_id=1, source_target_pairs={{0,2},{1,3},{2,0},{3,1},{4,6},{5,7},{6,4},{7,5},{8,10},{9,11},{10,... | collective-permute-start | bytes 36872 | tf_op jit(solution)/shard_map/ppermute | solution.py:387
  133.2 7.9 %collective-permute-start.8 = (bf16[48,128]{1,0:T(8,128)(2,1)S(1)}, bf16[48,128]{1,0:T(8,128)(2,1)S(1)}, u32[]{:S(2)}, u32[]{:S(2)}) collective-permute-start(bf16[48,128]{1,0:T(8,128)(2,1)S(1)} %get-tuple-element.45), channel_id=1, source_target_pairs={{0,3},{1,2},{2,1},{3,0},{4,7},{5,6},{6,5},{7,4},{8,11},{9,10},{10,... | collective-permute-start | bytes 36872 | tf_op jit(solution)/shard_map/ppermute | solution.py:387

commit v11 on v10

--- a/solution.py
+++ b/solution.py
@@ -175,52 +175,60 @@
     new_keys, new_values = new_ref[0], new_ref[1]
     fresh = new_keys.shape[0]
     every = queries_ref[...]
-    for i in range(RI):
-        queries = every[i * HD : (i + 1) * HD, :]
-        row_pos = jnp.concatenate([rowpos_ref[i]] * GQ, axis=0)
-        peak = jnp.full((HD, BLK), least_peak, f32)
-        for x in range(NX):
-            keys = jnp.concatenate([cache_refs[x][b] for b in range(blocks)], axis=1)
-            score = jnp.dot(queries, keys, preferred_element_type=f32)
+    row_pos = [jnp.concatenate([rowpos_ref[i]] * GQ, axis=0) for i in range(RI)]
+    peaks = [jnp.full((HD, BLK), least_peak, f32)] * RI
+    for x in range(NX):
+        keys = jnp.concatenate([cache_refs[x][b] for b in range(blocks)], axis=1)
+        score = jnp.dot(every, keys, preferred_element_type=f32)
+        for i in range(RI):
+            at = i * HD
             for b in range(blocks):
                 n = x * blocks + b
                 cut = jnp.where(
-                    keypos_ref[n : n + 1, :] <= row_pos,
-                    score[:, b * BLK : (b + 1) * BLK],
+                    keypos_ref[n : n + 1, :] <= row_pos[i],
+                    score[at : at + HD, b * BLK : (b + 1) * BLK],
                     masked_score,
                 )
-                score_ref[:, n * BLK : (n + 1) * BLK] = cut
-                peak = jnp.maximum(peak, cut)
-        n = NX * blocks
-        score = lax.dot_general(queries, new_keys, contract_last, preferred_element_type=f32)
-        last = jnp.where(keypos_ref[n : n + 1, :fresh] <= row_pos[:, :fresh], score, masked_score)
-        top = jnp.maximum(
-            jnp.max(peak, axis=1, keepdims=True), jnp.max(last, axis=1, keepdims=True)
-        )
-        top = top * scale
+                score_ref[at : at + HD, n * BLK : (n + 1) * BLK] = cut
+                peaks[i] = jnp.maximum(peaks[i], cut)
+    n = NX * blocks
+    score = lax.dot_general(every, new_keys, contract_last, preferred_element_type=f32)
+    tops, totals, weights = [], [], []
+    for i in range(RI):
+        allowed = keypos_ref[n : n + 1, :fresh] <= row_pos[i][:, :fresh]
+        last = jnp.where(allowed, score[i * HD : (i + 1) * HD, :], masked_score)
+        top = scale * jnp.maximum(
+            jnp.max(peaks[i], axis=1, keepdims=True), jnp.max(last, axis=1, keepdims=True)
+        )
         weight = jnp.exp2(last * scale - top)
-        total_last = jnp.sum(weight, axis=1, keepdims=True)
-        numer = jnp.dot(weight.astype(bf16), new_values, preferred_element_type=f32)
-        total = jnp.zeros((HD, BLK), f32)
-        for x in range(NX):
+        tops.append(top)
+        totals.append(jnp.sum(weight, axis=1, keepdims=True))
+        weights.append(weight.astype(bf16))
+    numer = jnp.dot(jnp.concatenate(weights, axis=0), new_values, preferred_element_type=f32)
+    sums = [jnp.zeros((HD, BLK), f32)] * RI
+    for x in range(NX):
+        bands = []
+        for i in range(RI):
             weights = []
             for b in range(blocks):
                 n = x * blocks + b
-                weight = jnp.exp2(score_ref[:, n * BLK : (n + 1) * BLK] * scale - top)
-                total = total + weight
+                cut = score_ref[i * HD : (i + 1) * HD, n * BLK : (n + 1) * BLK]
+                weight = jnp.exp2(cut * scale - tops[i])
+                sums[i] = sums[i] + weight
                 weights.append(weight.astype(bf16))
-            values = jnp.concatenate([cache_refs[x][blocks + b] for b in range(blocks)], axis=0)
-            numer = numer + jnp.dot(
-                jnp.concatenate(weights, axis=1), values, preferred_element_type=f32
-            )
-        total = jnp.sum(total, axis=1, keepdims=True) + total_last
+            bands.append(jnp.concatenate(weights, axis=1))
+        values = jnp.concatenate([cache_refs[x][blocks + b] for b in range(blocks)], axis=0)
+        numer = numer + jnp.dot(
+            jnp.concatenate(bands, axis=0), values, preferred_element_type=f32
+        )
+    shares, levels = [], []
+    for i in range(RI):
+        total = jnp.sum(sums[i], axis=1, keepdims=True) + totals[i]
         some = total > 0.0
-        share = numer * jnp.where(some, 1.0 / jnp.where(some, total, 1.0), 0.0)
-        level = top + jnp.where(some, jnp.log2(jnp.where(some, total, 1.0)), 0.0)
-        share_at = (NX * blocks + i) * BLK
-        score_ref[:, share_at : share_at + BLK] = share
-        level_at = (NX * blocks + RI + i) * BLK
-        score_ref[:, level_at : level_at + BLK] = jnp.broadcast_to(level, (HD, BLK))
+        factor = jnp.where(some, 1.0 / jnp.where(some, total, 1.0), 0.0)
+        shares.append(numer[i * HD : (i + 1) * HD, :] * factor)
+        level = tops[i] + jnp.where(some, jnp.log2(jnp.where(some, total, 1.0)), 0.0)
+        levels.append(jnp.broadcast_to(level, (HD, BLK)))
     lane = lax.broadcasted_iota(jnp.int32, (8, HD), 1)
     for z in range(NZ):
         parts = []
@@ -228,10 +236,8 @@
         for k in range(RI):
             row = 24 * z + 8 * k
             i, r = row // HD, row % HD
-            share_at = (NX * blocks + i) * BLK
-            level_at = (NX * blocks + RI + i) * BLK
-            parts.append(score_ref[r : r + 8, share_at : share_at + BLK])
-            for p, piece in enumerate(three_pieces(score_ref[r : r + 8, level_at : level_at + BLK])):
+            parts.append(shares[i][r : r + 8, :])
+            for p, piece in enumerate(three_pieces(levels[i][r : r + 8, :])):
                 tail = jnp.where(lane == 3 * k + p, piece, tail)
         out_ref[z] = jnp.concatenate(parts + [tail], axis=0).astype(bf16)
 
@@ -275,14 +281,12 @@
 
 
 def next_kernel(terms_ref, *refs):
-    wide = range(GQ, 2 * GQ + 2)
-    weights = [jnp.concatenate([ref[j] for j in wide], axis=1) for ref in refs[:NX]]
+    gained = []
     resid_refs, (out_ref, cut_ref) = refs[NX : 2 * NX], refs[2 * NX :]
     attended = terms_ref[0].astype(f32)
     for h in range(1, NH):
         attended = attended + terms_ref[h].astype(f32)
     squares = jnp.zeros((XR, 1), f32)
-    product = jnp.zeros((XR, (GQ + 2) * HD), f32)
     for x in range(NX):
         rest = refs[x][WB - 1].astype(f32)
         before = rest[:XR]
@@ -290,13 +294,19 @@
         resid = before + attended[:, x * HD : (x + 1) * HD]
         resid_refs[x][...] = resid.astype(bf16)
         squares = squares + jnp.sum(resid * resid, axis=1, keepdims=True)
-        gained = (resid * gain).astype(bf16)
-        product = product + jnp.dot(gained, weights[x], preferred_element_type=f32)
-    for i in range(RI):
-        for j in range(GQ + 2):
-            cut_ref[:, i * (GQ + 2) + j, :] = product[
-                i * TILE : (i + 1) * TILE, j * HD : (j + 1) * HD
-            ]
+        gained.append((resid * gain).astype(bf16))
+    gained = jnp.concatenate(gained, axis=1)
+    for first in range(0, GQ + 2, 2):
+        pair = range(GQ + first, GQ + first + 2)
+        columns = [jnp.concatenate([ref[j] for j in pair], axis=1) for ref in refs[:NX]]
+        product = jnp.dot(
+            gained, jnp.concatenate(columns, axis=0), preferred_element_type=f32
+        )
+        for i in range(RI):
+            for j in range(2):
+                cut_ref[:, i * (GQ + 2) + first + j, :] = product[
+                    i * TILE : (i + 1) * TILE, j * HD : (j + 1) * HD
+                ]
     lane = lax.broadcasted_iota(jnp.int32, (TILE, HD), 1)
     tail = jnp.zeros((TILE, HD), f32)
     for i in range(RI):
@@ -458,7 +468,8 @@
         attend_kernel,
         shaped((NZ, 32, HD), bf16),
         (queries, key_pos, wide_row_pos, new, *caches),
-        scratch=[pltpu.VMEM((HD, (NX * blocks + 2 * RI) * BLK), f32)],
+        scratch=[pltpu.VMEM((XR * GQ, NX * blocks * BLK), f32)],
+        limit=20,
     )
     for step in (1, 3):
         weights_x[step] = swapped(after(bundles[step], parts, weights_x[2]), step)

time: 144 us -> 145 us (level)
  no operation moved by 1% of the time
where the time goes in v11:
time: 145 us; the launch traced here: 142 us
  starting transfers between devices  67.2 us (46%)
  blocking collectives  30.7 us (21%)
  waiting for transfers between devices  26.6 us (18%)
  Pallas kernels  11.1 us (8%)
  local copies, waits for them, and re-layouts  3.55 us (2%)
  other arithmetic  2.01 us (1%)
    ppermute x9, starting transfers between devices, swapped(): return lax.ppermute(array, 'x', [(n, n ^ step) for n in range(NX)])  30.7 us
    all_to_all x1, blocking collectives, on_device(): heads_out = a2a(share, 'z').reshape(XR * GQ, HD)  18.1 us
    all_to_all x1, starting transfers between devices, on_device(): a2a(tiles, 'z')  13.5 us
    all_to_all x1, blocking collectives, on_device(): a2a(terms, ('core', 'y'))  12.6 us
    pallas_call x10, Pallas kernels, vmem_call(): pl.pallas_call(kernel, out_shape=out_shape, in_specs=[small] * scalars +...  11.1 us
    all_to_all x1, starting transfers between devices, on_device(): payload = a2a(payload, 'x')  9.46 us
    all_to_all x1, waiting for transfers between devices, on_device(): queries = a2a(copies, 'z').reshape(XR * GQ, HD)  8.51 us
    all_to_all x1, waiting for transfers between devices, on_device(): a2a(parts, 'z')  6.69 us
  transfers between devices with their start and end apart: 14, of which 5 were waited for; matrix products, arithmetic and copies ran while one was open for 2% of the time, Pallas kernels for 4%

profile of v11, /device:TPU:6, one launch (start us, length us, event | category | flops | bytes accessed | tf_op | source)
XLA Modules:
  0.0 142.3 jit_solution(4775435473605780888)
XLA Ops:
  0.6 2.2 %shard_map.122 = (bf16[4,48,16,128]{3,2,1,0:T(8,128)(2,1)}, bf16[4,128,128]{2,1,0:T(8,128)(2,1)}) custom-call(bf16[192,128]{1,0:T(8,128)(2,1)} %hidden_hbm.1, bf16[128,1280]{1,0:T(8,128)(2,1)} %weight_hbm.1, f32[1,128]{1,0:T(1,128)} %bitcast.13), custom_call_target="tpu_custom_call" | custom-call | tf_op jit(solution)/shard_map/pallas_call | solution.py:43
  2.9 0.0 copy-start.11
  2.9 0.0 copy-start.9
  2.9 0.0 copy-start.10
  2.9 0.0 copy-start.8
  2.9 0.0 copy-start
  2.9 0.0 copy-start.1
  3.0 0.0 copy-start.2
  3.0 0.0 copy-start.3
  3.0 9.5 %all-to-all-start = ((bf16[4,48,16,128]{3,2,1,0:T(8,128)(2,1)}), bf16[4,48,16,128]{3,2,1,0:T(8,128)(2,1)S(1)}, u32[]{:S(2)}, u32[]{:S(2)}) async-start(bf16[4,48,16,128]{3,2,1,0:T(8,128)(2,1)} %get-tuple-element.27), calls=%async_computation | async-start | bytes 1572864 | tf_op jit(solution)/shard_map/all_to_all | solution.py:415
  12.5 0.1 fusion.3
  12.6 0.1 compare_select_fusion
  12.7 0.1 select_reduce_fusion
  12.8 0.4 select_reduce_fusion.1
  13.2 0.1 slice_reduce_fusion
  13.4 0.2 reshape.203
  13.6 0.1 copy.19
  13.7 0.1 concatenate.25
  13.7 0.1 broadcast_in_dim.41
  13.8 0.2 select_reduce_fusion.3
  14.0 0.1 add_convert_fusion
  14.1 0.2 fusion.2
  14.3 0.1 pad_maximum_fusion.2
  14.4 0.5 shard_map.124
  14.9 0.8 copy-done.5
  15.7 0.8 copy-done.6
  16.6 0.8 copy-done.7
  17.4 2.5 %all-to-all-done.in_ref = bf16[4,48,16,128]{3,2,1,0:T(8,128)(2,1)S(1)} async-done(((bf16[4,48,16,128]{3,2,1,0:T(8,128)(2,1)}), bf16[4,48,16,128]{3,2,1,0:T(8,128)(2,1)S(1)}, u32[]{:S(2)}, u32[]{:S(2)}) %all-to-all-start) | async-done | bytes 786464 | tf_op jit(solution)/shard_map/all_to_all | solution.py:415
  19.9 0.9 shard_map.123
  20.7 13.5 %all-to-all-start.1 = ((bf16[16,48,128]{2,1,0:T(8,128)(2,1)}), bf16[16,48,128]{2,1,0:T(8,128)(2,1)S(1)}, u32[]{:S(2)}, u32[]{:S(2)}) async-start(bf16[16,48,128]{2,1,0:T(8,128)(2,1)} %shard_map.123), calls=%async_computation.1 | async-start | bytes 393216 | tf_op jit(solution)/shard_map/all_to_all | solution.py:461
  34.2 0.1 copy.21
  34.3 0.1 add.107
  34.4 0.1 copy.20
  34.5 0.1 gt.11
  34.6 0.1 pad_maximum_fusion
  34.7 0.1 iota_add_fusion
  34.7 4.0 %collective-permute-start.2 = (bf16[12,128,128]{2,1,0:T(8,128)(2,1)S(1)}, bf16[12,128,128]{2,1,0:T(8,128)(2,1)S(1)}, u32[]{:S(2)}, u32[]{:S(2)}) collective-permute-start(bf16[12,128,128]{2,1,0:T(8,128)(2,1)S(1)} %get-tuple-element.34.refs_0_), channel_id=1, source_target_pairs={{0,3},{1,2},{2,1},{3,0},{4,7},{5,6},{6,5},{7,4},{8,11},{9,10},{10,... | collective-permute-start | bytes 1179656 | tf_op jit(solution)/shard_map/ppermute | solution.py:397
  38.7 1.9 %collective-permute-start.1 = (bf16[12,128,128]{2,1,0:T(8,128)(2,1)S(1)}, bf16[12,128,128]{2,1,0:T(8,128)(2,1)S(1)}, u32[]{:S(2)}, u32[]{:S(2)}) collective-permute-start(bf16[12,128,128]{2,1,0:T(8,128)(2,1)S(1)} %get-tuple-element.34.refs_0_), channel_id=1, source_target_pairs={{0,2},{1,3},{2,0},{3,1},{4,6},{5,7},{6,4},{7,5},{8,10},{9,11},{10,... | collective-permute-start | bytes 1179656 | tf_op jit(solution)/shard_map/ppermute | solution.py:397
  40.7 3.9 %collective-permute-start = (bf16[12,128,128]{2,1,0:T(8,128)(2,1)S(1)}, bf16[12,128,128]{2,1,0:T(8,128)(2,1)S(1)}, u32[]{:S(2)}, u32[]{:S(2)}) collective-permute-start(bf16[12,128,128]{2,1,0:T(8,128)(2,1)S(1)} %get-tuple-element.34.refs_0_), channel_id=1, source_target_pairs={{0,1},{1,0},{2,3},{3,2},{4,5},{5,4},{6,7},{7,6},{8,9},{9,8},{10,11... | collective-permute-start | bytes 1179656 | tf_op jit(solution)/shard_map/ppermute | solution.py:397
  44.6 5.4 %all-to-all-done.1.in_ref = bf16[16,48,128]{2,1,0:T(8,128)(2,1)S(1)} async-done(((bf16[16,48,128]{2,1,0:T(8,128)(2,1)}), bf16[16,48,128]{2,1,0:T(8,128)(2,1)S(1)}, u32[]{:S(2)}, u32[]{:S(2)}) %all-to-all-start.1) | async-done | bytes 196640 | tf_op jit(solution)/shard_map/all_to_all | solution.py:461
  50.0 0.7 shard_map.125
  50.7 6.6 %all-to-all-start.2 = ((bf16[16,24,128]{2,1,0:T(8,128)(2,1)}), bf16[16,24,128]{2,1,0:T(8,128)(2,1)S(1)}, u32[]{:S(2)}, u32[]{:S(2)}) async-start(bf16[16,24,128]{2,1,0:T(8,128)(2,1)} %get-tuple-element.31), calls=%async_computation.2 | async-start | bytes 196608 | tf_op jit(solution)/shard_map/all_to_all | solution.py:464
  57.4 4.0 %collective-permute-start.3 = (bf16[19,128,128]{2,1,0:T(8,128)(2,1)}, bf16[19,128,128]{2,1,0:T(8,128)(2,1)S(1)}, u32[]{:S(2)}, u32[]{:S(2)}) collective-permute-start(bf16[19,128,128]{2,1,0:T(8,128)(2,1)} %copy-done.7), channel_id=1, source_target_pairs={{0,2},{1,3},{2,0},{3,1},{4,6},{5,7},{6,4},{7,5},{8,10},{9,11},{10,... | collective-permute-start | bytes 1867784 | tf_op jit(solution)/shard_map/ppermute | solution.py:397
  61.4 0.5 compare_reduce_fusion
  61.9 0.1 add_select_fusion
  62.0 8.5 %all-to-all-done.2 = bf16[16,24,128]{2,1,0:T(8,128)(2,1)S(1)} async-done(((bf16[16,24,128]{2,1,0:T(8,128)(2,1)}), bf16[16,24,128]{2,1,0:T(8,128)(2,1)S(1)}, u32[]{:S(2)}, u32[]{:S(2)}) %all-to-all-start.2) | async-done | bytes 98336 | tf_op jit(solution)/shard_map/all_to_all | solution.py:464
  70.5 0.1 broadcast_in_dim.49.rowpos_ref
  70.6 3.5 %shard_map.126 = bf16[16,32,128]{2,1,0:T(8,128)(2,1)} custom-call(bf16[384,128]{1,0:T(8,128)(2,1)S(1)} %bitcast.9, s32[25,128]{1,0:T(8,128)S(1)} %pad_add_fusion.keypos_ref, s32[3,16,128]{2,1,0:T(8,128)S(1)} %broadcast_in_dim.49.rowpos_ref, bf16[2,16,128]{2,1,0:T(8,128)(2,1)S(1)} %get-tuple-element.33.new_ref, ...), custom_call_target="tpu_custom_call" | custom-call | tf_op jit(solution)/shard_map/pallas_call | solution.py:43
  74.1 3.5 %all-to-all-start.3 = ((bf16[16,32,128]{2,1,0:T(8,128)(2,1)}), bf16[16,32,128]{2,1,0:T(8,128)(2,1)S(1)}, u32[]{:S(2)}, u32[]{:S(2)}) async-start(bf16[16,32,128]{2,1,0:T(8,128)(2,1)} %shard_map.126), calls=%async_computation.3 | async-start | bytes 262144 | tf_op jit(solution)/shard_map/all_to_all | solution.py:478
  77.6 2.8 %collective-permute-start.4 = (bf16[19,128,128]{2,1,0:T(8,128)(2,1)}, bf16[19,128,128]{2,1,0:T(8,128)(2,1)S(1)}, u32[]{:S(2)}, u32[]{:S(2)}) collective-permute-start(bf16[19,128,128]{2,1,0:T(8,128)(2,1)} %copy-done.6), channel_id=1, source_target_pairs={{0,1},{1,0},{2,3},{3,2},{4,5},{5,4},{6,7},{7,6},{8,9},{9,8},{10,11... | collective-permute-start | bytes 1867784 | tf_op jit(solution)/shard_map/ppermute | solution.py:397
  80.4 3.7 %collective-permute-start.5 = (bf16[19,128,128]{2,1,0:T(8,128)(2,1)}, bf16[19,128,128]{2,1,0:T(8,128)(2,1)S(1)}, u32[]{:S(2)}, u32[]{:S(2)}) collective-permute-start(bf16[19,128,128]{2,1,0:T(8,128)(2,1)} %copy-done.5), channel_id=1, source_target_pairs={{0,3},{1,2},{2,1},{3,0},{4,7},{5,6},{6,5},{7,4},{8,11},{9,10},{10,... | collective-permute-start | bytes 1867784 | tf_op jit(solution)/shard_map/ppermute | solution.py:397
  84.1 6.7 %all-to-all-done.3.in_ref = bf16[16,32,128]{2,1,0:T(8,128)(2,1)S(1)} async-done(((bf16[16,32,128]{2,1,0:T(8,128)(2,1)}), bf16[16,32,128]{2,1,0:T(8,128)(2,1)S(1)}, u32[]{:S(2)}, u32[]{:S(2)}) %all-to-all-start.3) | async-done | bytes 131104 | tf_op jit(solution)/shard_map/all_to_all | solution.py:478
  90.7 0.3 shard_map.127
  91.0 18.1 %all_to_all.35 = bf16[16,24,128]{2,1,0:T(8,128)(2,1)S(1)} all-to-all(bf16[16,24,128]{2,1,0:T(8,128)(2,1)S(1)} %shard_map.127), channel_id=1, replica_groups=mesh['y'=4,'core'=2,'z'=16,'x'=4] {'z'}, dimensions={0} | all-to-all | bytes 196608 | tf_op jit(solution)/shard_map/all_to_all | solution.py:480
  109.1 0.3 shard_map.128
  109.4 12.6 %all_to_all.36.terms_ref = bf16[8,48,512]{2,1,0:T(8,128)(2,1)S(1)} all-to-all(bf16[8,48,512]{2,1,0:T(8,128)(2,1)S(1)} %shard_map.128), channel_id=1, replica_groups=mesh['y'=4,'core'=2,'z'=16,'x'=4] {'core','y'}, dimensions={0} | all-to-all | bytes 786432 | tf_op jit(solution)/shard_map/all_to_all | solution.py:487
  122.1 1.1 shard_map.129
  123.2 3.5 %all-to-all-start.6 = ((bf16[16,32,128]{2,1,0:T(8,128)(2,1)}), bf16[16,32,128]{2,1,0:T(8,128)(2,1)S(1)}, u32[]{:S(2)}, u32[]{:S(2)}) async-start(bf16[16,32,128]{2,1,0:T(8,128)(2,1)} %get-tuple-element.46), calls=%async_computation.6 | async-start | bytes 262144 | tf_op jit(solution)/shard_map/all_to_all | solution.py:492
  126.7 2.8 %collective-permute-start.6 = (bf16[48,128]{1,0:T(8,128)(2,1)S(1)}, bf16[48,128]{1,0:T(8,128)(2,1)S(1)}, u32[]{:S(2)}, u32[]{:S(2)}) collective-permute-start(bf16[48,128]{1,0:T(8,128)(2,1)S(1)} %get-tuple-element.43), channel_id=1, source_target_pairs={{0,1},{1,0},{2,3},{3,2},{4,5},{5,4},{6,7},{7,6},{8,9},{9,8},{10,11... | collective-permute-start | bytes 36872 | tf_op jit(solution)/shard_map/ppermute | solution.py:397
  129.5 4.1 %collective-permute-start.7 = (bf16[48,128]{1,0:T(8,128)(2,1)S(1)}, bf16[48,128]{1,0:T(8,128)(2,1)S(1)}, u32[]{:S(2)}, u32[]{:S(2)}) collective-permute-start(bf16[48,128]{1,0:T(8,128)(2,1)S(1)} %get-tuple-element.44), channel_id=1, source_target_pairs={{0,2},{1,3},{2,0},{3,1},{4,6},{5,7},{6,4},{7,5},{8,10},{9,11},{10,... | collective-permute-start | bytes 36872 | tf_op jit(solution)/shard_map/ppermute | solution.py:397
  133.5 3.6 %collective-permute-start.8 = (bf16[48,128]{1,0:T(8,128)(2,1)S(1)}, bf16[48,128]{1,0:T(8,128)(2,1)S(1)}, u32[]{:S(2)}, u32[]{:S(2)}) collective-permute-start(bf16[48,128]{1,0:T(8,128)(2,1)S(1)} %get-tuple-element.45), channel_id=1, source_target_pairs={{0,3},{1,2},{2,1},{3,0},{4,7},{5,6},{6,5},{7,4},{8,11},{9,10},{10,... | collective-permute-start | bytes 36872 | tf_op jit(solution)/shard_map/ppermute | solution.py:397
  137.1 3.5 %all-to-all-done.6.in_ref = bf16[16,32,128]{2,1,0:T(8,128)(2,1)S(1)} async-done(((bf16[16,32,128]{2,1,0:T(8,128)(2,1)}), bf16[16,32,128]{2,1,0:T(8,128)(2,1)S(1)}, u32[]{:S(2)}, u32[]{:S(2)}) %all-to-all-start.6) | async-done | bytes 131104 | tf_op jit(solution)/shard_map/all_to_all | solution.py:492
  140.7 0.8 shard_map.130
  141.4 0.8 shard_map.131
  (36 shorter events, 0.2 us)
Async XLA Ops:
  2.9 9.6 %copy-start.11 = (s32[128]{0:T(128)S(1)}, s32[128]{0:T(128)}, u32[]{:S(2)}) copy-start(s32[128]{0:T(128)} %param.18) | copy-start | bytes 1540
  2.9 9.6 %copy-start.9 = (s32[128]{0:T(128)S(1)}, s32[128]{0:T(128)}, u32[]{:S(2)}) copy-start(s32[128]{0:T(128)} %param.19) | copy-start | bytes 1540
  2.9 9.9 %copy-start.10 = (s32[128]{0:T(128)S(1)}, s32[128]{0:T(128)}, u32[]{:S(2)}) copy-start(s32[128]{0:T(128)} %param.20) | copy-start | bytes 1540
  2.9 10.4 %copy-start.8 = (s32[192]{0:T(256)S(1)}, s32[192]{0:T(256)}, u32[]{:S(2)}) copy-start(s32[192]{0:T(256)} %param.21) | copy-start | bytes 2308
  2.9 11.4 %copy-start = (bf16[128,1280]{1,0:T(8,128)(2,1)S(1)}, bf16[128,1280]{1,0:T(8,128)(2,1)}, u32[]{:S(2)}) copy-start(bf16[128,1280]{1,0:T(8,128)(2,1)} %next_weight_ref.1) | copy-start | bytes 983044
  2.9 11.4 %copy-start.1 = (bf16[1024,128]{1,0:T(8,128)(2,1)S(1)}, bf16[1024,128]{1,0:T(8,128)(2,1)}, u32[]{:S(2)}) copy-start(bf16[1024,128]{1,0:T(8,128)(2,1)} %out_weight_ref.1) | copy-start | bytes 786436
  3.0 11.4 %copy-start.2 = (bf16[768,128]{1,0:T(8,128)(2,1)S(1)}, bf16[768,128]{1,0:T(8,128)(2,1)}, u32[]{:S(2)}) copy-start(bf16[768,128]{1,0:T(8,128)(2,1)} %keys_ref.1) | copy-start | bytes 589828
  3.0 11.4 %copy-start.3 = (bf16[768,128]{1,0:T(8,128)(2,1)S(1)}, bf16[768,128]{1,0:T(8,128)(2,1)}, u32[]{:S(2)}) copy-start(bf16[768,128]{1,0:T(8,128)(2,1)} %values_ref.1) | copy-start | bytes 589828
  3.0 11.4 %copy-start.4 = (bf16[4,128,128]{2,1,0:T(8,128)(2,1)S(1)}, bf16[4,128,128]{2,1,0:T(8,128)(2,1)}, u32[]{:S(2)}) copy-start(bf16[4,128,128]{2,1,0:T(8,128)(2,1)} %get-tuple-element.28.hidden_ref) | copy-start | bytes 393220
  3.0 16.9 %all-to-all-start = ((bf16[4,48,16,128]{3,2,1,0:T(8,128)(2,1)}), bf16[4,48,16,128]{3,2,1,0:T(8,128)(2,1)S(1)}, u32[]{:S(2)}, u32[]{:S(2)}) async-start(bf16[4,48,16,128]{3,2,1,0:T(8,128)(2,1)} %get-tuple-element.27), calls=%async_computation | async-start | bytes 1572864 | tf_op jit(solution)/shard_map/all_to_all | solution.py:415
  14.9 0.8 copy-start.5
  15.7 0.8 copy-start.6
  16.6 0.8 copy-start.7
  20.7 29.2 %all-to-all-start.1 = ((bf16[16,48,128]{2,1,0:T(8,128)(2,1)}), bf16[16,48,128]{2,1,0:T(8,128)(2,1)S(1)}, u32[]{:S(2)}, u32[]{:S(2)}) async-start(bf16[16,48,128]{2,1,0:T(8,128)(2,1)} %shard_map.123), calls=%async_computation.1 | async-start | bytes 393216 | tf_op jit(solution)/shard_map/all_to_all | solution.py:461
  34.7 27.2 %collective-permute-start.2 = (bf16[12,128,128]{2,1,0:T(8,128)(2,1)S(1)}, bf16[12,128,128]{2,1,0:T(8,128)(2,1)S(1)}, u32[]{:S(2)}, u32[]{:S(2)}) collective-permute-start(bf16[12,128,128]{2,1,0:T(8,128)(2,1)S(1)} %get-tuple-element.34.refs_0_), channel_id=1, source_target_pairs={{0,3},{1,2},{2,1},{3,0},{4,7},{5,6},{6,5},{7,4},{8,11},{9,10},{10,... | collective-permute-start | bytes 1179656 | tf_op jit(solution)/shard_map/ppermute | solution.py:397
  38.7 23.3 %collective-permute-start.1 = (bf16[12,128,128]{2,1,0:T(8,128)(2,1)S(1)}, bf16[12,128,128]{2,1,0:T(8,128)(2,1)S(1)}, u32[]{:S(2)}, u32[]{:S(2)}) collective-permute-start(bf16[12,128,128]{2,1,0:T(8,128)(2,1)S(1)} %get-tuple-element.34.refs_0_), channel_id=1, source_target_pairs={{0,2},{1,3},{2,0},{3,1},{4,6},{5,7},{6,4},{7,5},{8,10},{9,11},{10,... | collective-permute-start | bytes 1179656 | tf_op jit(solution)/shard_map/ppermute | solution.py:397
  40.7 21.4 %collective-permute-start = (bf16[12,128,128]{2,1,0:T(8,128)(2,1)S(1)}, bf16[12,128,128]{2,1,0:T(8,128)(2,1)S(1)}, u32[]{:S(2)}, u32[]{:S(2)}) collective-permute-start(bf16[12,128,128]{2,1,0:T(8,128)(2,1)S(1)} %get-tuple-element.34.refs_0_), channel_id=1, source_target_pairs={{0,1},{1,0},{2,3},{3,2},{4,5},{5,4},{6,7},{7,6},{8,9},{9,8},{10,11... | collective-permute-start | bytes 1179656 | tf_op jit(solution)/shard_map/ppermute | solution.py:397
  50.7 19.8 %all-to-all-start.2 = ((bf16[16,24,128]{2,1,0:T(8,128)(2,1)}), bf16[16,24,128]{2,1,0:T(8,128)(2,1)S(1)}, u32[]{:S(2)}, u32[]{:S(2)}) async-start(bf16[16,24,128]{2,1,0:T(8,128)(2,1)} %get-tuple-element.31), calls=%async_computation.2 | async-start | bytes 196608 | tf_op jit(solution)/shard_map/all_to_all | solution.py:464
  57.4 20.2 %collective-permute-start.3 = (bf16[19,128,128]{2,1,0:T(8,128)(2,1)}, bf16[19,128,128]{2,1,0:T(8,128)(2,1)S(1)}, u32[]{:S(2)}, u32[]{:S(2)}) collective-permute-start(bf16[19,128,128]{2,1,0:T(8,128)(2,1)} %copy-done.7), channel_id=1, source_target_pairs={{0,2},{1,3},{2,0},{3,1},{4,6},{5,7},{6,4},{7,5},{8,10},{9,11},{10,... | collective-permute-start | bytes 1867784 | tf_op jit(solution)/shard_map/ppermute | solution.py:397
  74.1 16.7 %all-to-all-start.3 = ((bf16[16,32,128]{2,1,0:T(8,128)(2,1)}), bf16[16,32,128]{2,1,0:T(8,128)(2,1)S(1)}, u32[]{:S(2)}, u32[]{:S(2)}) async-start(bf16[16,32,128]{2,1,0:T(8,128)(2,1)} %shard_map.126), calls=%async_computation.3 | async-start | bytes 262144 | tf_op jit(solution)/shard_map/all_to_all | solution.py:478
  77.6 31.5 %collective-permute-start.4 = (bf16[19,128,128]{2,1,0:T(8,128)(2,1)}, bf16[19,128,128]{2,1,0:T(8,128)(2,1)S(1)}, u32[]{:S(2)}, u32[]{:S(2)}) collective-permute-start(bf16[19,128,128]{2,1,0:T(8,128)(2,1)} %copy-done.6), channel_id=1, source_target_pairs={{0,1},{1,0},{2,3},{3,2},{4,5},{5,4},{6,7},{7,6},{8,9},{9,8},{10,11... | collective-permute-start | bytes 1867784 | tf_op jit(solution)/shard_map/ppermute | solution.py:397
  80.4 28.8 %collective-permute-start.5 = (bf16[19,128,128]{2,1,0:T(8,128)(2,1)}, bf16[19,128,128]{2,1,0:T(8,128)(2,1)S(1)}, u32[]{:S(2)}, u32[]{:S(2)}) collective-permute-start(bf16[19,128,128]{2,1,0:T(8,128)(2,1)} %copy-done.5), channel_id=1, source_target_pairs={{0,3},{1,2},{2,1},{3,0},{4,7},{5,6},{6,5},{7,4},{8,11},{9,10},{10,... | collective-permute-start | bytes 1867784 | tf_op jit(solution)/shard_map/ppermute | solution.py:397
  123.2 17.5 %all-to-all-start.6 = ((bf16[16,32,128]{2,1,0:T(8,128)(2,1)}), bf16[16,32,128]{2,1,0:T(8,128)(2,1)S(1)}, u32[]{:S(2)}, u32[]{:S(2)}) async-start(bf16[16,32,128]{2,1,0:T(8,128)(2,1)} %get-tuple-element.46), calls=%async_computation.6 | async-start | bytes 262144 | tf_op jit(solution)/shard_map/all_to_all | solution.py:492
  126.7 14.7 %collective-permute-start.6 = (bf16[48,128]{1,0:T(8,128)(2,1)S(1)}, bf16[48,128]{1,0:T(8,128)(2,1)S(1)}, u32[]{:S(2)}, u32[]{:S(2)}) collective-permute-start(bf16[48,128]{1,0:T(8,128)(2,1)S(1)} %get-tuple-element.43), channel_id=1, source_target_pairs={{0,1},{1,0},{2,3},{3,2},{4,5},{5,4},{6,7},{7,6},{8,9},{9,8},{10,11... | collective-permute-start | bytes 36872 | tf_op jit(solution)/shard_map/ppermute | solution.py:397
  129.5 12.0 %collective-permute-start.7 = (bf16[48,128]{1,0:T(8,128)(2,1)S(1)}, bf16[48,128]{1,0:T(8,128)(2,1)S(1)}, u32[]{:S(2)}, u32[]{:S(2)}) collective-permute-start(bf16[48,128]{1,0:T(8,128)(2,1)S(1)} %get-tuple-element.44), channel_id=1, source_target_pairs={{0,2},{1,3},{2,0},{3,1},{4,6},{5,7},{6,4},{7,5},{8,10},{9,11},{10,... | collective-permute-start | bytes 36872 | tf_op jit(solution)/shard_map/ppermute | solution.py:397
  133.5 7.9 %collective-permute-start.8 = (bf16[48,128]{1,0:T(8,128)(2,1)S(1)}, bf16[48,128]{1,0:T(8,128)(2,1)S(1)}, u32[]{:S(2)}, u32[]{:S(2)}) collective-permute-start(bf16[48,128]{1,0:T(8,128)(2,1)S(1)} %get-tuple-element.45), channel_id=1, source_target_pairs={{0,3},{1,2},{2,1},{3,0},{4,7},{5,6},{6,5},{7,4},{8,11},{9,10},{10,... | collective-permute-start | bytes 36872 | tf_op jit(solution)/shard_map/ppermute | solution.py:397

commit v12 on v10

--- a/solution.py
+++ b/solution.py
@@ -180,17 +180,18 @@
         row_pos = jnp.concatenate([rowpos_ref[i]] * GQ, axis=0)
         peak = jnp.full((HD, BLK), least_peak, f32)
         for x in range(NX):
-            keys = jnp.concatenate([cache_refs[x][b] for b in range(blocks)], axis=1)
-            score = jnp.dot(queries, keys, preferred_element_type=f32)
-            for b in range(blocks):
-                n = x * blocks + b
-                cut = jnp.where(
-                    keypos_ref[n : n + 1, :] <= row_pos,
-                    score[:, b * BLK : (b + 1) * BLK],
-                    masked_score,
-                )
-                score_ref[:, n * BLK : (n + 1) * BLK] = cut
-                peak = jnp.maximum(peak, cut)
+            for first in range(0, blocks, 2):
+                keys = jnp.concatenate([cache_refs[x][first], cache_refs[x][first + 1]], axis=1)
+                score = jnp.dot(queries, keys, preferred_element_type=f32)
+                for b in range(2):
+                    n = x * blocks + first + b
+                    cut = jnp.where(
+                        keypos_ref[n : n + 1, :] <= row_pos,
+                        score[:, b * BLK : (b + 1) * BLK],
+                        masked_score,
+                    )
+                    score_ref[:, n * BLK : (n + 1) * BLK] = cut
+                    peak = jnp.maximum(peak, cut)
         n = NX * blocks
         score = lax.dot_general(queries, new_keys, contract_last, preferred_element_type=f32)
         last = jnp.where(keypos_ref[n : n + 1, :fresh] <= row_pos[:, :fresh], score, masked_score)
@@ -203,16 +204,17 @@
         numer = jnp.dot(weight.astype(bf16), new_values, preferred_element_type=f32)
         total = jnp.zeros((HD, BLK), f32)
         for x in range(NX):
-            weights = []
-            for b in range(blocks):
-                n = x * blocks + b
-                weight = jnp.exp2(score_ref[:, n * BLK : (n + 1) * BLK] * scale - top)
-                total = total + weight
-                weights.append(weight.astype(bf16))
-            values = jnp.concatenate([cache_refs[x][blocks + b] for b in range(blocks)], axis=0)
-            numer = numer + jnp.dot(
-                jnp.concatenate(weights, axis=1), values, preferred_element_type=f32
-            )
+            for first in range(blocks, 2 * blocks, 2):
+                weights = []
+                for b in range(2):
+                    n = (x - 1) * blocks + first + b
+                    weight = jnp.exp2(score_ref[:, n * BLK : (n + 1) * BLK] * scale - top)
+                    total = total + weight
+                    weights.append(weight.astype(bf16))
+                values = jnp.concatenate([cache_refs[x][first], cache_refs[x][first + 1]], axis=0)
+                numer = numer + jnp.dot(
+                    jnp.concatenate(weights, axis=1), values, preferred_element_type=f32
+                )
         total = jnp.sum(total, axis=1, keepdims=True) + total_last
         some = total > 0.0
         share = numer * jnp.where(some, 1.0 / jnp.where(some, total, 1.0), 0.0)

time: 144 us -> 144 us (level)
  no operation moved by 1% of the time
where the time goes in v12:
time: 144 us; the launch traced here: 142 us
  starting transfers between devices  67.2 us (47%)
  blocking collectives  30.7 us (21%)
  waiting for transfers between devices  26.6 us (18%)
  Pallas kernels  10.8 us (8%)
  local copies, waits for them, and re-layouts  3.55 us (2%)
  other arithmetic  2.01 us (1%)
    ppermute x9, starting transfers between devices, swapped(): return lax.ppermute(array, 'x', [(n, n ^ step) for n in range(NX)])  30.7 us
    all_to_all x1, blocking collectives, on_device(): heads_out = a2a(share, 'z').reshape(XR * GQ, HD)  18.1 us
    all_to_all x1, starting transfers between devices, on_device(): a2a(tiles, 'z')  13.5 us
    all_to_all x1, blocking collectives, on_device(): a2a(terms, ('core', 'y'))  12.6 us
    pallas_call x10, Pallas kernels, vmem_call(): pl.pallas_call(kernel, out_shape=out_shape, in_specs=[small] * scalars +...  10.8 us
    all_to_all x1, starting transfers between devices, on_device(): payload = a2a(payload, 'x')  9.46 us
    all_to_all x1, waiting for transfers between devices, on_device(): queries = a2a(copies, 'z').reshape(XR * GQ, HD)  8.51 us
    all_to_all x1, waiting for transfers between devices, on_device(): a2a(parts, 'z')  6.68 us
  transfers between devices with their start and end apart: 14, of which 5 were waited for; matrix products, arithmetic and copies ran while one was open for 2% of the time, Pallas kernels for 4%

profile of v12, /device:TPU:6, one launch (start us, length us, event | category | flops | bytes accessed | tf_op | source)
XLA Modules:
  0.0 141.9 jit_solution(2001798424447362756)
XLA Ops:
  0.6 2.2 %shard_map.122 = (bf16[4,48,16,128]{3,2,1,0:T(8,128)(2,1)}, bf16[4,128,128]{2,1,0:T(8,128)(2,1)}) custom-call(bf16[192,128]{1,0:T(8,128)(2,1)} %hidden_hbm.1, bf16[128,1280]{1,0:T(8,128)(2,1)} %weight_hbm.1, f32[1,128]{1,0:T(1,128)} %bitcast.13), custom_call_target="tpu_custom_call" | custom-call | tf_op jit(solution)/shard_map/pallas_call | solution.py:43
  2.9 0.0 copy-start.11
  2.9 0.0 copy-start.9
  2.9 0.0 copy-start.10
  2.9 0.0 copy-start.8
  2.9 0.0 copy-start
  2.9 0.0 copy-start.1
  3.0 0.0 copy-start.2
  3.0 0.0 copy-start.3
  3.0 9.5 %all-to-all-start = ((bf16[4,48,16,128]{3,2,1,0:T(8,128)(2,1)}), bf16[4,48,16,128]{3,2,1,0:T(8,128)(2,1)S(1)}, u32[]{:S(2)}, u32[]{:S(2)}) async-start(bf16[4,48,16,128]{3,2,1,0:T(8,128)(2,1)} %get-tuple-element.27), calls=%async_computation | async-start | bytes 1572864 | tf_op jit(solution)/shard_map/all_to_all | solution.py:407
  12.5 0.1 fusion.3
  12.6 0.1 compare_select_fusion
  12.7 0.1 select_reduce_fusion
  12.8 0.4 select_reduce_fusion.1
  13.2 0.1 slice_reduce_fusion
  13.4 0.2 reshape.203
  13.6 0.1 copy.19
  13.7 0.1 concatenate.25
  13.7 0.1 broadcast_in_dim.41
  13.8 0.2 select_reduce_fusion.3
  14.0 0.1 add_convert_fusion
  14.1 0.2 fusion.2
  14.3 0.1 pad_maximum_fusion.2
  14.4 0.5 shard_map.124
  14.9 0.8 copy-done.5
  15.7 0.8 copy-done.6
  16.6 0.8 copy-done.7
  17.4 2.5 %all-to-all-done.in_ref = bf16[4,48,16,128]{3,2,1,0:T(8,128)(2,1)S(1)} async-done(((bf16[4,48,16,128]{3,2,1,0:T(8,128)(2,1)}), bf16[4,48,16,128]{3,2,1,0:T(8,128)(2,1)S(1)}, u32[]{:S(2)}, u32[]{:S(2)}) %all-to-all-start) | async-done | bytes 786464 | tf_op jit(solution)/shard_map/all_to_all | solution.py:407
  19.9 0.9 shard_map.123
  20.7 13.5 %all-to-all-start.1 = ((bf16[16,48,128]{2,1,0:T(8,128)(2,1)}), bf16[16,48,128]{2,1,0:T(8,128)(2,1)S(1)}, u32[]{:S(2)}, u32[]{:S(2)}) async-start(bf16[16,48,128]{2,1,0:T(8,128)(2,1)} %shard_map.123), calls=%async_computation.1 | async-start | bytes 393216 | tf_op jit(solution)/shard_map/all_to_all | solution.py:453
  34.2 0.1 copy.21
  34.3 0.1 add.107
  34.4 0.1 copy.20
  34.5 0.1 gt.11
  34.6 0.1 pad_maximum_fusion
  34.7 0.1 iota_add_fusion
  34.7 4.0 %collective-permute-start.2 = (bf16[12,128,128]{2,1,0:T(8,128)(2,1)S(1)}, bf16[12,128,128]{2,1,0:T(8,128)(2,1)S(1)}, u32[]{:S(2)}, u32[]{:S(2)}) collective-permute-start(bf16[12,128,128]{2,1,0:T(8,128)(2,1)S(1)} %get-tuple-element.34.refs_0_), channel_id=1, source_target_pairs={{0,3},{1,2},{2,1},{3,0},{4,7},{5,6},{6,5},{7,4},{8,11},{9,10},{10,... | collective-permute-start | bytes 1179656 | tf_op jit(solution)/shard_map/ppermute | solution.py:389
  38.7 1.9 %collective-permute-start.1 = (bf16[12,128,128]{2,1,0:T(8,128)(2,1)S(1)}, bf16[12,128,128]{2,1,0:T(8,128)(2,1)S(1)}, u32[]{:S(2)}, u32[]{:S(2)}) collective-permute-start(bf16[12,128,128]{2,1,0:T(8,128)(2,1)S(1)} %get-tuple-element.34.refs_0_), channel_id=1, source_target_pairs={{0,2},{1,3},{2,0},{3,1},{4,6},{5,7},{6,4},{7,5},{8,10},{9,11},{10,... | collective-permute-start | bytes 1179656 | tf_op jit(solution)/shard_map/ppermute | solution.py:389
  40.7 3.9 %collective-permute-start = (bf16[12,128,128]{2,1,0:T(8,128)(2,1)S(1)}, bf16[12,128,128]{2,1,0:T(8,128)(2,1)S(1)}, u32[]{:S(2)}, u32[]{:S(2)}) collective-permute-start(bf16[12,128,128]{2,1,0:T(8,128)(2,1)S(1)} %get-tuple-element.34.refs_0_), channel_id=1, source_target_pairs={{0,1},{1,0},{2,3},{3,2},{4,5},{5,4},{6,7},{7,6},{8,9},{9,8},{10,11... | collective-permute-start | bytes 1179656 | tf_op jit(solution)/shard_map/ppermute | solution.py:389
  44.6 5.4 %all-to-all-done.1.in_ref = bf16[16,48,128]{2,1,0:T(8,128)(2,1)S(1)} async-done(((bf16[16,48,128]{2,1,0:T(8,128)(2,1)}), bf16[16,48,128]{2,1,0:T(8,128)(2,1)S(1)}, u32[]{:S(2)}, u32[]{:S(2)}) %all-to-all-start.1) | async-done | bytes 196640 | tf_op jit(solution)/shard_map/all_to_all | solution.py:453
  50.0 0.7 shard_map.125
  50.7 6.6 %all-to-all-start.2 = ((bf16[16,24,128]{2,1,0:T(8,128)(2,1)}), bf16[16,24,128]{2,1,0:T(8,128)(2,1)S(1)}, u32[]{:S(2)}, u32[]{:S(2)}) async-start(bf16[16,24,128]{2,1,0:T(8,128)(2,1)} %get-tuple-element.31), calls=%async_computation.2 | async-start | bytes 196608 | tf_op jit(solution)/shard_map/all_to_all | solution.py:456
  57.4 4.0 %collective-permute-start.3 = (bf16[19,128,128]{2,1,0:T(8,128)(2,1)}, bf16[19,128,128]{2,1,0:T(8,128)(2,1)S(1)}, u32[]{:S(2)}, u32[]{:S(2)}) collective-permute-start(bf16[19,128,128]{2,1,0:T(8,128)(2,1)} %copy-done.7), channel_id=1, source_target_pairs={{0,2},{1,3},{2,0},{3,1},{4,6},{5,7},{6,4},{7,5},{8,10},{9,11},{10,... | collective-permute-start | bytes 1867784 | tf_op jit(solution)/shard_map/ppermute | solution.py:389
  61.4 0.5 compare_reduce_fusion
  61.9 0.1 add_select_fusion
  62.0 8.5 %all-to-all-done.2 = bf16[16,24,128]{2,1,0:T(8,128)(2,1)S(1)} async-done(((bf16[16,24,128]{2,1,0:T(8,128)(2,1)}), bf16[16,24,128]{2,1,0:T(8,128)(2,1)S(1)}, u32[]{:S(2)}, u32[]{:S(2)}) %all-to-all-start.2) | async-done | bytes 98336 | tf_op jit(solution)/shard_map/all_to_all | solution.py:456
  70.5 0.1 broadcast_in_dim.49.rowpos_ref
  70.6 3.1 %shard_map.126 = bf16[16,32,128]{2,1,0:T(8,128)(2,1)} custom-call(bf16[384,128]{1,0:T(8,128)(2,1)S(1)} %bitcast.9, s32[25,128]{1,0:T(8,128)S(1)} %pad_add_fusion.keypos_ref, s32[3,16,128]{2,1,0:T(8,128)S(1)} %broadcast_in_dim.49.rowpos_ref, bf16[2,16,128]{2,1,0:T(8,128)(2,1)S(1)} %get-tuple-element.33.new_ref, ...), custom_call_target="tpu_custom_call" | custom-call | tf_op jit(solution)/shard_map/pallas_call | solution.py:43
  73.7 3.5 %all-to-all-start.3 = ((bf16[16,32,128]{2,1,0:T(8,128)(2,1)}), bf16[16,32,128]{2,1,0:T(8,128)(2,1)S(1)}, u32[]{:S(2)}, u32[]{:S(2)}) async-start(bf16[16,32,128]{2,1,0:T(8,128)(2,1)} %shard_map.126), calls=%async_computation.3 | async-start | bytes 262144 | tf_op jit(solution)/shard_map/all_to_all | solution.py:469
  77.2 2.8 %collective-permute-start.4 = (bf16[19,128,128]{2,1,0:T(8,128)(2,1)}, bf16[19,128,128]{2,1,0:T(8,128)(2,1)S(1)}, u32[]{:S(2)}, u32[]{:S(2)}) collective-permute-start(bf16[19,128,128]{2,1,0:T(8,128)(2,1)} %copy-done.6), channel_id=1, source_target_pairs={{0,1},{1,0},{2,3},{3,2},{4,5},{5,4},{6,7},{7,6},{8,9},{9,8},{10,11... | collective-permute-start | bytes 1867784 | tf_op jit(solution)/shard_map/ppermute | solution.py:389
  80.0 3.7 %collective-permute-start.5 = (bf16[19,128,128]{2,1,0:T(8,128)(2,1)}, bf16[19,128,128]{2,1,0:T(8,128)(2,1)S(1)}, u32[]{:S(2)}, u32[]{:S(2)}) collective-permute-start(bf16[19,128,128]{2,1,0:T(8,128)(2,1)} %copy-done.5), channel_id=1, source_target_pairs={{0,3},{1,2},{2,1},{3,0},{4,7},{5,6},{6,5},{7,4},{8,11},{9,10},{10,... | collective-permute-start | bytes 1867784 | tf_op jit(solution)/shard_map/ppermute | solution.py:389
  83.7 6.7 %all-to-all-done.3.in_ref = bf16[16,32,128]{2,1,0:T(8,128)(2,1)S(1)} async-done(((bf16[16,32,128]{2,1,0:T(8,128)(2,1)}), bf16[16,32,128]{2,1,0:T(8,128)(2,1)S(1)}, u32[]{:S(2)}, u32[]{:S(2)}) %all-to-all-start.3) | async-done | bytes 131104 | tf_op jit(solution)/shard_map/all_to_all | solution.py:469
  90.3 0.3 shard_map.127
  90.6 18.1 %all_to_all.35 = bf16[16,24,128]{2,1,0:T(8,128)(2,1)S(1)} all-to-all(bf16[16,24,128]{2,1,0:T(8,128)(2,1)S(1)} %shard_map.127), channel_id=1, replica_groups=mesh['y'=4,'core'=2,'z'=16,'x'=4] {'z'}, dimensions={0} | all-to-all | bytes 196608 | tf_op jit(solution)/shard_map/all_to_all | solution.py:471
  108.7 0.3 shard_map.128
  109.0 12.6 %all_to_all.36.terms_ref = bf16[8,48,512]{2,1,0:T(8,128)(2,1)S(1)} all-to-all(bf16[8,48,512]{2,1,0:T(8,128)(2,1)S(1)} %shard_map.128), channel_id=1, replica_groups=mesh['y'=4,'core'=2,'z'=16,'x'=4] {'core','y'}, dimensions={0} | all-to-all | bytes 786432 | tf_op jit(solution)/shard_map/all_to_all | solution.py:478
  121.7 1.1 shard_map.129
  122.8 3.5 %all-to-all-start.6 = ((bf16[16,32,128]{2,1,0:T(8,128)(2,1)}), bf16[16,32,128]{2,1,0:T(8,128)(2,1)S(1)}, u32[]{:S(2)}, u32[]{:S(2)}) async-start(bf16[16,32,128]{2,1,0:T(8,128)(2,1)} %get-tuple-element.46), calls=%async_computation.6 | async-start | bytes 262144 | tf_op jit(solution)/shard_map/all_to_all | solution.py:483
  126.3 2.8 %collective-permute-start.6 = (bf16[48,128]{1,0:T(8,128)(2,1)S(1)}, bf16[48,128]{1,0:T(8,128)(2,1)S(1)}, u32[]{:S(2)}, u32[]{:S(2)}) collective-permute-start(bf16[48,128]{1,0:T(8,128)(2,1)S(1)} %get-tuple-element.43), channel_id=1, source_target_pairs={{0,1},{1,0},{2,3},{3,2},{4,5},{5,4},{6,7},{7,6},{8,9},{9,8},{10,11... | collective-permute-start | bytes 36872 | tf_op jit(solution)/shard_map/ppermute | solution.py:389
  129.1 4.1 %collective-permute-start.7 = (bf16[48,128]{1,0:T(8,128)(2,1)S(1)}, bf16[48,128]{1,0:T(8,128)(2,1)S(1)}, u32[]{:S(2)}, u32[]{:S(2)}) collective-permute-start(bf16[48,128]{1,0:T(8,128)(2,1)S(1)} %get-tuple-element.44), channel_id=1, source_target_pairs={{0,2},{1,3},{2,0},{3,1},{4,6},{5,7},{6,4},{7,5},{8,10},{9,11},{10,... | collective-permute-start | bytes 36872 | tf_op jit(solution)/shard_map/ppermute | solution.py:389
  133.2 3.6 %collective-permute-start.8 = (bf16[48,128]{1,0:T(8,128)(2,1)S(1)}, bf16[48,128]{1,0:T(8,128)(2,1)S(1)}, u32[]{:S(2)}, u32[]{:S(2)}) collective-permute-start(bf16[48,128]{1,0:T(8,128)(2,1)S(1)} %get-tuple-element.45), channel_id=1, source_target_pairs={{0,3},{1,2},{2,1},{3,0},{4,7},{5,6},{6,5},{7,4},{8,11},{9,10},{10,... | collective-permute-start | bytes 36872 | tf_op jit(solution)/shard_map/ppermute | solution.py:389
  136.8 3.5 %all-to-all-done.6.in_ref = bf16[16,32,128]{2,1,0:T(8,128)(2,1)S(1)} async-done(((bf16[16,32,128]{2,1,0:T(8,128)(2,1)}), bf16[16,32,128]{2,1,0:T(8,128)(2,1)S(1)}, u32[]{:S(2)}, u32[]{:S(2)}) %all-to-all-start.6) | async-done | bytes 131104 | tf_op jit(solution)/shard_map/all_to_all | solution.py:483
  140.3 0.8 shard_map.130
  141.1 0.8 shard_map.131
  (36 shorter events, 0.2 us)
Async XLA Ops:
  2.9 9.6 %copy-start.11 = (s32[128]{0:T(128)S(1)}, s32[128]{0:T(128)}, u32[]{:S(2)}) copy-start(s32[128]{0:T(128)} %param.18) | copy-start | bytes 1540
  2.9 9.6 %copy-start.9 = (s32[128]{0:T(128)S(1)}, s32[128]{0:T(128)}, u32[]{:S(2)}) copy-start(s32[128]{0:T(128)} %param.19) | copy-start | bytes 1540
  2.9 9.9 %copy-start.10 = (s32[128]{0:T(128)S(1)}, s32[128]{0:T(128)}, u32[]{:S(2)}) copy-start(s32[128]{0:T(128)} %param.20) | copy-start | bytes 1540
  2.9 10.4 %copy-start.8 = (s32[192]{0:T(256)S(1)}, s32[192]{0:T(256)}, u32[]{:S(2)}) copy-start(s32[192]{0:T(256)} %param.21) | copy-start | bytes 2308
  2.9 11.4 %copy-start = (bf16[128,1280]{1,0:T(8,128)(2,1)S(1)}, bf16[128,1280]{1,0:T(8,128)(2,1)}, u32[]{:S(2)}) copy-start(bf16[128,1280]{1,0:T(8,128)(2,1)} %next_weight_ref.1) | copy-start | bytes 983044
  2.9 11.4 %copy-start.1 = (bf16[1024,128]{1,0:T(8,128)(2,1)S(1)}, bf16[1024,128]{1,0:T(8,128)(2,1)}, u32[]{:S(2)}) copy-start(bf16[1024,128]{1,0:T(8,128)(2,1)} %out_weight_ref.1) | copy-start | bytes 786436
  3.0 11.4 %copy-start.2 = (bf16[768,128]{1,0:T(8,128)(2,1)S(1)}, bf16[768,128]{1,0:T(8,128)(2,1)}, u32[]{:S(2)}) copy-start(bf16[768,128]{1,0:T(8,128)(2,1)} %keys_ref.1) | copy-start | bytes 589828
  3.0 11.4 %copy-start.3 = (bf16[768,128]{1,0:T(8,128)(2,1)S(1)}, bf16[768,128]{1,0:T(8,128)(2,1)}, u32[]{:S(2)}) copy-start(bf16[768,128]{1,0:T(8,128)(2,1)} %values_ref.1) | copy-start | bytes 589828
  3.0 11.4 %copy-start.4 = (bf16[4,128,128]{2,1,0:T(8,128)(2,1)S(1)}, bf16[4,128,128]{2,1,0:T(8,128)(2,1)}, u32[]{:S(2)}) copy-start(bf16[4,128,128]{2,1,0:T(8,128)(2,1)} %get-tuple-element.28.hidden_ref) | copy-start | bytes 393220
  3.0 16.9 %all-to-all-start = ((bf16[4,48,16,128]{3,2,1,0:T(8,128)(2,1)}), bf16[4,48,16,128]{3,2,1,0:T(8,128)(2,1)S(1)}, u32[]{:S(2)}, u32[]{:S(2)}) async-start(bf16[4,48,16,128]{3,2,1,0:T(8,128)(2,1)} %get-tuple-element.27), calls=%async_computation | async-start | bytes 1572864 | tf_op jit(solution)/shard_map/all_to_all | solution.py:407
  14.9 0.8 copy-start.5
  15.7 0.8 copy-start.6
  16.6 0.8 copy-start.7
  20.7 29.2 %all-to-all-start.1 = ((bf16[16,48,128]{2,1,0:T(8,128)(2,1)}), bf16[16,48,128]{2,1,0:T(8,128)(2,1)S(1)}, u32[]{:S(2)}, u32[]{:S(2)}) async-start(bf16[16,48,128]{2,1,0:T(8,128)(2,1)} %shard_map.123), calls=%async_computation.1 | async-start | bytes 393216 | tf_op jit(solution)/shard_map/all_to_all | solution.py:453
  34.7 27.2 %collective-permute-start.2 = (bf16[12,128,128]{2,1,0:T(8,128)(2,1)S(1)}, bf16[12,128,128]{2,1,0:T(8,128)(2,1)S(1)}, u32[]{:S(2)}, u32[]{:S(2)}) collective-permute-start(bf16[12,128,128]{2,1,0:T(8,128)(2,1)S(1)} %get-tuple-element.34.refs_0_), channel_id=1, source_target_pairs={{0,3},{1,2},{2,1},{3,0},{4,7},{5,6},{6,5},{7,4},{8,11},{9,10},{10,... | collective-permute-start | bytes 1179656 | tf_op jit(solution)/shard_map/ppermute | solution.py:389
  38.7 23.3 %collective-permute-start.1 = (bf16[12,128,128]{2,1,0:T(8,128)(2,1)S(1)}, bf16[12,128,128]{2,1,0:T(8,128)(2,1)S(1)}, u32[]{:S(2)}, u32[]{:S(2)}) collective-permute-start(bf16[12,128,128]{2,1,0:T(8,128)(2,1)S(1)} %get-tuple-element.34.refs_0_), channel_id=1, source_target_pairs={{0,2},{1,3},{2,0},{3,1},{4,6},{5,7},{6,4},{7,5},{8,10},{9,11},{10,... | collective-permute-start | bytes 1179656 | tf_op jit(solution)/shard_map/ppermute | solution.py:389
  40.7 21.4 %collective-permute-start = (bf16[12,128,128]{2,1,0:T(8,128)(2,1)S(1)}, bf16[12,128,128]{2,1,0:T(8,128)(2,1)S(1)}, u32[]{:S(2)}, u32[]{:S(2)}) collective-permute-start(bf16[12,128,128]{2,1,0:T(8,128)(2,1)S(1)} %get-tuple-element.34.refs_0_), channel_id=1, source_target_pairs={{0,1},{1,0},{2,3},{3,2},{4,5},{5,4},{6,7},{7,6},{8,9},{9,8},{10,11... | collective-permute-start | bytes 1179656 | tf_op jit(solution)/shard_map/ppermute | solution.py:389
  50.7 19.8 %all-to-all-start.2 = ((bf16[16,24,128]{2,1,0:T(8,128)(2,1)}), bf16[16,24,128]{2,1,0:T(8,128)(2,1)S(1)}, u32[]{:S(2)}, u32[]{:S(2)}) async-start(bf16[16,24,128]{2,1,0:T(8,128)(2,1)} %get-tuple-element.31), calls=%async_computation.2 | async-start | bytes 196608 | tf_op jit(solution)/shard_map/all_to_all | solution.py:456
  57.4 19.8 %collective-permute-start.3 = (bf16[19,128,128]{2,1,0:T(8,128)(2,1)}, bf16[19,128,128]{2,1,0:T(8,128)(2,1)S(1)}, u32[]{:S(2)}, u32[]{:S(2)}) collective-permute-start(bf16[19,128,128]{2,1,0:T(8,128)(2,1)} %copy-done.7), channel_id=1, source_target_pairs={{0,2},{1,3},{2,0},{3,1},{4,6},{5,7},{6,4},{7,5},{8,10},{9,11},{10,... | collective-permute-start | bytes 1867784 | tf_op jit(solution)/shard_map/ppermute | solution.py:389
  73.7 16.7 %all-to-all-start.3 = ((bf16[16,32,128]{2,1,0:T(8,128)(2,1)}), bf16[16,32,128]{2,1,0:T(8,128)(2,1)S(1)}, u32[]{:S(2)}, u32[]{:S(2)}) async-start(bf16[16,32,128]{2,1,0:T(8,128)(2,1)} %shard_map.126), calls=%async_computation.3 | async-start | bytes 262144 | tf_op jit(solution)/shard_map/all_to_all | solution.py:469
  77.2 31.5 %collective-permute-start.4 = (bf16[19,128,128]{2,1,0:T(8,128)(2,1)}, bf16[19,128,128]{2,1,0:T(8,128)(2,1)S(1)}, u32[]{:S(2)}, u32[]{:S(2)}) collective-permute-start(bf16[19,128,128]{2,1,0:T(8,128)(2,1)} %copy-done.6), channel_id=1, source_target_pairs={{0,1},{1,0},{2,3},{3,2},{4,5},{5,4},{6,7},{7,6},{8,9},{9,8},{10,11... | collective-permute-start | bytes 1867784 | tf_op jit(solution)/shard_map/ppermute | solution.py:389
  80.0 28.8 %collective-permute-start.5 = (bf16[19,128,128]{2,1,0:T(8,128)(2,1)}, bf16[19,128,128]{2,1,0:T(8,128)(2,1)S(1)}, u32[]{:S(2)}, u32[]{:S(2)}) collective-permute-start(bf16[19,128,128]{2,1,0:T(8,128)(2,1)} %copy-done.5), channel_id=1, source_target_pairs={{0,3},{1,2},{2,1},{3,0},{4,7},{5,6},{6,5},{7,4},{8,11},{9,10},{10,... | collective-permute-start | bytes 1867784 | tf_op jit(solution)/shard_map/ppermute | solution.py:389
  122.8 17.5 %all-to-all-start.6 = ((bf16[16,32,128]{2,1,0:T(8,128)(2,1)}), bf16[16,32,128]{2,1,0:T(8,128)(2,1)S(1)}, u32[]{:S(2)}, u32[]{:S(2)}) async-start(bf16[16,32,128]{2,1,0:T(8,128)(2,1)} %get-tuple-element.46), calls=%async_computation.6 | async-start | bytes 262144 | tf_op jit(solution)/shard_map/all_to_all | solution.py:483
  126.3 14.7 %collective-permute-start.6 = (bf16[48,128]{1,0:T(8,128)(2,1)S(1)}, bf16[48,128]{1,0:T(8,128)(2,1)S(1)}, u32[]{:S(2)}, u32[]{:S(2)}) collective-permute-start(bf16[48,128]{1,0:T(8,128)(2,1)S(1)} %get-tuple-element.43), channel_id=1, source_target_pairs={{0,1},{1,0},{2,3},{3,2},{4,5},{5,4},{6,7},{7,6},{8,9},{9,8},{10,11... | collective-permute-start | bytes 36872 | tf_op jit(solution)/shard_map/ppermute | solution.py:389
  129.1 12.0 %collective-permute-start.7 = (bf16[48,128]{1,0:T(8,128)(2,1)S(1)}, bf16[48,128]{1,0:T(8,128)(2,1)S(1)}, u32[]{:S(2)}, u32[]{:S(2)}) collective-permute-start(bf16[48,128]{1,0:T(8,128)(2,1)S(1)} %get-tuple-element.44), channel_id=1, source_target_pairs={{0,2},{1,3},{2,0},{3,1},{4,6},{5,7},{6,4},{7,5},{8,10},{9,11},{10,... | collective-permute-start | bytes 36872 | tf_op jit(solution)/shard_map/ppermute | solution.py:389
  133.2 7.9 %collective-permute-start.8 = (bf16[48,128]{1,0:T(8,128)(2,1)S(1)}, bf16[48,128]{1,0:T(8,128)(2,1)S(1)}, u32[]{:S(2)}, u32[]{:S(2)}) collective-permute-start(bf16[48,128]{1,0:T(8,128)(2,1)S(1)} %get-tuple-element.45), channel_id=1, source_target_pairs={{0,3},{1,2},{2,1},{3,0},{4,7},{5,6},{6,5},{7,4},{8,11},{9,10},{10,... | collective-permute-start | bytes 36872 | tf_op jit(solution)/shard_map/ppermute | solution.py:389
